TPU v7x, 32 devices: a whole 2x2x4 slice. The times are simulated.
32 devices in a mesh: rows: 8 (over y, x, core), grp: 4 (over z).
Axes of the slice: x: 2, y: 2, z: 4, core: 2. Of those that a mesh axis runs over, the one named last changes fastest.
Arguments:
- single: bfloat16 [768, 384], P('grp'), may hold values from -6 to 6
- pair: bfloat16 [768, 768, 128], P('rows', 'grp'), may hold values from -6 to 6
- chains: int32 [768], replicated, may hold values from 0 to 3, as said below
- noised: bfloat16 [8, 768, 768], P('rows', 'grp'), may hold values from -6 to 6
- w_gamma: bfloat16 [384, 768], replicated, may hold values from -0.3125 to 0.3125
- w_beta: bfloat16 [384, 768], replicated, may hold values from -0.3125 to 0.3125
- w_outgate: bfloat16 [384, 768], replicated, may hold values from -0.3125 to 0.3125
- w_query: bfloat16 [768, 768], replicated, may hold values from -0.21875 to 0.21875
- w_key: bfloat16 [768, 768], replicated, may hold values from -0.21875 to 0.21875
- w_value: bfloat16 [768, 768], replicated, may hold values from -0.21875 to 0.21875
- w_out: bfloat16 [768, 768], replicated, may hold values from -0.21875 to 0.21875
- w_pair: bfloat16 [128, 16], replicated, may hold values from -0.5 to 0.5
- chain_gain: float32 [16], replicated, may hold values from -3 to 6
- cotangent: bfloat16 [8, 768, 768], P('rows', 'grp'), may hold values from -6 to 6
Outputs:
- updated: bfloat16 [8, 768, 768], P('rows', 'grp')
- d_single: float32 [768, 384], P('grp')
- d_pair: bfloat16 [768, 768, 128], P('rows', 'grp')
Inputs may be any that keep to these rules, and one draw needn't show every extreme that they name: `chains`: chain numbers never fall along the tokens; each chain has 1 to 384 tokens, one exactly 384.
All inputs are finite; a program needn't handle non-finite values.
Results may differ from a plain program's by a relative error of at most 0.022.
Values may be sent and summed in bfloat16 or wider, within the bound.
No kernel may reach another device: no remote copies, remote signals or barrier semaphores. Data moves between devices by JAX's collectives and lax.ppermute only.
A program may use at most 128 MiB of HBM per device.

v0:
```python
import functools
import math

import jax
import jax.numpy as jnp
from jax import lax
from jax.experimental import pallas as pl
from jax.experimental.pallas import tpu as pltpu
from jax.sharding import PartitionSpec as P

EPSILON = 1e-05
BF16 = jnp.bfloat16
F32 = jnp.float32
VMEM_LIMIT = 56 * 1024 * 1024


def norm_rows(values):
    center = values - jnp.mean(values, axis=-1, keepdims=True)
    inverse = lax.rsqrt(jnp.mean(center * center, axis=-1, keepdims=True) + EPSILON)
    return (center * inverse, inverse)


def norm_back(grad_in, normed, inverse):
    grad_mean = jnp.mean(grad_in, axis=-1, keepdims=True)
    cross_mean = jnp.mean(grad_in * normed, axis=-1, keepdims=True)
    return inverse * (grad_in - grad_mean - normed * cross_mean)


def mm(left, right):
    return lax.dot_general(left, right, (((1,), (0,)), ((), ())), preferred_element_type=F32)


def mm_nt(left, right):
    return lax.dot_general(left, right, (((1,), (1,)), ((), ())), preferred_element_type=F32)


def mm_tn(left, right):
    return lax.dot_general(left, right, (((0,), (0,)), ((), ())), preferred_element_type=F32)


def sigmoid(values):
    return 1.0 / (1.0 + jnp.exp(-values))


def params():
    return pltpu.CompilerParams(vmem_limit_bytes=VMEM_LIMIT)


def smem():
    return pl.BlockSpec(memory_space=pltpu.SMEM)


def vmem():
    return pl.BlockSpec(memory_space=pltpu.VMEM)


def project_kernel(
    group_ref,
    single_ref,
    noised_ref,
    cot_ref,
    w_gamma_ref,
    w_beta_ref,
    w_outgate_ref,
    w_query_ref,
    w_key_ref,
    w_value_ref,
    w_out_ref,
    *rest,
    groups,
    calls,
):
    send_refs = rest[:groups]
    gamma_ref, gate_ref, stage_ref = rest[groups:]
    width = stage_ref.shape[2]
    part = width // (4 * calls)
    group_own = group_ref[0]
    single_norm, _ = norm_rows(single_ref[...].astype(F32))
    single_b = single_norm.astype(BF16)
    cond_gamma = sigmoid(mm(single_b, w_gamma_ref[...]))
    gamma_ref[...] = cond_gamma
    out_gate = sigmoid(mm(single_b, w_outgate_ref[...]))
    gate_ref[...] = out_gate
    cond_beta = mm(single_b, w_beta_ref[...])
    noised_norm, _ = norm_rows(noised_ref[...].astype(F32))
    x_b = (noised_norm * cond_gamma + cond_beta).astype(BF16)

    def put(kind, values):
        rounded = values.astype(BF16)
        for group in range(groups):
            slot = lax.rem(group - group_own + groups, groups)
            for call in range(calls):
                feature = (group * calls + call) * part
                lane = (call * 4 + kind) * part
                stage_ref[slot, :, lane : lane + part] = rounded[:, feature : feature + part]

    put(0, mm(x_b, w_query_ref[...]))
    put(1, mm(x_b, w_key_ref[...]))
    put(2, mm(x_b, w_value_ref[...]))
    grad_update = (cot_ref[...].astype(F32) * out_gate).astype(BF16)
    put(3, mm_nt(grad_update, w_out_ref[...]))
    for slot in range(groups):
        send_refs[slot][...] = stage_ref[slot]


def lane_tiles(cols):
    return [(tile, tile * 128, min(cols, tile * 128 + 128)) for tile in range(-(-cols // 128))]


def mean_matrix(channels):
    first = lax.broadcasted_iota(jnp.int32, (2 * channels, 2 * channels), 0) >= channels
    second = lax.broadcasted_iota(jnp.int32, (2 * channels, 2 * channels), 1) >= channels
    return jnp.where(first == second, 1.0 / channels, 0.0).astype(BF16)


def center_rows(pair_ref, first, batch, means):
    _, _, cols, channels = pair_ref.shape
    both = jnp.concatenate(
        [pair_ref[side, pl.ds(first, batch)].reshape(batch * cols, channels) for side in range(2)],
        axis=1,
    )
    return both.astype(F32) - mm(both, means)


def bias_kernel(
    group_ref,
    rows_ref,
    chains_ref,
    gain_ref,
    pair_ref,
    w_pair_ref,
    cols_ref,
    *rest,
    groups,
    batch,
):
    send_refs = rest[:groups]
    stats_ref, flat_ref, gains_ref, stage_ref = rest[groups:]
    _, step, cols, channels = pair_ref.shape
    heads = gain_ref.shape[0]
    per_group = heads // groups
    half = step * pl.num_programs(0)
    group_own = group_ref[0]
    row_base = rows_ref[0] * 2 * half + pl.program_id(0) * step
    means = mean_matrix(channels)
    weight = w_pair_ref[...]
    left = jnp.concatenate(
        [
            jnp.concatenate([weight, jnp.zeros((heads, channels), BF16)], axis=1),
            jnp.concatenate(
                [
                    jnp.zeros((heads, channels), BF16),
                    jnp.full((heads, channels), 1.0 / channels, BF16),
                ],
                axis=1,
            ),
        ],
        axis=0,
    )
    chain_cols = cols_ref[:, :cols]
    for group in range(1, groups):
        here = cols_ref[:, group * cols : (group + 1) * cols]
        chain_cols = jnp.where(group_own == group, here, chain_cols)
    for head in range(heads):
        gains_ref[head : head + 1, :] = jnp.full((1, cols), gain_ref[head], F32)

    def some_rows(index, carry):
        first = index * batch
        center = center_rows(pair_ref, first, batch, means)
        center_b = center.astype(BF16)
        square = (center * center).astype(BF16)
        for inner in range(batch):
            rows = slice(inner * cols, (inner + 1) * cols)
            for side in range(2):
                lanes = slice(side * channels, (side + 1) * channels)
                right = jnp.concatenate([center_b[rows, lanes], square[rows, lanes]], axis=1)
                sums = mm_nt(left, right)
                inverse = lax.rsqrt(sums[heads : heads + 8] + EPSILON)
                projected = sums[:heads] * inverse[:1]
                stats_ref[side, first + inner, :heads, :] = projected
                stats_ref[side, first + inner, heads:, :] = inverse
                chain = chains_ref[row_base + side * half + first + inner]
                same = (chain_cols == chain).astype(F32)
                values = projected + gains_ref[...] * same
                for tile, start, end in lane_tiles(cols):
                    piece = values[:, start:end]
                    if end - start < 128:
                        blank = jnp.zeros((heads, 128 - end + start), F32)
                        piece = jnp.concatenate([piece, blank], axis=1)
                    flat_ref[side, tile, pl.ds(first + inner, heads, stride=step), :] = piece
        return carry

    lax.fori_loop(0, step // batch, some_rows, 0)
    for head in range(heads):
        slot = lax.rem(head // per_group - group_own + groups, groups)
        values = jnp.concatenate(
            [
                flat_ref[side, tile, head * step : (head + 1) * step, : end - start]
                for side in range(2)
                for tile, start, end in lane_tiles(cols)
            ],
            axis=1,
        )
        stage_ref[slot, head % per_group] = values.astype(BF16)
    for slot in range(groups):
        send_refs[slot][...] = stage_ref[slot]


def pair_bias(pair, w_pair, chain_gain, chains, group_index, row_index, groups):
    rows, cols, channels = pair.shape
    heads = w_pair.shape[1]
    per_group = heads // groups
    half = rows // 2
    step = 16
    tiles = -(-cols // 128)
    *sends, stats = pl.pallas_call(
        functools.partial(bias_kernel, groups=groups, batch=4),
        grid=(half // step,),
        in_specs=[
            smem(),
            smem(),
            smem(),
            smem(),
            pl.BlockSpec((2, step, cols, channels), lambda t: (0, t, 0, 0)),
            pl.BlockSpec((heads, channels), lambda t: (0, 0)),
            pl.BlockSpec((1, groups * cols), lambda t: (0, 0)),
        ],
        out_specs=[
            pl.BlockSpec((per_group, step, 2 * cols), lambda t: (0, t, 0)) for _ in range(groups)
        ]
        + [pl.BlockSpec((2, step, heads + 8, cols), lambda t: (0, t, 0, 0))],
        out_shape=[
            jax.ShapeDtypeStruct((per_group, half, 2 * cols), BF16) for _ in range(groups)
        ]
        + [jax.ShapeDtypeStruct((2, half, heads + 8, cols), F32)],
        scratch_shapes=[
            pltpu.VMEM((2, tiles, heads * step, 128), F32),
            pltpu.VMEM((heads, cols), F32),
            pltpu.VMEM((groups, per_group, step, 2 * cols), BF16),
        ],
        compiler_params=params(),
    )(
        group_index,
        row_index,
        chains,
        chain_gain,
        pair.reshape(2, half, cols, channels),
        w_pair.T,
        chains.reshape(1, groups * cols),
    )
    return sends, stats


def pair_back_kernel(
    group_ref, pair_ref, stats_ref, w_pair_ref, *rest, groups, calls, factor, batch
):
    grad_refs = rest[: groups * calls]
    out_ref, flat_ref = rest[groups * calls :]
    _, step, cols, channels = pair_ref.shape
    per_call = grad_refs[0].shape[0]
    heads = groups * calls * per_call
    group_own = group_ref[0]
    means = mean_matrix(channels)
    weight = w_pair_ref[...].astype(F32)
    weight = weight - jnp.mean(weight, axis=-1, keepdims=True)
    high = weight.astype(BF16)
    low = (weight - high.astype(F32)).astype(BF16)
    weights = jnp.concatenate([high, low, jnp.zeros((16, channels), BF16)], axis=0)
    spread = lax.broadcasted_iota(jnp.int32, (2 * heads + 16, channels), 0)
    spread = ((spread >= 2 * heads) & (spread < 2 * heads + 2)).astype(F32).astype(BF16)
    weights = jnp.concatenate([weights, spread], axis=1)
    blank = jnp.zeros((14, cols), F32)
    for number in range(groups * calls):
        call, slot = divmod(number, groups)
        source = lax.rem(group_own + slot, groups) * calls + call
        for head in range(per_call):
            values = grad_refs[number][head].astype(F32)
            top = pl.multiple_of((source * per_call + head) * step, step)
            for side in range(2):
                for tile, start, end in lane_tiles(cols):
                    flat_ref[side, tile, pl.ds(top, step), : end - start] = values[
                        :, side * cols + start : side * cols + end
                    ]

    def some_rows(index, carry):
        first = index * batch
        center = center_rows(pair_ref, first, batch, means)
        for side in range(2):
            lefts = []
            for inner in range(batch):
                grads = jnp.concatenate(
                    [
                        flat_ref[side, tile, pl.ds(first + inner, heads, stride=step), :][
                            :, : end - start
                        ]
                        for tile, start, end in lane_tiles(cols)
                    ],
                    axis=1,
                )
                projected = stats_ref[side, first + inner, :heads, :]
                inverse = stats_ref[side, first + inner, heads : heads + 1, :]
                cross = jnp.sum(grads * projected, axis=0, keepdims=True) * (1.0 / channels)
                scaled = grads * (inverse * factor)
                cross = cross * (inverse * inverse * factor)
                cross_high = cross.astype(BF16).astype(F32)
                lefts.append(
                    jnp.concatenate(
                        [scaled, scaled, cross_high, cross - cross_high, blank], axis=0
                    )
                )
            for inner in range(batch):
                rows = slice(inner * cols, (inner + 1) * cols)
                lanes = slice(side * channels, (side + 1) * channels)
                both = mm_tn(lefts[inner].astype(BF16), weights)
                out_ref[side, first + inner] = (
                    both[:, :channels] - center[rows, lanes] * both[:, channels:]
                ).astype(BF16)
        return carry

    lax.fori_loop(0, step // batch, some_rows, 0)


def pair_back(pair, stats, grads, w_pair, group_index, groups, factor):
    rows, cols, channels = pair.shape
    per_call = grads[0].shape[0]
    heads = len(grads) * per_call
    half = rows // 2
    step = 16
    tiles = -(-cols // 128)
    out = pl.pallas_call(
        functools.partial(
            pair_back_kernel, groups=groups, calls=len(grads) // groups, factor=factor, batch=4
        ),
        grid=(half // step,),
        in_specs=[
            smem(),
            pl.BlockSpec((2, step, cols, channels), lambda t: (0, t, 0, 0)),
            pl.BlockSpec((2, step, heads + 8, cols), lambda t: (0, t, 0, 0)),
            pl.BlockSpec((heads, channels), lambda t: (0, 0)),
        ]
        + [pl.BlockSpec((per_call, step, 2 * cols), lambda t: (0, t, 0)) for _ in grads],
        out_specs=pl.BlockSpec((2, step, cols, channels), lambda t: (0, t, 0, 0)),
        out_shape=jax.ShapeDtypeStruct((2, half, cols, channels), BF16),
        scratch_shapes=[pltpu.VMEM((2, tiles, heads * step, 128), F32)],
        compiler_params=params(),
    )(group_index, pair.reshape(2, half, cols, channels), stats, w_pair.T, *grads)
    return out.reshape(rows, cols, channels)


def unit_order(heads):
    first, second = range(heads // 2), range(heads // 2, heads)
    order = [(0, head) for head in range(heads)]
    order += [(1, head) for head in first] + [(3, head) for head in first]
    order += [(2, head) for head in second] + [(3, head) for head in second]
    order += [(2, head) for head in first] + [(1, head) for head in second]
    return order


def attention_kernel(group_ref, row_ref, *rest, groups, row_parts, head_size, row_block):
    bias_refs = rest[: row_parts + 2]
    acts_refs = rest[row_parts + 2 : row_parts + 2 + groups]
    rest = rest[row_parts + 2 + groups :]
    out_refs = rest[:groups]
    (
        keep_ref,
        give_ref,
        query_ref,
        keys_ref,
        values_ref,
        grads_ref,
        query_t_ref,
        keys_t_ref,
        values_t_ref,
        grads_t_ref,
        bias_full,
        score_full,
        att_sum,
        gq_sum,
        gk_sum,
        gv_sum,
    ) = rest[groups:]
    head = pl.program_id(0)
    heads = keep_ref.shape[0] * 2 // row_parts
    group_own = group_ref[0]
    cols, width = acts_refs[0].shape
    tokens = groups * cols
    part = width // 4
    half = bias_refs[0].shape[2]
    scale = 1.0 / math.sqrt(head_size)
    extra = att_sum.shape[1] - part
    plain = (query_ref, keys_ref, values_ref, grads_ref)
    turned = (query_t_ref, keys_t_ref, values_t_ref, grads_t_ref)

    @pl.when(head == 0)
    def _():
        for kind in range(4):
            for slot in range(groups):
                plain[kind][slot * cols : (slot + 1) * cols, :] = acts_refs[slot][
                    :, kind * part : (kind + 1) * part
                ]
            turned[kind][...] = plain[kind][...].T
        att_sum[...] = jnp.zeros_like(att_sum)
        gq_sum[...] = jnp.zeros_like(gq_sum)

    def places(row_part):
        first = row_part * (2 * half)
        slot = lax.rem(group_own - first // cols + groups, groups)
        for side in range(2):
            top = slot * cols + lax.rem(first, cols) + side * half
            top = pl.multiple_of(top, 16)
            for column in range(groups):
                yield column, side, pl.ds(top, half)

    for other in range(row_parts):
        for column, side, rows in places(row_ref[0] ^ other):
            block, place = bias_refs[other], column
            if other >= row_parts - 2 and column >= groups // 2:
                block, place = bias_refs[other + 2], column - groups // 2
            bias_full[rows, column * cols : (column + 1) * cols] = block[
                place, 0, :, side * cols : (side + 1) * cols
            ]

    lane = lax.broadcasted_iota(jnp.int32, (1, part), 1)
    mine = (lane >= head * head_size) & (lane < (head + 1) * head_size)
    zero = jnp.zeros((), BF16)
    keys_m = jnp.where(mine, keys_ref[...], zero)
    values_m = jnp.concatenate(
        [jnp.where(mine, values_ref[...], zero), jnp.ones((tokens, extra), BF16)], axis=1
    )
    feature = pl.multiple_of(head * head_size, head_size)
    query_t = query_t_ref[pl.ds(feature, head_size), :]
    grads_t = grads_t_ref[pl.ds(feature, head_size), :]
    gk_t = jnp.zeros((head_size, tokens), F32)
    gv_t = jnp.zeros((head_size, tokens), F32)
    for top in range(0, tokens, row_block):
        rows = slice(top, top + row_block)
        query = jnp.where(mine, query_ref[rows, :], zero)
        grads = jnp.where(mine, grads_ref[rows, :], zero)
        scores = mm(query, keys_t_ref[...]) * scale + bias_full[rows, :].astype(F32)
        weights = jnp.exp(scores)
        attended = mm(weights.astype(BF16), values_m)
        inverse = 1.0 / attended[:, part : part + 1]
        attended = attended[:, :part] * inverse
        att_sum[rows, :part] += attended
        delta = jnp.sum(attended * grads.astype(F32), axis=-1, keepdims=True)
        prob = weights * inverse
        grad_prob = mm(grads, values_t_ref[...])
        score = (prob * (grad_prob - delta)).astype(BF16)
        score_full[rows, :] = score
        gq_sum[rows, :] += mm(score, keys_m)
        gk_t = gk_t + mm(query_t[:, rows], score)
        gv_t = gv_t + mm(grads_t[:, rows], prob.astype(BF16))
    gk_sum[pl.ds(feature, head_size), :] = gk_t
    gv_sum[pl.ds(feature, head_size), :] = gv_t

    for other in range(row_parts):
        dbias_ref = give_ref if other % 2 else keep_ref
        unit = 0
        for place, (chip, unit_head) in enumerate(unit_order(heads)):
            if chip == other // 2:
                unit = jnp.where(head == unit_head, place, unit)
        for column, side, rows in places(row_ref[0] ^ other):
            dbias_ref[unit, column, :, side * cols : (side + 1) * cols] = score_full[
                rows, column * cols : (column + 1) * cols
            ]

    @pl.when(head == heads - 1)
    def _():
        results = (
            gq_sum[...] * scale,
            (gk_sum[...] * scale).T,
            gv_sum[...].T,
            att_sum[:, :part],
        )
        for kind, values in enumerate(results):
            rounded = values.astype(BF16)
            for slot in range(groups):
                out_refs[slot][:, kind * part : (kind + 1) * part] = rounded[
                    slot * cols : (slot + 1) * cols
                ]


def attention(group_index, row_index, acts, bias, head_size):
    groups = len(acts)
    row_parts = len(bias) - 2
    cols, width = acts[0].shape
    tokens = groups * cols
    part = width // 4
    _, heads, half, lanes = bias[0].shape
    row_block = 256 if tokens % 256 == 0 else cols
    padded = (part // 128 + 1) * 128
    units = (row_parts // 2 * heads, groups, half, lanes)
    *grads, keep, give = pl.pallas_call(
        functools.partial(
            attention_kernel,
            groups=groups,
            row_parts=row_parts,
            head_size=head_size,
            row_block=row_block,
        ),
        grid=(heads,),
        in_specs=[smem(), smem()]
        + [
            pl.BlockSpec((block.shape[0], 1, half, lanes), lambda h: (0, h, 0, 0))
            for block in bias
        ]
        + [pl.BlockSpec((cols, width), lambda h: (0, 0))] * groups,
        out_specs=[pl.BlockSpec((cols, width), lambda h: (0, 0))] * groups
        + [pl.BlockSpec(units, lambda h: (0, 0, 0, 0))] * 2,
        out_shape=[jax.ShapeDtypeStruct((cols, width), BF16)] * groups
        + [jax.ShapeDtypeStruct(units, BF16)] * 2,
        scratch_shapes=[pltpu.VMEM((tokens, part), BF16) for _ in range(4)]
        + [pltpu.VMEM((part, tokens), BF16) for _ in range(4)]
        + [
            pltpu.VMEM((tokens, tokens), BF16),
            pltpu.VMEM((tokens, tokens), BF16),
            pltpu.VMEM((tokens, padded), F32),
            pltpu.VMEM((tokens, part), F32),
            pltpu.VMEM((part, tokens), F32),
            pltpu.VMEM((part, tokens), F32),
        ],
        compiler_params=params(),
    )(group_index, row_index, *bias, *acts)
    return grads, keep, give


def finish_kernel(
    group_ref,
    single_ref,
    noised_ref,
    cot_ref,
    gamma_ref,
    gate_ref,
    w_gamma_ref,
    w_beta_ref,
    w_outgate_ref,
    w_query_ref,
    w_key_ref,
    w_value_ref,
    w_out_ref,
    *rest,
    groups,
    calls,
):
    got_refs = rest[: groups * calls]
    updated_ref, d_single_ref, stage_ref = rest[groups * calls :]
    width = stage_ref.shape[3]
    part = width // 4
    for slot in range(groups):
        for call in range(calls):
            stage_ref[lax.rem(group_ref[0] + slot, groups), call] = got_refs[
                call * groups + slot
            ][...]

    def take(kind):
        return jnp.concatenate(
            [
                stage_ref[group, call, :, kind * part : (kind + 1) * part]
                for group in range(groups)
                for call in range(calls)
            ],
            axis=1,
        )

    out_gate = gate_ref[...]
    cond_gamma = gamma_ref[...]
    block_update = mm(take(3), w_out_ref[...])
    noised = noised_ref[...].astype(F32)
    updated_ref[...] = (noised + out_gate * block_update).astype(BF16)
    gate_part = cot_ref[...].astype(F32) * block_update
    pre_gate = (gate_part * out_gate * (1.0 - out_gate)).astype(BF16)
    grad_input = mm_nt(take(0), w_query_ref[...])
    grad_input += mm_nt(take(1), w_key_ref[...])
    grad_input += mm_nt(take(2), w_value_ref[...])
    noised_norm, _ = norm_rows(noised)
    pre_gamma = (grad_input * noised_norm * cond_gamma * (1.0 - cond_gamma)).astype(BF16)
    grad_snorm = mm_nt(pre_gamma, w_gamma_ref[...])
    grad_snorm += mm_nt(grad_input.astype(BF16), w_beta_ref[...])
    grad_snorm += mm_nt(pre_gate, w_outgate_ref[...])
    single_norm, single_inv = norm_rows(single_ref[...].astype(F32))
    d_single_ref[...] = norm_back(grad_snorm, single_norm, single_inv)


def swap_groups(sends, direction):
    groups = len(sends)
    got = [sends[0]]
    for shift in range(1, groups):
        perm = [(index, (index + direction * shift) % groups) for index in range(groups)]
        got.append(lax.ppermute(sends[shift], "grp", perm))
    return got


def flip_rows(values, bits, row_total):
    return lax.ppermute(values, "rows", [(index, index ^ bits) for index in range(row_total)])


def gather_rows(own, acts, row_total):
    half = own.shape[0] // 2
    near = flip_rows(own, 2, row_total)
    far = flip_rows(own, 4, row_total)
    first = flip_rows(near[:half], 4, row_total)
    second = flip_rows(far[half:], 2, row_total)
    first, second, acts[1], acts[2], acts[3] = lax.optimization_barrier(
        (first, second, acts[1], acts[2], acts[3])
    )
    blocks = []
    for block in (own, near, far, first, second):
        blocks += [block, flip_rows(block, 1, row_total)]
    return blocks, acts


def add_last_kernel(keep_ref, got_ref, near_ref, far_ref, near_two_ref, far_two_ref, *out_refs):
    head = pl.program_id(0)
    lower = head < pl.num_programs(0) // 2
    total = keep_ref[0].astype(F32) + got_ref[0].astype(F32)
    total += jnp.where(lower, near_ref[0].astype(F32), far_ref[0].astype(F32))
    total += jnp.where(lower, far_two_ref[0].astype(F32), near_two_ref[0].astype(F32))
    total = total.astype(BF16)
    for slot, out_ref in enumerate(out_refs):
        out_ref[0] = total[slot]


def scatter_rows(keep, give, grads, row_total):
    got = flip_rows(give, 1, row_total)
    units, groups, half, lanes = keep.shape
    heads = units // 4
    part = heads // 2

    def add(first, count, *others):
        total = keep[first : first + count].astype(F32) + got[first : first + count].astype(F32)
        for other in others:
            total += other.astype(F32)
        return total.astype(BF16)

    near = flip_rows(add(heads, heads), 2, row_total)
    far = flip_rows(add(2 * heads, heads), 4, row_total)
    far_two = add(3 * heads, part, near[part:])
    near_two = add(3 * heads + part, part, far[part:])
    far_two = flip_rows(far_two, 4, row_total)
    near_two = flip_rows(near_two, 2, row_total)
    far_two, near_two, grads = lax.optimization_barrier((far_two, near_two, grads))
    block = (1, groups, half, lanes)
    whole = pl.BlockSpec(block, lambda h: (h, 0, 0, 0))
    wrapped = pl.BlockSpec(block, lambda h: (lax.rem(h, part), 0, 0, 0))
    sums = pl.pallas_call(
        add_last_kernel,
        grid=(heads,),
        in_specs=[whole, whole] + [wrapped] * 4,
        out_specs=[pl.BlockSpec((1, half, lanes), lambda h: (h, 0, 0))] * groups,
        out_shape=[jax.ShapeDtypeStruct((heads, half, lanes), BF16)] * groups,
        compiler_params=params(),
    )(keep, got, near, far, near_two, far_two)
    sums, grads = lax.optimization_barrier((sums, grads))
    return sums, grads


def sum_rows(values, row_total):
    mine = values.astype(BF16)
    both = (mine.astype(F32) + flip_rows(mine, 1, row_total).astype(F32)).astype(BF16)
    near, far, last = (flip_rows(both, bits, row_total).astype(F32) for bits in (2, 4, 6))
    return (both.astype(F32) + near) + (far + last)


def split_heads(
    single,
    pair,
    chains,
    noised,
    w_gamma,
    w_beta,
    w_outgate,
    w_query,
    w_key,
    w_value,
    w_out,
    w_pair,
    chain_gain,
    cotangent,
    *,
    groups,
    row_total,
):
    cols, _ = single.shape
    tokens = chains.shape[0]
    width = noised.shape[2]
    head_size = width // w_pair.shape[1]
    calls = 1
    row_index = lax.axis_index("rows").reshape(1)
    group_index = lax.axis_index("grp").reshape(1)
    bias_send, stats = pair_bias(
        pair, w_pair, chain_gain, chains, group_index, row_index, groups
    )
    bias_got = swap_groups(bias_send, 1)
    noised = noised[0]
    cotangent = cotangent[0]
    *acts_send, cond_gamma, out_gate = pl.pallas_call(
        functools.partial(project_kernel, groups=groups, calls=calls),
        in_specs=[smem()] + [vmem()] * 10,
        out_shape=[
            jax.ShapeDtypeStruct((cols, 4 * width // groups), BF16) for _ in range(groups)
        ]
        + [
            jax.ShapeDtypeStruct((cols, width), F32),
            jax.ShapeDtypeStruct((cols, width), F32),
        ],
        scratch_shapes=[pltpu.VMEM((groups, cols, 4 * width // groups), BF16)],
        compiler_params=params(),
    )(
        group_index,
        single,
        noised,
        cotangent,
        w_gamma,
        w_beta,
        w_outgate,
        w_query,
        w_key,
        w_value,
        w_out,
    )
    bias_got, _ = lax.optimization_barrier((bias_got, acts_send))
    acts = swap_groups(acts_send, 1)
    bias_all, acts = gather_rows(jnp.stack(bias_got), acts, row_total)
    grads_send, keep, give = attention(group_index, row_index, acts, bias_all, head_size)
    grads = swap_groups(grads_send, -1)
    dbias_own, grads = scatter_rows(keep, give, grads, row_total)
    dbias_back = swap_groups(dbias_own, -1)
    updated, d_part = pl.pallas_call(
        functools.partial(finish_kernel, groups=groups, calls=calls),
        in_specs=[smem()] + [vmem()] * (12 + groups * calls),
        out_shape=[
            jax.ShapeDtypeStruct((cols, width), BF16),
            jax.ShapeDtypeStruct(single.shape, F32),
        ],
        scratch_shapes=[pltpu.VMEM((groups, calls, cols, 4 * width // (groups * calls)), BF16)],
        compiler_params=params(),
    )(
        group_index,
        single,
        noised,
        cotangent,
        cond_gamma,
        out_gate,
        w_gamma,
        w_beta,
        w_outgate,
        w_query,
        w_key,
        w_value,
        w_out,
        *grads,
    )
    d_part, dbias_back = lax.optimization_barrier((d_part, dbias_back))
    d_single = sum_rows(d_part, row_total)
    d_pair = pair_back(pair, stats, dbias_back, w_pair, group_index, groups, float(tokens))
    return (updated[None], d_single, d_pair)


def project(acts, weight):
    return jnp.einsum("std,de->ste", acts, weight, preferred_element_type=F32)


def project_back(acts, weight):
    return jnp.einsum("ste,de->std", acts, weight, preferred_element_type=F32)


def split_keys(
    single,
    pair,
    chains,
    noised,
    w_gamma,
    w_beta,
    w_outgate,
    w_query,
    w_key,
    w_value,
    w_out,
    w_pair,
    chain_gain,
    cotangent,
):
    col_count = single.shape[0]
    row_count = pair.shape[0]
    head_count = w_pair.shape[1]
    model_width = w_query.shape[0]
    head_size = model_width // head_count
    sample_count = noised.shape[0]
    token_total = chains.shape[0]
    score_scale = 1.0 / math.sqrt(head_size)
    row_index = lax.axis_index("rows")
    group_index = lax.axis_index("grp")
    chain_rows = lax.dynamic_slice_in_dim(chains, row_index * row_count, row_count)
    chain_cols = lax.dynamic_slice_in_dim(chains, group_index * col_count, col_count)
    pair_norm, pair_inv = norm_rows(pair.astype(jnp.float32))
    projected = jnp.einsum(
        "ijc,ch->hij", pair_norm.astype(jnp.bfloat16), w_pair, preferred_element_type=jnp.float32
    )
    same_chain = (chain_rows[:, None] == chain_cols[None, :]).astype(jnp.float32)
    bias_block = (projected + chain_gain[:, None, None] * same_chain[None]).astype(jnp.bfloat16)
    bias_keys = lax.all_gather(bias_block, "rows", axis=1, tiled=True)
    single_norm, single_inv = norm_rows(single.astype(jnp.float32))
    single_b = single_norm.astype(jnp.bfloat16)
    cond_gamma = jax.nn.sigmoid(jnp.dot(single_b, w_gamma, preferred_element_type=jnp.float32))
    cond_beta = jnp.dot(single_b, w_beta, preferred_element_type=jnp.float32)
    out_gate = jax.nn.sigmoid(jnp.dot(single_b, w_outgate, preferred_element_type=jnp.float32))
    noised_f = noised.astype(jnp.float32)
    noised_norm, noised_inv = norm_rows(noised_f)
    x_b = (noised_norm * cond_gamma[None] + cond_beta[None]).astype(jnp.bfloat16)
    queries = project(x_b, w_query).astype(jnp.bfloat16)
    keys_own = project(x_b, w_key).astype(jnp.bfloat16)
    values_own = project(x_b, w_value).astype(jnp.bfloat16)
    queries_all = lax.all_gather(queries, "grp", axis=1, tiled=True)
    query_heads = queries_all.reshape(sample_count, token_total, head_count, head_size)
    key_heads = keys_own.reshape(sample_count, col_count, head_count, head_size)
    value_heads = values_own.reshape(sample_count, col_count, head_count, head_size)
    scores = (
        jnp.einsum("sihe,sjhe->shij", query_heads, key_heads, preferred_element_type=jnp.float32)
        * score_scale
        + bias_keys.astype(jnp.float32)[None]
    )
    exp_scores = jnp.exp(scores)
    exp_total = lax.psum(jnp.sum(exp_scores, axis=-1).astype(jnp.bfloat16), "grp").astype(
        jnp.float32
    )
    attn_prob = exp_scores / exp_total[..., None]
    prob_b = attn_prob.astype(jnp.bfloat16)
    attended_part = jnp.einsum(
        "shij,sjhe->sihe", prob_b, value_heads, preferred_element_type=jnp.float32
    )
    attended_part = attended_part.reshape(sample_count, token_total, model_width)
    attended = lax.psum_scatter(
        attended_part.astype(jnp.bfloat16), "grp", scatter_dimension=1, tiled=True
    )
    block_update = project(attended, w_out)
    updated = (noised_f + out_gate[None] * block_update).astype(jnp.bfloat16)
    grad_out = cotangent.astype(jnp.float32)
    gate_part = jnp.sum(grad_out * block_update, axis=0)
    grad_update = (grad_out * out_gate[None]).astype(jnp.bfloat16)
    grad_attn = project_back(grad_update, w_out).astype(jnp.bfloat16)
    grads_all = lax.all_gather(grad_attn, "grp", axis=1, tiled=True)
    grad_heads = grads_all.reshape(sample_count, token_total, head_count, head_size)
    grad_prob = jnp.einsum(
        "sihe,sjhe->shij", grad_heads, value_heads, preferred_element_type=jnp.float32
    )
    row_delta = lax.psum(
        jnp.sum(attn_prob * grad_prob, axis=-1).astype(jnp.bfloat16), "grp"
    ).astype(jnp.float32)
    grad_score = attn_prob * (grad_prob - row_delta[..., None])
    score_b = grad_score.astype(jnp.bfloat16)
    query_part = (
        jnp.einsum("shij,sjhe->sihe", score_b, key_heads, preferred_element_type=jnp.float32)
        * score_scale
    )
    query_part = query_part.reshape(sample_count, token_total, model_width)
    grad_query = lax.psum_scatter(
        query_part.astype(jnp.bfloat16), "grp", scatter_dimension=1, tiled=True
    )
    grad_key = (
        jnp.einsum("shij,sihe->sjhe", score_b, query_heads, preferred_element_type=jnp.float32)
        * score_scale
    )
    grad_value = jnp.einsum(
        "shij,sihe->sjhe", prob_b, grad_heads, preferred_element_type=jnp.float32
    )
    grad_key = grad_key.reshape(sample_count, col_count, model_width).astype(jnp.bfloat16)
    grad_value = grad_value.reshape(sample_count, col_count, model_width).astype(jnp.bfloat16)
    grad_input = (
        project_back(grad_query, w_query)
        + project_back(grad_key, w_key)
        + project_back(grad_value, w_value)
    )
    gamma_part = jnp.sum(grad_input * noised_norm, axis=0)
    beta_part = jnp.sum(grad_input, axis=0)
    gamma_sum, beta_sum, gate_sum = lax.psum((gamma_part, beta_part, gate_part), "rows")
    pre_gamma = (gamma_sum * cond_gamma * (1.0 - cond_gamma)).astype(jnp.bfloat16)
    pre_gate = (gate_sum * out_gate * (1.0 - out_gate)).astype(jnp.bfloat16)
    grad_snorm = jnp.dot(pre_gamma, w_gamma.T, preferred_element_type=jnp.float32)
    grad_snorm = grad_snorm + jnp.dot(
        beta_sum.astype(jnp.bfloat16), w_beta.T, preferred_element_type=jnp.float32
    )
    grad_snorm = grad_snorm + jnp.dot(pre_gate, w_outgate.T, preferred_element_type=jnp.float32)
    d_single = norm_back(grad_snorm, single_norm, single_inv)
    bias_part = jnp.sum(score_b, axis=0, dtype=jnp.float32)
    bias_own = lax.psum_scatter(bias_part, "rows", scatter_dimension=1, tiled=True)
    bias_grad = (bias_own * token_total).astype(jnp.bfloat16)
    grad_pairn = jnp.einsum("hij,ch->ijc", bias_grad, w_pair, preferred_element_type=jnp.float32)
    d_pair = norm_back(grad_pairn, pair_norm, pair_inv).astype(jnp.bfloat16)
    return (updated, d_single, d_pair)


def solution(mesh):
    in_specs = (
        P("grp", None),
        P("rows", "grp", None),
        P(),
        P("rows", "grp", None),
        P(),
        P(),
        P(),
        P(),
        P(),
        P(),
        P(),
        P(),
        P(),
        P("rows", "grp", None),
    )
    out_specs = (P("rows", "grp", None), P("grp", None), P("rows", "grp", None))
    groups = mesh.shape["grp"]
    row_total = mesh.shape["rows"]

    def on_device(*args):
        pair, noised, w_pair = args[1], args[3], args[11]
        fits = (
            pair.shape[0] % 32 == 0
            and pair.shape[1] % pair.shape[0] == 0
            and row_total == 8
            and noised.shape[0] == 1
            and noised.shape[1] % 64 == 0
            and w_pair.shape[1] % (2 * groups) == 0
        )
        if fits:
            return split_heads(*args, groups=groups, row_total=row_total)
        return split_keys(*args)

    return jax.shard_map(
        on_device, mesh=mesh, in_specs=in_specs, out_specs=out_specs, check_vma=False
    )
```

profile of v0, /device:TPU:0, one launch (start us, length us, event | category | flops | bytes accessed | tf_op | source)
XLA Modules:
  0.0 156.6 jit_solution(5870201827958969806)
XLA Ops:
  0.6 1.3 reshape.25.cols_ref
  1.9 10.8 %shard_map.158 = (bf16[4,48,384]{2,1,0:T(8,128)(2,1)}, bf16[4,48,384]{2,1,0:T(8,128)(2,1)}, bf16[4,48,384]{2,1,0:T(8,128)(2,1)}, bf16[4,48,384]{2,1,0:T(8,128)(2,1)}, f32[2,48,24,192]{3,2,1,0:T(8,128)}) custom-call(s32[1]{0:T(128)} %bitcast.group_ref, s32[1]{0:T(128)} %bitcast.3.rows_ref.row_ref, s32[768]{0:T(1024)} %chains_ref.1, f32[16]{0:T(128)} %gain_ref.1, ...), custom_call_target="tpu_custom_call" | custom-call | tf_op jit(solution)/shard_map/pallas_call | solution.py:216
  12.7 3.0 %collective-permute-start = (bf16[4,48,384]{2,1,0:T(8,128)(2,1)}, bf16[4,48,384]{2,1,0:T(8,128)(2,1)S(1)}, u32[]{:S(2)}, u32[]{:S(2)}) collective-permute-start(bf16[4,48,384]{2,1,0:T(8,128)(2,1)} %get-tuple-element.57), channel_id=1, source_target_pairs={{0,1},{1,2},{2,3},{3,0},{4,5},{5,6},{6,7},{7,4},{8,9},{9,10},{10,1... | collective-permute-start | bytes 442376 | tf_op jit(solution)/shard_map/ppermute | solution.py:589
  15.7 2.6 %collective-permute-start.1 = (bf16[4,48,384]{2,1,0:T(8,128)(2,1)}, bf16[4,48,384]{2,1,0:T(8,128)(2,1)S(1)}, u32[]{:S(2)}, u32[]{:S(2)}) collective-permute-start(bf16[4,48,384]{2,1,0:T(8,128)(2,1)} %get-tuple-element.58), channel_id=1, source_target_pairs={{0,2},{1,3},{2,0},{3,1},{4,6},{5,7},{6,4},{7,5},{8,10},{9,11},{10,... | collective-permute-start | bytes 442376 | tf_op jit(solution)/shard_map/ppermute | solution.py:589
  18.3 1.3 collective-permute-start.2
  19.7 6.6 %shard_map.157 = (bf16[192,768]{1,0:T(8,128)(2,1)}, bf16[192,768]{1,0:T(8,128)(2,1)}, bf16[192,768]{1,0:T(8,128)(2,1)}, bf16[192,768]{1,0:T(8,128)(2,1)}, f32[192,768]{1,0:T(8,128)}, /*index=5*/f32[192,768]{1,0:T(8,128)}) custom-call(s32[1]{0:T(128)} %bitcast.group_ref, bf16[192,384]{1,0:T(8,128)(2,1)} %single_ref.3, bf16[192,768]{1,0:T(8,128)(2,1)} %bitcast.15, ...), custom_call_target="tpu_custom_call" | custom-call | tf_op jit(solution)/shard_map/pallas_call | solution.py:696
  26.2 2.0 %collective-permute-done.1 = bf16[4,48,384]{2,1,0:T(8,128)(2,1)S(1)} collective-permute-done((bf16[4,48,384]{2,1,0:T(8,128)(2,1)}, bf16[4,48,384]{2,1,0:T(8,128)(2,1)S(1)}, u32[]{:S(2)}, u32[]{:S(2)}) %collective-permute-start.1) | collective-permute-done | bytes 147488 | tf_op jit(solution)/shard_map/ppermute | solution.py:589
  28.2 0.0 collective-permute-done.2
  28.2 0.1 pad_maximum_fusion.rest_0_
  28.3 1.6 %collective-permute-start.6 = (bf16[4,4,48,384]{3,2,1,0:T(8,128)(2,1)S(1)}, bf16[4,4,48,384]{3,2,1,0:T(8,128)(2,1)S(1)}, u32[]{:S(2)}, u32[]{:S(2)}) collective-permute-start(bf16[4,4,48,384]{3,2,1,0:T(8,128)(2,1)S(1)} %pad_maximum_fusion.rest_0_), channel_id=1, source_target_pairs={{0,16},{4,20},{8,24},{12,28},{16,0},{20,4},{24,8},{28,12},{1,17},{... | collective-permute-start | bytes 1769480 | tf_op jit(solution)/shard_map/ppermute | solution.py:594
  29.9 1.5 collective-permute-start.4
  31.4 3.6 %collective-permute-start.10 = (bf16[192,768]{1,0:T(8,128)(2,1)}, bf16[192,768]{1,0:T(8,128)(2,1)S(1)}, u32[]{:S(2)}, u32[]{:S(2)}) collective-permute-start(bf16[192,768]{1,0:T(8,128)(2,1)} %get-tuple-element.61), channel_id=1, source_target_pairs={{0,1},{1,2},{2,3},{3,0},{4,5},{5,6},{6,7},{7,4},{8,9},{9,10},{10,1... | collective-permute-start | bytes 884744 | tf_op jit(solution)/shard_map/ppermute | solution.py:589
  35.0 1.6 %collective-permute-start.11 = (bf16[192,768]{1,0:T(8,128)(2,1)}, bf16[192,768]{1,0:T(8,128)(2,1)S(1)}, u32[]{:S(2)}, u32[]{:S(2)}) collective-permute-start(bf16[192,768]{1,0:T(8,128)(2,1)} %get-tuple-element.62), channel_id=1, source_target_pairs={{0,2},{1,3},{2,0},{3,1},{4,6},{5,7},{6,4},{7,5},{8,10},{9,11},{10,... | collective-permute-start | bytes 884744 | tf_op jit(solution)/shard_map/ppermute | solution.py:589
  36.7 0.7 collective-permute-start.12
  37.4 6.2 %collective-permute-done.6.rest_4_ = bf16[4,4,48,384]{3,2,1,0:T(8,128)(2,1)S(1)} collective-permute-done((bf16[4,4,48,384]{3,2,1,0:T(8,128)(2,1)S(1)}, bf16[4,4,48,384]{3,2,1,0:T(8,128)(2,1)S(1)}, u32[]{:S(2)}, u32[]{:S(2)}) %collective-permute-start.6) | collective-permute-done | bytes 589856 | tf_op jit(solution)/shard_map/ppermute | solution.py:594
  43.6 1.6 collective-permute-start.9
  45.2 1.6 %collective-permute-start.8 = (bf16[2,4,48,384]{3,2,1,0:T(8,128)(2,1)S(1)}, bf16[2,4,48,384]{3,2,1,0:T(8,128)(2,1)S(1)}, u32[]{:S(2)}, u32[]{:S(2)}) collective-permute-start(bf16[2,4,48,384]{3,2,1,0:T(8,128)(2,1)S(1)} %slice.48), channel_id=1, source_target_pairs={{0,16},{4,20},{8,24},{12,28},{16,0},{20,4},{24,8},{28,12},{1,17},{... | collective-permute-start | bytes 884744 | tf_op jit(solution)/shard_map/ppermute | solution.py:594
  46.8 0.0 collective-permute-done.10.rest_11_
  46.8 7.9 %collective-permute-done.11.rest_12_ = bf16[192,768]{1,0:T(8,128)(2,1)S(1)} collective-permute-done((bf16[192,768]{1,0:T(8,128)(2,1)}, bf16[192,768]{1,0:T(8,128)(2,1)S(1)}, u32[]{:S(2)}, u32[]{:S(2)}) %collective-permute-start.11) | collective-permute-done | bytes 294944 | tf_op jit(solution)/shard_map/ppermute | solution.py:589
  54.7 0.0 collective-permute-start.7
  54.7 0.0 collective-permute-done.12.rest_13_
  54.7 0.5 collective-permute-start.5
  55.2 0.0 copy-start.16
  55.2 0.1 collective-permute-start.13
  55.4 0.4 collective-permute-start.14
  55.8 0.9 collective-permute-done.7.rest_5_
  56.7 0.8 collective-permute-done.5.rest_3_
  57.5 0.4 collective-permute-done.13.rest_7_
  57.9 0.4 collective-permute-done.14.rest_9_
  58.5 0.2 copy-done.17
  58.7 0.7 copy-done.18
  59.4 17.5 %shard_map.159 = (bf16[192,768]{1,0:T(8,128)(2,1)}, bf16[192,768]{1,0:T(8,128)(2,1)}, bf16[192,768]{1,0:T(8,128)(2,1)}, bf16[192,768]{1,0:T(8,128)(2,1)}, bf16[1...) custom-call(s32[1]{0:T(128)} %bitcast.group_ref, s32[1]{0:T(128)} %bitcast.3.rows_ref.row_ref, ...), custom_call_target="tpu_custom_call" | custom-call | tf_op jit(solution)/shard_map/pallas_call | solution.py:493
  76.9 0.2 collective-permute-start.15
  77.1 4.6 %collective-permute-done.15.got_ref = bf16[16,4,48,384]{3,2,1,0:T(8,128)(2,1)S(1)} collective-permute-done((bf16[16,4,48,384]{3,2,1,0:T(8,128)(2,1)}, bf16[16,4,48,384]{3,2,1,0:T(8,128)(2,1)S(1)}, u32[]{:S(2)}, u32[]{:S(2)}) %collective-permute-start.15) | collective-permute-done | bytes 2359328 | tf_op jit(solution)/shard_map/ppermute | solution.py:594
  81.7 2.4 %add_convert_fusion = (bf16[4,4,48,384]{3,2,1,0:T(8,128)(2,1)S(1)}, bf16[4,4,48,384]{3,2,1,0:T(8,128)(2,1)S(1)}) fusion(bf16[16,4,48,384]{3,2,1,0:T(8,128)(2,1)S(1)} %collective-permute-done.15.got_ref, bf16[16,4,48,384]{3,2,1,0:T(8,128)(2,1)} %get-tuple-element.73.keep_ref), kind=kLoop, calls=%fused_computation | loop fusion | flops 2359296 | bytes 3538944 | tf_op jit(solution)/shard_map/convert_element_type | solution.py:633
  84.1 0.6 collective-permute-start.17
  84.7 0.5 collective-permute-start.16
  85.2 8.5 %collective-permute-start.20 = (bf16[192,768]{1,0:T(8,128)(2,1)S(1)}, bf16[192,768]{1,0:T(8,128)(2,1)S(1)}, u32[]{:S(2)}, u32[]{:S(2)}) collective-permute-start(bf16[192,768]{1,0:T(8,128)(2,1)S(1)} %copy-done.27), channel_id=1, source_target_pairs={{0,3},{1,0},{2,1},{3,2},{4,7},{5,4},{6,5},{7,6},{8,11},{9,8},{10,9... | collective-permute-start | bytes 884744 | tf_op jit(solution)/shard_map/ppermute | solution.py:589
  93.7 0.6 collective-permute-start.22
  94.4 5.2 %collective-permute-done.17.far_ref = bf16[4,4,48,384]{3,2,1,0:T(8,128)(2,1)S(1)} collective-permute-done((bf16[4,4,48,384]{3,2,1,0:T(8,128)(2,1)S(1)}, bf16[4,4,48,384]{3,2,1,0:T(8,128)(2,1)S(1)}, u32[]{:S(2)}, u32[]{:S(2)}) %collective-permute-start.17) | collective-permute-done | bytes 589856 | tf_op jit(solution)/shard_map/ppermute | solution.py:594
  99.5 0.2 collective-permute-done.16.near_ref
  99.8 1.5 add_convert_fusion.2
  101.3 0.6 collective-permute-start.19
  101.9 1.5 collective-permute-start.18
  103.4 14.6 %collective-permute-done.21.rest_2_ = bf16[192,768]{1,0:T(8,128)(2,1)S(1)} collective-permute-done((bf16[192,768]{1,0:T(8,128)(2,1)S(1)}, bf16[192,768]{1,0:T(8,128)(2,1)S(1)}, u32[]{:S(2)}, u32[]{:S(2)}) %collective-permute-start.21) | collective-permute-done | bytes 294944 | tf_op jit(solution)/shard_map/ppermute | solution.py:589
  118.1 0.0 copy-start.19
  118.1 0.7 copy-done.19
  118.8 0.1 copy-done.20
  118.9 3.9 %shard_map.160 = (bf16[4,48,384]{2,1,0:T(8,128)(2,1)}, bf16[4,48,384]{2,1,0:T(8,128)(2,1)}, bf16[4,48,384]{2,1,0:T(8,128)(2,1)}, bf16[4,48,384]{2,1,0:T(8,128)(2,1)}) custom-call(bf16[16,4,48,384]{3,2,1,0:T(8,128)(2,1)} %get-tuple-element.73.keep_ref, bf16[16,4,48,384]{3,2,1,0:T(8,128)(2,1)} %copy-done, bf16[4,4,48,384]{3,2,1,0:T(8,128)(2,1)} %copy-done.3, ...), custom_call_target="tpu_custom_call" | custom-call | tf_op jit(solution)/shard_map/pallas_call | solution.py:645
  122.9 0.2 collective-permute-start.23
  123.0 3.2 %collective-permute-start.24 = (bf16[4,48,384]{2,1,0:T(8,128)(2,1)}, bf16[4,48,384]{2,1,0:T(8,128)(2,1)S(1)}, u32[]{:S(2)}, u32[]{:S(2)}) collective-permute-start(bf16[4,48,384]{2,1,0:T(8,128)(2,1)} %get-tuple-element.97), channel_id=1, source_target_pairs={{0,2},{1,3},{2,0},{3,1},{4,6},{5,7},{6,4},{7,5},{8,10},{9,11},{10,... | collective-permute-start | bytes 442376 | tf_op jit(solution)/shard_map/ppermute | solution.py:589
  126.3 1.9 %collective-permute-start.25 = (bf16[4,48,384]{2,1,0:T(8,128)(2,1)}, bf16[4,48,384]{2,1,0:T(8,128)(2,1)S(1)}, u32[]{:S(2)}, u32[]{:S(2)}) collective-permute-start(bf16[4,48,384]{2,1,0:T(8,128)(2,1)} %get-tuple-element.98), channel_id=1, source_target_pairs={{0,1},{1,2},{2,3},{3,0},{4,5},{5,6},{6,7},{7,4},{8,9},{9,10},{10,1... | collective-permute-start | bytes 442376 | tf_op jit(solution)/shard_map/ppermute | solution.py:589
  128.2 7.5 %shard_map.161 = (bf16[192,768]{1,0:T(8,128)(2,1)}, f32[192,384]{1,0:T(8,128)}) custom-call(s32[1]{0:T(128)} %bitcast.group_ref, bf16[192,384]{1,0:T(8,128)(2,1)} %single_ref.3, bf16[192,768]{1,0:T(8,128)(2,1)} %bitcast.16, bf16[192,768]{1,0:T(8,128)(2,1)} %bitcast.18, f32[192,768]{1,0:T(8,128)} %get-tuple-element.54.gamma_ref, ...), custom_call_target="tpu_custom_call" | custom-call | tf_op jit(solution)/shard_map/pallas_call | solution.py:728
  135.8 0.0 copy-start.22
  135.8 3.3 %collective-permute-done.24.rest_2_ = bf16[4,48,384]{2,1,0:T(8,128)(2,1)S(1)} collective-permute-done((bf16[4,48,384]{2,1,0:T(8,128)(2,1)}, bf16[4,48,384]{2,1,0:T(8,128)(2,1)S(1)}, u32[]{:S(2)}, u32[]{:S(2)}) %collective-permute-start.24) | collective-permute-done | bytes 147488 | tf_op jit(solution)/shard_map/ppermute | solution.py:589
  139.1 1.1 convert_element_type.80
  140.1 0.1 collective-permute-start.26
  140.2 1.4 collective-permute-done.26
  141.6 1.0 add_convert_fusion.4
  142.6 2.5 %collective-permute-start.29 = (bf16[192,384]{1,0:T(8,128)(2,1)S(1)}, bf16[192,384]{1,0:T(8,128)(2,1)S(1)}, u32[]{:S(2)}, u32[]{:S(2)}) collective-permute-start(bf16[192,384]{1,0:T(8,128)(2,1)S(1)} %add_convert_fusion.4), channel_id=1, source_target_pairs={{0,24},{4,28},{8,16},{12,20},{16,8},{20,12},{24,0},{28,4},{1,25},{... | collective-permute-start | bytes 442376 | tf_op jit(solution)/shard_map/ppermute | solution.py:594
  145.1 0.5 collective-permute-start.28
  145.6 0.5 collective-permute-start.27
  146.2 9.6 %shard_map.162 = bf16[2,48,192,128]{3,2,1,0:T(8,128)(2,1)} custom-call(s32[1]{0:T(128)} %bitcast.group_ref, bf16[2,48,192,128]{3,2,1,0:T(8,128)(2,1)} %bitcast.13, f32[2,48,24,192]{3,2,1,0:T(8,128)} %get-tuple-element.100.stats_ref, bf16[16,128]{1,0:T(8,128)(2,1)} %bitcast.24, bf16[4,48,384]{2,1,0:T(8,128)(2,1)} %get-tuple-element.101.rest_0_, ...), custom_call_target="tpu_custom_call" | custom-call | tf_op jit(solution)/shard_map/pallas_call | solution.py:330
  155.8 0.8 add_add_fusion
  (67 shorter events, 0.2 us)
Async XLA Ops:
  12.7 13.5 %collective-permute-start = (bf16[4,48,384]{2,1,0:T(8,128)(2,1)}, bf16[4,48,384]{2,1,0:T(8,128)(2,1)S(1)}, u32[]{:S(2)}, u32[]{:S(2)}) collective-permute-start(bf16[4,48,384]{2,1,0:T(8,128)(2,1)} %get-tuple-element.57), channel_id=1, source_target_pairs={{0,1},{1,2},{2,3},{3,0},{4,5},{5,6},{6,7},{7,4},{8,9},{9,10},{10,1... | collective-permute-start | bytes 442376 | tf_op jit(solution)/shard_map/ppermute | solution.py:589
  15.7 12.5 %collective-permute-start.1 = (bf16[4,48,384]{2,1,0:T(8,128)(2,1)}, bf16[4,48,384]{2,1,0:T(8,128)(2,1)S(1)}, u32[]{:S(2)}, u32[]{:S(2)}) collective-permute-start(bf16[4,48,384]{2,1,0:T(8,128)(2,1)} %get-tuple-element.58), channel_id=1, source_target_pairs={{0,2},{1,3},{2,0},{3,1},{4,6},{5,7},{6,4},{7,5},{8,10},{9,11},{10,... | collective-permute-start | bytes 442376 | tf_op jit(solution)/shard_map/ppermute | solution.py:589
  18.3 9.9 %collective-permute-start.2 = (bf16[4,48,384]{2,1,0:T(8,128)(2,1)}, bf16[4,48,384]{2,1,0:T(8,128)(2,1)S(1)}, u32[]{:S(2)}, u32[]{:S(2)}) collective-permute-start(bf16[4,48,384]{2,1,0:T(8,128)(2,1)} %get-tuple-element.59), channel_id=1, source_target_pairs={{0,3},{1,0},{2,1},{3,2},{4,7},{5,4},{6,5},{7,6},{8,11},{9,8},{10,9... | collective-permute-start | bytes 442376 | tf_op jit(solution)/shard_map/ppermute | solution.py:589
  19.7 8.6 %copy-start.21 = (bf16[4,48,384]{2,1,0:T(8,128)(2,1)S(1)}, bf16[4,48,384]{2,1,0:T(8,128)(2,1)}, u32[]{:S(2)}) copy-start(bf16[4,48,384]{2,1,0:T(8,128)(2,1)} %get-tuple-element.64) | copy-start | bytes 442372
  28.3 30.0 %copy-start.1 = (bf16[4,4,48,384]{3,2,1,0:T(8,128)(2,1)}, bf16[4,4,48,384]{3,2,1,0:T(8,128)(2,1)S(1)}, u32[]{:S(2)}) copy-start(bf16[4,4,48,384]{3,2,1,0:T(8,128)(2,1)S(1)} %pad_maximum_fusion.rest_0_) | copy-start | bytes 1769476
  28.3 15.2 %collective-permute-start.6 = (bf16[4,4,48,384]{3,2,1,0:T(8,128)(2,1)S(1)}, bf16[4,4,48,384]{3,2,1,0:T(8,128)(2,1)S(1)}, u32[]{:S(2)}, u32[]{:S(2)}) collective-permute-start(bf16[4,4,48,384]{3,2,1,0:T(8,128)(2,1)S(1)} %pad_maximum_fusion.rest_0_), channel_id=1, source_target_pairs={{0,16},{4,20},{8,24},{12,28},{16,0},{20,4},{24,8},{28,12},{1,17},{... | collective-permute-start | bytes 1769480 | tf_op jit(solution)/shard_map/ppermute | solution.py:594
  29.9 15.2 %collective-permute-start.4 = (bf16[4,4,48,384]{3,2,1,0:T(8,128)(2,1)S(1)}, bf16[4,4,48,384]{3,2,1,0:T(8,128)(2,1)S(1)}, u32[]{:S(2)}, u32[]{:S(2)}) collective-permute-start(bf16[4,4,48,384]{3,2,1,0:T(8,128)(2,1)S(1)} %pad_maximum_fusion.rest_0_), channel_id=1, source_target_pairs={{0,8},{4,12},{8,0},{12,4},{16,24},{20,28},{24,16},{28,20},{1,9},{5... | collective-permute-start | bytes 1769480 | tf_op jit(solution)/shard_map/ppermute | solution.py:594
  31.4 15.4 %collective-permute-start.10 = (bf16[192,768]{1,0:T(8,128)(2,1)}, bf16[192,768]{1,0:T(8,128)(2,1)S(1)}, u32[]{:S(2)}, u32[]{:S(2)}) collective-permute-start(bf16[192,768]{1,0:T(8,128)(2,1)} %get-tuple-element.61), channel_id=1, source_target_pairs={{0,1},{1,2},{2,3},{3,0},{4,5},{5,6},{6,7},{7,4},{8,9},{9,10},{10,1... | collective-permute-start | bytes 884744 | tf_op jit(solution)/shard_map/ppermute | solution.py:589
  35.0 19.6 %collective-permute-start.11 = (bf16[192,768]{1,0:T(8,128)(2,1)}, bf16[192,768]{1,0:T(8,128)(2,1)S(1)}, u32[]{:S(2)}, u32[]{:S(2)}) collective-permute-start(bf16[192,768]{1,0:T(8,128)(2,1)} %get-tuple-element.62), channel_id=1, source_target_pairs={{0,2},{1,3},{2,0},{3,1},{4,6},{5,7},{6,4},{7,5},{8,10},{9,11},{10,... | collective-permute-start | bytes 884744 | tf_op jit(solution)/shard_map/ppermute | solution.py:589
  36.7 18.0 %collective-permute-start.12 = (bf16[192,768]{1,0:T(8,128)(2,1)}, bf16[192,768]{1,0:T(8,128)(2,1)S(1)}, u32[]{:S(2)}, u32[]{:S(2)}) collective-permute-start(bf16[192,768]{1,0:T(8,128)(2,1)} %get-tuple-element.63), channel_id=1, source_target_pairs={{0,3},{1,0},{2,1},{3,2},{4,7},{5,4},{6,5},{7,6},{8,11},{9,8},{10,9... | collective-permute-start | bytes 884744 | tf_op jit(solution)/shard_map/ppermute | solution.py:589
  43.6 14.8 %copy-start.4 = (bf16[4,4,48,384]{3,2,1,0:T(8,128)(2,1)}, bf16[4,4,48,384]{3,2,1,0:T(8,128)(2,1)S(1)}, u32[]{:S(2)}) copy-start(bf16[4,4,48,384]{3,2,1,0:T(8,128)(2,1)S(1)} %collective-permute-done.6.rest_4_) | copy-start | bytes 1769476
  43.6 11.6 %collective-permute-start.9 = (bf16[2,4,48,384]{3,2,1,0:T(8,128)(2,1)S(1)}, bf16[2,4,48,384]{3,2,1,0:T(8,128)(2,1)S(1)}, u32[]{:S(2)}, u32[]{:S(2)}) collective-permute-start(bf16[2,4,48,384]{3,2,1,0:T(8,128)(2,1)S(1)} %slice.49), channel_id=1, source_target_pairs={{0,8},{4,12},{8,0},{12,4},{16,24},{20,28},{24,16},{28,20},{1,9},{5... | collective-permute-start | bytes 884744 | tf_op jit(solution)/shard_map/ppermute | solution.py:594
  45.2 13.2 %copy-start.5 = (bf16[4,4,48,384]{3,2,1,0:T(8,128)(2,1)}, bf16[4,4,48,384]{3,2,1,0:T(8,128)(2,1)S(1)}, u32[]{:S(2)}) copy-start(bf16[4,4,48,384]{3,2,1,0:T(8,128)(2,1)S(1)} %collective-permute-done.4.rest_2_) | copy-start | bytes 1769476
  45.2 10.0 %collective-permute-start.8 = (bf16[2,4,48,384]{3,2,1,0:T(8,128)(2,1)S(1)}, bf16[2,4,48,384]{3,2,1,0:T(8,128)(2,1)S(1)}, u32[]{:S(2)}, u32[]{:S(2)}) collective-permute-start(bf16[2,4,48,384]{3,2,1,0:T(8,128)(2,1)S(1)} %slice.48), channel_id=1, source_target_pairs={{0,16},{4,20},{8,24},{12,28},{16,0},{20,4},{24,8},{28,12},{1,17},{... | collective-permute-start | bytes 884744 | tf_op jit(solution)/shard_map/ppermute | solution.py:594
  46.8 11.6 %copy-start.9 = (bf16[192,768]{1,0:T(8,128)(2,1)}, bf16[192,768]{1,0:T(8,128)(2,1)S(1)}, u32[]{:S(2)}) copy-start(bf16[192,768]{1,0:T(8,128)(2,1)S(1)} %collective-permute-done.10.rest_11_) | copy-start | bytes 884740
  46.8 9.0 %collective-permute-start.3 = (bf16[4,4,48,384]{3,2,1,0:T(8,128)(2,1)S(1)}, bf16[4,4,48,384]{3,2,1,0:T(8,128)(2,1)S(1)}, u32[]{:S(2)}, u32[]{:S(2)}) collective-permute-start(bf16[4,4,48,384]{3,2,1,0:T(8,128)(2,1)S(1)} %pad_maximum_fusion.rest_0_), channel_id=1, source_target_pairs={{0,4},{4,0},{8,12},{12,8},{16,20},{20,16},{24,28},{28,24},{1,5},{5... | collective-permute-start | bytes 1769480 | tf_op jit(solution)/shard_map/ppermute | solution.py:594
  54.7 3.7 %copy-start.10 = (bf16[192,768]{1,0:T(8,128)(2,1)}, bf16[192,768]{1,0:T(8,128)(2,1)S(1)}, u32[]{:S(2)}) copy-start(bf16[192,768]{1,0:T(8,128)(2,1)S(1)} %collective-permute-done.11.rest_12_) | copy-start | bytes 884740
  54.7 2.0 %collective-permute-start.7 = (bf16[4,4,48,384]{3,2,1,0:T(8,128)(2,1)S(1)}, bf16[4,4,48,384]{3,2,1,0:T(8,128)(2,1)S(1)}, u32[]{:S(2)}, u32[]{:S(2)}) collective-permute-start(bf16[4,4,48,384]{3,2,1,0:T(8,128)(2,1)S(1)} %collective-permute-done.6.rest_4_), channel_id=1, source_target_pairs={{0,4},{4,0},{8,12},{12,8},{16,20},{20,16},{24,28},{28,24},{1,5},{5... | collective-permute-start | bytes 1769480 | tf_op jit(solution)/shard_map/ppermute | solution.py:594
  54.7 3.7 %copy-start.11 = (bf16[192,768]{1,0:T(8,128)(2,1)}, bf16[192,768]{1,0:T(8,128)(2,1)S(1)}, u32[]{:S(2)}) copy-start(bf16[192,768]{1,0:T(8,128)(2,1)S(1)} %collective-permute-done.12.rest_13_) | copy-start | bytes 884740
  54.7 2.8 %collective-permute-start.5 = (bf16[4,4,48,384]{3,2,1,0:T(8,128)(2,1)S(1)}, bf16[4,4,48,384]{3,2,1,0:T(8,128)(2,1)S(1)}, u32[]{:S(2)}, u32[]{:S(2)}) collective-permute-start(bf16[4,4,48,384]{3,2,1,0:T(8,128)(2,1)S(1)} %collective-permute-done.4.rest_2_), channel_id=1, source_target_pairs={{0,4},{4,0},{8,12},{12,8},{16,20},{20,16},{24,28},{28,24},{1,5},{5... | collective-permute-start | bytes 1769480 | tf_op jit(solution)/shard_map/ppermute | solution.py:594
  55.2 3.2 %copy-start.13 = (bf16[2,4,48,384]{3,2,1,0:T(8,128)(2,1)}, bf16[2,4,48,384]{3,2,1,0:T(8,128)(2,1)S(1)}, u32[]{:S(2)}) copy-start(bf16[2,4,48,384]{3,2,1,0:T(8,128)(2,1)S(1)} %collective-permute-done.9.rest_8_) | copy-start | bytes 884740
  55.2 3.2 %copy-start.16 = (bf16[2,4,48,384]{3,2,1,0:T(8,128)(2,1)}, bf16[2,4,48,384]{3,2,1,0:T(8,128)(2,1)S(1)}, u32[]{:S(2)}) copy-start(bf16[2,4,48,384]{3,2,1,0:T(8,128)(2,1)S(1)} %collective-permute-done.8.rest_6_) | copy-start | bytes 884740
  55.2 2.7 %collective-permute-start.13 = (bf16[2,4,48,384]{3,2,1,0:T(8,128)(2,1)S(1)}, bf16[2,4,48,384]{3,2,1,0:T(8,128)(2,1)S(1)}, u32[]{:S(2)}, u32[]{:S(2)}) collective-permute-start(bf16[2,4,48,384]{3,2,1,0:T(8,128)(2,1)S(1)} %collective-permute-done.8.rest_6_), channel_id=1, source_target_pairs={{0,4},{4,0},{8,12},{12,8},{16,20},{20,16},{24,28},{28,24},{1,5},{5... | collective-permute-start | bytes 884744 | tf_op jit(solution)/shard_map/ppermute | solution.py:594
  55.4 3.0 %collective-permute-start.14 = (bf16[2,4,48,384]{3,2,1,0:T(8,128)(2,1)S(1)}, bf16[2,4,48,384]{3,2,1,0:T(8,128)(2,1)S(1)}, u32[]{:S(2)}, u32[]{:S(2)}) collective-permute-start(bf16[2,4,48,384]{3,2,1,0:T(8,128)(2,1)S(1)} %collective-permute-done.9.rest_8_), channel_id=1, source_target_pairs={{0,4},{4,0},{8,12},{12,8},{16,20},{20,16},{24,28},{28,24},{1,5},{5... | collective-permute-start | bytes 884744 | tf_op jit(solution)/shard_map/ppermute | solution.py:594
  55.8 2.6 %copy-start.6 = (bf16[4,4,48,384]{3,2,1,0:T(8,128)(2,1)}, bf16[4,4,48,384]{3,2,1,0:T(8,128)(2,1)S(1)}, u32[]{:S(2)}) copy-start(bf16[4,4,48,384]{3,2,1,0:T(8,128)(2,1)S(1)} %collective-permute-done.3.rest_1_) | copy-start | bytes 1769476
  56.7 1.8 %copy-start.7 = (bf16[4,4,48,384]{3,2,1,0:T(8,128)(2,1)}, bf16[4,4,48,384]{3,2,1,0:T(8,128)(2,1)S(1)}, u32[]{:S(2)}) copy-start(bf16[4,4,48,384]{3,2,1,0:T(8,128)(2,1)S(1)} %collective-permute-done.7.rest_5_) | copy-start | bytes 1769476
  57.5 0.9 copy-start.8
  57.9 0.7 copy-start.17
  58.7 0.7 copy-start.18
  76.9 8.4 %copy-start.27 = (bf16[192,768]{1,0:T(8,128)(2,1)S(1)}, bf16[192,768]{1,0:T(8,128)(2,1)}, u32[]{:S(2)}) copy-start(bf16[192,768]{1,0:T(8,128)(2,1)} %get-tuple-element.76) | copy-start | bytes 884740
  76.9 16.9 %copy-start.26 = (bf16[192,768]{1,0:T(8,128)(2,1)S(1)}, bf16[192,768]{1,0:T(8,128)(2,1)}, u32[]{:S(2)}) copy-start(bf16[192,768]{1,0:T(8,128)(2,1)} %get-tuple-element.77) | copy-start | bytes 884740
  76.9 16.9 %copy-start.25 = (bf16[192,768]{1,0:T(8,128)(2,1)S(1)}, bf16[192,768]{1,0:T(8,128)(2,1)}, u32[]{:S(2)}) copy-start(bf16[192,768]{1,0:T(8,128)(2,1)} %get-tuple-element.78) | copy-start | bytes 884740
  76.9 4.8 %collective-permute-start.15 = (bf16[16,4,48,384]{3,2,1,0:T(8,128)(2,1)}, bf16[16,4,48,384]{3,2,1,0:T(8,128)(2,1)S(1)}, u32[]{:S(2)}, u32[]{:S(2)}) collective-permute-start(bf16[16,4,48,384]{3,2,1,0:T(8,128)(2,1)} %get-tuple-element.74), channel_id=1, source_target_pairs={{0,4},{4,0},{8,12},{12,8},{16,20},{20,16},{24,28},{28,24},{1,5},{5... | collective-permute-start | bytes 7077896 | tf_op jit(solution)/shard_map/ppermute | solution.py:594
  81.7 19.6 %copy-start = (bf16[16,4,48,384]{3,2,1,0:T(8,128)(2,1)}, bf16[16,4,48,384]{3,2,1,0:T(8,128)(2,1)S(1)}, u32[]{:S(2)}) copy-start(bf16[16,4,48,384]{3,2,1,0:T(8,128)(2,1)S(1)} %collective-permute-done.15.got_ref) | copy-start | bytes 7077892
  84.1 15.4 %collective-permute-start.17 = (bf16[4,4,48,384]{3,2,1,0:T(8,128)(2,1)S(1)}, bf16[4,4,48,384]{3,2,1,0:T(8,128)(2,1)S(1)}, u32[]{:S(2)}, u32[]{:S(2)}) collective-permute-start(bf16[4,4,48,384]{3,2,1,0:T(8,128)(2,1)S(1)} %get-tuple-element.107), channel_id=1, source_target_pairs={{0,16},{4,20},{8,24},{12,28},{16,0},{20,4},{24,8},{28,12},{1,17},{... | collective-permute-start | bytes 1769480 | tf_op jit(solution)/shard_map/ppermute | solution.py:594
  84.7 15.1 %collective-permute-start.16 = (bf16[4,4,48,384]{3,2,1,0:T(8,128)(2,1)S(1)}, bf16[4,4,48,384]{3,2,1,0:T(8,128)(2,1)S(1)}, u32[]{:S(2)}, u32[]{:S(2)}) collective-permute-start(bf16[4,4,48,384]{3,2,1,0:T(8,128)(2,1)S(1)} %get-tuple-element.108), channel_id=1, source_target_pairs={{0,8},{4,12},{8,0},{12,4},{16,24},{20,28},{24,16},{28,20},{1,9},{5... | collective-permute-start | bytes 1769480 | tf_op jit(solution)/shard_map/ppermute | solution.py:594
  85.2 18.2 %collective-permute-start.20 = (bf16[192,768]{1,0:T(8,128)(2,1)S(1)}, bf16[192,768]{1,0:T(8,128)(2,1)S(1)}, u32[]{:S(2)}, u32[]{:S(2)}) collective-permute-start(bf16[192,768]{1,0:T(8,128)(2,1)S(1)} %copy-done.27), channel_id=1, source_target_pairs={{0,3},{1,0},{2,1},{3,2},{4,7},{5,4},{6,5},{7,6},{8,11},{9,8},{10,9... | collective-permute-start | bytes 884744 | tf_op jit(solution)/shard_map/ppermute | solution.py:589
  93.7 24.3 %collective-permute-start.21 = (bf16[192,768]{1,0:T(8,128)(2,1)S(1)}, bf16[192,768]{1,0:T(8,128)(2,1)S(1)}, u32[]{:S(2)}, u32[]{:S(2)}) collective-permute-start(bf16[192,768]{1,0:T(8,128)(2,1)S(1)} %copy-done.26), channel_id=1, source_target_pairs={{0,2},{1,3},{2,0},{3,1},{4,6},{5,7},{6,4},{7,5},{8,10},{9,11},{10,... | collective-permute-start | bytes 884744 | tf_op jit(solution)/shard_map/ppermute | solution.py:589
  93.7 24.3 %collective-permute-start.22 = (bf16[192,768]{1,0:T(8,128)(2,1)S(1)}, bf16[192,768]{1,0:T(8,128)(2,1)S(1)}, u32[]{:S(2)}, u32[]{:S(2)}) collective-permute-start(bf16[192,768]{1,0:T(8,128)(2,1)S(1)} %copy-done.25), channel_id=1, source_target_pairs={{0,1},{1,2},{2,3},{3,0},{4,5},{5,6},{6,7},{7,4},{8,9},{9,10},{10,1... | collective-permute-start | bytes 884744 | tf_op jit(solution)/shard_map/ppermute | solution.py:589
  99.5 18.6 %copy-start.2 = (bf16[4,4,48,384]{3,2,1,0:T(8,128)(2,1)}, bf16[4,4,48,384]{3,2,1,0:T(8,128)(2,1)S(1)}, u32[]{:S(2)}) copy-start(bf16[4,4,48,384]{3,2,1,0:T(8,128)(2,1)S(1)} %collective-permute-done.17.far_ref) | copy-start | bytes 1769476
  99.8 18.3 %copy-start.3 = (bf16[4,4,48,384]{3,2,1,0:T(8,128)(2,1)}, bf16[4,4,48,384]{3,2,1,0:T(8,128)(2,1)S(1)}, u32[]{:S(2)}) copy-start(bf16[4,4,48,384]{3,2,1,0:T(8,128)(2,1)S(1)} %collective-permute-done.16.near_ref) | copy-start | bytes 1769476
  101.3 16.8 %collective-permute-start.19 = (bf16[2,4,48,384]{3,2,1,0:T(8,128)(2,1)S(1)}, bf16[2,4,48,384]{3,2,1,0:T(8,128)(2,1)S(1)}, u32[]{:S(2)}, u32[]{:S(2)}) collective-permute-start(bf16[2,4,48,384]{3,2,1,0:T(8,128)(2,1)S(1)} %get-tuple-element.105), channel_id=1, source_target_pairs={{0,8},{4,12},{8,0},{12,4},{16,24},{20,28},{24,16},{28,20},{1,9},{5... | collective-permute-start | bytes 884744 | tf_op jit(solution)/shard_map/ppermute | solution.py:594
  101.9 16.2 %collective-permute-start.18 = (bf16[2,4,48,384]{3,2,1,0:T(8,128)(2,1)S(1)}, bf16[2,4,48,384]{3,2,1,0:T(8,128)(2,1)S(1)}, u32[]{:S(2)}, u32[]{:S(2)}) collective-permute-start(bf16[2,4,48,384]{3,2,1,0:T(8,128)(2,1)S(1)} %get-tuple-element.106), channel_id=1, source_target_pairs={{0,16},{4,20},{8,24},{12,28},{16,0},{20,4},{24,8},{28,12},{1,17},{... | collective-permute-start | bytes 884744 | tf_op jit(solution)/shard_map/ppermute | solution.py:594
  103.4 19.5 %copy-start.12 = (bf16[192,768]{1,0:T(8,128)(2,1)}, bf16[192,768]{1,0:T(8,128)(2,1)S(1)}, u32[]{:S(2)}) copy-start(bf16[192,768]{1,0:T(8,128)(2,1)S(1)} %collective-permute-done.20.rest_1_) | copy-start | bytes 884740
  118.0 4.8 %copy-start.14 = (bf16[192,768]{1,0:T(8,128)(2,1)}, bf16[192,768]{1,0:T(8,128)(2,1)S(1)}, u32[]{:S(2)}) copy-start(bf16[192,768]{1,0:T(8,128)(2,1)S(1)} %collective-permute-done.21.rest_2_) | copy-start | bytes 884740
  118.0 4.8 %copy-start.15 = (bf16[192,768]{1,0:T(8,128)(2,1)}, bf16[192,768]{1,0:T(8,128)(2,1)S(1)}, u32[]{:S(2)}) copy-start(bf16[192,768]{1,0:T(8,128)(2,1)S(1)} %collective-permute-done.22.rest_3_) | copy-start | bytes 884740
  118.1 0.8 copy-start.19
  118.1 0.9 copy-start.20
  122.9 12.9 %collective-permute-start.23 = (bf16[4,48,384]{2,1,0:T(8,128)(2,1)}, bf16[4,48,384]{2,1,0:T(8,128)(2,1)S(1)}, u32[]{:S(2)}, u32[]{:S(2)}) collective-permute-start(bf16[4,48,384]{2,1,0:T(8,128)(2,1)} %get-tuple-element.96), channel_id=1, source_target_pairs={{0,3},{1,0},{2,1},{3,2},{4,7},{5,4},{6,5},{7,6},{8,11},{9,8},{10,9... | collective-permute-start | bytes 442376 | tf_op jit(solution)/shard_map/ppermute | solution.py:589
  123.0 16.0 %collective-permute-start.24 = (bf16[4,48,384]{2,1,0:T(8,128)(2,1)}, bf16[4,48,384]{2,1,0:T(8,128)(2,1)S(1)}, u32[]{:S(2)}, u32[]{:S(2)}) collective-permute-start(bf16[4,48,384]{2,1,0:T(8,128)(2,1)} %get-tuple-element.97), channel_id=1, source_target_pairs={{0,2},{1,3},{2,0},{3,1},{4,6},{5,7},{6,4},{7,5},{8,10},{9,11},{10,... | collective-permute-start | bytes 442376 | tf_op jit(solution)/shard_map/ppermute | solution.py:589
  126.3 12.8 %collective-permute-start.25 = (bf16[4,48,384]{2,1,0:T(8,128)(2,1)}, bf16[4,48,384]{2,1,0:T(8,128)(2,1)S(1)}, u32[]{:S(2)}, u32[]{:S(2)}) collective-permute-start(bf16[4,48,384]{2,1,0:T(8,128)(2,1)} %get-tuple-element.98), channel_id=1, source_target_pairs={{0,1},{1,2},{2,3},{3,0},{4,5},{5,6},{6,7},{7,4},{8,9},{9,10},{10,1... | collective-permute-start | bytes 442376 | tf_op jit(solution)/shard_map/ppermute | solution.py:589
  135.8 10.4 %copy-start.22 = (bf16[4,48,384]{2,1,0:T(8,128)(2,1)}, bf16[4,48,384]{2,1,0:T(8,128)(2,1)S(1)}, u32[]{:S(2)}) copy-start(bf16[4,48,384]{2,1,0:T(8,128)(2,1)S(1)} %collective-permute-done.23.rest_1_) | copy-start | bytes 442372
  139.1 7.1 %copy-start.23 = (bf16[4,48,384]{2,1,0:T(8,128)(2,1)}, bf16[4,48,384]{2,1,0:T(8,128)(2,1)S(1)}, u32[]{:S(2)}) copy-start(bf16[4,48,384]{2,1,0:T(8,128)(2,1)S(1)} %collective-permute-done.24.rest_2_) | copy-start | bytes 442372
  139.1 7.1 %copy-start.24 = (bf16[4,48,384]{2,1,0:T(8,128)(2,1)}, bf16[4,48,384]{2,1,0:T(8,128)(2,1)S(1)}, u32[]{:S(2)}) copy-start(bf16[4,48,384]{2,1,0:T(8,128)(2,1)S(1)} %collective-permute-done.25.rest_3_) | copy-start | bytes 442372
  140.1 1.4 collective-permute-start.26
  142.6 13.2 %collective-permute-start.29 = (bf16[192,384]{1,0:T(8,128)(2,1)S(1)}, bf16[192,384]{1,0:T(8,128)(2,1)S(1)}, u32[]{:S(2)}, u32[]{:S(2)}) collective-permute-start(bf16[192,384]{1,0:T(8,128)(2,1)S(1)} %add_convert_fusion.4), channel_id=1, source_target_pairs={{0,24},{4,28},{8,16},{12,20},{16,8},{20,12},{24,0},{28,4},{1,25},{... | collective-permute-start | bytes 442376 | tf_op jit(solution)/shard_map/ppermute | solution.py:594
  145.1 10.7 %collective-permute-start.28 = (bf16[192,384]{1,0:T(8,128)(2,1)S(1)}, bf16[192,384]{1,0:T(8,128)(2,1)S(1)}, u32[]{:S(2)}, u32[]{:S(2)}) collective-permute-start(bf16[192,384]{1,0:T(8,128)(2,1)S(1)} %add_convert_fusion.4), channel_id=1, source_target_pairs={{0,16},{4,20},{8,24},{12,28},{16,0},{20,4},{24,8},{28,12},{1,17},{... | collective-permute-start | bytes 442376 | tf_op jit(solution)/shard_map/ppermute | solution.py:594
  145.6 10.2 %collective-permute-start.27 = (bf16[192,384]{1,0:T(8,128)(2,1)S(1)}, bf16[192,384]{1,0:T(8,128)(2,1)S(1)}, u32[]{:S(2)}, u32[]{:S(2)}) collective-permute-start(bf16[192,384]{1,0:T(8,128)(2,1)S(1)} %add_convert_fusion.4), channel_id=1, source_target_pairs={{0,8},{4,12},{8,0},{12,4},{16,24},{20,28},{24,16},{28,20},{1,9},{5... | collective-permute-start | bytes 442376 | tf_op jit(solution)/shard_map/ppermute | solution.py:594
where the time goes:
time: 157 us
  Pallas kernels  55.9 us (36%)
  waiting for transfers between devices  47.9 us (31%)
  starting transfers between devices  41.8 us (27%)
  other arithmetic  6.84 us (4%)
  local copies, waits for them, and re-layouts  3.21 us (2%)
    ppermute x12, waiting for transfers between devices, swap_groups(): got.append(lax.ppermute(sends[shift], 'grp', perm))  27.8 us
    ppermute x12, starting transfers between devices, swap_groups(): got.append(lax.ppermute(sends[shift], 'grp', perm))  27.5 us
    ppermute x18, waiting for transfers between devices, flip_rows(): lax.ppermute(values, 'rows', [(index, index ^ bits) for index in range(ro...  20.1 us
    pallas_call x1, Pallas kernels, attention(): pl.pallas_call(functools.partial(attention_kernel, groups=groups, row_par...  17.5 us
    ppermute x18, starting transfers between devices, flip_rows(): lax.ppermute(values, 'rows', [(index, index ^ bits) for index in range(ro...  14.4 us
    pallas_call x1, Pallas kernels, pair_bias(): pl.pallas_call(functools.partial(bias_kernel, groups=groups, batch=4), gr...  10.8 us
    pallas_call x1, Pallas kernels, pair_back(): pl.pallas_call(functools.partial(pair_back_kernel, groups=groups, calls=l...  9.62 us
    pallas_call x1, Pallas kernels, split_heads(): pl.pallas_call(functools.partial(finish_kernel, groups=groups, calls=call...  7.5 us
  transfers between devices with their start and end apart: 30, of which 13 were waited for; matrix products, arithmetic and copies ran while one was open for 1% of the time, Pallas kernels for 15%

commit v1 on v0

--- a/solution.py
+++ b/solution.py
@@ -122,6 +122,16 @@
     return both.astype(F32) - mm(both, means)
 
 
+def lane_pad(block, before, total):
+    rows, width = block.shape
+    pieces = [block]
+    if before:
+        pieces = [jnp.zeros((rows, before), block.dtype)] + pieces
+    if total > before + width:
+        pieces = pieces + [jnp.zeros((rows, total - before - width), block.dtype)]
+    return jnp.concatenate(pieces, axis=1)
+
+
 def bias_kernel(
     group_ref,
     rows_ref,
@@ -143,23 +153,18 @@
     group_own = group_ref[0]
     row_base = rows_ref[0] * 2 * half + pl.program_id(0) * step
     means = mean_matrix(channels)
-    weight = w_pair_ref[...]
-    left = jnp.concatenate(
-        [
-            jnp.concatenate([weight, jnp.zeros((heads, channels), BF16)], axis=1),
-            jnp.concatenate(
-                [
-                    jnp.zeros((heads, channels), BF16),
-                    jnp.full((heads, channels), 1.0 / channels, BF16),
-                ],
-                axis=1,
-            ),
-        ],
-        axis=0,
-    )
-    chain_cols = cols_ref[:, :cols]
+    weight = w_pair_ref[...].astype(F32).T.astype(BF16)
+    mean_part = jnp.full((channels, heads), 1.0 / channels, BF16)
+    mixed = []
+    for inner in range(2):
+        for part, offset in ((weight, 0), (mean_part, heads)):
+            for side in range(2):
+                mixed.append(lane_pad(part, 2 * heads * (2 * inner + side) + offset, 8 * heads))
+    mixed = jnp.concatenate(mixed, axis=0)
+    chain_all = cols_ref[...].reshape(1, groups * cols)
+    chain_cols = chain_all[:, :cols]
     for group in range(1, groups):
-        here = cols_ref[:, group * cols : (group + 1) * cols]
+        here = chain_all[:, group * cols : (group + 1) * cols]
         chain_cols = jnp.where(group_own == group, here, chain_cols)
     for head in range(heads):
         gains_ref[head : head + 1, :] = jnp.full((1, cols), gain_ref[head], F32)
@@ -169,25 +174,27 @@
         center = center_rows(pair_ref, first, batch, means)
         center_b = center.astype(BF16)
         square = (center * center).astype(BF16)
-        for inner in range(batch):
-            rows = slice(inner * cols, (inner + 1) * cols)
-            for side in range(2):
-                lanes = slice(side * channels, (side + 1) * channels)
-                right = jnp.concatenate([center_b[rows, lanes], square[rows, lanes]], axis=1)
-                sums = mm_nt(left, right)
-                inverse = lax.rsqrt(sums[heads : heads + 8] + EPSILON)
-                projected = sums[:heads] * inverse[:1]
-                stats_ref[side, first + inner, :heads, :] = projected
-                stats_ref[side, first + inner, heads:, :] = inverse
-                chain = chains_ref[row_base + side * half + first + inner]
-                same = (chain_cols == chain).astype(F32)
-                values = projected + gains_ref[...] * same
-                for tile, start, end in lane_tiles(cols):
-                    piece = values[:, start:end]
-                    if end - start < 128:
-                        blank = jnp.zeros((heads, 128 - end + start), F32)
-                        piece = jnp.concatenate([piece, blank], axis=1)
-                    flat_ref[side, tile, pl.ds(first + inner, heads, stride=step), :] = piece
+        for base in range(0, batch, 2):
+            one = slice(base * cols, (base + 1) * cols)
+            two = slice((base + 1) * cols, (base + 2) * cols)
+            left = jnp.concatenate(
+                [center_b[one], square[one], center_b[two], square[two]], axis=1
+            )
+            sums = mm(left, mixed).T
+            for inner in range(2):
+                row = first + base + inner
+                for side in range(2):
+                    top = 2 * heads * (2 * inner + side)
+                    inverse = lax.rsqrt(sums[top + heads : top + 2 * heads] + EPSILON)
+                    projected = sums[top : top + heads] * inverse
+                    stats_ref[side, row, :heads, :] = projected
+                    stats_ref[side, row, heads:, :] = inverse[:8]
+                    chain = chains_ref[row_base + side * half + row]
+                    same = (chain_cols == chain).astype(F32)
+                    values = projected + gains_ref[...] * same
+                    for tile, start, end in lane_tiles(cols):
+                        piece = lane_pad(values[:, start:end], 0, 128)
+                        flat_ref[side, tile, pl.ds(row, heads, stride=step), :] = piece
         return carry
 
     lax.fori_loop(0, step // batch, some_rows, 0)
@@ -223,7 +230,7 @@
             smem(),
             pl.BlockSpec((2, step, cols, channels), lambda t: (0, t, 0, 0)),
             pl.BlockSpec((heads, channels), lambda t: (0, 0)),
-            pl.BlockSpec((1, groups * cols), lambda t: (0, 0)),
+            pl.BlockSpec((groups * cols,), lambda t: (0,)),
         ],
         out_specs=[
             pl.BlockSpec((per_group, step, 2 * cols), lambda t: (0, t, 0)) for _ in range(groups)
@@ -246,7 +253,7 @@
         chain_gain,
         pair.reshape(2, half, cols, channels),
         w_pair.T,
-        chains.reshape(1, groups * cols),
+        chains,
     )
     return sends, stats
 
@@ -262,14 +269,16 @@
     group_own = group_ref[0]
     means = mean_matrix(channels)
     weight = w_pair_ref[...].astype(F32)
-    weight = weight - jnp.mean(weight, axis=-1, keepdims=True)
-    high = weight.astype(BF16)
-    low = (weight - high.astype(F32)).astype(BF16)
-    weights = jnp.concatenate([high, low, jnp.zeros((16, channels), BF16)], axis=0)
-    spread = lax.broadcasted_iota(jnp.int32, (2 * heads + 16, channels), 0)
-    spread = ((spread >= 2 * heads) & (spread < 2 * heads + 2)).astype(F32).astype(BF16)
-    weights = jnp.concatenate([weights, spread], axis=1)
-    blank = jnp.zeros((14, cols), F32)
+    weight = (weight - jnp.mean(weight, axis=-1, keepdims=True)).astype(BF16)
+    spread = lax.broadcasted_iota(jnp.int32, (heads, channels), 0)
+    spread = (spread < 2).astype(F32).astype(BF16)
+    block = jnp.concatenate(
+        [lane_pad(weight, 0, 2 * channels), lane_pad(spread, channels, 2 * channels)], axis=0
+    )
+    weights = jnp.concatenate(
+        [lane_pad(block, 2 * channels * place, 8 * channels) for place in range(4)], axis=0
+    )
+    blank = jnp.zeros((heads - 2, cols), F32)
     for number in range(groups * calls):
         call, slot = divmod(number, groups)
         source = lax.rem(group_own + slot, groups) * calls + call
@@ -285,9 +294,10 @@
     def some_rows(index, carry):
         first = index * batch
         center = center_rows(pair_ref, first, batch, means)
-        for side in range(2):
-            lefts = []
-            for inner in range(batch):
+        for base in range(0, batch, 2):
+            places = [(base + inner, side) for inner in range(2) for side in range(2)]
+            left = []
+            for inner, side in places:
                 grads = jnp.concatenate(
                     [
                         flat_ref[side, tile, pl.ds(first + inner, heads, stride=step), :][
@@ -303,17 +313,15 @@
                 scaled = grads * (inverse * factor)
                 cross = cross * (inverse * inverse * factor)
                 cross_high = cross.astype(BF16).astype(F32)
-                lefts.append(
-                    jnp.concatenate(
-                        [scaled, scaled, cross_high, cross - cross_high, blank], axis=0
-                    )
-                )
-            for inner in range(batch):
+                left += [scaled, cross_high, cross - cross_high, blank]
+            both = mm_tn(jnp.concatenate(left, axis=0).astype(BF16), weights)
+            for place, (inner, side) in enumerate(places):
                 rows = slice(inner * cols, (inner + 1) * cols)
                 lanes = slice(side * channels, (side + 1) * channels)
-                both = mm_tn(lefts[inner].astype(BF16), weights)
+                start = 2 * channels * place
+                middle, end = start + channels, start + 2 * channels
                 out_ref[side, first + inner] = (
-                    both[:, :channels] - center[rows, lanes] * both[:, channels:]
+                    both[:, start:middle] - center[rows, lanes] * both[:, middle:end]
                 ).astype(BF16)
         return carry
 
@@ -609,21 +617,19 @@
     return blocks, acts
 
 
-def add_last_kernel(keep_ref, got_ref, near_ref, far_ref, near_two_ref, far_two_ref, *out_refs):
-    head = pl.program_id(0)
-    lower = head < pl.num_programs(0) // 2
-    total = keep_ref[0].astype(F32) + got_ref[0].astype(F32)
-    total += jnp.where(lower, near_ref[0].astype(F32), far_ref[0].astype(F32))
-    total += jnp.where(lower, far_two_ref[0].astype(F32), near_two_ref[0].astype(F32))
-    total = total.astype(BF16)
-    for slot, out_ref in enumerate(out_refs):
-        out_ref[0] = total[slot]
-
-
-def scatter_rows(keep, give, grads, row_total):
+def add_last_kernel(own_ref, far_ref, near_ref, *out_refs):
+    heads = own_ref.shape[0]
+    half = heads // 2
+    for head in range(heads):
+        other = far_ref[head] if head < half else near_ref[head - half]
+        total = (own_ref[head].astype(F32) + other.astype(F32)).astype(BF16)
+        for slot, out_ref in enumerate(out_refs):
+            out_ref[head] = total[slot]
+
+
+def scatter_rows(keep, give, row_total):
     got = flip_rows(give, 1, row_total)
-    units, groups, half, lanes = keep.shape
-    heads = units // 4
+    heads = keep.shape[0] // 4
     part = heads // 2
 
     def add(first, count, *others):
@@ -634,24 +640,21 @@
 
     near = flip_rows(add(heads, heads), 2, row_total)
     far = flip_rows(add(2 * heads, heads), 4, row_total)
-    far_two = add(3 * heads, part, near[part:])
-    near_two = add(3 * heads + part, part, far[part:])
-    far_two = flip_rows(far_two, 4, row_total)
-    near_two = flip_rows(near_two, 2, row_total)
-    far_two, near_two, grads = lax.optimization_barrier((far_two, near_two, grads))
-    block = (1, groups, half, lanes)
-    whole = pl.BlockSpec(block, lambda h: (h, 0, 0, 0))
-    wrapped = pl.BlockSpec(block, lambda h: (lax.rem(h, part), 0, 0, 0))
-    sums = pl.pallas_call(
+    far_two = flip_rows(add(3 * heads, part, near[part:]), 4, row_total)
+    near_two = flip_rows(add(3 * heads + part, part, far[part:]), 2, row_total)
+    own = add(0, heads, jnp.concatenate([near[:part], far[:part]]))
+    return own, far_two, near_two
+
+
+def add_last(own, far_two, near_two):
+    heads, groups, half, lanes = own.shape
+    return pl.pallas_call(
         add_last_kernel,
-        grid=(heads,),
-        in_specs=[whole, whole] + [wrapped] * 4,
-        out_specs=[pl.BlockSpec((1, half, lanes), lambda h: (h, 0, 0))] * groups,
+        in_specs=[vmem()] * 3,
+        out_specs=[vmem()] * groups,
         out_shape=[jax.ShapeDtypeStruct((heads, half, lanes), BF16)] * groups,
         compiler_params=params(),
-    )(keep, got, near, far, near_two, far_two)
-    sums, grads = lax.optimization_barrier((sums, grads))
-    return sums, grads
+    )(own, far_two, near_two)
 
 
 def sum_rows(values, row_total):
@@ -723,8 +726,8 @@
     bias_all, acts = gather_rows(jnp.stack(bias_got), acts, row_total)
     grads_send, keep, give = attention(group_index, row_index, acts, bias_all, head_size)
     grads = swap_groups(grads_send, -1)
-    dbias_own, grads = scatter_rows(keep, give, grads, row_total)
-    dbias_back = swap_groups(dbias_own, -1)
+    own, far_two, near_two = scatter_rows(keep, give, row_total)
+    own, grads = lax.optimization_barrier((own, grads))
     updated, d_part = pl.pallas_call(
         functools.partial(finish_kernel, groups=groups, calls=calls),
         in_specs=[smem()] + [vmem()] * (12 + groups * calls),
@@ -750,7 +753,8 @@
         w_out,
         *grads,
     )
-    d_part, dbias_back = lax.optimization_barrier((d_part, dbias_back))
+    far_two, near_two, d_part = lax.optimization_barrier((far_two, near_two, d_part))
+    dbias_back = swap_groups(add_last(own, far_two, near_two), -1)
     d_single = sum_rows(d_part, row_total)
     d_pair = pair_back(pair, stats, dbias_back, w_pair, group_index, groups, float(tokens))
     return (updated[None], d_single, d_pair)

time: 157 us -> 157 us (level)
  waiting for transfers between devices: 47.9 us -> 51.8 us
  other arithmetic: 6.84 us -> 5.11 us
    ppermute x12, waiting for transfers between devices: 27.8 us -> 33.1 us  [swap_groups(): got.append(lax.ppermute(sends[shift], 'grp', perm))]
    pallas_call x1, Pallas kernels: 3.91 us -> 2.12 us  [add_last(): pl.pallas_call(add_last_kernel, in_specs=[vmem()] * 3, out_specs=[vmem()]...]
    convert_element_type x2 -> x3, other arithmetic: 3.87 us -> 2.98 us  [add(): return total.astype(BF16)]
  transfers between devices with their start and end apart: 30 -> 30, of which waited for: 13 -> 12; matrix products, arithmetic and copies ran while one was open for 1% -> 1% of each run, Pallas kernels for 15% -> 16%
where the time goes in v1:
time: 157 us
  Pallas kernels  55 us (35%)
  waiting for transfers between devices  51.8 us (33%)
  starting transfers between devices  41.6 us (26%)
  other arithmetic  5.11 us (3%)
  local copies, waits for them, and re-layouts  2.65 us (2%)
    ppermute x12, waiting for transfers between devices, swap_groups(): got.append(lax.ppermute(sends[shift], 'grp', perm))  33.1 us
    ppermute x12, starting transfers between devices, swap_groups(): got.append(lax.ppermute(sends[shift], 'grp', perm))  27.3 us
    ppermute x18, waiting for transfers between devices, flip_rows(): lax.ppermute(values, 'rows', [(index, index ^ bits) for index in range(ro...  18.7 us
    pallas_call x1, Pallas kernels, attention(): pl.pallas_call(functools.partial(attention_kernel, groups=groups, row_par...  17.4 us
    ppermute x18, starting transfers between devices, flip_rows(): lax.ppermute(values, 'rows', [(index, index ^ bits) for index in range(ro...  14.3 us
    pallas_call x1, Pallas kernels, pair_bias(): pl.pallas_call(functools.partial(bias_kernel, groups=groups, batch=4), gr...  11.9 us
    pallas_call x1, Pallas kernels, pair_back(): pl.pallas_call(functools.partial(pair_back_kernel, groups=groups, calls=l...  9.49 us
    pallas_call x1, Pallas kernels, split_heads(): pl.pallas_call(functools.partial(finish_kernel, groups=groups, calls=call...  7.5 us
  transfers between devices with their start and end apart: 30, of which 12 were waited for; matrix products, arithmetic and copies ran while one was open for 1% of the time, Pallas kernels for 16%

profile of v1, /device:TPU:0, one launch (start us, length us, event | category | flops | bytes accessed | tf_op | source)
XLA Modules:
  0.0 157.1 jit_solution(16496792034952824426)
XLA Ops:
  0.6 11.9 %shard_map.158 = (bf16[4,48,384]{2,1,0:T(8,128)(2,1)}, bf16[4,48,384]{2,1,0:T(8,128)(2,1)}, bf16[4,48,384]{2,1,0:T(8,128)(2,1)}, bf16[4,48,384]{2,1,0:T(8,128)(2,1)}, f32[2,48,24,192]{3,2,1,0:T(8,128)}) custom-call(s32[1]{0:T(128)} %bitcast.group_ref, s32[1]{0:T(128)} %bitcast.3.rows_ref.row_ref, s32[768]{0:T(1024)} %cols_ref.1, f32[16]{0:T(128)} %gain_ref.1, ...), custom_call_target="tpu_custom_call" | custom-call | tf_op jit(solution)/shard_map/pallas_call | solution.py:223
  12.6 3.0 %collective-permute-start = (bf16[4,48,384]{2,1,0:T(8,128)(2,1)}, bf16[4,48,384]{2,1,0:T(8,128)(2,1)S(1)}, u32[]{:S(2)}, u32[]{:S(2)}) collective-permute-start(bf16[4,48,384]{2,1,0:T(8,128)(2,1)} %get-tuple-element.46), channel_id=1, source_target_pairs={{0,1},{1,2},{2,3},{3,0},{4,5},{5,6},{6,7},{7,4},{8,9},{9,10},{10,1... | collective-permute-start | bytes 442376 | tf_op jit(solution)/shard_map/ppermute | solution.py:597
  15.6 2.6 %collective-permute-start.1 = (bf16[4,48,384]{2,1,0:T(8,128)(2,1)}, bf16[4,48,384]{2,1,0:T(8,128)(2,1)S(1)}, u32[]{:S(2)}, u32[]{:S(2)}) collective-permute-start(bf16[4,48,384]{2,1,0:T(8,128)(2,1)} %get-tuple-element.47), channel_id=1, source_target_pairs={{0,2},{1,3},{2,0},{3,1},{4,6},{5,7},{6,4},{7,5},{8,10},{9,11},{10,... | collective-permute-start | bytes 442376 | tf_op jit(solution)/shard_map/ppermute | solution.py:597
  18.2 1.3 collective-permute-start.2
  19.5 6.5 %shard_map.157 = (bf16[192,768]{1,0:T(8,128)(2,1)}, bf16[192,768]{1,0:T(8,128)(2,1)}, bf16[192,768]{1,0:T(8,128)(2,1)}, bf16[192,768]{1,0:T(8,128)(2,1)}, f32[192,768]{1,0:T(8,128)}, /*index=5*/f32[192,768]{1,0:T(8,128)}) custom-call(s32[1]{0:T(128)} %bitcast.group_ref, bf16[192,384]{1,0:T(8,128)(2,1)} %single_ref.3, bf16[192,768]{1,0:T(8,128)(2,1)} %bitcast.15, ...), custom_call_target="tpu_custom_call" | custom-call | tf_op jit(solution)/shard_map/pallas_call | solution.py:699
  26.1 0.0 collective-permute-done
  26.1 2.0 %collective-permute-done.1 = bf16[4,48,384]{2,1,0:T(8,128)(2,1)S(1)} collective-permute-done((bf16[4,48,384]{2,1,0:T(8,128)(2,1)}, bf16[4,48,384]{2,1,0:T(8,128)(2,1)S(1)}, u32[]{:S(2)}, u32[]{:S(2)}) %collective-permute-start.1) | collective-permute-done | bytes 147488 | tf_op jit(solution)/shard_map/ppermute | solution.py:597
  28.1 0.0 collective-permute-done.2
  28.1 0.1 pad_maximum_fusion.rest_0_
  28.2 1.6 %collective-permute-start.6 = (bf16[4,4,48,384]{3,2,1,0:T(8,128)(2,1)S(1)}, bf16[4,4,48,384]{3,2,1,0:T(8,128)(2,1)S(1)}, u32[]{:S(2)}, u32[]{:S(2)}) collective-permute-start(bf16[4,4,48,384]{3,2,1,0:T(8,128)(2,1)S(1)} %pad_maximum_fusion.rest_0_), channel_id=1, source_target_pairs={{0,16},{4,20},{8,24},{12,28},{16,0},{20,4},{24,8},{28,12},{1,17},{... | collective-permute-start | bytes 1769480 | tf_op jit(solution)/shard_map/ppermute | solution.py:602
  29.8 1.5 collective-permute-start.4
  31.3 3.6 %collective-permute-start.10 = (bf16[192,768]{1,0:T(8,128)(2,1)S(1)}, bf16[192,768]{1,0:T(8,128)(2,1)S(1)}, u32[]{:S(2)}, u32[]{:S(2)}) collective-permute-start(bf16[192,768]{1,0:T(8,128)(2,1)S(1)} %copy-done.29), channel_id=1, source_target_pairs={{0,1},{1,2},{2,3},{3,0},{4,5},{5,6},{6,7},{7,4},{8,9},{9,10},{10,1... | collective-permute-start | bytes 884744 | tf_op jit(solution)/shard_map/ppermute | solution.py:597
  34.9 1.6 %collective-permute-start.11 = (bf16[192,768]{1,0:T(8,128)(2,1)S(1)}, bf16[192,768]{1,0:T(8,128)(2,1)S(1)}, u32[]{:S(2)}, u32[]{:S(2)}) collective-permute-start(bf16[192,768]{1,0:T(8,128)(2,1)S(1)} %copy-done.28), channel_id=1, source_target_pairs={{0,2},{1,3},{2,0},{3,1},{4,6},{5,7},{6,4},{7,5},{8,10},{9,11},{10,... | collective-permute-start | bytes 884744 | tf_op jit(solution)/shard_map/ppermute | solution.py:597
  36.6 0.8 collective-permute-start.12
  37.4 6.1 %collective-permute-done.6.rest_4_ = bf16[4,4,48,384]{3,2,1,0:T(8,128)(2,1)S(1)} collective-permute-done((bf16[4,4,48,384]{3,2,1,0:T(8,128)(2,1)S(1)}, bf16[4,4,48,384]{3,2,1,0:T(8,128)(2,1)S(1)}, u32[]{:S(2)}, u32[]{:S(2)}) %collective-permute-start.6) | collective-permute-done | bytes 589856 | tf_op jit(solution)/shard_map/ppermute | solution.py:602
  43.5 1.6 collective-permute-start.9
  45.0 0.0 collective-permute-done.4.rest_2_
  45.1 1.6 %collective-permute-start.8 = (bf16[2,4,48,384]{3,2,1,0:T(8,128)(2,1)S(1)}, bf16[2,4,48,384]{3,2,1,0:T(8,128)(2,1)S(1)}, u32[]{:S(2)}, u32[]{:S(2)}) collective-permute-start(bf16[2,4,48,384]{3,2,1,0:T(8,128)(2,1)S(1)} %slice.64), channel_id=1, source_target_pairs={{0,16},{4,20},{8,24},{12,28},{16,0},{20,4},{24,8},{28,12},{1,17},{... | collective-permute-start | bytes 884744 | tf_op jit(solution)/shard_map/ppermute | solution.py:602
  46.7 0.0 collective-permute-start.3
  46.7 7.7 %collective-permute-done.11.rest_12_ = bf16[192,768]{1,0:T(8,128)(2,1)S(1)} collective-permute-done((bf16[192,768]{1,0:T(8,128)(2,1)S(1)}, bf16[192,768]{1,0:T(8,128)(2,1)S(1)}, u32[]{:S(2)}, u32[]{:S(2)}) %collective-permute-start.11) | collective-permute-done | bytes 294944 | tf_op jit(solution)/shard_map/ppermute | solution.py:597
  54.3 0.0 collective-permute-start.7
  54.3 0.0 collective-permute-done.12.rest_13_
  54.4 0.5 collective-permute-start.5
  54.9 0.0 copy-start.12
  54.9 0.1 collective-permute-start.13
  55.0 0.4 collective-permute-start.14
  55.5 0.9 collective-permute-done.7.rest_5_
  56.3 0.8 collective-permute-done.5.rest_3_
  57.2 0.4 collective-permute-done.13.rest_7_
  57.6 0.4 collective-permute-done.14.rest_9_
  58.1 0.2 copy-done.16
  58.3 0.7 copy-done.17
  59.0 17.4 %shard_map.159 = (bf16[192,768]{1,0:T(8,128)(2,1)}, bf16[192,768]{1,0:T(8,128)(2,1)}, bf16[192,768]{1,0:T(8,128)(2,1)}, bf16[192,768]{1,0:T(8,128)(2,1)}, bf16[1...) custom-call(s32[1]{0:T(128)} %bitcast.group_ref, s32[1]{0:T(128)} %bitcast.3.rows_ref.row_ref, ...), custom_call_target="tpu_custom_call" | custom-call | tf_op jit(solution)/shard_map/pallas_call | solution.py:501
  76.5 0.2 collective-permute-start.15
  76.7 4.6 %collective-permute-done.15 = bf16[16,4,48,384]{3,2,1,0:T(8,128)(2,1)S(1)} collective-permute-done((bf16[16,4,48,384]{3,2,1,0:T(8,128)(2,1)}, bf16[16,4,48,384]{3,2,1,0:T(8,128)(2,1)S(1)}, u32[]{:S(2)}, u32[]{:S(2)}) %collective-permute-start.15) | collective-permute-done | bytes 2359328 | tf_op jit(solution)/shard_map/ppermute | solution.py:602
  81.3 1.7 %add_convert_fusion.2 = (bf16[4,4,48,384]{3,2,1,0:T(8,128)(2,1)S(1)}, bf16[4,4,48,384]{3,2,1,0:T(8,128)(2,1)S(1)}) fusion(bf16[16,4,48,384]{3,2,1,0:T(8,128)(2,1)S(1)} %collective-permute-done.15, bf16[16,4,48,384]{3,2,1,0:T(8,128)(2,1)} %get-tuple-element.62), kind=kLoop, calls=%fused_computation.2 | loop fusion | flops 2359296 | bytes 3538944 | tf_op jit(solution)/shard_map/convert_element_type | solution.py:639
  83.0 0.6 collective-permute-start.16
  83.6 0.5 collective-permute-start.17
  84.1 8.5 %collective-permute-start.18 = (bf16[192,768]{1,0:T(8,128)(2,1)S(1)}, bf16[192,768]{1,0:T(8,128)(2,1)S(1)}, u32[]{:S(2)}, u32[]{:S(2)}) collective-permute-start(bf16[192,768]{1,0:T(8,128)(2,1)S(1)} %copy-done.26), channel_id=1, source_target_pairs={{0,3},{1,0},{2,1},{3,2},{4,7},{5,4},{6,5},{7,6},{8,11},{9,8},{10,9... | collective-permute-start | bytes 884744 | tf_op jit(solution)/shard_map/ppermute | solution.py:597
  92.7 0.6 collective-permute-start.20
  93.3 5.1 %collective-permute-done.16 = bf16[4,4,48,384]{3,2,1,0:T(8,128)(2,1)S(1)} collective-permute-done((bf16[4,4,48,384]{3,2,1,0:T(8,128)(2,1)S(1)}, bf16[4,4,48,384]{3,2,1,0:T(8,128)(2,1)S(1)}, u32[]{:S(2)}, u32[]{:S(2)}) %collective-permute-start.16) | collective-permute-done | bytes 589856 | tf_op jit(solution)/shard_map/ppermute | solution.py:602
  98.5 0.3 collective-permute-done.17
  98.7 0.2 add_convert_fusion.3
  99.0 1.6 collective-permute-start.22
  100.5 0.5 collective-permute-start.21
  101.1 1.0 add_convert_fusion.own_ref
  102.1 14.8 %collective-permute-done.19.rest_2_ = bf16[192,768]{1,0:T(8,128)(2,1)S(1)} collective-permute-done((bf16[192,768]{1,0:T(8,128)(2,1)S(1)}, bf16[192,768]{1,0:T(8,128)(2,1)S(1)}, u32[]{:S(2)}, u32[]{:S(2)}) %collective-permute-start.19) | collective-permute-done | bytes 294944 | tf_op jit(solution)/shard_map/ppermute | solution.py:597
  117.0 0.7 copy-done.14
  117.7 0.1 copy-done.15
  117.8 7.5 %shard_map.160 = (bf16[192,768]{1,0:T(8,128)(2,1)}, f32[192,384]{1,0:T(8,128)}) custom-call(s32[1]{0:T(128)} %bitcast.group_ref, bf16[192,384]{1,0:T(8,128)(2,1)} %single_ref.3, bf16[192,768]{1,0:T(8,128)(2,1)} %bitcast.16, bf16[192,768]{1,0:T(8,128)(2,1)} %bitcast.18, f32[192,768]{1,0:T(8,128)} %get-tuple-element.43.gamma_ref, ...), custom_call_target="tpu_custom_call" | custom-call | tf_op jit(solution)/shard_map/pallas_call | solution.py:731
  125.3 0.0 copy-start.19
  125.3 1.2 convert_element_type.96
  126.5 0.1 collective-permute-start.23
  126.6 2.1 %shard_map.161 = (bf16[4,48,384]{2,1,0:T(8,128)(2,1)}, bf16[4,48,384]{2,1,0:T(8,128)(2,1)}, bf16[4,48,384]{2,1,0:T(8,128)(2,1)}, bf16[4,48,384]{2,1,0:T(8,128)(2,1)}) custom-call(bf16[4,4,48,384]{3,2,1,0:T(8,128)(2,1)} %add_convert_fusion.own_ref, bf16[2,4,48,384]{3,2,1,0:T(8,128)(2,1)} %copy-done.19, bf16[2,4,48,384]{3,2,1,0:T(8,128)(2,1)} %copy-done.18), custom_call_target="tpu_custom_call" | custom-call | tf_op jit(solution)/shard_map/pallas_call | solution.py:651
  128.8 3.2 %collective-permute-start.28 = (bf16[4,48,384]{2,1,0:T(8,128)(2,1)}, bf16[4,48,384]{2,1,0:T(8,128)(2,1)S(1)}, u32[]{:S(2)}, u32[]{:S(2)}) collective-permute-start(bf16[4,48,384]{2,1,0:T(8,128)(2,1)} %get-tuple-element.81), channel_id=1, source_target_pairs={{0,2},{1,3},{2,0},{3,1},{4,6},{5,7},{6,4},{7,5},{8,10},{9,11},{10,... | collective-permute-start | bytes 442376 | tf_op jit(solution)/shard_map/ppermute | solution.py:597
  131.9 2.0 %collective-permute-start.29 = (bf16[4,48,384]{2,1,0:T(8,128)(2,1)}, bf16[4,48,384]{2,1,0:T(8,128)(2,1)S(1)}, u32[]{:S(2)}, u32[]{:S(2)}) collective-permute-start(bf16[4,48,384]{2,1,0:T(8,128)(2,1)} %get-tuple-element.82), channel_id=1, source_target_pairs={{0,1},{1,2},{2,3},{3,0},{4,5},{5,6},{6,7},{7,4},{8,9},{9,10},{10,1... | collective-permute-start | bytes 442376 | tf_op jit(solution)/shard_map/ppermute | solution.py:597
  134.0 2.5 %collective-permute-start.26 = (bf16[192,384]{1,0:T(8,128)(2,1)S(1)}, bf16[192,384]{1,0:T(8,128)(2,1)S(1)}, u32[]{:S(2)}, u32[]{:S(2)}) collective-permute-start(bf16[192,384]{1,0:T(8,128)(2,1)S(1)} %add_convert_fusion.5), channel_id=1, source_target_pairs={{0,24},{4,28},{8,16},{12,20},{16,8},{20,12},{24,0},{28,4},{1,25},{... | collective-permute-start | bytes 442376 | tf_op jit(solution)/shard_map/ppermute | solution.py:602
  136.5 0.5 collective-permute-start.25
  137.0 0.5 collective-permute-start.24
  137.6 8.6 %collective-permute-done.28.rest_2_ = bf16[4,48,384]{2,1,0:T(8,128)(2,1)S(1)} collective-permute-done((bf16[4,48,384]{2,1,0:T(8,128)(2,1)}, bf16[4,48,384]{2,1,0:T(8,128)(2,1)S(1)}, u32[]{:S(2)}, u32[]{:S(2)}) %collective-permute-start.28) | collective-permute-done | bytes 147488 | tf_op jit(solution)/shard_map/ppermute | solution.py:597
  146.1 0.7 copy-done.22
  146.8 0.0 copy-done.23
  146.8 9.5 %shard_map.162 = bf16[2,48,192,128]{3,2,1,0:T(8,128)(2,1)} custom-call(s32[1]{0:T(128)} %bitcast.group_ref, bf16[2,48,192,128]{3,2,1,0:T(8,128)(2,1)} %bitcast.13, f32[2,48,24,192]{3,2,1,0:T(8,128)} %get-tuple-element.75.stats_ref, bf16[16,128]{1,0:T(8,128)(2,1)} %bitcast.24, bf16[4,48,384]{2,1,0:T(8,128)(2,1)} %get-tuple-element.79.rest_0_, ...), custom_call_target="tpu_custom_call" | custom-call | tf_op jit(solution)/shard_map/pallas_call | solution.py:338
  156.3 0.8 add_add_fusion
  (73 shorter events, 0.3 us)
Async XLA Ops:
  12.6 13.5 %collective-permute-start = (bf16[4,48,384]{2,1,0:T(8,128)(2,1)}, bf16[4,48,384]{2,1,0:T(8,128)(2,1)S(1)}, u32[]{:S(2)}, u32[]{:S(2)}) collective-permute-start(bf16[4,48,384]{2,1,0:T(8,128)(2,1)} %get-tuple-element.46), channel_id=1, source_target_pairs={{0,1},{1,2},{2,3},{3,0},{4,5},{5,6},{6,7},{7,4},{8,9},{9,10},{10,1... | collective-permute-start | bytes 442376 | tf_op jit(solution)/shard_map/ppermute | solution.py:597
  15.6 12.5 %collective-permute-start.1 = (bf16[4,48,384]{2,1,0:T(8,128)(2,1)}, bf16[4,48,384]{2,1,0:T(8,128)(2,1)S(1)}, u32[]{:S(2)}, u32[]{:S(2)}) collective-permute-start(bf16[4,48,384]{2,1,0:T(8,128)(2,1)} %get-tuple-element.47), channel_id=1, source_target_pairs={{0,2},{1,3},{2,0},{3,1},{4,6},{5,7},{6,4},{7,5},{8,10},{9,11},{10,... | collective-permute-start | bytes 442376 | tf_op jit(solution)/shard_map/ppermute | solution.py:597
  18.2 9.9 %collective-permute-start.2 = (bf16[4,48,384]{2,1,0:T(8,128)(2,1)}, bf16[4,48,384]{2,1,0:T(8,128)(2,1)S(1)}, u32[]{:S(2)}, u32[]{:S(2)}) collective-permute-start(bf16[4,48,384]{2,1,0:T(8,128)(2,1)} %get-tuple-element.48), channel_id=1, source_target_pairs={{0,3},{1,0},{2,1},{3,2},{4,7},{5,4},{6,5},{7,6},{8,11},{9,8},{10,9... | collective-permute-start | bytes 442376 | tf_op jit(solution)/shard_map/ppermute | solution.py:597
  19.5 8.6 %copy-start.20 = (bf16[4,48,384]{2,1,0:T(8,128)(2,1)S(1)}, bf16[4,48,384]{2,1,0:T(8,128)(2,1)}, u32[]{:S(2)}) copy-start(bf16[4,48,384]{2,1,0:T(8,128)(2,1)} %get-tuple-element.53) | copy-start | bytes 442372
  26.1 5.2 %copy-start.29 = (bf16[192,768]{1,0:T(8,128)(2,1)S(1)}, bf16[192,768]{1,0:T(8,128)(2,1)}, u32[]{:S(2)}) copy-start(bf16[192,768]{1,0:T(8,128)(2,1)} %get-tuple-element.50) | copy-start | bytes 884740
  26.1 8.8 %copy-start.28 = (bf16[192,768]{1,0:T(8,128)(2,1)S(1)}, bf16[192,768]{1,0:T(8,128)(2,1)}, u32[]{:S(2)}) copy-start(bf16[192,768]{1,0:T(8,128)(2,1)} %get-tuple-element.51) | copy-start | bytes 884740
  26.1 10.5 %copy-start.27 = (bf16[192,768]{1,0:T(8,128)(2,1)S(1)}, bf16[192,768]{1,0:T(8,128)(2,1)}, u32[]{:S(2)}) copy-start(bf16[192,768]{1,0:T(8,128)(2,1)} %get-tuple-element.52) | copy-start | bytes 884740
  28.2 29.8 %copy-start = (bf16[4,4,48,384]{3,2,1,0:T(8,128)(2,1)}, bf16[4,4,48,384]{3,2,1,0:T(8,128)(2,1)S(1)}, u32[]{:S(2)}) copy-start(bf16[4,4,48,384]{3,2,1,0:T(8,128)(2,1)S(1)} %pad_maximum_fusion.rest_0_) | copy-start | bytes 1769476
  28.2 15.2 %collective-permute-start.6 = (bf16[4,4,48,384]{3,2,1,0:T(8,128)(2,1)S(1)}, bf16[4,4,48,384]{3,2,1,0:T(8,128)(2,1)S(1)}, u32[]{:S(2)}, u32[]{:S(2)}) collective-permute-start(bf16[4,4,48,384]{3,2,1,0:T(8,128)(2,1)S(1)} %pad_maximum_fusion.rest_0_), channel_id=1, source_target_pairs={{0,16},{4,20},{8,24},{12,28},{16,0},{20,4},{24,8},{28,12},{1,17},{... | collective-permute-start | bytes 1769480 | tf_op jit(solution)/shard_map/ppermute | solution.py:602
  29.8 15.2 %collective-permute-start.4 = (bf16[4,4,48,384]{3,2,1,0:T(8,128)(2,1)S(1)}, bf16[4,4,48,384]{3,2,1,0:T(8,128)(2,1)S(1)}, u32[]{:S(2)}, u32[]{:S(2)}) collective-permute-start(bf16[4,4,48,384]{3,2,1,0:T(8,128)(2,1)S(1)} %pad_maximum_fusion.rest_0_), channel_id=1, source_target_pairs={{0,8},{4,12},{8,0},{12,4},{16,24},{20,28},{24,16},{28,20},{1,9},{5... | collective-permute-start | bytes 1769480 | tf_op jit(solution)/shard_map/ppermute | solution.py:602
  31.3 15.4 %collective-permute-start.10 = (bf16[192,768]{1,0:T(8,128)(2,1)S(1)}, bf16[192,768]{1,0:T(8,128)(2,1)S(1)}, u32[]{:S(2)}, u32[]{:S(2)}) collective-permute-start(bf16[192,768]{1,0:T(8,128)(2,1)S(1)} %copy-done.29), channel_id=1, source_target_pairs={{0,1},{1,2},{2,3},{3,0},{4,5},{5,6},{6,7},{7,4},{8,9},{9,10},{10,1... | collective-permute-start | bytes 884744 | tf_op jit(solution)/shard_map/ppermute | solution.py:597
  34.9 19.4 %collective-permute-start.11 = (bf16[192,768]{1,0:T(8,128)(2,1)S(1)}, bf16[192,768]{1,0:T(8,128)(2,1)S(1)}, u32[]{:S(2)}, u32[]{:S(2)}) collective-permute-start(bf16[192,768]{1,0:T(8,128)(2,1)S(1)} %copy-done.28), channel_id=1, source_target_pairs={{0,2},{1,3},{2,0},{3,1},{4,6},{5,7},{6,4},{7,5},{8,10},{9,11},{10,... | collective-permute-start | bytes 884744 | tf_op jit(solution)/shard_map/ppermute | solution.py:597
  36.6 17.8 %collective-permute-start.12 = (bf16[192,768]{1,0:T(8,128)(2,1)S(1)}, bf16[192,768]{1,0:T(8,128)(2,1)S(1)}, u32[]{:S(2)}, u32[]{:S(2)}) collective-permute-start(bf16[192,768]{1,0:T(8,128)(2,1)S(1)} %copy-done.27), channel_id=1, source_target_pairs={{0,3},{1,0},{2,1},{3,2},{4,7},{5,4},{6,5},{7,6},{8,11},{9,8},{10,9... | collective-permute-start | bytes 884744 | tf_op jit(solution)/shard_map/ppermute | solution.py:597
  43.4 14.6 %copy-start.2 = (bf16[4,4,48,384]{3,2,1,0:T(8,128)(2,1)}, bf16[4,4,48,384]{3,2,1,0:T(8,128)(2,1)S(1)}, u32[]{:S(2)}) copy-start(bf16[4,4,48,384]{3,2,1,0:T(8,128)(2,1)S(1)} %collective-permute-done.6.rest_4_) | copy-start | bytes 1769476
  43.5 11.4 %collective-permute-start.9 = (bf16[2,4,48,384]{3,2,1,0:T(8,128)(2,1)S(1)}, bf16[2,4,48,384]{3,2,1,0:T(8,128)(2,1)S(1)}, u32[]{:S(2)}, u32[]{:S(2)}) collective-permute-start(bf16[2,4,48,384]{3,2,1,0:T(8,128)(2,1)S(1)} %slice.65), channel_id=1, source_target_pairs={{0,8},{4,12},{8,0},{12,4},{16,24},{20,28},{24,16},{28,20},{1,9},{5... | collective-permute-start | bytes 884744 | tf_op jit(solution)/shard_map/ppermute | solution.py:602
  45.0 13.0 %copy-start.3 = (bf16[4,4,48,384]{3,2,1,0:T(8,128)(2,1)}, bf16[4,4,48,384]{3,2,1,0:T(8,128)(2,1)S(1)}, u32[]{:S(2)}) copy-start(bf16[4,4,48,384]{3,2,1,0:T(8,128)(2,1)S(1)} %collective-permute-done.4.rest_2_) | copy-start | bytes 1769476
  45.1 9.8 %collective-permute-start.8 = (bf16[2,4,48,384]{3,2,1,0:T(8,128)(2,1)S(1)}, bf16[2,4,48,384]{3,2,1,0:T(8,128)(2,1)S(1)}, u32[]{:S(2)}, u32[]{:S(2)}) collective-permute-start(bf16[2,4,48,384]{3,2,1,0:T(8,128)(2,1)S(1)} %slice.64), channel_id=1, source_target_pairs={{0,16},{4,20},{8,24},{12,28},{16,0},{20,4},{24,8},{28,12},{1,17},{... | collective-permute-start | bytes 884744 | tf_op jit(solution)/shard_map/ppermute | solution.py:602
  46.6 11.4 %copy-start.8 = (bf16[192,768]{1,0:T(8,128)(2,1)}, bf16[192,768]{1,0:T(8,128)(2,1)S(1)}, u32[]{:S(2)}) copy-start(bf16[192,768]{1,0:T(8,128)(2,1)S(1)} %collective-permute-done.10.rest_11_) | copy-start | bytes 884740
  46.7 8.8 %collective-permute-start.3 = (bf16[4,4,48,384]{3,2,1,0:T(8,128)(2,1)S(1)}, bf16[4,4,48,384]{3,2,1,0:T(8,128)(2,1)S(1)}, u32[]{:S(2)}, u32[]{:S(2)}) collective-permute-start(bf16[4,4,48,384]{3,2,1,0:T(8,128)(2,1)S(1)} %pad_maximum_fusion.rest_0_), channel_id=1, source_target_pairs={{0,4},{4,0},{8,12},{12,8},{16,20},{20,16},{24,28},{28,24},{1,5},{5... | collective-permute-start | bytes 1769480 | tf_op jit(solution)/shard_map/ppermute | solution.py:602
  54.3 3.7 %copy-start.9 = (bf16[192,768]{1,0:T(8,128)(2,1)}, bf16[192,768]{1,0:T(8,128)(2,1)S(1)}, u32[]{:S(2)}) copy-start(bf16[192,768]{1,0:T(8,128)(2,1)S(1)} %collective-permute-done.11.rest_12_) | copy-start | bytes 884740
  54.3 2.0 %collective-permute-start.7 = (bf16[4,4,48,384]{3,2,1,0:T(8,128)(2,1)S(1)}, bf16[4,4,48,384]{3,2,1,0:T(8,128)(2,1)S(1)}, u32[]{:S(2)}, u32[]{:S(2)}) collective-permute-start(bf16[4,4,48,384]{3,2,1,0:T(8,128)(2,1)S(1)} %collective-permute-done.6.rest_4_), channel_id=1, source_target_pairs={{0,4},{4,0},{8,12},{12,8},{16,20},{20,16},{24,28},{28,24},{1,5},{5... | collective-permute-start | bytes 1769480 | tf_op jit(solution)/shard_map/ppermute | solution.py:602
  54.3 3.7 %copy-start.10 = (bf16[192,768]{1,0:T(8,128)(2,1)}, bf16[192,768]{1,0:T(8,128)(2,1)S(1)}, u32[]{:S(2)}) copy-start(bf16[192,768]{1,0:T(8,128)(2,1)S(1)} %collective-permute-done.12.rest_13_) | copy-start | bytes 884740
  54.4 2.8 %collective-permute-start.5 = (bf16[4,4,48,384]{3,2,1,0:T(8,128)(2,1)S(1)}, bf16[4,4,48,384]{3,2,1,0:T(8,128)(2,1)S(1)}, u32[]{:S(2)}, u32[]{:S(2)}) collective-permute-start(bf16[4,4,48,384]{3,2,1,0:T(8,128)(2,1)S(1)} %collective-permute-done.4.rest_2_), channel_id=1, source_target_pairs={{0,4},{4,0},{8,12},{12,8},{16,20},{20,16},{24,28},{28,24},{1,5},{5... | collective-permute-start | bytes 1769480 | tf_op jit(solution)/shard_map/ppermute | solution.py:602
  54.9 3.2 %copy-start.11 = (bf16[2,4,48,384]{3,2,1,0:T(8,128)(2,1)}, bf16[2,4,48,384]{3,2,1,0:T(8,128)(2,1)S(1)}, u32[]{:S(2)}) copy-start(bf16[2,4,48,384]{3,2,1,0:T(8,128)(2,1)S(1)} %collective-permute-done.9.rest_8_) | copy-start | bytes 884740
  54.9 3.2 %copy-start.12 = (bf16[2,4,48,384]{3,2,1,0:T(8,128)(2,1)}, bf16[2,4,48,384]{3,2,1,0:T(8,128)(2,1)S(1)}, u32[]{:S(2)}) copy-start(bf16[2,4,48,384]{3,2,1,0:T(8,128)(2,1)S(1)} %collective-permute-done.8.rest_6_) | copy-start | bytes 884740
  54.9 2.7 %collective-permute-start.13 = (bf16[2,4,48,384]{3,2,1,0:T(8,128)(2,1)S(1)}, bf16[2,4,48,384]{3,2,1,0:T(8,128)(2,1)S(1)}, u32[]{:S(2)}, u32[]{:S(2)}) collective-permute-start(bf16[2,4,48,384]{3,2,1,0:T(8,128)(2,1)S(1)} %collective-permute-done.8.rest_6_), channel_id=1, source_target_pairs={{0,4},{4,0},{8,12},{12,8},{16,20},{20,16},{24,28},{28,24},{1,5},{5... | collective-permute-start | bytes 884744 | tf_op jit(solution)/shard_map/ppermute | solution.py:602
  55.0 3.0 %collective-permute-start.14 = (bf16[2,4,48,384]{3,2,1,0:T(8,128)(2,1)S(1)}, bf16[2,4,48,384]{3,2,1,0:T(8,128)(2,1)S(1)}, u32[]{:S(2)}, u32[]{:S(2)}) collective-permute-start(bf16[2,4,48,384]{3,2,1,0:T(8,128)(2,1)S(1)} %collective-permute-done.9.rest_8_), channel_id=1, source_target_pairs={{0,4},{4,0},{8,12},{12,8},{16,20},{20,16},{24,28},{28,24},{1,5},{5... | collective-permute-start | bytes 884744 | tf_op jit(solution)/shard_map/ppermute | solution.py:602
  55.5 2.6 %copy-start.5 = (bf16[4,4,48,384]{3,2,1,0:T(8,128)(2,1)}, bf16[4,4,48,384]{3,2,1,0:T(8,128)(2,1)S(1)}, u32[]{:S(2)}) copy-start(bf16[4,4,48,384]{3,2,1,0:T(8,128)(2,1)S(1)} %collective-permute-done.3.rest_1_) | copy-start | bytes 1769476
  56.3 1.8 %copy-start.6 = (bf16[4,4,48,384]{3,2,1,0:T(8,128)(2,1)}, bf16[4,4,48,384]{3,2,1,0:T(8,128)(2,1)S(1)}, u32[]{:S(2)}) copy-start(bf16[4,4,48,384]{3,2,1,0:T(8,128)(2,1)S(1)} %collective-permute-done.7.rest_5_) | copy-start | bytes 1769476
  57.2 0.9 copy-start.7
  57.6 0.7 copy-start.16
  58.3 0.7 copy-start.17
  76.5 4.8 %collective-permute-start.15 = (bf16[16,4,48,384]{3,2,1,0:T(8,128)(2,1)}, bf16[16,4,48,384]{3,2,1,0:T(8,128)(2,1)S(1)}, u32[]{:S(2)}, u32[]{:S(2)}) collective-permute-start(bf16[16,4,48,384]{3,2,1,0:T(8,128)(2,1)} %get-tuple-element.63), channel_id=1, source_target_pairs={{0,4},{4,0},{8,12},{12,8},{16,20},{20,16},{24,28},{28,24},{1,5},{5... | collective-permute-start | bytes 7077896 | tf_op jit(solution)/shard_map/ppermute | solution.py:602
  81.3 2.8 %copy-start.26 = (bf16[192,768]{1,0:T(8,128)(2,1)S(1)}, bf16[192,768]{1,0:T(8,128)(2,1)}, u32[]{:S(2)}) copy-start(bf16[192,768]{1,0:T(8,128)(2,1)} %get-tuple-element.65) | copy-start | bytes 884740
  81.3 11.4 %copy-start.25 = (bf16[192,768]{1,0:T(8,128)(2,1)S(1)}, bf16[192,768]{1,0:T(8,128)(2,1)}, u32[]{:S(2)}) copy-start(bf16[192,768]{1,0:T(8,128)(2,1)} %get-tuple-element.66) | copy-start | bytes 884740
  81.3 11.4 %copy-start.24 = (bf16[192,768]{1,0:T(8,128)(2,1)S(1)}, bf16[192,768]{1,0:T(8,128)(2,1)}, u32[]{:S(2)}) copy-start(bf16[192,768]{1,0:T(8,128)(2,1)} %get-tuple-element.67) | copy-start | bytes 884740
  81.3 17.4 %copy-start.1 = (bf16[16,4,48,384]{3,2,1,0:T(8,128)(2,1)S(1)}, bf16[16,4,48,384]{3,2,1,0:T(8,128)(2,1)}, u32[]{:S(2)}) copy-start(bf16[16,4,48,384]{3,2,1,0:T(8,128)(2,1)} %get-tuple-element.62) | copy-start | bytes 7077892
  83.0 15.4 %collective-permute-start.16 = (bf16[4,4,48,384]{3,2,1,0:T(8,128)(2,1)S(1)}, bf16[4,4,48,384]{3,2,1,0:T(8,128)(2,1)S(1)}, u32[]{:S(2)}, u32[]{:S(2)}) collective-permute-start(bf16[4,4,48,384]{3,2,1,0:T(8,128)(2,1)S(1)} %get-tuple-element.85), channel_id=1, source_target_pairs={{0,8},{4,12},{8,0},{12,4},{16,24},{20,28},{24,16},{28,20},{1,9},{5... | collective-permute-start | bytes 1769480 | tf_op jit(solution)/shard_map/ppermute | solution.py:602
  83.6 15.1 %collective-permute-start.17 = (bf16[4,4,48,384]{3,2,1,0:T(8,128)(2,1)S(1)}, bf16[4,4,48,384]{3,2,1,0:T(8,128)(2,1)S(1)}, u32[]{:S(2)}, u32[]{:S(2)}) collective-permute-start(bf16[4,4,48,384]{3,2,1,0:T(8,128)(2,1)S(1)} %get-tuple-element.86), channel_id=1, source_target_pairs={{0,16},{4,20},{8,24},{12,28},{16,0},{20,4},{24,8},{28,12},{1,17},{... | collective-permute-start | bytes 1769480 | tf_op jit(solution)/shard_map/ppermute | solution.py:602
  84.1 18.0 %collective-permute-start.18 = (bf16[192,768]{1,0:T(8,128)(2,1)S(1)}, bf16[192,768]{1,0:T(8,128)(2,1)S(1)}, u32[]{:S(2)}, u32[]{:S(2)}) collective-permute-start(bf16[192,768]{1,0:T(8,128)(2,1)S(1)} %copy-done.26), channel_id=1, source_target_pairs={{0,3},{1,0},{2,1},{3,2},{4,7},{5,4},{6,5},{7,6},{8,11},{9,8},{10,9... | collective-permute-start | bytes 884744 | tf_op jit(solution)/shard_map/ppermute | solution.py:597
  92.7 24.3 %collective-permute-start.19 = (bf16[192,768]{1,0:T(8,128)(2,1)S(1)}, bf16[192,768]{1,0:T(8,128)(2,1)S(1)}, u32[]{:S(2)}, u32[]{:S(2)}) collective-permute-start(bf16[192,768]{1,0:T(8,128)(2,1)S(1)} %copy-done.25), channel_id=1, source_target_pairs={{0,2},{1,3},{2,0},{3,1},{4,6},{5,7},{6,4},{7,5},{8,10},{9,11},{10,... | collective-permute-start | bytes 884744 | tf_op jit(solution)/shard_map/ppermute | solution.py:597
  92.7 24.3 %collective-permute-start.20 = (bf16[192,768]{1,0:T(8,128)(2,1)S(1)}, bf16[192,768]{1,0:T(8,128)(2,1)S(1)}, u32[]{:S(2)}, u32[]{:S(2)}) collective-permute-start(bf16[192,768]{1,0:T(8,128)(2,1)S(1)} %copy-done.24), channel_id=1, source_target_pairs={{0,1},{1,2},{2,3},{3,0},{4,5},{5,6},{6,7},{7,4},{8,9},{9,10},{10,1... | collective-permute-start | bytes 884744 | tf_op jit(solution)/shard_map/ppermute | solution.py:597
  99.0 26.3 %collective-permute-start.22 = (bf16[2,4,48,384]{3,2,1,0:T(8,128)(2,1)S(1)}, bf16[2,4,48,384]{3,2,1,0:T(8,128)(2,1)S(1)}, u32[]{:S(2)}, u32[]{:S(2)}) collective-permute-start(bf16[2,4,48,384]{3,2,1,0:T(8,128)(2,1)S(1)} %get-tuple-element.83), channel_id=1, source_target_pairs={{0,8},{4,12},{8,0},{12,4},{16,24},{20,28},{24,16},{28,20},{1,9},{5... | collective-permute-start | bytes 884744 | tf_op jit(solution)/shard_map/ppermute | solution.py:602
  100.5 24.8 %collective-permute-start.21 = (bf16[2,4,48,384]{3,2,1,0:T(8,128)(2,1)S(1)}, bf16[2,4,48,384]{3,2,1,0:T(8,128)(2,1)S(1)}, u32[]{:S(2)}, u32[]{:S(2)}) collective-permute-start(bf16[2,4,48,384]{3,2,1,0:T(8,128)(2,1)S(1)} %get-tuple-element.84), channel_id=1, source_target_pairs={{0,16},{4,20},{8,24},{12,28},{16,0},{20,4},{24,8},{28,12},{1,17},{... | collective-permute-start | bytes 884744 | tf_op jit(solution)/shard_map/ppermute | solution.py:602
  102.1 14.8 %copy-start.13 = (bf16[192,768]{1,0:T(8,128)(2,1)}, bf16[192,768]{1,0:T(8,128)(2,1)S(1)}, u32[]{:S(2)}) copy-start(bf16[192,768]{1,0:T(8,128)(2,1)S(1)} %collective-permute-done.18.rest_1_) | copy-start | bytes 884740
  117.0 0.7 copy-start.14
  117.0 0.8 copy-start.15
  125.3 8.7 %copy-start.4 = (f32[192,384]{1,0:T(8,128)S(1)}, f32[192,384]{1,0:T(8,128)}, u32[]{:S(2)}) copy-start(f32[192,384]{1,0:T(8,128)} %get-tuple-element.74) | copy-start | bytes 884740
  125.3 1.3 copy-start.18
  125.3 1.3 copy-start.19
  126.5 7.4 %collective-permute-start.23 = (bf16[192,384]{1,0:T(8,128)(2,1)S(1)}, bf16[192,384]{1,0:T(8,128)(2,1)S(1)}, u32[]{:S(2)}, u32[]{:S(2)}) collective-permute-start(bf16[192,384]{1,0:T(8,128)(2,1)S(1)} %convert_element_type.96), channel_id=1, source_target_pairs={{0,4},{4,0},{8,12},{12,8},{16,20},{20,16},{24,28},{28,24},{1,5},{5... | collective-permute-start | bytes 442376 | tf_op jit(solution)/shard_map/ppermute | solution.py:602
  128.8 8.2 %collective-permute-start.27 = (bf16[4,48,384]{2,1,0:T(8,128)(2,1)}, bf16[4,48,384]{2,1,0:T(8,128)(2,1)S(1)}, u32[]{:S(2)}, u32[]{:S(2)}) collective-permute-start(bf16[4,48,384]{2,1,0:T(8,128)(2,1)} %get-tuple-element.80), channel_id=1, source_target_pairs={{0,3},{1,0},{2,1},{3,2},{4,7},{5,4},{6,5},{7,6},{8,11},{9,8},{10,9... | collective-permute-start | bytes 442376 | tf_op jit(solution)/shard_map/ppermute | solution.py:597
  128.8 17.3 %collective-permute-start.28 = (bf16[4,48,384]{2,1,0:T(8,128)(2,1)}, bf16[4,48,384]{2,1,0:T(8,128)(2,1)S(1)}, u32[]{:S(2)}, u32[]{:S(2)}) collective-permute-start(bf16[4,48,384]{2,1,0:T(8,128)(2,1)} %get-tuple-element.81), channel_id=1, source_target_pairs={{0,2},{1,3},{2,0},{3,1},{4,6},{5,7},{6,4},{7,5},{8,10},{9,11},{10,... | collective-permute-start | bytes 442376 | tf_op jit(solution)/shard_map/ppermute | solution.py:597
  131.9 14.2 %collective-permute-start.29 = (bf16[4,48,384]{2,1,0:T(8,128)(2,1)}, bf16[4,48,384]{2,1,0:T(8,128)(2,1)S(1)}, u32[]{:S(2)}, u32[]{:S(2)}) collective-permute-start(bf16[4,48,384]{2,1,0:T(8,128)(2,1)} %get-tuple-element.82), channel_id=1, source_target_pairs={{0,1},{1,2},{2,3},{3,0},{4,5},{5,6},{6,7},{7,4},{8,9},{9,10},{10,1... | collective-permute-start | bytes 442376 | tf_op jit(solution)/shard_map/ppermute | solution.py:597
  134.0 22.3 %collective-permute-start.26 = (bf16[192,384]{1,0:T(8,128)(2,1)S(1)}, bf16[192,384]{1,0:T(8,128)(2,1)S(1)}, u32[]{:S(2)}, u32[]{:S(2)}) collective-permute-start(bf16[192,384]{1,0:T(8,128)(2,1)S(1)} %add_convert_fusion.5), channel_id=1, source_target_pairs={{0,24},{4,28},{8,16},{12,20},{16,8},{20,12},{24,0},{28,4},{1,25},{... | collective-permute-start | bytes 442376 | tf_op jit(solution)/shard_map/ppermute | solution.py:602
  136.5 19.8 %collective-permute-start.25 = (bf16[192,384]{1,0:T(8,128)(2,1)S(1)}, bf16[192,384]{1,0:T(8,128)(2,1)S(1)}, u32[]{:S(2)}, u32[]{:S(2)}) collective-permute-start(bf16[192,384]{1,0:T(8,128)(2,1)S(1)} %add_convert_fusion.5), channel_id=1, source_target_pairs={{0,16},{4,20},{8,24},{12,28},{16,0},{20,4},{24,8},{28,12},{1,17},{... | collective-permute-start | bytes 442376 | tf_op jit(solution)/shard_map/ppermute | solution.py:602
  137.0 9.1 %copy-start.21 = (bf16[4,48,384]{2,1,0:T(8,128)(2,1)}, bf16[4,48,384]{2,1,0:T(8,128)(2,1)S(1)}, u32[]{:S(2)}) copy-start(bf16[4,48,384]{2,1,0:T(8,128)(2,1)S(1)} %collective-permute-done.27.rest_1_) | copy-start | bytes 442372
  137.0 19.3 %collective-permute-start.24 = (bf16[192,384]{1,0:T(8,128)(2,1)S(1)}, bf16[192,384]{1,0:T(8,128)(2,1)S(1)}, u32[]{:S(2)}, u32[]{:S(2)}) collective-permute-start(bf16[192,384]{1,0:T(8,128)(2,1)S(1)} %add_convert_fusion.5), channel_id=1, source_target_pairs={{0,8},{4,12},{8,0},{12,4},{16,24},{20,28},{24,16},{28,20},{1,9},{5... | collective-permute-start | bytes 442376 | tf_op jit(solution)/shard_map/ppermute | solution.py:602
  146.1 0.7 copy-start.22
  146.1 0.7 copy-start.23

commit v2 on v1

--- a/solution.py
+++ b/solution.py
@@ -88,7 +88,7 @@
     def put(kind, values):
         rounded = values.astype(BF16)
         for group in range(groups):
-            slot = lax.rem(group - group_own + groups, groups)
+            slot = group_own ^ group
             for call in range(calls):
                 feature = (group * calls + call) * part
                 lane = (call * 4 + kind) * part
@@ -116,7 +116,7 @@
 def center_rows(pair_ref, first, batch, means):
     _, _, cols, channels = pair_ref.shape
     both = jnp.concatenate(
-        [pair_ref[side, pl.ds(first, batch)].reshape(batch * cols, channels) for side in range(2)],
+        [pair_ref[side, first : first + batch].reshape(batch * cols, channels) for side in range(2)],
         axis=1,
     )
     return both.astype(F32) - mm(both, means)
@@ -169,8 +169,7 @@
     for head in range(heads):
         gains_ref[head : head + 1, :] = jnp.full((1, cols), gain_ref[head], F32)
 
-    def some_rows(index, carry):
-        first = index * batch
+    for first in range(0, step, batch):
         center = center_rows(pair_ref, first, batch, means)
         center_b = center.astype(BF16)
         square = (center * center).astype(BF16)
@@ -195,11 +194,8 @@
                     for tile, start, end in lane_tiles(cols):
                         piece = lane_pad(values[:, start:end], 0, 128)
                         flat_ref[side, tile, pl.ds(row, heads, stride=step), :] = piece
-        return carry
-
-    lax.fori_loop(0, step // batch, some_rows, 0)
     for head in range(heads):
-        slot = lax.rem(head // per_group - group_own + groups, groups)
+        slot = group_own ^ (head // per_group)
         values = jnp.concatenate(
             [
                 flat_ref[side, tile, head * step : (head + 1) * step, : end - start]
@@ -281,7 +277,7 @@
     blank = jnp.zeros((heads - 2, cols), F32)
     for number in range(groups * calls):
         call, slot = divmod(number, groups)
-        source = lax.rem(group_own + slot, groups) * calls + call
+        source = (group_own ^ slot) * calls + call
         for head in range(per_call):
             values = grad_refs[number][head].astype(F32)
             top = pl.multiple_of((source * per_call + head) * step, step)
@@ -291,8 +287,7 @@
                         :, side * cols + start : side * cols + end
                     ]
 
-    def some_rows(index, carry):
-        first = index * batch
+    for first in range(0, step, batch):
         center = center_rows(pair_ref, first, batch, means)
         for base in range(0, batch, 2):
             places = [(base + inner, side) for inner in range(2) for side in range(2)]
@@ -323,9 +318,6 @@
                 out_ref[side, first + inner] = (
                     both[:, start:middle] - center[rows, lanes] * both[:, middle:end]
                 ).astype(BF16)
-        return carry
-
-    lax.fori_loop(0, step // batch, some_rows, 0)
 
 
 def pair_back(pair, stats, grads, w_pair, group_index, groups, factor):
@@ -412,7 +404,7 @@
 
     def places(row_part):
         first = row_part * (2 * half)
-        slot = lax.rem(group_own - first // cols + groups, groups)
+        slot = group_own ^ (first // cols)
         for side in range(2):
             top = slot * cols + lax.rem(first, cols) + side * half
             top = pl.multiple_of(top, 16)
@@ -556,7 +548,7 @@
     part = width // 4
     for slot in range(groups):
         for call in range(calls):
-            stage_ref[lax.rem(group_ref[0] + slot, groups), call] = got_refs[
+            stage_ref[group_ref[0] ^ slot, call] = got_refs[
                 call * groups + slot
             ][...]
 
@@ -586,15 +578,15 @@
     grad_snorm += mm_nt(grad_input.astype(BF16), w_beta_ref[...])
     grad_snorm += mm_nt(pre_gate, w_outgate_ref[...])
     single_norm, single_inv = norm_rows(single_ref[...].astype(F32))
-    d_single_ref[...] = norm_back(grad_snorm, single_norm, single_inv)
-
-
-def swap_groups(sends, direction):
+    d_single_ref[...] = norm_back(grad_snorm, single_norm, single_inv).astype(BF16)
+
+
+def swap_groups(sends):
     groups = len(sends)
     got = [sends[0]]
-    for shift in range(1, groups):
-        perm = [(index, (index + direction * shift) % groups) for index in range(groups)]
-        got.append(lax.ppermute(sends[shift], "grp", perm))
+    for bits in range(1, groups):
+        perm = [(index, index ^ bits) for index in range(groups)]
+        got.append(lax.ppermute(sends[bits], "grp", perm))
     return got
 
 
@@ -657,9 +649,11 @@
     )(own, far_two, near_two)
 
 
-def sum_rows(values, row_total):
-    mine = values.astype(BF16)
-    both = (mine.astype(F32) + flip_rows(mine, 1, row_total).astype(F32)).astype(BF16)
+def sum_cores(mine, row_total):
+    return (mine.astype(F32) + flip_rows(mine, 1, row_total).astype(F32)).astype(BF16)
+
+
+def sum_chips(both, row_total):
     near, far, last = (flip_rows(both, bits, row_total).astype(F32) for bits in (2, 4, 6))
     return (both.astype(F32) + near) + (far + last)
 
@@ -693,7 +687,7 @@
     bias_send, stats = pair_bias(
         pair, w_pair, chain_gain, chains, group_index, row_index, groups
     )
-    bias_got = swap_groups(bias_send, 1)
+    bias_got = swap_groups(bias_send)
     noised = noised[0]
     cotangent = cotangent[0]
     *acts_send, cond_gamma, out_gate = pl.pallas_call(
@@ -722,18 +716,20 @@
         w_out,
     )
     bias_got, _ = lax.optimization_barrier((bias_got, acts_send))
-    acts = swap_groups(acts_send, 1)
+    acts = swap_groups(acts_send)
     bias_all, acts = gather_rows(jnp.stack(bias_got), acts, row_total)
     grads_send, keep, give = attention(group_index, row_index, acts, bias_all, head_size)
-    grads = swap_groups(grads_send, -1)
+    grads = swap_groups(grads_send)
     own, far_two, near_two = scatter_rows(keep, give, row_total)
-    own, grads = lax.optimization_barrier((own, grads))
+    far_two, near_two, grads = lax.optimization_barrier((far_two, near_two, grads))
+    dbias_own, grads = lax.optimization_barrier((add_last(own, far_two, near_two), grads))
+    dbias_back = swap_groups(dbias_own)
     updated, d_part = pl.pallas_call(
         functools.partial(finish_kernel, groups=groups, calls=calls),
         in_specs=[smem()] + [vmem()] * (12 + groups * calls),
         out_shape=[
             jax.ShapeDtypeStruct((cols, width), BF16),
-            jax.ShapeDtypeStruct(single.shape, F32),
+            jax.ShapeDtypeStruct(single.shape, BF16),
         ],
         scratch_shapes=[pltpu.VMEM((groups, calls, cols, 4 * width // (groups * calls)), BF16)],
         compiler_params=params(),
@@ -753,9 +749,9 @@
         w_out,
         *grads,
     )
-    far_two, near_two, d_part = lax.optimization_barrier((far_two, near_two, d_part))
-    dbias_back = swap_groups(add_last(own, far_two, near_two), -1)
-    d_single = sum_rows(d_part, row_total)
+    d_part, dbias_back = lax.optimization_barrier((d_part, dbias_back))
+    d_both = sum_cores(d_part, row_total)
+    d_single = sum_chips(d_both, row_total)
     d_pair = pair_back(pair, stats, dbias_back, w_pair, group_index, groups, float(tokens))
     return (updated[None], d_single, d_pair)
 
@@ -917,7 +913,8 @@
     def on_device(*args):
         pair, noised, w_pair = args[1], args[3], args[11]
         fits = (
-            pair.shape[0] % 32 == 0
+            groups in (2, 4)
+            and pair.shape[0] % 32 == 0
             and pair.shape[1] % pair.shape[0] == 0
             and row_total == 8
             and noised.shape[0] == 1

time: 157 us -> 148 us (0.943)
  Pallas kernels: 55 us -> 50.1 us
  starting transfers between devices: 41.6 us -> 37 us
    ppermute x18, waiting for transfers between devices: 18.7 us -> 24.1 us  [flip_rows(): lax.ppermute(values, 'rows', [(index, index ^ bits) for index in range(ro...]
    ppermute x12, waiting for transfers between devices: 33.1 us -> 28.9 us  [swap_groups(): got.append(lax.ppermute(sends[bits], 'grp', perm))]
    pallas_call x1, Pallas kernels: 11.9 us -> 8.45 us  [pair_bias(): pl.pallas_call(functools.partial(bias_kernel, groups=groups, batch=4), gr...]
    ppermute x12, starting transfers between devices: 27.3 us -> 23.9 us  [swap_groups(): got.append(lax.ppermute(sends[bits], 'grp', perm))]
  transfers between devices with their start and end apart: 30 -> 30, of which waited for: 12 -> 14; matrix products, arithmetic and copies ran while one was open for 1% -> 1% of each run, Pallas kernels for 16% -> 15%
where the time goes in v2:
time: 148 us
  waiting for transfers between devices  53 us (36%)
  Pallas kernels  50.1 us (34%)
  starting transfers between devices  37 us (25%)
  other arithmetic  4.81 us (3%)
  local copies, waits for them, and re-layouts  2 us (1%)
    ppermute x12, waiting for transfers between devices, swap_groups(): got.append(lax.ppermute(sends[bits], 'grp', perm))  28.9 us
    ppermute x18, waiting for transfers between devices, flip_rows(): lax.ppermute(values, 'rows', [(index, index ^ bits) for index in range(ro...  24.1 us
    ppermute x12, starting transfers between devices, swap_groups(): got.append(lax.ppermute(sends[bits], 'grp', perm))  23.9 us
    pallas_call x1, Pallas kernels, attention(): pl.pallas_call(functools.partial(attention_kernel, groups=groups, row_par...  17.5 us
    ppermute x18, starting transfers between devices, flip_rows(): lax.ppermute(values, 'rows', [(index, index ^ bits) for index in range(ro...  13.1 us
    pallas_call x1, Pallas kernels, pair_bias(): pl.pallas_call(functools.partial(bias_kernel, groups=groups, batch=4), gr...  8.45 us
    pallas_call x1, Pallas kernels, pair_back(): pl.pallas_call(functools.partial(pair_back_kernel, groups=groups, calls=l...  8.2 us
    pallas_call x1, Pallas kernels, split_heads(): pl.pallas_call(functools.partial(finish_kernel, groups=groups, calls=call...  7.5 us
  transfers between devices with their start and end apart: 30, of which 14 were waited for; matrix products, arithmetic and copies ran while one was open for 1% of the time, Pallas kernels for 15%

profile of v2, /device:TPU:0, one launch (start us, length us, event | category | flops | bytes accessed | tf_op | source)
XLA Modules:
  0.0 147.8 jit_solution(12162707412524291423)
XLA Ops:
  0.6 8.4 %shard_map.158 = (bf16[4,48,384]{2,1,0:T(8,128)(2,1)}, bf16[4,48,384]{2,1,0:T(8,128)(2,1)}, bf16[4,48,384]{2,1,0:T(8,128)(2,1)}, bf16[4,48,384]{2,1,0:T(8,128)(2,1)}, f32[2,48,24,192]{3,2,1,0:T(8,128)}) custom-call(s32[1]{0:T(128)} %bitcast.group_ref, s32[1]{0:T(128)} %bitcast.3.rows_ref.row_ref, s32[768]{0:T(1024)} %cols_ref.1, f32[16]{0:T(128)} %gain_ref.1, ...), custom_call_target="tpu_custom_call" | custom-call | tf_op jit(solution)/shard_map/pallas_call | solution.py:219
  9.1 3.0 %collective-permute-start = (bf16[4,48,384]{2,1,0:T(8,128)(2,1)}, bf16[4,48,384]{2,1,0:T(8,128)(2,1)S(1)}, u32[]{:S(2)}, u32[]{:S(2)}) collective-permute-start(bf16[4,48,384]{2,1,0:T(8,128)(2,1)} %get-tuple-element.57), channel_id=1, source_target_pairs={{0,1},{1,0},{2,3},{3,2},{4,5},{5,4},{6,7},{7,6},{8,9},{9,8},{10,11... | collective-permute-start | bytes 442376 | tf_op jit(solution)/shard_map/ppermute | solution.py:589
  12.1 2.6 %collective-permute-start.1 = (bf16[4,48,384]{2,1,0:T(8,128)(2,1)}, bf16[4,48,384]{2,1,0:T(8,128)(2,1)S(1)}, u32[]{:S(2)}, u32[]{:S(2)}) collective-permute-start(bf16[4,48,384]{2,1,0:T(8,128)(2,1)} %get-tuple-element.58), channel_id=1, source_target_pairs={{0,2},{1,3},{2,0},{3,1},{4,6},{5,7},{6,4},{7,5},{8,10},{9,11},{10,... | collective-permute-start | bytes 442376 | tf_op jit(solution)/shard_map/ppermute | solution.py:589
  14.7 0.0 collective-permute-start.2
  14.7 6.4 %shard_map.157 = (bf16[192,768]{1,0:T(8,128)(2,1)}, bf16[192,768]{1,0:T(8,128)(2,1)}, bf16[192,768]{1,0:T(8,128)(2,1)}, bf16[192,768]{1,0:T(8,128)(2,1)}, f32[192,768]{1,0:T(8,128)}, /*index=5*/f32[192,768]{1,0:T(8,128)}) custom-call(s32[1]{0:T(128)} %bitcast.group_ref, bf16[192,384]{1,0:T(8,128)(2,1)} %single_ref.3, bf16[192,768]{1,0:T(8,128)(2,1)} %bitcast.15, ...), custom_call_target="tpu_custom_call" | custom-call | tf_op jit(solution)/shard_map/pallas_call | solution.py:693
  21.1 0.0 copy-start.27
  21.1 0.0 collective-permute-done
  21.1 5.2 %collective-permute-done.1 = bf16[4,48,384]{2,1,0:T(8,128)(2,1)S(1)} collective-permute-done((bf16[4,48,384]{2,1,0:T(8,128)(2,1)}, bf16[4,48,384]{2,1,0:T(8,128)(2,1)S(1)}, u32[]{:S(2)}, u32[]{:S(2)}) %collective-permute-start.1) | collective-permute-done | bytes 147488 | tf_op jit(solution)/shard_map/ppermute | solution.py:589
  26.3 0.1 pad_maximum_fusion.rest_0_
  26.4 1.6 %collective-permute-start.6 = (bf16[4,4,48,384]{3,2,1,0:T(8,128)(2,1)S(1)}, bf16[4,4,48,384]{3,2,1,0:T(8,128)(2,1)S(1)}, u32[]{:S(2)}, u32[]{:S(2)}) collective-permute-start(bf16[4,4,48,384]{3,2,1,0:T(8,128)(2,1)S(1)} %pad_maximum_fusion.rest_0_), channel_id=1, source_target_pairs={{0,16},{4,20},{8,24},{12,28},{16,0},{20,4},{24,8},{28,12},{1,17},{... | collective-permute-start | bytes 1769480 | tf_op jit(solution)/shard_map/ppermute | solution.py:594
  28.0 1.5 %collective-permute-start.4 = (bf16[4,4,48,384]{3,2,1,0:T(8,128)(2,1)S(1)}, bf16[4,4,48,384]{3,2,1,0:T(8,128)(2,1)S(1)}, u32[]{:S(2)}, u32[]{:S(2)}) collective-permute-start(bf16[4,4,48,384]{3,2,1,0:T(8,128)(2,1)S(1)} %pad_maximum_fusion.rest_0_), channel_id=1, source_target_pairs={{0,8},{4,12},{8,0},{12,4},{16,24},{20,28},{24,16},{28,20},{1,9},{5... | collective-permute-start | bytes 1769480 | tf_op jit(solution)/shard_map/ppermute | solution.py:594
  29.5 2.3 %collective-permute-start.10 = (bf16[192,768]{1,0:T(8,128)(2,1)S(1)}, bf16[192,768]{1,0:T(8,128)(2,1)S(1)}, u32[]{:S(2)}, u32[]{:S(2)}) collective-permute-start(bf16[192,768]{1,0:T(8,128)(2,1)S(1)} %copy-done.28), channel_id=1, source_target_pairs={{0,1},{1,0},{2,3},{3,2},{4,5},{5,4},{6,7},{7,6},{8,9},{9,8},{10,11... | collective-permute-start | bytes 884744 | tf_op jit(solution)/shard_map/ppermute | solution.py:589
  31.8 1.1 collective-permute-start.11
  32.9 1.5 collective-permute-start.12
  34.4 4.7 %collective-permute-done.6.rest_4_ = bf16[4,4,48,384]{3,2,1,0:T(8,128)(2,1)S(1)} collective-permute-done((bf16[4,4,48,384]{3,2,1,0:T(8,128)(2,1)S(1)}, bf16[4,4,48,384]{3,2,1,0:T(8,128)(2,1)S(1)}, u32[]{:S(2)}, u32[]{:S(2)}) %collective-permute-start.6) | collective-permute-done | bytes 589856 | tf_op jit(solution)/shard_map/ppermute | solution.py:594
  39.1 1.6 %collective-permute-start.9 = (bf16[2,4,48,384]{3,2,1,0:T(8,128)(2,1)S(1)}, bf16[2,4,48,384]{3,2,1,0:T(8,128)(2,1)S(1)}, u32[]{:S(2)}, u32[]{:S(2)}) collective-permute-start(bf16[2,4,48,384]{3,2,1,0:T(8,128)(2,1)S(1)} %slice.65), channel_id=1, source_target_pairs={{0,8},{4,12},{8,0},{12,4},{16,24},{20,28},{24,16},{28,20},{1,9},{5... | collective-permute-start | bytes 884744 | tf_op jit(solution)/shard_map/ppermute | solution.py:594
  40.7 1.7 %collective-permute-done.4.rest_2_ = bf16[4,4,48,384]{3,2,1,0:T(8,128)(2,1)S(1)} collective-permute-done((bf16[4,4,48,384]{3,2,1,0:T(8,128)(2,1)S(1)}, bf16[4,4,48,384]{3,2,1,0:T(8,128)(2,1)S(1)}, u32[]{:S(2)}, u32[]{:S(2)}) %collective-permute-start.4) | collective-permute-done | bytes 589856 | tf_op jit(solution)/shard_map/ppermute | solution.py:594
  42.4 0.4 collective-permute-start.8
  42.7 0.0 collective-permute-done.10.rest_11_
  42.8 12.5 %collective-permute-done.11.rest_12_ = bf16[192,768]{1,0:T(8,128)(2,1)S(1)} collective-permute-done((bf16[192,768]{1,0:T(8,128)(2,1)S(1)}, bf16[192,768]{1,0:T(8,128)(2,1)S(1)}, u32[]{:S(2)}, u32[]{:S(2)}) %collective-permute-start.11) | collective-permute-done | bytes 294944 | tf_op jit(solution)/shard_map/ppermute | solution.py:589
  55.3 0.5 collective-permute-start.5
  55.8 0.0 copy-start.14
  55.8 0.1 collective-permute-start.13
  56.0 0.4 collective-permute-start.14
  56.4 0.9 collective-permute-done.7.rest_5_
  57.3 0.8 collective-permute-done.5.rest_3_
  58.1 0.4 collective-permute-done.13.rest_7_
  58.6 0.4 collective-permute-done.14.rest_9_
  59.1 0.2 copy-done.15
  59.3 0.7 copy-done.16
  60.0 17.5 %shard_map.159 = (bf16[192,768]{1,0:T(8,128)(2,1)}, bf16[192,768]{1,0:T(8,128)(2,1)}, bf16[192,768]{1,0:T(8,128)(2,1)}, bf16[192,768]{1,0:T(8,128)(2,1)}, bf16[1...) custom-call(s32[1]{0:T(128)} %bitcast.group_ref, s32[1]{0:T(128)} %bitcast.3.rows_ref.row_ref, ...), custom_call_target="tpu_custom_call" | custom-call | tf_op jit(solution)/shard_map/pallas_call | solution.py:493
  77.5 0.2 collective-permute-start.15
  77.7 4.6 %collective-permute-done.15 = bf16[16,4,48,384]{3,2,1,0:T(8,128)(2,1)S(1)} collective-permute-done((bf16[16,4,48,384]{3,2,1,0:T(8,128)(2,1)}, bf16[16,4,48,384]{3,2,1,0:T(8,128)(2,1)S(1)}, u32[]{:S(2)}, u32[]{:S(2)}) %collective-permute-start.15) | collective-permute-done | bytes 2359328 | tf_op jit(solution)/shard_map/ppermute | solution.py:594
  82.3 1.7 %add_convert_fusion.2 = (bf16[4,4,48,384]{3,2,1,0:T(8,128)(2,1)S(1)}, bf16[4,4,48,384]{3,2,1,0:T(8,128)(2,1)S(1)}) fusion(bf16[16,4,48,384]{3,2,1,0:T(8,128)(2,1)S(1)} %collective-permute-done.15, bf16[16,4,48,384]{3,2,1,0:T(8,128)(2,1)} %get-tuple-element.73), kind=kLoop, calls=%fused_computation.2 | loop fusion | flops 2359296 | bytes 3538944 | tf_op jit(solution)/shard_map/convert_element_type | solution.py:631
  84.0 0.6 collective-permute-start.16
  84.6 0.5 collective-permute-start.17
  85.1 2.9 %collective-permute-start.20 = (bf16[192,768]{1,0:T(8,128)(2,1)S(1)}, bf16[192,768]{1,0:T(8,128)(2,1)S(1)}, u32[]{:S(2)}, u32[]{:S(2)}) collective-permute-start(bf16[192,768]{1,0:T(8,128)(2,1)S(1)} %copy-done.25), channel_id=1, source_target_pairs={{0,1},{1,0},{2,3},{3,2},{4,5},{5,4},{6,7},{7,6},{8,9},{9,8},{10,11... | collective-permute-start | bytes 884744 | tf_op jit(solution)/shard_map/ppermute | solution.py:589
  88.0 1.3 collective-permute-start.21
  89.3 1.5 collective-permute-start.22
  90.7 8.7 %collective-permute-done.16 = bf16[4,4,48,384]{3,2,1,0:T(8,128)(2,1)S(1)} collective-permute-done((bf16[4,4,48,384]{3,2,1,0:T(8,128)(2,1)S(1)}, bf16[4,4,48,384]{3,2,1,0:T(8,128)(2,1)S(1)}, u32[]{:S(2)}, u32[]{:S(2)}) %collective-permute-start.16) | collective-permute-done | bytes 589856 | tf_op jit(solution)/shard_map/ppermute | solution.py:594
  99.4 0.3 collective-permute-done.17
  99.7 0.2 add_convert_fusion.3
  99.9 1.6 %collective-permute-start.19 = (bf16[2,4,48,384]{3,2,1,0:T(8,128)(2,1)S(1)}, bf16[2,4,48,384]{3,2,1,0:T(8,128)(2,1)S(1)}, u32[]{:S(2)}, u32[]{:S(2)}) collective-permute-start(bf16[2,4,48,384]{3,2,1,0:T(8,128)(2,1)S(1)} %get-tuple-element.105), channel_id=1, source_target_pairs={{0,8},{4,12},{8,0},{12,4},{16,24},{20,28},{24,16},{28,20},{1,9},{5... | collective-permute-start | bytes 884744 | tf_op jit(solution)/shard_map/ppermute | solution.py:594
  101.5 0.5 collective-permute-start.18
  102.1 1.0 add_convert_fusion.own_ref
  103.1 8.4 %collective-permute-done.21.rest_2_ = bf16[192,768]{1,0:T(8,128)(2,1)S(1)} collective-permute-done((bf16[192,768]{1,0:T(8,128)(2,1)S(1)}, bf16[192,768]{1,0:T(8,128)(2,1)S(1)}, u32[]{:S(2)}, u32[]{:S(2)}) %collective-permute-start.21) | collective-permute-done | bytes 294944 | tf_op jit(solution)/shard_map/ppermute | solution.py:589
  111.5 0.0 copy-start.18
  111.5 0.7 copy-done.17
  112.3 0.1 copy-done.18
  112.4 2.1 %shard_map.160 = (bf16[4,48,384]{2,1,0:T(8,128)(2,1)}, bf16[4,48,384]{2,1,0:T(8,128)(2,1)}, bf16[4,48,384]{2,1,0:T(8,128)(2,1)}, bf16[4,48,384]{2,1,0:T(8,128)(2,1)}) custom-call(bf16[4,4,48,384]{3,2,1,0:T(8,128)(2,1)} %add_convert_fusion.own_ref, bf16[2,4,48,384]{3,2,1,0:T(8,128)(2,1)} %copy-done.18, bf16[2,4,48,384]{3,2,1,0:T(8,128)(2,1)} %copy-done.17), custom_call_target="tpu_custom_call" | custom-call | tf_op jit(solution)/shard_map/pallas_call | solution.py:643
  114.5 5.2 %collective-permute-start.23 = (bf16[4,48,384]{2,1,0:T(8,128)(2,1)}, bf16[4,48,384]{2,1,0:T(8,128)(2,1)S(1)}, u32[]{:S(2)}, u32[]{:S(2)}) collective-permute-start(bf16[4,48,384]{2,1,0:T(8,128)(2,1)} %get-tuple-element.96), channel_id=1, source_target_pairs={{0,1},{1,0},{2,3},{3,2},{4,5},{5,4},{6,7},{7,6},{8,9},{9,8},{10,11... | collective-permute-start | bytes 442376 | tf_op jit(solution)/shard_map/ppermute | solution.py:589
  119.7 1.2 collective-permute-start.24
  120.9 1.5 collective-permute-start.25
  122.4 7.5 %shard_map.161 = (bf16[192,768]{1,0:T(8,128)(2,1)}, bf16[192,384]{1,0:T(8,128)(2,1)}) custom-call(s32[1]{0:T(128)} %bitcast.group_ref, bf16[192,384]{1,0:T(8,128)(2,1)} %single_ref.3, bf16[192,768]{1,0:T(8,128)(2,1)} %bitcast.16, bf16[192,768]{1,0:T(8,128)(2,1)} %bitcast.18, f32[192,768]{1,0:T(8,128)} %get-tuple-element.54.gamma_ref, ...), custom_call_target="tpu_custom_call" | custom-call | tf_op jit(solution)/shard_map/pallas_call | solution.py:727
  129.9 0.0 copy-start.20
  129.9 2.8 %collective-permute-done.24.rest_2_ = bf16[4,48,384]{2,1,0:T(8,128)(2,1)S(1)} collective-permute-done((bf16[4,48,384]{2,1,0:T(8,128)(2,1)}, bf16[4,48,384]{2,1,0:T(8,128)(2,1)S(1)}, u32[]{:S(2)}, u32[]{:S(2)}) %collective-permute-start.24) | collective-permute-done | bytes 147488 | tf_op jit(solution)/shard_map/ppermute | solution.py:589
  132.7 0.1 collective-permute-start.26
  132.7 1.6 %collective-permute-done.26 = bf16[192,384]{1,0:T(8,128)(2,1)S(1)} collective-permute-done((bf16[192,384]{1,0:T(8,128)(2,1)}, bf16[192,384]{1,0:T(8,128)(2,1)S(1)}, u32[]{:S(2)}, u32[]{:S(2)}) %collective-permute-start.26) | collective-permute-done | bytes 147488 | tf_op jit(solution)/shard_map/ppermute | solution.py:594
  134.3 1.0 add_convert_fusion.5
  135.3 2.5 %collective-permute-start.29 = (bf16[192,384]{1,0:T(8,128)(2,1)S(1)}, bf16[192,384]{1,0:T(8,128)(2,1)S(1)}, u32[]{:S(2)}, u32[]{:S(2)}) collective-permute-start(bf16[192,384]{1,0:T(8,128)(2,1)S(1)} %add_convert_fusion.5), channel_id=1, source_target_pairs={{0,24},{4,28},{8,16},{12,20},{16,8},{20,12},{24,0},{28,4},{1,25},{... | collective-permute-start | bytes 442376 | tf_op jit(solution)/shard_map/ppermute | solution.py:594
  137.8 0.5 collective-permute-start.28
  138.3 0.5 collective-permute-start.27
  138.8 8.2 %shard_map.162 = bf16[2,48,192,128]{3,2,1,0:T(8,128)(2,1)} custom-call(s32[1]{0:T(128)} %bitcast.group_ref, bf16[2,48,192,128]{3,2,1,0:T(8,128)(2,1)} %bitcast.13, f32[2,48,24,192]{3,2,1,0:T(8,128)} %get-tuple-element.100.stats_ref, bf16[16,128]{1,0:T(8,128)(2,1)} %bitcast.24, bf16[4,48,384]{2,1,0:T(8,128)(2,1)} %get-tuple-element.101.rest_0_, ...), custom_call_target="tpu_custom_call" | custom-call | tf_op jit(solution)/shard_map/pallas_call | solution.py:330
  147.1 0.8 add_add_fusion
  (70 shorter events, 0.3 us)
Async XLA Ops:
  9.1 12.0 %collective-permute-start = (bf16[4,48,384]{2,1,0:T(8,128)(2,1)}, bf16[4,48,384]{2,1,0:T(8,128)(2,1)S(1)}, u32[]{:S(2)}, u32[]{:S(2)}) collective-permute-start(bf16[4,48,384]{2,1,0:T(8,128)(2,1)} %get-tuple-element.57), channel_id=1, source_target_pairs={{0,1},{1,0},{2,3},{3,2},{4,5},{5,4},{6,7},{7,6},{8,9},{9,8},{10,11... | collective-permute-start | bytes 442376 | tf_op jit(solution)/shard_map/ppermute | solution.py:589
  12.1 14.2 %collective-permute-start.1 = (bf16[4,48,384]{2,1,0:T(8,128)(2,1)}, bf16[4,48,384]{2,1,0:T(8,128)(2,1)S(1)}, u32[]{:S(2)}, u32[]{:S(2)}) collective-permute-start(bf16[4,48,384]{2,1,0:T(8,128)(2,1)} %get-tuple-element.58), channel_id=1, source_target_pairs={{0,2},{1,3},{2,0},{3,1},{4,6},{5,7},{6,4},{7,5},{8,10},{9,11},{10,... | collective-permute-start | bytes 442376 | tf_op jit(solution)/shard_map/ppermute | solution.py:589
  14.7 11.6 %collective-permute-start.2 = (bf16[4,48,384]{2,1,0:T(8,128)(2,1)}, bf16[4,48,384]{2,1,0:T(8,128)(2,1)S(1)}, u32[]{:S(2)}, u32[]{:S(2)}) collective-permute-start(bf16[4,48,384]{2,1,0:T(8,128)(2,1)} %get-tuple-element.59), channel_id=1, source_target_pairs={{0,3},{1,2},{2,1},{3,0},{4,7},{5,6},{6,5},{7,4},{8,11},{9,10},{10,... | collective-permute-start | bytes 442376 | tf_op jit(solution)/shard_map/ppermute | solution.py:589
  14.7 11.6 %copy-start.19 = (bf16[4,48,384]{2,1,0:T(8,128)(2,1)S(1)}, bf16[4,48,384]{2,1,0:T(8,128)(2,1)}, u32[]{:S(2)}) copy-start(bf16[4,48,384]{2,1,0:T(8,128)(2,1)} %get-tuple-element.64) | copy-start | bytes 442372
  21.1 8.4 %copy-start.28 = (bf16[192,768]{1,0:T(8,128)(2,1)S(1)}, bf16[192,768]{1,0:T(8,128)(2,1)}, u32[]{:S(2)}) copy-start(bf16[192,768]{1,0:T(8,128)(2,1)} %get-tuple-element.61) | copy-start | bytes 884740
  21.1 10.7 %copy-start.27 = (bf16[192,768]{1,0:T(8,128)(2,1)S(1)}, bf16[192,768]{1,0:T(8,128)(2,1)}, u32[]{:S(2)}) copy-start(bf16[192,768]{1,0:T(8,128)(2,1)} %get-tuple-element.62) | copy-start | bytes 884740
  21.1 11.8 %copy-start.26 = (bf16[192,768]{1,0:T(8,128)(2,1)S(1)}, bf16[192,768]{1,0:T(8,128)(2,1)}, u32[]{:S(2)}) copy-start(bf16[192,768]{1,0:T(8,128)(2,1)} %get-tuple-element.63) | copy-start | bytes 884740
  26.4 32.6 %copy-start = (bf16[4,4,48,384]{3,2,1,0:T(8,128)(2,1)}, bf16[4,4,48,384]{3,2,1,0:T(8,128)(2,1)S(1)}, u32[]{:S(2)}) copy-start(bf16[4,4,48,384]{3,2,1,0:T(8,128)(2,1)S(1)} %pad_maximum_fusion.rest_0_) | copy-start | bytes 1769476
  26.4 12.7 %collective-permute-start.6 = (bf16[4,4,48,384]{3,2,1,0:T(8,128)(2,1)S(1)}, bf16[4,4,48,384]{3,2,1,0:T(8,128)(2,1)S(1)}, u32[]{:S(2)}, u32[]{:S(2)}) collective-permute-start(bf16[4,4,48,384]{3,2,1,0:T(8,128)(2,1)S(1)} %pad_maximum_fusion.rest_0_), channel_id=1, source_target_pairs={{0,16},{4,20},{8,24},{12,28},{16,0},{20,4},{24,8},{28,12},{1,17},{... | collective-permute-start | bytes 1769480 | tf_op jit(solution)/shard_map/ppermute | solution.py:594
  28.0 14.3 %collective-permute-start.4 = (bf16[4,4,48,384]{3,2,1,0:T(8,128)(2,1)S(1)}, bf16[4,4,48,384]{3,2,1,0:T(8,128)(2,1)S(1)}, u32[]{:S(2)}, u32[]{:S(2)}) collective-permute-start(bf16[4,4,48,384]{3,2,1,0:T(8,128)(2,1)S(1)} %pad_maximum_fusion.rest_0_), channel_id=1, source_target_pairs={{0,8},{4,12},{8,0},{12,4},{16,24},{20,28},{24,16},{28,20},{1,9},{5... | collective-permute-start | bytes 1769480 | tf_op jit(solution)/shard_map/ppermute | solution.py:594
  29.5 13.2 %collective-permute-start.10 = (bf16[192,768]{1,0:T(8,128)(2,1)S(1)}, bf16[192,768]{1,0:T(8,128)(2,1)S(1)}, u32[]{:S(2)}, u32[]{:S(2)}) collective-permute-start(bf16[192,768]{1,0:T(8,128)(2,1)S(1)} %copy-done.28), channel_id=1, source_target_pairs={{0,1},{1,0},{2,3},{3,2},{4,5},{5,4},{6,7},{7,6},{8,9},{9,8},{10,11... | collective-permute-start | bytes 884744 | tf_op jit(solution)/shard_map/ppermute | solution.py:589
  31.8 23.5 %collective-permute-start.11 = (bf16[192,768]{1,0:T(8,128)(2,1)S(1)}, bf16[192,768]{1,0:T(8,128)(2,1)S(1)}, u32[]{:S(2)}, u32[]{:S(2)}) collective-permute-start(bf16[192,768]{1,0:T(8,128)(2,1)S(1)} %copy-done.27), channel_id=1, source_target_pairs={{0,2},{1,3},{2,0},{3,1},{4,6},{5,7},{6,4},{7,5},{8,10},{9,11},{10,... | collective-permute-start | bytes 884744 | tf_op jit(solution)/shard_map/ppermute | solution.py:589
  32.9 22.4 %collective-permute-start.12 = (bf16[192,768]{1,0:T(8,128)(2,1)S(1)}, bf16[192,768]{1,0:T(8,128)(2,1)S(1)}, u32[]{:S(2)}, u32[]{:S(2)}) collective-permute-start(bf16[192,768]{1,0:T(8,128)(2,1)S(1)} %copy-done.26), channel_id=1, source_target_pairs={{0,3},{1,2},{2,1},{3,0},{4,7},{5,6},{6,5},{7,4},{8,11},{9,10},{10,... | collective-permute-start | bytes 884744 | tf_op jit(solution)/shard_map/ppermute | solution.py:589
  39.1 19.9 %copy-start.2 = (bf16[4,4,48,384]{3,2,1,0:T(8,128)(2,1)}, bf16[4,4,48,384]{3,2,1,0:T(8,128)(2,1)S(1)}, u32[]{:S(2)}) copy-start(bf16[4,4,48,384]{3,2,1,0:T(8,128)(2,1)S(1)} %collective-permute-done.6.rest_4_) | copy-start | bytes 1769476
  39.1 16.7 %collective-permute-start.9 = (bf16[2,4,48,384]{3,2,1,0:T(8,128)(2,1)S(1)}, bf16[2,4,48,384]{3,2,1,0:T(8,128)(2,1)S(1)}, u32[]{:S(2)}, u32[]{:S(2)}) collective-permute-start(bf16[2,4,48,384]{3,2,1,0:T(8,128)(2,1)S(1)} %slice.65), channel_id=1, source_target_pairs={{0,8},{4,12},{8,0},{12,4},{16,24},{20,28},{24,16},{28,20},{1,9},{5... | collective-permute-start | bytes 884744 | tf_op jit(solution)/shard_map/ppermute | solution.py:594
  42.4 16.6 %copy-start.3 = (bf16[4,4,48,384]{3,2,1,0:T(8,128)(2,1)}, bf16[4,4,48,384]{3,2,1,0:T(8,128)(2,1)S(1)}, u32[]{:S(2)}) copy-start(bf16[4,4,48,384]{3,2,1,0:T(8,128)(2,1)S(1)} %collective-permute-done.4.rest_2_) | copy-start | bytes 1769476
  42.4 13.4 %collective-permute-start.8 = (bf16[2,4,48,384]{3,2,1,0:T(8,128)(2,1)S(1)}, bf16[2,4,48,384]{3,2,1,0:T(8,128)(2,1)S(1)}, u32[]{:S(2)}, u32[]{:S(2)}) collective-permute-start(bf16[2,4,48,384]{3,2,1,0:T(8,128)(2,1)S(1)} %slice.64), channel_id=1, source_target_pairs={{0,16},{4,20},{8,24},{12,28},{16,0},{20,4},{24,8},{28,12},{1,17},{... | collective-permute-start | bytes 884744 | tf_op jit(solution)/shard_map/ppermute | solution.py:594
  42.8 16.2 %copy-start.7 = (bf16[192,768]{1,0:T(8,128)(2,1)}, bf16[192,768]{1,0:T(8,128)(2,1)S(1)}, u32[]{:S(2)}) copy-start(bf16[192,768]{1,0:T(8,128)(2,1)S(1)} %collective-permute-done.10.rest_11_) | copy-start | bytes 884740
  42.8 13.7 %collective-permute-start.3 = (bf16[4,4,48,384]{3,2,1,0:T(8,128)(2,1)S(1)}, bf16[4,4,48,384]{3,2,1,0:T(8,128)(2,1)S(1)}, u32[]{:S(2)}, u32[]{:S(2)}) collective-permute-start(bf16[4,4,48,384]{3,2,1,0:T(8,128)(2,1)S(1)} %pad_maximum_fusion.rest_0_), channel_id=1, source_target_pairs={{0,4},{4,0},{8,12},{12,8},{16,20},{20,16},{24,28},{28,24},{1,5},{5... | collective-permute-start | bytes 1769480 | tf_op jit(solution)/shard_map/ppermute | solution.py:594
  55.3 3.7 %copy-start.8 = (bf16[192,768]{1,0:T(8,128)(2,1)}, bf16[192,768]{1,0:T(8,128)(2,1)S(1)}, u32[]{:S(2)}) copy-start(bf16[192,768]{1,0:T(8,128)(2,1)S(1)} %collective-permute-done.11.rest_12_) | copy-start | bytes 884740
  55.3 2.0 %collective-permute-start.7 = (bf16[4,4,48,384]{3,2,1,0:T(8,128)(2,1)S(1)}, bf16[4,4,48,384]{3,2,1,0:T(8,128)(2,1)S(1)}, u32[]{:S(2)}, u32[]{:S(2)}) collective-permute-start(bf16[4,4,48,384]{3,2,1,0:T(8,128)(2,1)S(1)} %collective-permute-done.6.rest_4_), channel_id=1, source_target_pairs={{0,4},{4,0},{8,12},{12,8},{16,20},{20,16},{24,28},{28,24},{1,5},{5... | collective-permute-start | bytes 1769480 | tf_op jit(solution)/shard_map/ppermute | solution.py:594
  55.3 3.7 %copy-start.10 = (bf16[192,768]{1,0:T(8,128)(2,1)}, bf16[192,768]{1,0:T(8,128)(2,1)S(1)}, u32[]{:S(2)}) copy-start(bf16[192,768]{1,0:T(8,128)(2,1)S(1)} %collective-permute-done.12.rest_13_) | copy-start | bytes 884740
  55.3 2.8 %collective-permute-start.5 = (bf16[4,4,48,384]{3,2,1,0:T(8,128)(2,1)S(1)}, bf16[4,4,48,384]{3,2,1,0:T(8,128)(2,1)S(1)}, u32[]{:S(2)}, u32[]{:S(2)}) collective-permute-start(bf16[4,4,48,384]{3,2,1,0:T(8,128)(2,1)S(1)} %collective-permute-done.4.rest_2_), channel_id=1, source_target_pairs={{0,4},{4,0},{8,12},{12,8},{16,20},{20,16},{24,28},{28,24},{1,5},{5... | collective-permute-start | bytes 1769480 | tf_op jit(solution)/shard_map/ppermute | solution.py:594
  55.8 3.2 %copy-start.13 = (bf16[2,4,48,384]{3,2,1,0:T(8,128)(2,1)}, bf16[2,4,48,384]{3,2,1,0:T(8,128)(2,1)S(1)}, u32[]{:S(2)}) copy-start(bf16[2,4,48,384]{3,2,1,0:T(8,128)(2,1)S(1)} %collective-permute-done.9.rest_8_) | copy-start | bytes 884740
  55.8 3.2 %copy-start.14 = (bf16[2,4,48,384]{3,2,1,0:T(8,128)(2,1)}, bf16[2,4,48,384]{3,2,1,0:T(8,128)(2,1)S(1)}, u32[]{:S(2)}) copy-start(bf16[2,4,48,384]{3,2,1,0:T(8,128)(2,1)S(1)} %collective-permute-done.8.rest_6_) | copy-start | bytes 884740
  55.8 2.7 %collective-permute-start.13 = (bf16[2,4,48,384]{3,2,1,0:T(8,128)(2,1)S(1)}, bf16[2,4,48,384]{3,2,1,0:T(8,128)(2,1)S(1)}, u32[]{:S(2)}, u32[]{:S(2)}) collective-permute-start(bf16[2,4,48,384]{3,2,1,0:T(8,128)(2,1)S(1)} %collective-permute-done.8.rest_6_), channel_id=1, source_target_pairs={{0,4},{4,0},{8,12},{12,8},{16,20},{20,16},{24,28},{28,24},{1,5},{5... | collective-permute-start | bytes 884744 | tf_op jit(solution)/shard_map/ppermute | solution.py:594
  56.0 3.0 %collective-permute-start.14 = (bf16[2,4,48,384]{3,2,1,0:T(8,128)(2,1)S(1)}, bf16[2,4,48,384]{3,2,1,0:T(8,128)(2,1)S(1)}, u32[]{:S(2)}, u32[]{:S(2)}) collective-permute-start(bf16[2,4,48,384]{3,2,1,0:T(8,128)(2,1)S(1)} %collective-permute-done.9.rest_8_), channel_id=1, source_target_pairs={{0,4},{4,0},{8,12},{12,8},{16,20},{20,16},{24,28},{28,24},{1,5},{5... | collective-permute-start | bytes 884744 | tf_op jit(solution)/shard_map/ppermute | solution.py:594
  56.4 2.6 %copy-start.4 = (bf16[4,4,48,384]{3,2,1,0:T(8,128)(2,1)}, bf16[4,4,48,384]{3,2,1,0:T(8,128)(2,1)S(1)}, u32[]{:S(2)}) copy-start(bf16[4,4,48,384]{3,2,1,0:T(8,128)(2,1)S(1)} %collective-permute-done.3.rest_1_) | copy-start | bytes 1769476
  57.3 1.8 %copy-start.5 = (bf16[4,4,48,384]{3,2,1,0:T(8,128)(2,1)}, bf16[4,4,48,384]{3,2,1,0:T(8,128)(2,1)S(1)}, u32[]{:S(2)}) copy-start(bf16[4,4,48,384]{3,2,1,0:T(8,128)(2,1)S(1)} %collective-permute-done.7.rest_5_) | copy-start | bytes 1769476
  58.1 0.9 copy-start.6
  58.6 0.7 copy-start.15
  59.3 0.7 copy-start.16
  77.5 4.8 %collective-permute-start.15 = (bf16[16,4,48,384]{3,2,1,0:T(8,128)(2,1)}, bf16[16,4,48,384]{3,2,1,0:T(8,128)(2,1)S(1)}, u32[]{:S(2)}, u32[]{:S(2)}) collective-permute-start(bf16[16,4,48,384]{3,2,1,0:T(8,128)(2,1)} %get-tuple-element.74), channel_id=1, source_target_pairs={{0,4},{4,0},{8,12},{12,8},{16,20},{20,16},{24,28},{28,24},{1,5},{5... | collective-permute-start | bytes 7077896 | tf_op jit(solution)/shard_map/ppermute | solution.py:594
  82.3 2.8 %copy-start.25 = (bf16[192,768]{1,0:T(8,128)(2,1)S(1)}, bf16[192,768]{1,0:T(8,128)(2,1)}, u32[]{:S(2)}) copy-start(bf16[192,768]{1,0:T(8,128)(2,1)} %get-tuple-element.76) | copy-start | bytes 884740
  82.3 5.7 %copy-start.24 = (bf16[192,768]{1,0:T(8,128)(2,1)S(1)}, bf16[192,768]{1,0:T(8,128)(2,1)}, u32[]{:S(2)}) copy-start(bf16[192,768]{1,0:T(8,128)(2,1)} %get-tuple-element.77) | copy-start | bytes 884740
  82.3 7.0 %copy-start.23 = (bf16[192,768]{1,0:T(8,128)(2,1)S(1)}, bf16[192,768]{1,0:T(8,128)(2,1)}, u32[]{:S(2)}) copy-start(bf16[192,768]{1,0:T(8,128)(2,1)} %get-tuple-element.78) | copy-start | bytes 884740
  82.3 17.4 %copy-start.1 = (bf16[16,4,48,384]{3,2,1,0:T(8,128)(2,1)S(1)}, bf16[16,4,48,384]{3,2,1,0:T(8,128)(2,1)}, u32[]{:S(2)}) copy-start(bf16[16,4,48,384]{3,2,1,0:T(8,128)(2,1)} %get-tuple-element.73) | copy-start | bytes 7077892
  84.0 15.4 %collective-permute-start.16 = (bf16[4,4,48,384]{3,2,1,0:T(8,128)(2,1)S(1)}, bf16[4,4,48,384]{3,2,1,0:T(8,128)(2,1)S(1)}, u32[]{:S(2)}, u32[]{:S(2)}) collective-permute-start(bf16[4,4,48,384]{3,2,1,0:T(8,128)(2,1)S(1)} %get-tuple-element.107), channel_id=1, source_target_pairs={{0,8},{4,12},{8,0},{12,4},{16,24},{20,28},{24,16},{28,20},{1,9},{5... | collective-permute-start | bytes 1769480 | tf_op jit(solution)/shard_map/ppermute | solution.py:594
  84.6 15.1 %collective-permute-start.17 = (bf16[4,4,48,384]{3,2,1,0:T(8,128)(2,1)S(1)}, bf16[4,4,48,384]{3,2,1,0:T(8,128)(2,1)S(1)}, u32[]{:S(2)}, u32[]{:S(2)}) collective-permute-start(bf16[4,4,48,384]{3,2,1,0:T(8,128)(2,1)S(1)} %get-tuple-element.108), channel_id=1, source_target_pairs={{0,16},{4,20},{8,24},{12,28},{16,0},{20,4},{24,8},{28,12},{1,17},{... | collective-permute-start | bytes 1769480 | tf_op jit(solution)/shard_map/ppermute | solution.py:594
  85.1 18.0 %collective-permute-start.20 = (bf16[192,768]{1,0:T(8,128)(2,1)S(1)}, bf16[192,768]{1,0:T(8,128)(2,1)S(1)}, u32[]{:S(2)}, u32[]{:S(2)}) collective-permute-start(bf16[192,768]{1,0:T(8,128)(2,1)S(1)} %copy-done.25), channel_id=1, source_target_pairs={{0,1},{1,0},{2,3},{3,2},{4,5},{5,4},{6,7},{7,6},{8,9},{9,8},{10,11... | collective-permute-start | bytes 884744 | tf_op jit(solution)/shard_map/ppermute | solution.py:589
  88.0 23.5 %collective-permute-start.21 = (bf16[192,768]{1,0:T(8,128)(2,1)S(1)}, bf16[192,768]{1,0:T(8,128)(2,1)S(1)}, u32[]{:S(2)}, u32[]{:S(2)}) collective-permute-start(bf16[192,768]{1,0:T(8,128)(2,1)S(1)} %copy-done.24), channel_id=1, source_target_pairs={{0,2},{1,3},{2,0},{3,1},{4,6},{5,7},{6,4},{7,5},{8,10},{9,11},{10,... | collective-permute-start | bytes 884744 | tf_op jit(solution)/shard_map/ppermute | solution.py:589
  89.3 22.2 %collective-permute-start.22 = (bf16[192,768]{1,0:T(8,128)(2,1)S(1)}, bf16[192,768]{1,0:T(8,128)(2,1)S(1)}, u32[]{:S(2)}, u32[]{:S(2)}) collective-permute-start(bf16[192,768]{1,0:T(8,128)(2,1)S(1)} %copy-done.23), channel_id=1, source_target_pairs={{0,3},{1,2},{2,1},{3,0},{4,7},{5,6},{6,5},{7,4},{8,11},{9,10},{10,... | collective-permute-start | bytes 884744 | tf_op jit(solution)/shard_map/ppermute | solution.py:589
  99.9 11.6 %collective-permute-start.19 = (bf16[2,4,48,384]{3,2,1,0:T(8,128)(2,1)S(1)}, bf16[2,4,48,384]{3,2,1,0:T(8,128)(2,1)S(1)}, u32[]{:S(2)}, u32[]{:S(2)}) collective-permute-start(bf16[2,4,48,384]{3,2,1,0:T(8,128)(2,1)S(1)} %get-tuple-element.105), channel_id=1, source_target_pairs={{0,8},{4,12},{8,0},{12,4},{16,24},{20,28},{24,16},{28,20},{1,9},{5... | collective-permute-start | bytes 884744 | tf_op jit(solution)/shard_map/ppermute | solution.py:594
  101.5 10.0 %collective-permute-start.18 = (bf16[2,4,48,384]{3,2,1,0:T(8,128)(2,1)S(1)}, bf16[2,4,48,384]{3,2,1,0:T(8,128)(2,1)S(1)}, u32[]{:S(2)}, u32[]{:S(2)}) collective-permute-start(bf16[2,4,48,384]{3,2,1,0:T(8,128)(2,1)S(1)} %get-tuple-element.106), channel_id=1, source_target_pairs={{0,16},{4,20},{8,24},{12,28},{16,0},{20,4},{24,8},{28,12},{1,17},{... | collective-permute-start | bytes 884744 | tf_op jit(solution)/shard_map/ppermute | solution.py:594
  103.1 19.3 %copy-start.9 = (bf16[192,768]{1,0:T(8,128)(2,1)}, bf16[192,768]{1,0:T(8,128)(2,1)S(1)}, u32[]{:S(2)}) copy-start(bf16[192,768]{1,0:T(8,128)(2,1)S(1)} %collective-permute-done.20.rest_1_) | copy-start | bytes 884740
  111.5 10.9 %copy-start.11 = (bf16[192,768]{1,0:T(8,128)(2,1)}, bf16[192,768]{1,0:T(8,128)(2,1)S(1)}, u32[]{:S(2)}) copy-start(bf16[192,768]{1,0:T(8,128)(2,1)S(1)} %collective-permute-done.21.rest_2_) | copy-start | bytes 884740
  111.5 10.9 %copy-start.12 = (bf16[192,768]{1,0:T(8,128)(2,1)}, bf16[192,768]{1,0:T(8,128)(2,1)S(1)}, u32[]{:S(2)}) copy-start(bf16[192,768]{1,0:T(8,128)(2,1)S(1)} %collective-permute-done.22.rest_3_) | copy-start | bytes 884740
  111.5 0.8 copy-start.17
  111.5 0.9 copy-start.18
  114.5 15.4 %collective-permute-start.23 = (bf16[4,48,384]{2,1,0:T(8,128)(2,1)}, bf16[4,48,384]{2,1,0:T(8,128)(2,1)S(1)}, u32[]{:S(2)}, u32[]{:S(2)}) collective-permute-start(bf16[4,48,384]{2,1,0:T(8,128)(2,1)} %get-tuple-element.96), channel_id=1, source_target_pairs={{0,1},{1,0},{2,3},{3,2},{4,5},{5,4},{6,7},{7,6},{8,9},{9,8},{10,11... | collective-permute-start | bytes 442376 | tf_op jit(solution)/shard_map/ppermute | solution.py:589
  119.7 13.0 %collective-permute-start.24 = (bf16[4,48,384]{2,1,0:T(8,128)(2,1)}, bf16[4,48,384]{2,1,0:T(8,128)(2,1)S(1)}, u32[]{:S(2)}, u32[]{:S(2)}) collective-permute-start(bf16[4,48,384]{2,1,0:T(8,128)(2,1)} %get-tuple-element.97), channel_id=1, source_target_pairs={{0,2},{1,3},{2,0},{3,1},{4,6},{5,7},{6,4},{7,5},{8,10},{9,11},{10,... | collective-permute-start | bytes 442376 | tf_op jit(solution)/shard_map/ppermute | solution.py:589
  120.9 11.8 %collective-permute-start.25 = (bf16[4,48,384]{2,1,0:T(8,128)(2,1)}, bf16[4,48,384]{2,1,0:T(8,128)(2,1)S(1)}, u32[]{:S(2)}, u32[]{:S(2)}) collective-permute-start(bf16[4,48,384]{2,1,0:T(8,128)(2,1)} %get-tuple-element.98), channel_id=1, source_target_pairs={{0,3},{1,2},{2,1},{3,0},{4,7},{5,6},{6,5},{7,4},{8,11},{9,10},{10,... | collective-permute-start | bytes 442376 | tf_op jit(solution)/shard_map/ppermute | solution.py:589
  129.9 8.9 %copy-start.20 = (bf16[4,48,384]{2,1,0:T(8,128)(2,1)}, bf16[4,48,384]{2,1,0:T(8,128)(2,1)S(1)}, u32[]{:S(2)}) copy-start(bf16[4,48,384]{2,1,0:T(8,128)(2,1)S(1)} %collective-permute-done.23.rest_1_) | copy-start | bytes 442372
  132.7 6.2 %copy-start.21 = (bf16[4,48,384]{2,1,0:T(8,128)(2,1)}, bf16[4,48,384]{2,1,0:T(8,128)(2,1)S(1)}, u32[]{:S(2)}) copy-start(bf16[4,48,384]{2,1,0:T(8,128)(2,1)S(1)} %collective-permute-done.24.rest_2_) | copy-start | bytes 442372
  132.7 6.2 %copy-start.22 = (bf16[4,48,384]{2,1,0:T(8,128)(2,1)}, bf16[4,48,384]{2,1,0:T(8,128)(2,1)S(1)}, u32[]{:S(2)}) copy-start(bf16[4,48,384]{2,1,0:T(8,128)(2,1)S(1)} %collective-permute-done.25.rest_3_) | copy-start | bytes 442372
  132.7 1.6 %collective-permute-start.26 = (bf16[192,384]{1,0:T(8,128)(2,1)}, bf16[192,384]{1,0:T(8,128)(2,1)S(1)}, u32[]{:S(2)}, u32[]{:S(2)}) collective-permute-start(bf16[192,384]{1,0:T(8,128)(2,1)} %get-tuple-element.99), channel_id=1, source_target_pairs={{0,4},{4,0},{8,12},{12,8},{16,20},{20,16},{24,28},{28,24},{1,5},{5... | collective-permute-start | bytes 442376 | tf_op jit(solution)/shard_map/ppermute | solution.py:594
  135.3 11.8 %collective-permute-start.29 = (bf16[192,384]{1,0:T(8,128)(2,1)S(1)}, bf16[192,384]{1,0:T(8,128)(2,1)S(1)}, u32[]{:S(2)}, u32[]{:S(2)}) collective-permute-start(bf16[192,384]{1,0:T(8,128)(2,1)S(1)} %add_convert_fusion.5), channel_id=1, source_target_pairs={{0,24},{4,28},{8,16},{12,20},{16,8},{20,12},{24,0},{28,4},{1,25},{... | collective-permute-start | bytes 442376 | tf_op jit(solution)/shard_map/ppermute | solution.py:594
  137.8 9.2 %collective-permute-start.28 = (bf16[192,384]{1,0:T(8,128)(2,1)S(1)}, bf16[192,384]{1,0:T(8,128)(2,1)S(1)}, u32[]{:S(2)}, u32[]{:S(2)}) collective-permute-start(bf16[192,384]{1,0:T(8,128)(2,1)S(1)} %add_convert_fusion.5), channel_id=1, source_target_pairs={{0,16},{4,20},{8,24},{12,28},{16,0},{20,4},{24,8},{28,12},{1,17},{... | collective-permute-start | bytes 442376 | tf_op jit(solution)/shard_map/ppermute | solution.py:594
  138.3 8.8 %collective-permute-start.27 = (bf16[192,384]{1,0:T(8,128)(2,1)S(1)}, bf16[192,384]{1,0:T(8,128)(2,1)S(1)}, u32[]{:S(2)}, u32[]{:S(2)}) collective-permute-start(bf16[192,384]{1,0:T(8,128)(2,1)S(1)} %add_convert_fusion.5), channel_id=1, source_target_pairs={{0,8},{4,12},{8,0},{12,4},{16,24},{20,28},{24,16},{28,20},{1,9},{5... | collective-permute-start | bytes 442376 | tf_op jit(solution)/shard_map/ppermute | solution.py:594

commit v3 on v2

--- a/solution.py
+++ b/solution.py
@@ -349,9 +349,9 @@
 
 def unit_order(heads):
     first, second = range(heads // 2), range(heads // 2, heads)
-    order = [(0, head) for head in range(heads)]
-    order += [(1, head) for head in first] + [(3, head) for head in first]
+    order = [(1, head) for head in first] + [(3, head) for head in first]
     order += [(2, head) for head in second] + [(3, head) for head in second]
+    order += [(0, head) for head in range(heads)]
     order += [(2, head) for head in first] + [(1, head) for head in second]
     return order
 
@@ -364,6 +364,7 @@
     (
         keep_ref,
         give_ref,
+        give_late_ref,
         query_ref,
         keys_ref,
         values_ref,
@@ -453,16 +454,29 @@
     gk_sum[pl.ds(feature, head_size), :] = gk_t
     gv_sum[pl.ds(feature, head_size), :] = gv_t
 
-    for other in range(row_parts):
-        dbias_ref = give_ref if other % 2 else keep_ref
-        unit = 0
-        for place, (chip, unit_head) in enumerate(unit_order(heads)):
-            if chip == other // 2:
-                unit = jnp.where(head == unit_head, place, unit)
-        for column, side, rows in places(row_ref[0] ^ other):
-            dbias_ref[unit, column, :, side * cols : (side + 1) * cols] = score_full[
-                rows, column * cols : (column + 1) * cols
-            ]
+    order = unit_order(heads)
+    early = len(order) // 2
+
+    def give_back(some_heads):
+        for other in range(row_parts):
+            unit = order.index((other // 2, some_heads[0]))
+            dbias_ref = keep_ref
+            if other % 2:
+                dbias_ref = give_ref if unit < early else give_late_ref
+                unit = unit % early
+            unit = unit + head - some_heads[0]
+            for column, side, rows in places(row_ref[0] ^ other):
+                dbias_ref[unit, column, :, side * cols : (side + 1) * cols] = score_full[
+                    rows, column * cols : (column + 1) * cols
+                ]
+
+    @pl.when(head < heads // 2)
+    def _():
+        give_back(range(heads // 2))
+
+    @pl.when(head >= heads // 2)
+    def _():
+        give_back(range(heads // 2, heads))
 
     @pl.when(head == heads - 1)
     def _():
@@ -490,7 +504,8 @@
     row_block = 256 if tokens % 256 == 0 else cols
     padded = (part // 128 + 1) * 128
     units = (row_parts // 2 * heads, groups, half, lanes)
-    *grads, keep, give = pl.pallas_call(
+    some = (row_parts // 4 * heads, groups, half, lanes)
+    *grads, keep, give, give_late = pl.pallas_call(
         functools.partial(
             attention_kernel,
             groups=groups,
@@ -506,9 +521,9 @@
         ]
         + [pl.BlockSpec((cols, width), lambda h: (0, 0))] * groups,
         out_specs=[pl.BlockSpec((cols, width), lambda h: (0, 0))] * groups
-        + [pl.BlockSpec(units, lambda h: (0, 0, 0, 0))] * 2,
+        + [pl.BlockSpec(shape, lambda h: (0, 0, 0, 0)) for shape in (units, some, some)],
         out_shape=[jax.ShapeDtypeStruct((cols, width), BF16)] * groups
-        + [jax.ShapeDtypeStruct(units, BF16)] * 2,
+        + [jax.ShapeDtypeStruct(shape, BF16) for shape in (units, some, some)],
         scratch_shapes=[pltpu.VMEM((tokens, part), BF16) for _ in range(4)]
         + [pltpu.VMEM((part, tokens), BF16) for _ in range(4)]
         + [
@@ -521,7 +536,7 @@
         ],
         compiler_params=params(),
     )(group_index, row_index, *bias, *acts)
-    return grads, keep, give
+    return grads, keep, give, give_late
 
 
 def finish_kernel(
@@ -583,10 +598,10 @@
 
 def swap_groups(sends):
     groups = len(sends)
-    got = [sends[0]]
-    for bits in range(1, groups):
+    got = list(sends)
+    for bits in (*range(2, groups), 1):
         perm = [(index, index ^ bits) for index in range(groups)]
-        got.append(lax.ppermute(sends[bits], "grp", perm))
+        got[bits] = lax.ppermute(sends[bits], "grp", perm)
     return got
 
 
@@ -600,11 +615,13 @@
     far = flip_rows(own, 4, row_total)
     first = flip_rows(near[:half], 4, row_total)
     second = flip_rows(far[half:], 2, row_total)
-    first, second, acts[1], acts[2], acts[3] = lax.optimization_barrier(
-        (first, second, acts[1], acts[2], acts[3])
-    )
-    blocks = []
-    for block in (own, near, far, first, second):
+    own, acts[2] = lax.optimization_barrier((own, acts[2]))
+    own_other = flip_rows(own, 1, row_total)
+    first, second, own_other, acts[1], acts[3] = lax.optimization_barrier(
+        (first, second, own_other, acts[1], acts[3])
+    )
+    blocks = [own, own_other]
+    for block in (near, far, first, second):
         blocks += [block, flip_rows(block, 1, row_total)]
     return blocks, acts
 
@@ -619,22 +636,27 @@
             out_ref[head] = total[slot]
 
 
-def scatter_rows(keep, give, row_total):
+def scatter_rows(keep, give, give_late, row_total):
     got = flip_rows(give, 1, row_total)
-    heads = keep.shape[0] // 4
+    got, give_late = lax.optimization_barrier((got, give_late))
+    got_late = flip_rows(give_late, 1, row_total)
+    early = got.shape[0]
+    heads = early // 2
     part = heads // 2
 
     def add(first, count, *others):
-        total = keep[first : first + count].astype(F32) + got[first : first + count].astype(F32)
+        source, place = (got, first) if first < early else (got_late, first - early)
+        total = keep[first : first + count].astype(F32)
+        total += source[place : place + count].astype(F32)
         for other in others:
             total += other.astype(F32)
         return total.astype(BF16)
 
-    near = flip_rows(add(heads, heads), 2, row_total)
-    far = flip_rows(add(2 * heads, heads), 4, row_total)
-    far_two = flip_rows(add(3 * heads, part, near[part:]), 4, row_total)
-    near_two = flip_rows(add(3 * heads + part, part, far[part:]), 2, row_total)
-    own = add(0, heads, jnp.concatenate([near[:part], far[:part]]))
+    near = flip_rows(add(0, heads), 2, row_total)
+    far = flip_rows(add(heads, heads), 4, row_total)
+    far_two = flip_rows(add(early + heads, part, near[part:]), 4, row_total)
+    near_two = flip_rows(add(early + heads + part, part, far[part:]), 2, row_total)
+    own = add(early, heads, jnp.concatenate([near[:part], far[:part]]))
     return own, far_two, near_two
 
 
@@ -718,9 +740,9 @@
     bias_got, _ = lax.optimization_barrier((bias_got, acts_send))
     acts = swap_groups(acts_send)
     bias_all, acts = gather_rows(jnp.stack(bias_got), acts, row_total)
-    grads_send, keep, give = attention(group_index, row_index, acts, bias_all, head_size)
+    grads_send, keep, give, give_late = attention(group_index, row_index, acts, bias_all, head_size)
     grads = swap_groups(grads_send)
-    own, far_two, near_two = scatter_rows(keep, give, row_total)
+    own, far_two, near_two = scatter_rows(keep, give, give_late, row_total)
     far_two, near_two, grads = lax.optimization_barrier((far_two, near_two, grads))
     dbias_own, grads = lax.optimization_barrier((add_last(own, far_two, near_two), grads))
     dbias_back = swap_groups(dbias_own)

time: 148 us -> 150 us (1.014)
  starting transfers between devices: 37 us -> 40.4 us
  waiting for transfers between devices: 53 us -> 50.1 us
    ppermute x18 -> x19, waiting for transfers between devices: 24.1 us -> 18 us  [flip_rows(): lax.ppermute(values, 'rows', [(index, index ^ bits) for index in range(ro...]
    ppermute x18 -> x19, starting transfers between devices: 13.1 us -> 17 us  [flip_rows(): lax.ppermute(values, 'rows', [(index, index ^ bits) for index in range(ro...]
    ppermute x12, waiting for transfers between devices: 28.9 us -> 32.1 us  [swap_groups(): got[bits] = lax.ppermute(sends[bits], 'grp', perm)]
  transfers between devices with their start and end apart: 30 -> 31, of which waited for: 14 -> 14; matrix products, arithmetic and copies ran while one was open for 1% -> 2% of each run, Pallas kernels for 15% -> 15%
where the time goes in v3:
time: 150 us; the launch traced here: 149 us
  Pallas kernels  51.3 us (34%)
  waiting for transfers between devices  50.1 us (33%)
  starting transfers between devices  40.4 us (27%)
  other arithmetic  4.82 us (3%)
  local copies, waits for them, and re-layouts  1.85 us (1%)
    ppermute x12, waiting for transfers between devices, swap_groups(): got[bits] = lax.ppermute(sends[bits], 'grp', perm)  32.1 us
    ppermute x12, starting transfers between devices, swap_groups(): got[bits] = lax.ppermute(sends[bits], 'grp', perm)  23.4 us
    pallas_call x1, Pallas kernels, attention(): pl.pallas_call(functools.partial(attention_kernel, groups=groups, row_par...  18.6 us
    ppermute x19, waiting for transfers between devices, flip_rows(): lax.ppermute(values, 'rows', [(index, index ^ bits) for index in range(ro...  18 us
    ppermute x19, starting transfers between devices, flip_rows(): lax.ppermute(values, 'rows', [(index, index ^ bits) for index in range(ro...  17 us
    pallas_call x1, Pallas kernels, pair_bias(): pl.pallas_call(functools.partial(bias_kernel, groups=groups, batch=4), gr...  8.45 us
    pallas_call x1, Pallas kernels, pair_back(): pl.pallas_call(functools.partial(pair_back_kernel, groups=groups, calls=l...  8.2 us
    pallas_call x1, Pallas kernels, split_heads(): pl.pallas_call(functools.partial(finish_kernel, groups=groups, calls=call...  7.49 us
  transfers between devices with their start and end apart: 31, of which 14 were waited for; matrix products, arithmetic and copies ran while one was open for 2% of the time, Pallas kernels for 15%

profile of v3, /device:TPU:0, one launch (start us, length us, event | category | flops | bytes accessed | tf_op | source)
XLA Modules:
  0.0 149.3 jit_solution(7388655004269516801)
XLA Ops:
  0.6 8.4 %shard_map.158 = (bf16[4,48,384]{2,1,0:T(8,128)(2,1)}, bf16[4,48,384]{2,1,0:T(8,128)(2,1)}, bf16[4,48,384]{2,1,0:T(8,128)(2,1)}, bf16[4,48,384]{2,1,0:T(8,128)(2,1)}, f32[2,48,24,192]{3,2,1,0:T(8,128)}) custom-call(s32[1]{0:T(128)} %bitcast.group_ref, s32[1]{0:T(128)} %bitcast.3.rows_ref.row_ref, s32[768]{0:T(1024)} %cols_ref.1, f32[16]{0:T(128)} %gain_ref.1, ...), custom_call_target="tpu_custom_call" | custom-call | tf_op jit(solution)/shard_map/pallas_call | solution.py:219
  9.1 3.0 %collective-permute-start = (bf16[4,48,384]{2,1,0:T(8,128)(2,1)}, bf16[4,48,384]{2,1,0:T(8,128)(2,1)S(1)}, u32[]{:S(2)}, u32[]{:S(2)}) collective-permute-start(bf16[4,48,384]{2,1,0:T(8,128)(2,1)} %get-tuple-element.62), channel_id=1, source_target_pairs={{0,1},{1,0},{2,3},{3,2},{4,5},{5,4},{6,7},{7,6},{8,9},{9,8},{10,11... | collective-permute-start | bytes 442376 | tf_op jit(solution)/shard_map/ppermute | solution.py:604
  12.1 2.6 %collective-permute-start.1 = (bf16[4,48,384]{2,1,0:T(8,128)(2,1)}, bf16[4,48,384]{2,1,0:T(8,128)(2,1)S(1)}, u32[]{:S(2)}, u32[]{:S(2)}) collective-permute-start(bf16[4,48,384]{2,1,0:T(8,128)(2,1)} %get-tuple-element.63), channel_id=1, source_target_pairs={{0,2},{1,3},{2,0},{3,1},{4,6},{5,7},{6,4},{7,5},{8,10},{9,11},{10,... | collective-permute-start | bytes 442376 | tf_op jit(solution)/shard_map/ppermute | solution.py:604
  14.7 6.4 %shard_map.157 = (bf16[192,768]{1,0:T(8,128)(2,1)}, bf16[192,768]{1,0:T(8,128)(2,1)}, bf16[192,768]{1,0:T(8,128)(2,1)}, bf16[192,768]{1,0:T(8,128)(2,1)}, f32[192,768]{1,0:T(8,128)}, /*index=5*/f32[192,768]{1,0:T(8,128)}) custom-call(s32[1]{0:T(128)} %bitcast.group_ref, bf16[192,384]{1,0:T(8,128)(2,1)} %single_ref.3, bf16[192,768]{1,0:T(8,128)(2,1)} %bitcast.15, ...), custom_call_target="tpu_custom_call" | custom-call | tf_op jit(solution)/shard_map/pallas_call | solution.py:715
  21.1 2.0 %collective-permute-start.3 = (bf16[192,768]{1,0:T(8,128)(2,1)}, bf16[192,768]{1,0:T(8,128)(2,1)S(1)}, u32[]{:S(2)}, u32[]{:S(2)}) collective-permute-start(bf16[192,768]{1,0:T(8,128)(2,1)} %get-tuple-element.67), channel_id=1, source_target_pairs={{0,2},{1,3},{2,0},{3,1},{4,6},{5,7},{6,4},{7,5},{8,10},{9,11},{10,... | collective-permute-start | bytes 884744 | tf_op jit(solution)/shard_map/ppermute | solution.py:604
  23.0 9.6 %collective-permute-done.1 = bf16[4,48,384]{2,1,0:T(8,128)(2,1)S(1)} collective-permute-done((bf16[4,48,384]{2,1,0:T(8,128)(2,1)}, bf16[4,48,384]{2,1,0:T(8,128)(2,1)S(1)}, u32[]{:S(2)}, u32[]{:S(2)}) %collective-permute-start.1) | collective-permute-done | bytes 147488 | tf_op jit(solution)/shard_map/ppermute | solution.py:604
  32.6 0.0 collective-permute-done.2
  32.6 0.1 pad_maximum_fusion.rest_0_
  32.7 1.6 %collective-permute-start.6 = (bf16[4,4,48,384]{3,2,1,0:T(8,128)(2,1)S(1)}, bf16[4,4,48,384]{3,2,1,0:T(8,128)(2,1)S(1)}, u32[]{:S(2)}, u32[]{:S(2)}) collective-permute-start(bf16[4,4,48,384]{3,2,1,0:T(8,128)(2,1)S(1)} %pad_maximum_fusion.rest_0_), channel_id=1, source_target_pairs={{0,16},{4,20},{8,24},{12,28},{16,0},{20,4},{24,8},{28,12},{1,17},{... | collective-permute-start | bytes 1769480 | tf_op jit(solution)/shard_map/ppermute | solution.py:609
  34.3 1.5 %collective-permute-start.4 = (bf16[4,4,48,384]{3,2,1,0:T(8,128)(2,1)S(1)}, bf16[4,4,48,384]{3,2,1,0:T(8,128)(2,1)S(1)}, u32[]{:S(2)}, u32[]{:S(2)}) collective-permute-start(bf16[4,4,48,384]{3,2,1,0:T(8,128)(2,1)S(1)} %pad_maximum_fusion.rest_0_), channel_id=1, source_target_pairs={{0,8},{4,12},{8,0},{12,4},{16,24},{20,28},{24,16},{28,20},{1,9},{5... | collective-permute-start | bytes 1769480 | tf_op jit(solution)/shard_map/ppermute | solution.py:609
  35.8 4.9 %collective-permute-done.3.rest_12_ = bf16[192,768]{1,0:T(8,128)(2,1)S(1)} collective-permute-done((bf16[192,768]{1,0:T(8,128)(2,1)}, bf16[192,768]{1,0:T(8,128)(2,1)S(1)}, u32[]{:S(2)}, u32[]{:S(2)}) %collective-permute-start.3) | collective-permute-done | bytes 294944 | tf_op jit(solution)/shard_map/ppermute | solution.py:604
  40.7 0.0 collective-permute-start.8
  40.7 0.1 collective-permute-start.9
  40.8 2.5 %collective-permute-start.10 = (bf16[192,768]{1,0:T(8,128)(2,1)S(1)}, bf16[192,768]{1,0:T(8,128)(2,1)S(1)}, u32[]{:S(2)}, u32[]{:S(2)}) collective-permute-start(bf16[192,768]{1,0:T(8,128)(2,1)S(1)} %copy-done.26), channel_id=1, source_target_pairs={{0,3},{1,2},{2,1},{3,0},{4,7},{5,6},{6,5},{7,4},{8,11},{9,10},{10,... | collective-permute-start | bytes 884744 | tf_op jit(solution)/shard_map/ppermute | solution.py:604
  43.4 1.6 %collective-permute-start.7 = (bf16[2,4,48,384]{3,2,1,0:T(8,128)(2,1)S(1)}, bf16[2,4,48,384]{3,2,1,0:T(8,128)(2,1)S(1)}, u32[]{:S(2)}, u32[]{:S(2)}) collective-permute-start(bf16[2,4,48,384]{3,2,1,0:T(8,128)(2,1)S(1)} %slice.65), channel_id=1, source_target_pairs={{0,8},{4,12},{8,0},{12,4},{16,24},{20,28},{24,16},{28,20},{1,9},{5... | collective-permute-start | bytes 884744 | tf_op jit(solution)/shard_map/ppermute | solution.py:609
  44.9 0.0 collective-permute-done.4.rest_2_
  45.0 1.6 %collective-permute-start.5 = (bf16[2,4,48,384]{3,2,1,0:T(8,128)(2,1)S(1)}, bf16[2,4,48,384]{3,2,1,0:T(8,128)(2,1)S(1)}, u32[]{:S(2)}, u32[]{:S(2)}) collective-permute-start(bf16[2,4,48,384]{3,2,1,0:T(8,128)(2,1)S(1)} %slice.64), channel_id=1, source_target_pairs={{0,16},{4,20},{8,24},{12,28},{16,0},{20,4},{24,8},{28,12},{1,17},{... | collective-permute-start | bytes 884744 | tf_op jit(solution)/shard_map/ppermute | solution.py:609
  46.6 3.6 %collective-permute-done.9.rest_11_ = bf16[192,768]{1,0:T(8,128)(2,1)S(1)} collective-permute-done((bf16[192,768]{1,0:T(8,128)(2,1)S(1)}, bf16[192,768]{1,0:T(8,128)(2,1)S(1)}, u32[]{:S(2)}, u32[]{:S(2)}) %collective-permute-start.9) | collective-permute-done | bytes 294944 | tf_op jit(solution)/shard_map/ppermute | solution.py:604
  50.1 7.2 %collective-permute-done.10.rest_13_ = bf16[192,768]{1,0:T(8,128)(2,1)S(1)} collective-permute-done((bf16[192,768]{1,0:T(8,128)(2,1)S(1)}, bf16[192,768]{1,0:T(8,128)(2,1)S(1)}, u32[]{:S(2)}, u32[]{:S(2)}) %collective-permute-start.10) | collective-permute-done | bytes 294944 | tf_op jit(solution)/shard_map/ppermute | solution.py:604
  57.3 0.0 collective-permute-done.8.rest_1_
  57.3 0.0 collective-permute-done.5.rest_6_
  57.3 0.0 copy-start.14
  57.3 0.6 collective-permute-start.13
  57.9 0.1 collective-permute-start.14
  58.0 1.3 collective-permute-done.11.rest_3_
  59.3 0.4 collective-permute-done.13.rest_7_
  59.7 0.4 collective-permute-done.14.rest_9_
  60.2 0.2 copy-done.15
  60.4 0.7 copy-done.16
  61.1 18.6 %shard_map.159 = (bf16[192,768]{1,0:T(8,128)(2,1)}, bf16[192,768]{1,0:T(8,128)(2,1)}, bf16[192,768]{1,0:T(8,128)(2,1)}, bf16[192,768]{1,0:T(8,128)(2,1)}, bf16[1...) custom-call(s32[1]{0:T(128)} %bitcast.group_ref, ...), custom_call_target="tpu_custom_call" | custom-call | tf_op jit(solution)/shard_map/pallas_call | solution.py:508
  79.8 0.2 collective-permute-start.15
  80.0 2.9 %collective-permute-done.15 = bf16[8,4,48,384]{3,2,1,0:T(8,128)(2,1)S(1)} collective-permute-done((bf16[8,4,48,384]{3,2,1,0:T(8,128)(2,1)}, bf16[8,4,48,384]{3,2,1,0:T(8,128)(2,1)S(1)}, u32[]{:S(2)}, u32[]{:S(2)}) %collective-permute-start.15) | collective-permute-done | bytes 1179680 | tf_op jit(solution)/shard_map/ppermute | solution.py:609
  82.9 0.1 collective-permute-start.16
  83.0 1.7 %add_convert_fusion.2 = (bf16[4,4,48,384]{3,2,1,0:T(8,128)(2,1)S(1)}, bf16[4,4,48,384]{3,2,1,0:T(8,128)(2,1)S(1)}) fusion(bf16[8,4,48,384]{3,2,1,0:T(8,128)(2,1)S(1)} %collective-permute-done.15, bf16[16,4,48,384]{3,2,1,0:T(8,128)(2,1)} %get-tuple-element.80), kind=kLoop, calls=%fused_computation.2 | loop fusion | flops 2359296 | bytes 3538944 | tf_op jit(solution)/shard_map/convert_element_type | solution.py:653
  84.8 1.6 %collective-permute-start.17 = (bf16[4,4,48,384]{3,2,1,0:T(8,128)(2,1)S(1)}, bf16[4,4,48,384]{3,2,1,0:T(8,128)(2,1)S(1)}, u32[]{:S(2)}, u32[]{:S(2)}) collective-permute-start(bf16[4,4,48,384]{3,2,1,0:T(8,128)(2,1)S(1)} %get-tuple-element.117), channel_id=1, source_target_pairs={{0,8},{4,12},{8,0},{12,4},{16,24},{20,28},{24,16},{28,20},{1,9},{5... | collective-permute-start | bytes 1769480 | tf_op jit(solution)/shard_map/ppermute | solution.py:609
  86.3 1.5 %collective-permute-start.18 = (bf16[4,4,48,384]{3,2,1,0:T(8,128)(2,1)S(1)}, bf16[4,4,48,384]{3,2,1,0:T(8,128)(2,1)S(1)}, u32[]{:S(2)}, u32[]{:S(2)}) collective-permute-start(bf16[4,4,48,384]{3,2,1,0:T(8,128)(2,1)S(1)} %get-tuple-element.118), channel_id=1, source_target_pairs={{0,16},{4,20},{8,24},{12,28},{16,0},{20,4},{24,8},{28,12},{1,17},{... | collective-permute-start | bytes 1769480 | tf_op jit(solution)/shard_map/ppermute | solution.py:609
  87.8 0.9 collective-permute-start.21
  88.8 2.1 %collective-permute-start.22 = (bf16[192,768]{1,0:T(8,128)(2,1)S(1)}, bf16[192,768]{1,0:T(8,128)(2,1)S(1)}, u32[]{:S(2)}, u32[]{:S(2)}) collective-permute-start(bf16[192,768]{1,0:T(8,128)(2,1)S(1)} %copy-done.24), channel_id=1, source_target_pairs={{0,2},{1,3},{2,0},{3,1},{4,6},{5,7},{6,4},{7,5},{8,10},{9,11},{10,... | collective-permute-start | bytes 884744 | tf_op jit(solution)/shard_map/ppermute | solution.py:604
  90.9 9.5 %collective-permute-done.17 = bf16[4,4,48,384]{3,2,1,0:T(8,128)(2,1)S(1)} collective-permute-done((bf16[4,4,48,384]{3,2,1,0:T(8,128)(2,1)S(1)}, bf16[4,4,48,384]{3,2,1,0:T(8,128)(2,1)S(1)}, u32[]{:S(2)}, u32[]{:S(2)}) %collective-permute-start.17) | collective-permute-done | bytes 589856 | tf_op jit(solution)/shard_map/ppermute | solution.py:609
  100.4 2.5 %collective-permute-start.23 = (bf16[192,768]{1,0:T(8,128)(2,1)S(1)}, bf16[192,768]{1,0:T(8,128)(2,1)S(1)}, u32[]{:S(2)}, u32[]{:S(2)}) collective-permute-start(bf16[192,768]{1,0:T(8,128)(2,1)S(1)} %copy-done.23), channel_id=1, source_target_pairs={{0,3},{1,2},{2,1},{3,0},{4,7},{5,6},{6,5},{7,4},{8,11},{9,10},{10,... | collective-permute-start | bytes 884744 | tf_op jit(solution)/shard_map/ppermute | solution.py:604
  102.9 0.0 collective-permute-done.18
  102.9 0.2 add_convert_fusion.3
  103.2 1.6 %collective-permute-start.20 = (bf16[2,4,48,384]{3,2,1,0:T(8,128)(2,1)S(1)}, bf16[2,4,48,384]{3,2,1,0:T(8,128)(2,1)S(1)}, u32[]{:S(2)}, u32[]{:S(2)}) collective-permute-start(bf16[2,4,48,384]{3,2,1,0:T(8,128)(2,1)S(1)} %get-tuple-element.115), channel_id=1, source_target_pairs={{0,8},{4,12},{8,0},{12,4},{16,24},{20,28},{24,16},{28,20},{1,9},{5... | collective-permute-start | bytes 884744 | tf_op jit(solution)/shard_map/ppermute | solution.py:609
  104.7 1.5 %collective-permute-start.19 = (bf16[2,4,48,384]{3,2,1,0:T(8,128)(2,1)S(1)}, bf16[2,4,48,384]{3,2,1,0:T(8,128)(2,1)S(1)}, u32[]{:S(2)}, u32[]{:S(2)}) collective-permute-start(bf16[2,4,48,384]{3,2,1,0:T(8,128)(2,1)S(1)} %get-tuple-element.116), channel_id=1, source_target_pairs={{0,16},{4,20},{8,24},{12,28},{16,0},{20,4},{24,8},{28,12},{1,17},{... | collective-permute-start | bytes 884744 | tf_op jit(solution)/shard_map/ppermute | solution.py:609
  106.3 1.0 add_convert_fusion.own_ref
  107.4 3.5 %collective-permute-done.22.rest_2_ = bf16[192,768]{1,0:T(8,128)(2,1)S(1)} collective-permute-done((bf16[192,768]{1,0:T(8,128)(2,1)S(1)}, bf16[192,768]{1,0:T(8,128)(2,1)S(1)}, u32[]{:S(2)}, u32[]{:S(2)}) %collective-permute-start.22) | collective-permute-done | bytes 294944 | tf_op jit(solution)/shard_map/ppermute | solution.py:604
  110.8 0.6 collective-permute-done.20.near_ref
  111.4 1.2 collective-permute-done.19.far_ref
  112.6 0.7 copy-done.18
  113.3 2.1 %shard_map.160 = (bf16[4,48,384]{2,1,0:T(8,128)(2,1)}, bf16[4,48,384]{2,1,0:T(8,128)(2,1)}, bf16[4,48,384]{2,1,0:T(8,128)(2,1)}, bf16[4,48,384]{2,1,0:T(8,128)(2,1)}) custom-call(bf16[4,4,48,384]{3,2,1,0:T(8,128)(2,1)} %add_convert_fusion.own_ref, bf16[2,4,48,384]{3,2,1,0:T(8,128)(2,1)} %copy-done.18, bf16[2,4,48,384]{3,2,1,0:T(8,128)(2,1)} %copy-done.17), custom_call_target="tpu_custom_call" | custom-call | tf_op jit(solution)/shard_map/pallas_call | solution.py:665
  115.5 5.2 %collective-permute-start.24 = (bf16[4,48,384]{2,1,0:T(8,128)(2,1)}, bf16[4,48,384]{2,1,0:T(8,128)(2,1)S(1)}, u32[]{:S(2)}, u32[]{:S(2)}) collective-permute-start(bf16[4,48,384]{2,1,0:T(8,128)(2,1)} %get-tuple-element.106), channel_id=1, source_target_pairs={{0,1},{1,0},{2,3},{3,2},{4,5},{5,4},{6,7},{7,6},{8,9},{9,8},{10,11... | collective-permute-start | bytes 442376 | tf_op jit(solution)/shard_map/ppermute | solution.py:604
  120.7 1.0 collective-permute-start.25
  121.7 1.5 collective-permute-start.26
  123.2 7.5 %shard_map.161 = (bf16[192,768]{1,0:T(8,128)(2,1)}, bf16[192,384]{1,0:T(8,128)(2,1)}) custom-call(s32[1]{0:T(128)} %bitcast.group_ref, bf16[192,384]{1,0:T(8,128)(2,1)} %single_ref.3, bf16[192,768]{1,0:T(8,128)(2,1)} %bitcast.16, bf16[192,768]{1,0:T(8,128)(2,1)} %bitcast.18, f32[192,768]{1,0:T(8,128)} %get-tuple-element.59.gamma_ref, ...), custom_call_target="tpu_custom_call" | custom-call | tf_op jit(solution)/shard_map/pallas_call | solution.py:749
  130.7 0.0 copy-start.20
  130.7 3.5 %collective-permute-done.25.rest_2_ = bf16[4,48,384]{2,1,0:T(8,128)(2,1)S(1)} collective-permute-done((bf16[4,48,384]{2,1,0:T(8,128)(2,1)}, bf16[4,48,384]{2,1,0:T(8,128)(2,1)S(1)}, u32[]{:S(2)}, u32[]{:S(2)}) %collective-permute-start.25) | collective-permute-done | bytes 147488 | tf_op jit(solution)/shard_map/ppermute | solution.py:604
  134.1 0.1 collective-permute-start.27
  134.2 1.6 %collective-permute-done.27 = bf16[192,384]{1,0:T(8,128)(2,1)S(1)} collective-permute-done((bf16[192,384]{1,0:T(8,128)(2,1)}, bf16[192,384]{1,0:T(8,128)(2,1)S(1)}, u32[]{:S(2)}, u32[]{:S(2)}) %collective-permute-start.27) | collective-permute-done | bytes 147488 | tf_op jit(solution)/shard_map/ppermute | solution.py:609
  135.8 1.0 add_convert_fusion.5
  136.7 0.7 collective-permute-start.30
  137.4 1.5 %collective-permute-start.29 = (bf16[192,384]{1,0:T(8,128)(2,1)S(1)}, bf16[192,384]{1,0:T(8,128)(2,1)S(1)}, u32[]{:S(2)}, u32[]{:S(2)}) collective-permute-start(bf16[192,384]{1,0:T(8,128)(2,1)S(1)} %add_convert_fusion.5), channel_id=1, source_target_pairs={{0,16},{4,20},{8,24},{12,28},{16,0},{20,4},{24,8},{28,12},{1,17},{... | collective-permute-start | bytes 442376 | tf_op jit(solution)/shard_map/ppermute | solution.py:609
  139.0 1.3 collective-permute-start.28
  140.3 8.2 %shard_map.162 = bf16[2,48,192,128]{3,2,1,0:T(8,128)(2,1)} custom-call(s32[1]{0:T(128)} %bitcast.group_ref, bf16[2,48,192,128]{3,2,1,0:T(8,128)(2,1)} %bitcast.13, f32[2,48,24,192]{3,2,1,0:T(8,128)} %get-tuple-element.110.stats_ref, bf16[16,128]{1,0:T(8,128)(2,1)} %bitcast.24, bf16[4,48,384]{2,1,0:T(8,128)(2,1)} %get-tuple-element.111.rest_0_, ...), custom_call_target="tpu_custom_call" | custom-call | tf_op jit(solution)/shard_map/pallas_call | solution.py:330
  148.5 0.8 add_add_fusion
  (70 shorter events, 0.3 us)
Async XLA Ops:
  9.1 14.0 %collective-permute-start = (bf16[4,48,384]{2,1,0:T(8,128)(2,1)}, bf16[4,48,384]{2,1,0:T(8,128)(2,1)S(1)}, u32[]{:S(2)}, u32[]{:S(2)}) collective-permute-start(bf16[4,48,384]{2,1,0:T(8,128)(2,1)} %get-tuple-element.62), channel_id=1, source_target_pairs={{0,1},{1,0},{2,3},{3,2},{4,5},{5,4},{6,7},{7,6},{8,9},{9,8},{10,11... | collective-permute-start | bytes 442376 | tf_op jit(solution)/shard_map/ppermute | solution.py:604
  12.1 20.5 %collective-permute-start.1 = (bf16[4,48,384]{2,1,0:T(8,128)(2,1)}, bf16[4,48,384]{2,1,0:T(8,128)(2,1)S(1)}, u32[]{:S(2)}, u32[]{:S(2)}) collective-permute-start(bf16[4,48,384]{2,1,0:T(8,128)(2,1)} %get-tuple-element.63), channel_id=1, source_target_pairs={{0,2},{1,3},{2,0},{3,1},{4,6},{5,7},{6,4},{7,5},{8,10},{9,11},{10,... | collective-permute-start | bytes 442376 | tf_op jit(solution)/shard_map/ppermute | solution.py:604
  14.7 17.9 %collective-permute-start.2 = (bf16[4,48,384]{2,1,0:T(8,128)(2,1)}, bf16[4,48,384]{2,1,0:T(8,128)(2,1)S(1)}, u32[]{:S(2)}, u32[]{:S(2)}) collective-permute-start(bf16[4,48,384]{2,1,0:T(8,128)(2,1)} %get-tuple-element.64), channel_id=1, source_target_pairs={{0,3},{1,2},{2,1},{3,0},{4,7},{5,6},{6,5},{7,4},{8,11},{9,10},{10,... | collective-permute-start | bytes 442376 | tf_op jit(solution)/shard_map/ppermute | solution.py:604
  14.7 17.9 %copy-start.19 = (bf16[4,48,384]{2,1,0:T(8,128)(2,1)S(1)}, bf16[4,48,384]{2,1,0:T(8,128)(2,1)}, u32[]{:S(2)}) copy-start(bf16[4,48,384]{2,1,0:T(8,128)(2,1)} %get-tuple-element.69) | copy-start | bytes 442372
  21.1 19.6 %copy-start.27 = (bf16[192,768]{1,0:T(8,128)(2,1)S(1)}, bf16[192,768]{1,0:T(8,128)(2,1)}, u32[]{:S(2)}) copy-start(bf16[192,768]{1,0:T(8,128)(2,1)} %get-tuple-element.66) | copy-start | bytes 884740
  21.1 19.7 %copy-start.26 = (bf16[192,768]{1,0:T(8,128)(2,1)S(1)}, bf16[192,768]{1,0:T(8,128)(2,1)}, u32[]{:S(2)}) copy-start(bf16[192,768]{1,0:T(8,128)(2,1)} %get-tuple-element.68) | copy-start | bytes 884740
  21.1 19.6 %collective-permute-start.3 = (bf16[192,768]{1,0:T(8,128)(2,1)}, bf16[192,768]{1,0:T(8,128)(2,1)S(1)}, u32[]{:S(2)}, u32[]{:S(2)}) collective-permute-start(bf16[192,768]{1,0:T(8,128)(2,1)} %get-tuple-element.67), channel_id=1, source_target_pairs={{0,2},{1,3},{2,0},{3,1},{4,6},{5,7},{6,4},{7,5},{8,10},{9,11},{10,... | collective-permute-start | bytes 884744 | tf_op jit(solution)/shard_map/ppermute | solution.py:604
  32.7 27.4 %copy-start = (bf16[4,4,48,384]{3,2,1,0:T(8,128)(2,1)}, bf16[4,4,48,384]{3,2,1,0:T(8,128)(2,1)S(1)}, u32[]{:S(2)}) copy-start(bf16[4,4,48,384]{3,2,1,0:T(8,128)(2,1)S(1)} %pad_maximum_fusion.rest_0_) | copy-start | bytes 1769476
  32.7 10.6 %collective-permute-start.6 = (bf16[4,4,48,384]{3,2,1,0:T(8,128)(2,1)S(1)}, bf16[4,4,48,384]{3,2,1,0:T(8,128)(2,1)S(1)}, u32[]{:S(2)}, u32[]{:S(2)}) collective-permute-start(bf16[4,4,48,384]{3,2,1,0:T(8,128)(2,1)S(1)} %pad_maximum_fusion.rest_0_), channel_id=1, source_target_pairs={{0,16},{4,20},{8,24},{12,28},{16,0},{20,4},{24,8},{28,12},{1,17},{... | collective-permute-start | bytes 1769480 | tf_op jit(solution)/shard_map/ppermute | solution.py:609
  34.3 10.6 %collective-permute-start.4 = (bf16[4,4,48,384]{3,2,1,0:T(8,128)(2,1)S(1)}, bf16[4,4,48,384]{3,2,1,0:T(8,128)(2,1)S(1)}, u32[]{:S(2)}, u32[]{:S(2)}) collective-permute-start(bf16[4,4,48,384]{3,2,1,0:T(8,128)(2,1)S(1)} %pad_maximum_fusion.rest_0_), channel_id=1, source_target_pairs={{0,8},{4,12},{8,0},{12,4},{16,24},{20,28},{24,16},{28,20},{1,9},{5... | collective-permute-start | bytes 1769480 | tf_op jit(solution)/shard_map/ppermute | solution.py:609
  40.7 19.4 %copy-start.7 = (bf16[192,768]{1,0:T(8,128)(2,1)}, bf16[192,768]{1,0:T(8,128)(2,1)S(1)}, u32[]{:S(2)}) copy-start(bf16[192,768]{1,0:T(8,128)(2,1)S(1)} %collective-permute-done.3.rest_12_) | copy-start | bytes 884740
  40.7 16.6 %collective-permute-start.8 = (bf16[4,4,48,384]{3,2,1,0:T(8,128)(2,1)S(1)}, bf16[4,4,48,384]{3,2,1,0:T(8,128)(2,1)S(1)}, u32[]{:S(2)}, u32[]{:S(2)}) collective-permute-start(bf16[4,4,48,384]{3,2,1,0:T(8,128)(2,1)S(1)} %pad_maximum_fusion.rest_0_), channel_id=1, source_target_pairs={{0,4},{4,0},{8,12},{12,8},{16,20},{20,16},{24,28},{28,24},{1,5},{5... | collective-permute-start | bytes 1769480 | tf_op jit(solution)/shard_map/ppermute | solution.py:609
  40.7 9.4 %collective-permute-start.9 = (bf16[192,768]{1,0:T(8,128)(2,1)S(1)}, bf16[192,768]{1,0:T(8,128)(2,1)S(1)}, u32[]{:S(2)}, u32[]{:S(2)}) collective-permute-start(bf16[192,768]{1,0:T(8,128)(2,1)S(1)} %copy-done.27), channel_id=1, source_target_pairs={{0,1},{1,0},{2,3},{3,2},{4,5},{5,4},{6,7},{7,6},{8,9},{9,8},{10,11... | collective-permute-start | bytes 884744 | tf_op jit(solution)/shard_map/ppermute | solution.py:604
  40.8 16.5 %collective-permute-start.10 = (bf16[192,768]{1,0:T(8,128)(2,1)S(1)}, bf16[192,768]{1,0:T(8,128)(2,1)S(1)}, u32[]{:S(2)}, u32[]{:S(2)}) collective-permute-start(bf16[192,768]{1,0:T(8,128)(2,1)S(1)} %copy-done.26), channel_id=1, source_target_pairs={{0,3},{1,2},{2,1},{3,0},{4,7},{5,6},{6,5},{7,4},{8,11},{9,10},{10,... | collective-permute-start | bytes 884744 | tf_op jit(solution)/shard_map/ppermute | solution.py:604
  43.3 16.8 %copy-start.2 = (bf16[4,4,48,384]{3,2,1,0:T(8,128)(2,1)}, bf16[4,4,48,384]{3,2,1,0:T(8,128)(2,1)S(1)}, u32[]{:S(2)}) copy-start(bf16[4,4,48,384]{3,2,1,0:T(8,128)(2,1)S(1)} %collective-permute-done.6.rest_4_) | copy-start | bytes 1769476
  43.4 13.9 %collective-permute-start.7 = (bf16[2,4,48,384]{3,2,1,0:T(8,128)(2,1)S(1)}, bf16[2,4,48,384]{3,2,1,0:T(8,128)(2,1)S(1)}, u32[]{:S(2)}, u32[]{:S(2)}) collective-permute-start(bf16[2,4,48,384]{3,2,1,0:T(8,128)(2,1)S(1)} %slice.65), channel_id=1, source_target_pairs={{0,8},{4,12},{8,0},{12,4},{16,24},{20,28},{24,16},{28,20},{1,9},{5... | collective-permute-start | bytes 884744 | tf_op jit(solution)/shard_map/ppermute | solution.py:609
  44.9 15.2 %copy-start.3 = (bf16[4,4,48,384]{3,2,1,0:T(8,128)(2,1)}, bf16[4,4,48,384]{3,2,1,0:T(8,128)(2,1)S(1)}, u32[]{:S(2)}) copy-start(bf16[4,4,48,384]{3,2,1,0:T(8,128)(2,1)S(1)} %collective-permute-done.4.rest_2_) | copy-start | bytes 1769476
  45.0 12.4 %collective-permute-start.5 = (bf16[2,4,48,384]{3,2,1,0:T(8,128)(2,1)S(1)}, bf16[2,4,48,384]{3,2,1,0:T(8,128)(2,1)S(1)}, u32[]{:S(2)}, u32[]{:S(2)}) collective-permute-start(bf16[2,4,48,384]{3,2,1,0:T(8,128)(2,1)S(1)} %slice.64), channel_id=1, source_target_pairs={{0,16},{4,20},{8,24},{12,28},{16,0},{20,4},{24,8},{28,12},{1,17},{... | collective-permute-start | bytes 884744 | tf_op jit(solution)/shard_map/ppermute | solution.py:609
  50.1 10.0 %copy-start.10 = (bf16[192,768]{1,0:T(8,128)(2,1)}, bf16[192,768]{1,0:T(8,128)(2,1)S(1)}, u32[]{:S(2)}) copy-start(bf16[192,768]{1,0:T(8,128)(2,1)S(1)} %collective-permute-done.9.rest_11_) | copy-start | bytes 884740
  50.1 7.9 %collective-permute-start.12 = (bf16[4,4,48,384]{3,2,1,0:T(8,128)(2,1)S(1)}, bf16[4,4,48,384]{3,2,1,0:T(8,128)(2,1)S(1)}, u32[]{:S(2)}, u32[]{:S(2)}) collective-permute-start(bf16[4,4,48,384]{3,2,1,0:T(8,128)(2,1)S(1)} %collective-permute-done.6.rest_4_), channel_id=1, source_target_pairs={{0,4},{4,0},{8,12},{12,8},{16,20},{20,16},{24,28},{28,24},{1,5},{5... | collective-permute-start | bytes 1769480 | tf_op jit(solution)/shard_map/ppermute | solution.py:609
  57.3 2.9 %copy-start.12 = (bf16[192,768]{1,0:T(8,128)(2,1)}, bf16[192,768]{1,0:T(8,128)(2,1)S(1)}, u32[]{:S(2)}) copy-start(bf16[192,768]{1,0:T(8,128)(2,1)S(1)} %collective-permute-done.10.rest_13_) | copy-start | bytes 884740
  57.3 2.0 %collective-permute-start.11 = (bf16[4,4,48,384]{3,2,1,0:T(8,128)(2,1)S(1)}, bf16[4,4,48,384]{3,2,1,0:T(8,128)(2,1)S(1)}, u32[]{:S(2)}, u32[]{:S(2)}) collective-permute-start(bf16[4,4,48,384]{3,2,1,0:T(8,128)(2,1)S(1)} %collective-permute-done.4.rest_2_), channel_id=1, source_target_pairs={{0,4},{4,0},{8,12},{12,8},{16,20},{20,16},{24,28},{28,24},{1,5},{5... | collective-permute-start | bytes 1769480 | tf_op jit(solution)/shard_map/ppermute | solution.py:609
  57.3 2.9 %copy-start.4 = (bf16[4,4,48,384]{3,2,1,0:T(8,128)(2,1)}, bf16[4,4,48,384]{3,2,1,0:T(8,128)(2,1)S(1)}, u32[]{:S(2)}) copy-start(bf16[4,4,48,384]{3,2,1,0:T(8,128)(2,1)S(1)} %collective-permute-done.8.rest_1_) | copy-start | bytes 1769476
  57.3 2.9 %copy-start.13 = (bf16[2,4,48,384]{3,2,1,0:T(8,128)(2,1)}, bf16[2,4,48,384]{3,2,1,0:T(8,128)(2,1)S(1)}, u32[]{:S(2)}) copy-start(bf16[2,4,48,384]{3,2,1,0:T(8,128)(2,1)S(1)} %collective-permute-done.7.rest_8_) | copy-start | bytes 884740
  57.3 2.9 %copy-start.14 = (bf16[2,4,48,384]{3,2,1,0:T(8,128)(2,1)}, bf16[2,4,48,384]{3,2,1,0:T(8,128)(2,1)S(1)}, u32[]{:S(2)}) copy-start(bf16[2,4,48,384]{3,2,1,0:T(8,128)(2,1)S(1)} %collective-permute-done.5.rest_6_) | copy-start | bytes 884740
  57.3 2.4 %collective-permute-start.13 = (bf16[2,4,48,384]{3,2,1,0:T(8,128)(2,1)S(1)}, bf16[2,4,48,384]{3,2,1,0:T(8,128)(2,1)S(1)}, u32[]{:S(2)}, u32[]{:S(2)}) collective-permute-start(bf16[2,4,48,384]{3,2,1,0:T(8,128)(2,1)S(1)} %collective-permute-done.5.rest_6_), channel_id=1, source_target_pairs={{0,4},{4,0},{8,12},{12,8},{16,20},{20,16},{24,28},{28,24},{1,5},{5... | collective-permute-start | bytes 884744 | tf_op jit(solution)/shard_map/ppermute | solution.py:609
  57.9 2.2 %collective-permute-start.14 = (bf16[2,4,48,384]{3,2,1,0:T(8,128)(2,1)S(1)}, bf16[2,4,48,384]{3,2,1,0:T(8,128)(2,1)S(1)}, u32[]{:S(2)}, u32[]{:S(2)}) collective-permute-start(bf16[2,4,48,384]{3,2,1,0:T(8,128)(2,1)S(1)} %collective-permute-done.7.rest_8_), channel_id=1, source_target_pairs={{0,4},{4,0},{8,12},{12,8},{16,20},{20,16},{24,28},{28,24},{1,5},{5... | collective-permute-start | bytes 884744 | tf_op jit(solution)/shard_map/ppermute | solution.py:609
  58.0 2.2 %copy-start.5 = (bf16[4,4,48,384]{3,2,1,0:T(8,128)(2,1)}, bf16[4,4,48,384]{3,2,1,0:T(8,128)(2,1)S(1)}, u32[]{:S(2)}) copy-start(bf16[4,4,48,384]{3,2,1,0:T(8,128)(2,1)S(1)} %collective-permute-done.12.rest_5_) | copy-start | bytes 1769476
  59.3 0.9 copy-start.6
  59.7 0.7 copy-start.15
  60.4 0.7 copy-start.16
  79.8 3.1 %collective-permute-start.15 = (bf16[8,4,48,384]{3,2,1,0:T(8,128)(2,1)}, bf16[8,4,48,384]{3,2,1,0:T(8,128)(2,1)S(1)}, u32[]{:S(2)}, u32[]{:S(2)}) collective-permute-start(bf16[8,4,48,384]{3,2,1,0:T(8,128)(2,1)} %get-tuple-element.81), channel_id=1, source_target_pairs={{0,4},{4,0},{8,12},{12,8},{16,20},{20,16},{24,28},{28,24},{1,5},{5... | collective-permute-start | bytes 3538952 | tf_op jit(solution)/shard_map/ppermute | solution.py:609
  82.9 20.0 %collective-permute-start.16 = (bf16[8,4,48,384]{3,2,1,0:T(8,128)(2,1)}, bf16[8,4,48,384]{3,2,1,0:T(8,128)(2,1)S(1)}, u32[]{:S(2)}, u32[]{:S(2)}) collective-permute-start(bf16[8,4,48,384]{3,2,1,0:T(8,128)(2,1)} %get-tuple-element.83), channel_id=1, source_target_pairs={{0,4},{4,0},{8,12},{12,8},{16,20},{20,16},{24,28},{28,24},{1,5},{5... | collective-permute-start | bytes 3538952 | tf_op jit(solution)/shard_map/ppermute | solution.py:609
  83.0 4.8 %copy-start.25 = (bf16[192,768]{1,0:T(8,128)(2,1)S(1)}, bf16[192,768]{1,0:T(8,128)(2,1)}, u32[]{:S(2)}) copy-start(bf16[192,768]{1,0:T(8,128)(2,1)} %get-tuple-element.86) | copy-start | bytes 884740
  83.0 5.7 %copy-start.24 = (bf16[192,768]{1,0:T(8,128)(2,1)S(1)}, bf16[192,768]{1,0:T(8,128)(2,1)}, u32[]{:S(2)}) copy-start(bf16[192,768]{1,0:T(8,128)(2,1)} %get-tuple-element.87) | copy-start | bytes 884740
  83.0 17.4 %copy-start.23 = (bf16[192,768]{1,0:T(8,128)(2,1)S(1)}, bf16[192,768]{1,0:T(8,128)(2,1)}, u32[]{:S(2)}) copy-start(bf16[192,768]{1,0:T(8,128)(2,1)} %get-tuple-element.88) | copy-start | bytes 884740
  83.0 19.9 %copy-start.1 = (bf16[16,4,48,384]{3,2,1,0:T(8,128)(2,1)S(1)}, bf16[16,4,48,384]{3,2,1,0:T(8,128)(2,1)}, u32[]{:S(2)}) copy-start(bf16[16,4,48,384]{3,2,1,0:T(8,128)(2,1)} %get-tuple-element.80) | copy-start | bytes 7077892
  84.8 15.7 %collective-permute-start.17 = (bf16[4,4,48,384]{3,2,1,0:T(8,128)(2,1)S(1)}, bf16[4,4,48,384]{3,2,1,0:T(8,128)(2,1)S(1)}, u32[]{:S(2)}, u32[]{:S(2)}) collective-permute-start(bf16[4,4,48,384]{3,2,1,0:T(8,128)(2,1)S(1)} %get-tuple-element.117), channel_id=1, source_target_pairs={{0,8},{4,12},{8,0},{12,4},{16,24},{20,28},{24,16},{28,20},{1,9},{5... | collective-permute-start | bytes 1769480 | tf_op jit(solution)/shard_map/ppermute | solution.py:609
  86.3 16.6 %collective-permute-start.18 = (bf16[4,4,48,384]{3,2,1,0:T(8,128)(2,1)S(1)}, bf16[4,4,48,384]{3,2,1,0:T(8,128)(2,1)S(1)}, u32[]{:S(2)}, u32[]{:S(2)}) collective-permute-start(bf16[4,4,48,384]{3,2,1,0:T(8,128)(2,1)S(1)} %get-tuple-element.118), channel_id=1, source_target_pairs={{0,16},{4,20},{8,24},{12,28},{16,0},{20,4},{24,8},{28,12},{1,17},{... | collective-permute-start | bytes 1769480 | tf_op jit(solution)/shard_map/ppermute | solution.py:609
  87.8 19.5 %collective-permute-start.21 = (bf16[192,768]{1,0:T(8,128)(2,1)S(1)}, bf16[192,768]{1,0:T(8,128)(2,1)S(1)}, u32[]{:S(2)}, u32[]{:S(2)}) collective-permute-start(bf16[192,768]{1,0:T(8,128)(2,1)S(1)} %copy-done.25), channel_id=1, source_target_pairs={{0,1},{1,0},{2,3},{3,2},{4,5},{5,4},{6,7},{7,6},{8,9},{9,8},{10,11... | collective-permute-start | bytes 884744 | tf_op jit(solution)/shard_map/ppermute | solution.py:604
  88.8 22.1 %collective-permute-start.22 = (bf16[192,768]{1,0:T(8,128)(2,1)S(1)}, bf16[192,768]{1,0:T(8,128)(2,1)S(1)}, u32[]{:S(2)}, u32[]{:S(2)}) collective-permute-start(bf16[192,768]{1,0:T(8,128)(2,1)S(1)} %copy-done.24), channel_id=1, source_target_pairs={{0,2},{1,3},{2,0},{3,1},{4,6},{5,7},{6,4},{7,5},{8,10},{9,11},{10,... | collective-permute-start | bytes 884744 | tf_op jit(solution)/shard_map/ppermute | solution.py:604
  100.4 10.4 %collective-permute-start.23 = (bf16[192,768]{1,0:T(8,128)(2,1)S(1)}, bf16[192,768]{1,0:T(8,128)(2,1)S(1)}, u32[]{:S(2)}, u32[]{:S(2)}) collective-permute-start(bf16[192,768]{1,0:T(8,128)(2,1)S(1)} %copy-done.23), channel_id=1, source_target_pairs={{0,3},{1,2},{2,1},{3,0},{4,7},{5,6},{6,5},{7,4},{8,11},{9,10},{10,... | collective-permute-start | bytes 884744 | tf_op jit(solution)/shard_map/ppermute | solution.py:604
  103.2 8.3 %collective-permute-start.20 = (bf16[2,4,48,384]{3,2,1,0:T(8,128)(2,1)S(1)}, bf16[2,4,48,384]{3,2,1,0:T(8,128)(2,1)S(1)}, u32[]{:S(2)}, u32[]{:S(2)}) collective-permute-start(bf16[2,4,48,384]{3,2,1,0:T(8,128)(2,1)S(1)} %get-tuple-element.115), channel_id=1, source_target_pairs={{0,8},{4,12},{8,0},{12,4},{16,24},{20,28},{24,16},{28,20},{1,9},{5... | collective-permute-start | bytes 884744 | tf_op jit(solution)/shard_map/ppermute | solution.py:609
  104.7 7.9 %collective-permute-start.19 = (bf16[2,4,48,384]{3,2,1,0:T(8,128)(2,1)S(1)}, bf16[2,4,48,384]{3,2,1,0:T(8,128)(2,1)S(1)}, u32[]{:S(2)}, u32[]{:S(2)}) collective-permute-start(bf16[2,4,48,384]{3,2,1,0:T(8,128)(2,1)S(1)} %get-tuple-element.116), channel_id=1, source_target_pairs={{0,16},{4,20},{8,24},{12,28},{16,0},{20,4},{24,8},{28,12},{1,17},{... | collective-permute-start | bytes 884744 | tf_op jit(solution)/shard_map/ppermute | solution.py:609
  107.4 15.8 %copy-start.8 = (bf16[192,768]{1,0:T(8,128)(2,1)}, bf16[192,768]{1,0:T(8,128)(2,1)S(1)}, u32[]{:S(2)}) copy-start(bf16[192,768]{1,0:T(8,128)(2,1)S(1)} %collective-permute-done.21.rest_1_) | copy-start | bytes 884740
  110.8 12.3 %copy-start.9 = (bf16[192,768]{1,0:T(8,128)(2,1)}, bf16[192,768]{1,0:T(8,128)(2,1)S(1)}, u32[]{:S(2)}) copy-start(bf16[192,768]{1,0:T(8,128)(2,1)S(1)} %collective-permute-done.22.rest_2_) | copy-start | bytes 884740
  110.8 12.3 %copy-start.11 = (bf16[192,768]{1,0:T(8,128)(2,1)}, bf16[192,768]{1,0:T(8,128)(2,1)S(1)}, u32[]{:S(2)}) copy-start(bf16[192,768]{1,0:T(8,128)(2,1)S(1)} %collective-permute-done.23.rest_3_) | copy-start | bytes 884740
  111.4 1.2 copy-start.17
  112.6 0.7 copy-start.18
  115.5 15.2 %collective-permute-start.24 = (bf16[4,48,384]{2,1,0:T(8,128)(2,1)}, bf16[4,48,384]{2,1,0:T(8,128)(2,1)S(1)}, u32[]{:S(2)}, u32[]{:S(2)}) collective-permute-start(bf16[4,48,384]{2,1,0:T(8,128)(2,1)} %get-tuple-element.106), channel_id=1, source_target_pairs={{0,1},{1,0},{2,3},{3,2},{4,5},{5,4},{6,7},{7,6},{8,9},{9,8},{10,11... | collective-permute-start | bytes 442376 | tf_op jit(solution)/shard_map/ppermute | solution.py:604
  120.7 13.5 %collective-permute-start.25 = (bf16[4,48,384]{2,1,0:T(8,128)(2,1)}, bf16[4,48,384]{2,1,0:T(8,128)(2,1)S(1)}, u32[]{:S(2)}, u32[]{:S(2)}) collective-permute-start(bf16[4,48,384]{2,1,0:T(8,128)(2,1)} %get-tuple-element.107), channel_id=1, source_target_pairs={{0,2},{1,3},{2,0},{3,1},{4,6},{5,7},{6,4},{7,5},{8,10},{9,11},{10,... | collective-permute-start | bytes 442376 | tf_op jit(solution)/shard_map/ppermute | solution.py:604
  121.7 12.4 %collective-permute-start.26 = (bf16[4,48,384]{2,1,0:T(8,128)(2,1)}, bf16[4,48,384]{2,1,0:T(8,128)(2,1)S(1)}, u32[]{:S(2)}, u32[]{:S(2)}) collective-permute-start(bf16[4,48,384]{2,1,0:T(8,128)(2,1)} %get-tuple-element.108), channel_id=1, source_target_pairs={{0,3},{1,2},{2,1},{3,0},{4,7},{5,6},{6,5},{7,4},{8,11},{9,10},{10,... | collective-permute-start | bytes 442376 | tf_op jit(solution)/shard_map/ppermute | solution.py:604
  130.7 9.6 %copy-start.20 = (bf16[4,48,384]{2,1,0:T(8,128)(2,1)}, bf16[4,48,384]{2,1,0:T(8,128)(2,1)S(1)}, u32[]{:S(2)}) copy-start(bf16[4,48,384]{2,1,0:T(8,128)(2,1)S(1)} %collective-permute-done.24.rest_1_) | copy-start | bytes 442372
  134.1 6.2 %copy-start.21 = (bf16[4,48,384]{2,1,0:T(8,128)(2,1)}, bf16[4,48,384]{2,1,0:T(8,128)(2,1)S(1)}, u32[]{:S(2)}) copy-start(bf16[4,48,384]{2,1,0:T(8,128)(2,1)S(1)} %collective-permute-done.25.rest_2_) | copy-start | bytes 442372
  134.1 6.2 %copy-start.22 = (bf16[4,48,384]{2,1,0:T(8,128)(2,1)}, bf16[4,48,384]{2,1,0:T(8,128)(2,1)S(1)}, u32[]{:S(2)}) copy-start(bf16[4,48,384]{2,1,0:T(8,128)(2,1)S(1)} %collective-permute-done.26.rest_3_) | copy-start | bytes 442372
  134.1 1.6 %collective-permute-start.27 = (bf16[192,384]{1,0:T(8,128)(2,1)}, bf16[192,384]{1,0:T(8,128)(2,1)S(1)}, u32[]{:S(2)}, u32[]{:S(2)}) collective-permute-start(bf16[192,384]{1,0:T(8,128)(2,1)} %get-tuple-element.109), channel_id=1, source_target_pairs={{0,4},{4,0},{8,12},{12,8},{16,20},{20,16},{24,28},{28,24},{1,5},{5... | collective-permute-start | bytes 442376 | tf_op jit(solution)/shard_map/ppermute | solution.py:609
  136.7 11.8 %collective-permute-start.30 = (bf16[192,384]{1,0:T(8,128)(2,1)S(1)}, bf16[192,384]{1,0:T(8,128)(2,1)S(1)}, u32[]{:S(2)}, u32[]{:S(2)}) collective-permute-start(bf16[192,384]{1,0:T(8,128)(2,1)S(1)} %add_convert_fusion.5), channel_id=1, source_target_pairs={{0,24},{4,28},{8,16},{12,20},{16,8},{20,12},{24,0},{28,4},{1,25},{... | collective-permute-start | bytes 442376 | tf_op jit(solution)/shard_map/ppermute | solution.py:609
  137.4 11.1 %collective-permute-start.29 = (bf16[192,384]{1,0:T(8,128)(2,1)S(1)}, bf16[192,384]{1,0:T(8,128)(2,1)S(1)}, u32[]{:S(2)}, u32[]{:S(2)}) collective-permute-start(bf16[192,384]{1,0:T(8,128)(2,1)S(1)} %add_convert_fusion.5), channel_id=1, source_target_pairs={{0,16},{4,20},{8,24},{12,28},{16,0},{20,4},{24,8},{28,12},{1,17},{... | collective-permute-start | bytes 442376 | tf_op jit(solution)/shard_map/ppermute | solution.py:609
  139.0 9.6 %collective-permute-start.28 = (bf16[192,384]{1,0:T(8,128)(2,1)S(1)}, bf16[192,384]{1,0:T(8,128)(2,1)S(1)}, u32[]{:S(2)}, u32[]{:S(2)}) collective-permute-start(bf16[192,384]{1,0:T(8,128)(2,1)S(1)} %add_convert_fusion.5), channel_id=1, source_target_pairs={{0,8},{4,12},{8,0},{12,4},{16,24},{20,28},{24,16},{28,20},{1,9},{5... | collective-permute-start | bytes 442376 | tf_op jit(solution)/shard_map/ppermute | solution.py:609

commit v4 on v3

--- a/solution.py
+++ b/solution.py
@@ -196,15 +196,11 @@
                         flat_ref[side, tile, pl.ds(row, heads, stride=step), :] = piece
     for head in range(heads):
         slot = group_own ^ (head // per_group)
-        values = jnp.concatenate(
-            [
-                flat_ref[side, tile, head * step : (head + 1) * step, : end - start]
-                for side in range(2)
-                for tile, start, end in lane_tiles(cols)
-            ],
-            axis=1,
-        )
-        stage_ref[slot, head % per_group] = values.astype(BF16)
+        tops = slice(head * step, (head + 1) * step)
+        rest_lanes = [flat_ref[side, 1, tops, : cols - 128] for side in range(2)]
+        stage_ref[slot, head % per_group, 0] = flat_ref[0, 0, tops, :].astype(BF16)
+        stage_ref[slot, head % per_group, 1] = flat_ref[1, 0, tops, :].astype(BF16)
+        stage_ref[slot, head % per_group, 2] = jnp.concatenate(rest_lanes, axis=1).astype(BF16)
     for slot in range(groups):
         send_refs[slot][...] = stage_ref[slot]
 
@@ -229,17 +225,17 @@
             pl.BlockSpec((groups * cols,), lambda t: (0,)),
         ],
         out_specs=[
-            pl.BlockSpec((per_group, step, 2 * cols), lambda t: (0, t, 0)) for _ in range(groups)
+            pl.BlockSpec((per_group, 3, step, 128), lambda t: (0, 0, t, 0)) for _ in range(groups)
         ]
         + [pl.BlockSpec((2, step, heads + 8, cols), lambda t: (0, t, 0, 0))],
         out_shape=[
-            jax.ShapeDtypeStruct((per_group, half, 2 * cols), BF16) for _ in range(groups)
+            jax.ShapeDtypeStruct((per_group, 3, half, 128), BF16) for _ in range(groups)
         ]
         + [jax.ShapeDtypeStruct((2, half, heads + 8, cols), F32)],
         scratch_shapes=[
             pltpu.VMEM((2, tiles, heads * step, 128), F32),
             pltpu.VMEM((heads, cols), F32),
-            pltpu.VMEM((groups, per_group, step, 2 * cols), BF16),
+            pltpu.VMEM((groups, per_group, 3, step, 128), BF16),
         ],
         compiler_params=params(),
     )(
@@ -282,10 +278,10 @@
             values = grad_refs[number][head].astype(F32)
             top = pl.multiple_of((source * per_call + head) * step, step)
             for side in range(2):
-                for tile, start, end in lane_tiles(cols):
-                    flat_ref[side, tile, pl.ds(top, step), : end - start] = values[
-                        :, side * cols + start : side * cols + end
-                    ]
+                flat_ref[side, 0, pl.ds(top, step), :] = values[side]
+                flat_ref[side, 1, pl.ds(top, step), : cols - 128] = values[2][
+                    :, side * (cols - 128) : (side + 1) * (cols - 128)
+                ]
 
     for first in range(0, step, batch):
         center = center_rows(pair_ref, first, batch, means)
@@ -338,7 +334,7 @@
             pl.BlockSpec((2, step, heads + 8, cols), lambda t: (0, t, 0, 0)),
             pl.BlockSpec((heads, channels), lambda t: (0, 0)),
         ]
-        + [pl.BlockSpec((per_call, step, 2 * cols), lambda t: (0, t, 0)) for _ in grads],
+        + [pl.BlockSpec((per_call, 3, step, 128), lambda t: (0, 0, t, 0)) for _ in grads],
         out_specs=pl.BlockSpec((2, step, cols, channels), lambda t: (0, t, 0, 0)),
         out_shape=jax.ShapeDtypeStruct((2, half, cols, channels), BF16),
         scratch_shapes=[pltpu.VMEM((2, tiles, heads * step, 128), F32)],
@@ -386,19 +382,31 @@
     cols, width = acts_refs[0].shape
     tokens = groups * cols
     part = width // 4
-    half = bias_refs[0].shape[2]
+    half = bias_refs[0].shape[3]
+    rest_lanes = cols - 128
     scale = 1.0 / math.sqrt(head_size)
     extra = att_sum.shape[1] - part
     plain = (query_ref, keys_ref, values_ref, grads_ref)
     turned = (query_t_ref, keys_t_ref, values_t_ref, grads_t_ref)
 
+    turns = [(slot * cols, slot * 128, 128) for slot in range(groups)]
+    turns += [
+        (slot * cols + 128, groups * 128 + slot * rest_lanes, rest_lanes) for slot in range(groups)
+    ]
+
     @pl.when(head == 0)
     def _():
         for kind in range(4):
-            for slot in range(groups):
-                plain[kind][slot * cols : (slot + 1) * cols, :] = acts_refs[slot][
-                    :, kind * part : (kind + 1) * part
-                ]
+            lanes = slice(kind * part, (kind + 1) * part)
+            if kind in (0, 3):
+                for slot in range(groups):
+                    plain[kind][slot * cols : (slot + 1) * cols, :] = acts_refs[slot][:, lanes]
+            else:
+                for token, place, count in turns:
+                    slot, inside = divmod(token, cols)
+                    plain[kind][place : place + count, :] = acts_refs[slot][
+                        inside : inside + count, lanes
+                    ]
             turned[kind][...] = plain[kind][...].T
         att_sum[...] = jnp.zeros_like(att_sum)
         gq_sum[...] = jnp.zeros_like(gq_sum)
@@ -408,18 +416,20 @@
         slot = group_own ^ (first // cols)
         for side in range(2):
             top = slot * cols + lax.rem(first, cols) + side * half
-            top = pl.multiple_of(top, 16)
-            for column in range(groups):
-                yield column, side, pl.ds(top, half)
+            yield side, pl.ds(pl.multiple_of(top, 16), half)
 
     for other in range(row_parts):
-        for column, side, rows in places(row_ref[0] ^ other):
-            block, place = bias_refs[other], column
+
+        def block(column, which, other=other):
             if other >= row_parts - 2 and column >= groups // 2:
-                block, place = bias_refs[other + 2], column - groups // 2
-            bias_full[rows, column * cols : (column + 1) * cols] = block[
-                place, 0, :, side * cols : (side + 1) * cols
-            ]
+                return bias_refs[other + 2][column - groups // 2, 0, which]
+            return bias_refs[other][column, 0, which]
+
+        for side, rows in places(row_ref[0] ^ other):
+            lanes = slice(side * rest_lanes, (side + 1) * rest_lanes)
+            tiles = [block(column, side) for column in range(groups)]
+            tiles += [block(column, 2)[:, lanes] for column in range(groups)]
+            bias_full[rows, :] = jnp.concatenate(tiles, axis=1)
 
     lane = lax.broadcasted_iota(jnp.int32, (1, part), 1)
     mine = (lane >= head * head_size) & (lane < (head + 1) * head_size)
@@ -465,10 +475,17 @@
                 dbias_ref = give_ref if unit < early else give_late_ref
                 unit = unit % early
             unit = unit + head - some_heads[0]
-            for column, side, rows in places(row_ref[0] ^ other):
-                dbias_ref[unit, column, :, side * cols : (side + 1) * cols] = score_full[
-                    rows, column * cols : (column + 1) * cols
-                ]
+            scores = [score_full[rows, :] for _, rows in places(row_ref[0] ^ other)]
+            blocks = []
+            for column in range(groups):
+                start = groups * 128 + column * rest_lanes
+                blocks += [score[:, column * 128 : (column + 1) * 128] for score in scores]
+                blocks.append(
+                    jnp.concatenate(
+                        [score[:, start : start + rest_lanes] for score in scores], axis=1
+                    )
+                )
+            dbias_ref[unit] = jnp.stack(blocks).reshape(dbias_ref.shape[1:])
 
     @pl.when(head < heads // 2)
     def _():
@@ -488,10 +505,14 @@
         )
         for kind, values in enumerate(results):
             rounded = values.astype(BF16)
-            for slot in range(groups):
-                out_refs[slot][:, kind * part : (kind + 1) * part] = rounded[
-                    slot * cols : (slot + 1) * cols
-                ]
+            lanes = slice(kind * part, (kind + 1) * part)
+            if kind in (0, 3):
+                for slot in range(groups):
+                    out_refs[slot][:, lanes] = rounded[slot * cols : (slot + 1) * cols]
+            else:
+                for token, place, count in turns:
+                    slot, inside = divmod(token, cols)
+                    out_refs[slot][inside : inside + count, lanes] = rounded[place : place + count]
 
 
 def attention(group_index, row_index, acts, bias, head_size):
@@ -500,11 +521,11 @@
     cols, width = acts[0].shape
     tokens = groups * cols
     part = width // 4
-    _, heads, half, lanes = bias[0].shape
+    _, heads, _, half, lanes = bias[0].shape
     row_block = 256 if tokens % 256 == 0 else cols
     padded = (part // 128 + 1) * 128
-    units = (row_parts // 2 * heads, groups, half, lanes)
-    some = (row_parts // 4 * heads, groups, half, lanes)
+    units = (row_parts // 2 * heads, groups, 3, half, lanes)
+    some = (row_parts // 4 * heads, groups, 3, half, lanes)
     *grads, keep, give, give_late = pl.pallas_call(
         functools.partial(
             attention_kernel,
@@ -516,12 +537,12 @@
         grid=(heads,),
         in_specs=[smem(), smem()]
         + [
-            pl.BlockSpec((block.shape[0], 1, half, lanes), lambda h: (0, h, 0, 0))
+            pl.BlockSpec((block.shape[0], 1, 3, half, lanes), lambda h: (0, h, 0, 0, 0))
             for block in bias
         ]
         + [pl.BlockSpec((cols, width), lambda h: (0, 0))] * groups,
         out_specs=[pl.BlockSpec((cols, width), lambda h: (0, 0))] * groups
-        + [pl.BlockSpec(shape, lambda h: (0, 0, 0, 0)) for shape in (units, some, some)],
+        + [pl.BlockSpec(shape, lambda h: (0, 0, 0, 0, 0)) for shape in (units, some, some)],
         out_shape=[jax.ShapeDtypeStruct((cols, width), BF16)] * groups
         + [jax.ShapeDtypeStruct(shape, BF16) for shape in (units, some, some)],
         scratch_shapes=[pltpu.VMEM((tokens, part), BF16) for _ in range(4)]
@@ -598,11 +619,13 @@
 
 def swap_groups(sends):
     groups = len(sends)
-    got = list(sends)
-    for bits in (*range(2, groups), 1):
+    order = (*range(2, groups), 1)
+    got = []
+    for bits in order:
         perm = [(index, index ^ bits) for index in range(groups)]
-        got[bits] = lax.ppermute(sends[bits], "grp", perm)
-    return got
+        got.append(lax.ppermute(sends[bits], "grp", perm))
+    got = dict(zip(order, lax.optimization_barrier(got)))
+    return [sends[0]] + [got[bits] for bits in range(1, groups)]
 
 
 def flip_rows(values, bits, row_total):
@@ -615,13 +638,9 @@
     far = flip_rows(own, 4, row_total)
     first = flip_rows(near[:half], 4, row_total)
     second = flip_rows(far[half:], 2, row_total)
-    own, acts[2] = lax.optimization_barrier((own, acts[2]))
-    own_other = flip_rows(own, 1, row_total)
-    first, second, own_other, acts[1], acts[3] = lax.optimization_barrier(
-        (first, second, own_other, acts[1], acts[3])
-    )
-    blocks = [own, own_other]
-    for block in (near, far, first, second):
+    first, second, acts = lax.optimization_barrier((first, second, acts))
+    blocks = []
+    for block in (own, near, far, first, second):
         blocks += [block, flip_rows(block, 1, row_total)]
     return blocks, acts
 
@@ -661,12 +680,12 @@
 
 
 def add_last(own, far_two, near_two):
-    heads, groups, half, lanes = own.shape
+    heads, groups = own.shape[:2]
     return pl.pallas_call(
         add_last_kernel,
         in_specs=[vmem()] * 3,
         out_specs=[vmem()] * groups,
-        out_shape=[jax.ShapeDtypeStruct((heads, half, lanes), BF16)] * groups,
+        out_shape=[jax.ShapeDtypeStruct((heads,) + own.shape[2:], BF16)] * groups,
         compiler_params=params(),
     )(own, far_two, near_two)
 
@@ -940,7 +959,7 @@
             and pair.shape[1] % pair.shape[0] == 0
             and row_total == 8
             and noised.shape[0] == 1
-            and noised.shape[1] % 64 == 0
+            and noised.shape[1] == 192
             and w_pair.shape[1] % (2 * groups) == 0
         )
         if fits:

time: 150 us -> 149 us (level)
  starting transfers between devices: 40.4 us -> 38.3 us
  waiting for transfers between devices: 50.1 us -> 52.1 us
    ppermute x19, starting transfers between devices: 17 us -> 12.4 us  [flip_rows(): lax.ppermute(values, 'rows', [(index, index ^ bits) for index in range(ro...]
    ppermute x12, starting transfers between devices: 23.4 us -> 25.9 us  [swap_groups(): got.append(lax.ppermute(sends[bits], 'grp', perm))]
    ppermute x19, waiting for transfers between devices: 18 us -> 20.1 us  [flip_rows(): lax.ppermute(values, 'rows', [(index, index ^ bits) for index in range(ro...]
  transfers between devices with their start and end apart: 31 -> 31, of which waited for: 14 -> 17; matrix products, arithmetic and copies ran while one was open for 2% -> 2% of each run, Pallas kernels for 15% -> 15%
where the time goes in v4:
time: 149 us
  waiting for transfers between devices  52.1 us (35%)
  Pallas kernels  50.6 us (34%)
  starting transfers between devices  38.3 us (26%)
  other arithmetic  4.82 us (3%)
  local copies, waits for them, and re-layouts  1.89 us (1%)
    ppermute x12, waiting for transfers between devices, swap_groups(): got.append(lax.ppermute(sends[bits], 'grp', perm))  31.9 us
    ppermute x12, starting transfers between devices, swap_groups(): got.append(lax.ppermute(sends[bits], 'grp', perm))  25.9 us
    ppermute x19, waiting for transfers between devices, flip_rows(): lax.ppermute(values, 'rows', [(index, index ^ bits) for index in range(ro...  20.1 us
    pallas_call x1, Pallas kernels, attention(): pl.pallas_call(functools.partial(attention_kernel, groups=groups, row_par...  18 us
    ppermute x19, starting transfers between devices, flip_rows(): lax.ppermute(values, 'rows', [(index, index ^ bits) for index in range(ro...  12.4 us
    pallas_call x1, Pallas kernels, pair_bias(): pl.pallas_call(functools.partial(bias_kernel, groups=groups, batch=4), gr...  8.46 us
    pallas_call x1, Pallas kernels, pair_back(): pl.pallas_call(functools.partial(pair_back_kernel, groups=groups, calls=l...  8.18 us
    pallas_call x1, Pallas kernels, split_heads(): pl.pallas_call(functools.partial(finish_kernel, groups=groups, calls=call...  7.48 us
  transfers between devices with their start and end apart: 31, of which 17 were waited for; matrix products, arithmetic and copies ran while one was open for 2% of the time, Pallas kernels for 15%

profile of v4, /device:TPU:0, one launch (start us, length us, event | category | flops | bytes accessed | tf_op | source)
XLA Modules:
  0.0 148.6 jit_solution(15155371292611179333)
XLA Ops:
  0.6 8.5 %shard_map.158 = (bf16[4,3,48,128]{3,2,1,0:T(8,128)(2,1)}, bf16[4,3,48,128]{3,2,1,0:T(8,128)(2,1)}, bf16[4,3,48,128]{3,2,1,0:T(8,128)(2,1)}, bf16[4,3,48,128]{3,2,1,0:T(8,128)(2,1)}, f32[2,48,24,192]{3,2,1,0:T(8,128)}) custom-call(s32[1]{0:T(128)} %bitcast.group_ref, s32[1]{0:T(128)} %bitcast.3.rows_ref.row_ref, s32[768]{0:T(1024)} %cols_ref.1, f32[16]{0:T(128)} %gain_ref.1, ...), custom_call_target="tpu_custom_call" | custom-call | tf_op jit(solution)/shard_map/pallas_call | solution.py:215
  9.1 4.0 %collective-permute-start = (bf16[4,3,48,128]{3,2,1,0:T(8,128)(2,1)}, bf16[4,3,48,128]{3,2,1,0:T(8,128)(2,1)S(1)}, u32[]{:S(2)}, u32[]{:S(2)}) collective-permute-start(bf16[4,3,48,128]{3,2,1,0:T(8,128)(2,1)} %get-tuple-element.73), channel_id=1, source_target_pairs={{0,2},{1,3},{2,0},{3,1},{4,6},{5,7},{6,4},{7,5},{8,10},{9,11},{10,... | collective-permute-start | bytes 442376 | tf_op jit(solution)/shard_map/ppermute | solution.py:626
  13.1 1.3 collective-permute-start.1
  14.5 0.2 collective-permute-start.2
  14.7 6.4 %shard_map.157 = (bf16[192,768]{1,0:T(8,128)(2,1)}, bf16[192,768]{1,0:T(8,128)(2,1)}, bf16[192,768]{1,0:T(8,128)(2,1)}, bf16[192,768]{1,0:T(8,128)(2,1)}, f32[192,768]{1,0:T(8,128)}, /*index=5*/f32[192,768]{1,0:T(8,128)}) custom-call(s32[1]{0:T(128)} %bitcast.group_ref, bf16[192,384]{1,0:T(8,128)(2,1)} %single_ref.3, bf16[192,768]{1,0:T(8,128)(2,1)} %bitcast.15, ...), custom_call_target="tpu_custom_call" | custom-call | tf_op jit(solution)/shard_map/pallas_call | solution.py:734
  21.1 0.0 copy-start.27
  21.1 3.3 %collective-permute-done = bf16[4,3,48,128]{3,2,1,0:T(8,128)(2,1)S(1)} collective-permute-done((bf16[4,3,48,128]{3,2,1,0:T(8,128)(2,1)}, bf16[4,3,48,128]{3,2,1,0:T(8,128)(2,1)S(1)}, u32[]{:S(2)}, u32[]{:S(2)}) %collective-permute-start) | collective-permute-done | bytes 147488 | tf_op jit(solution)/shard_map/ppermute | solution.py:626
  24.4 0.5 collective-permute-done.2
  24.9 0.1 pad_maximum_fusion.rest_0_
  25.0 1.6 %collective-permute-start.6 = (bf16[4,4,3,48,128]{4,3,2,1,0:T(8,128)(2,1)S(1)}, bf16[4,4,3,48,128]{4,3,2,1,0:T(8,128)(2,1)S(1)}, u32[]{:S(2)}, u32[]{:S(2)}) collective-permute-start(bf16[4,4,3,48,128]{4,3,2,1,0:T(8,128)(2,1)S(1)} %pad_maximum_fusion.rest_0_), channel_id=1, source_target_pairs={{0,16},{4,20},{8,24},{12,28},{16,0},{20,4},{24,8},{28,12},{1,17},{... | collective-permute-start | bytes 1769480 | tf_op jit(solution)/shard_map/ppermute | solution.py:632
  26.6 1.5 %collective-permute-start.4 = (bf16[4,4,3,48,128]{4,3,2,1,0:T(8,128)(2,1)S(1)}, bf16[4,4,3,48,128]{4,3,2,1,0:T(8,128)(2,1)S(1)}, u32[]{:S(2)}, u32[]{:S(2)}) collective-permute-start(bf16[4,4,3,48,128]{4,3,2,1,0:T(8,128)(2,1)S(1)} %pad_maximum_fusion.rest_0_), channel_id=1, source_target_pairs={{0,8},{4,12},{8,0},{12,4},{16,24},{20,28},{24,16},{28,20},{1,9},{5... | collective-permute-start | bytes 1769480 | tf_op jit(solution)/shard_map/ppermute | solution.py:632
  28.1 2.6 %collective-permute-start.12 = (bf16[192,768]{1,0:T(8,128)(2,1)S(1)}, bf16[192,768]{1,0:T(8,128)(2,1)S(1)}, u32[]{:S(2)}, u32[]{:S(2)}) collective-permute-start(bf16[192,768]{1,0:T(8,128)(2,1)S(1)} %copy-done.28), channel_id=1, source_target_pairs={{0,1},{1,0},{2,3},{3,2},{4,5},{5,4},{6,7},{7,6},{8,9},{9,8},{10,11... | collective-permute-start | bytes 884744 | tf_op jit(solution)/shard_map/ppermute | solution.py:626
  30.7 1.9 %collective-permute-start.10 = (bf16[192,768]{1,0:T(8,128)(2,1)S(1)}, bf16[192,768]{1,0:T(8,128)(2,1)S(1)}, u32[]{:S(2)}, u32[]{:S(2)}) collective-permute-start(bf16[192,768]{1,0:T(8,128)(2,1)S(1)} %copy-done.27), channel_id=1, source_target_pairs={{0,2},{1,3},{2,0},{3,1},{4,6},{5,7},{6,4},{7,5},{8,10},{9,11},{10,... | collective-permute-start | bytes 884744 | tf_op jit(solution)/shard_map/ppermute | solution.py:626
  32.6 1.5 collective-permute-start.11
  34.1 4.2 %collective-permute-done.6.rest_4_ = bf16[4,4,3,48,128]{4,3,2,1,0:T(8,128)(2,1)S(1)} collective-permute-done((bf16[4,4,3,48,128]{4,3,2,1,0:T(8,128)(2,1)S(1)}, bf16[4,4,3,48,128]{4,3,2,1,0:T(8,128)(2,1)S(1)}, u32[]{:S(2)}, u32[]{:S(2)}) %collective-permute-start.6) | collective-permute-done | bytes 589856 | tf_op jit(solution)/shard_map/ppermute | solution.py:632
  38.3 1.3 collective-permute-start.9
  39.6 0.9 collective-permute-done.4.rest_2_
  40.5 0.7 collective-permute-start.8
  41.3 1.8 %collective-permute-done.12.rest_11_ = bf16[192,768]{1,0:T(8,128)(2,1)S(1)} collective-permute-done((bf16[192,768]{1,0:T(8,128)(2,1)S(1)}, bf16[192,768]{1,0:T(8,128)(2,1)S(1)}, u32[]{:S(2)}, u32[]{:S(2)}) %collective-permute-start.12) | collective-permute-done | bytes 294944 | tf_op jit(solution)/shard_map/ppermute | solution.py:626
  43.1 11.1 %collective-permute-done.10.rest_12_ = bf16[192,768]{1,0:T(8,128)(2,1)S(1)} collective-permute-done((bf16[192,768]{1,0:T(8,128)(2,1)S(1)}, bf16[192,768]{1,0:T(8,128)(2,1)S(1)}, u32[]{:S(2)}, u32[]{:S(2)}) %collective-permute-start.10) | collective-permute-done | bytes 294944 | tf_op jit(solution)/shard_map/ppermute | solution.py:626
  54.2 0.0 collective-permute-start.7
  54.2 0.5 collective-permute-start.5
  54.7 0.0 copy-start.14
  54.7 0.1 collective-permute-start.13
  54.9 0.4 collective-permute-start.14
  55.3 0.9 collective-permute-done.7.rest_5_
  56.2 0.8 collective-permute-done.5.rest_3_
  57.1 0.4 collective-permute-done.13.rest_7_
  57.5 0.4 collective-permute-done.14.rest_9_
  58.0 0.2 copy-done.15
  58.2 0.7 copy-done.16
  58.9 18.0 %shard_map.159 = (bf16[192,768]{1,0:T(8,128)(2,1)}, bf16[192,768]{1,0:T(8,128)(2,1)}, bf16[192,768]{1,0:T(8,128)(2,1)}, bf16[192,768]{1,0:T(8,128)(2,1)}, bf16[1...) custom-call(s32[1]{0:T(128)} %bitcast.group_ref, ...), custom_call_target="tpu_custom_call" | custom-call | tf_op jit(solution)/shard_map/pallas_call | solution.py:529
  77.0 0.2 collective-permute-start.15
  77.2 2.9 %collective-permute-done.15 = bf16[8,4,3,48,128]{4,3,2,1,0:T(8,128)(2,1)S(1)} collective-permute-done((bf16[8,4,3,48,128]{4,3,2,1,0:T(8,128)(2,1)}, bf16[8,4,3,48,128]{4,3,2,1,0:T(8,128)(2,1)S(1)}, u32[]{:S(2)}, u32[]{:S(2)}) %collective-permute-start.15) | collective-permute-done | bytes 1179680 | tf_op jit(solution)/shard_map/ppermute | solution.py:632
  80.1 0.1 collective-permute-start.16
  80.2 1.7 %add_convert_fusion.2 = (bf16[4,4,3,48,128]{4,3,2,1,0:T(8,128)(2,1)S(1)}, bf16[4,4,3,48,128]{4,3,2,1,0:T(8,128)(2,1)S(1)}) fusion(bf16[8,4,3,48,128]{4,3,2,1,0:T(8,128)(2,1)S(1)} %collective-permute-done.15, bf16[16,4,3,48,128]{4,3,2,1,0:T(8,128)(2,1)} %get-tuple-element.96), kind=kLoop, calls=%fused_computation.2 | loop fusion | flops 2359296 | bytes 3538944 | tf_op jit(solution)/shard_map/convert_element_type | solution.py:672
  82.0 0.6 collective-permute-start.17
  82.6 0.5 collective-permute-start.18
  83.1 6.0 %collective-permute-start.21 = (bf16[192,768]{1,0:T(8,128)(2,1)S(1)}, bf16[192,768]{1,0:T(8,128)(2,1)S(1)}, u32[]{:S(2)}, u32[]{:S(2)}) collective-permute-start(bf16[192,768]{1,0:T(8,128)(2,1)S(1)} %copy-done.25), channel_id=1, source_target_pairs={{0,2},{1,3},{2,0},{3,1},{4,6},{5,7},{6,4},{7,5},{8,10},{9,11},{10,... | collective-permute-start | bytes 884744 | tf_op jit(solution)/shard_map/ppermute | solution.py:626
  89.1 0.5 collective-permute-start.22
  89.7 7.9 %collective-permute-done.17 = bf16[4,4,3,48,128]{4,3,2,1,0:T(8,128)(2,1)S(1)} collective-permute-done((bf16[4,4,3,48,128]{4,3,2,1,0:T(8,128)(2,1)S(1)}, bf16[4,4,3,48,128]{4,3,2,1,0:T(8,128)(2,1)S(1)}, u32[]{:S(2)}, u32[]{:S(2)}) %collective-permute-start.17) | collective-permute-done | bytes 589856 | tf_op jit(solution)/shard_map/ppermute | solution.py:632
  97.6 4.2 %collective-permute-start.23 = (bf16[192,768]{1,0:T(8,128)(2,1)S(1)}, bf16[192,768]{1,0:T(8,128)(2,1)S(1)}, u32[]{:S(2)}, u32[]{:S(2)}) collective-permute-start(bf16[192,768]{1,0:T(8,128)(2,1)S(1)} %copy-done.23), channel_id=1, source_target_pairs={{0,1},{1,0},{2,3},{3,2},{4,5},{5,4},{6,7},{7,6},{8,9},{9,8},{10,11... | collective-permute-start | bytes 884744 | tf_op jit(solution)/shard_map/ppermute | solution.py:626
  101.9 0.2 add_convert_fusion.3
  102.1 0.6 collective-permute-start.20
  102.7 0.5 collective-permute-start.19
  103.2 5.9 %collective-permute-done.21.rest_2_ = bf16[192,768]{1,0:T(8,128)(2,1)S(1)} collective-permute-done((bf16[192,768]{1,0:T(8,128)(2,1)S(1)}, bf16[192,768]{1,0:T(8,128)(2,1)S(1)}, u32[]{:S(2)}, u32[]{:S(2)}) %collective-permute-start.21) | collective-permute-done | bytes 294944 | tf_op jit(solution)/shard_map/ppermute | solution.py:626
  109.1 5.9 %collective-permute-done.23.rest_1_ = bf16[192,768]{1,0:T(8,128)(2,1)S(1)} collective-permute-done((bf16[192,768]{1,0:T(8,128)(2,1)S(1)}, bf16[192,768]{1,0:T(8,128)(2,1)S(1)}, u32[]{:S(2)}, u32[]{:S(2)}) %collective-permute-start.23) | collective-permute-done | bytes 294944 | tf_op jit(solution)/shard_map/ppermute | solution.py:626
  115.1 1.0 add_convert_fusion.own_ref
  116.2 0.0 copy-start.18
  116.2 0.7 copy-done.17
  116.9 0.1 copy-done.18
  117.0 2.1 %shard_map.160 = (bf16[4,3,48,128]{3,2,1,0:T(8,128)(2,1)}, bf16[4,3,48,128]{3,2,1,0:T(8,128)(2,1)}, bf16[4,3,48,128]{3,2,1,0:T(8,128)(2,1)}, bf16[4,3,48,128]{3,2,1,0:T(8,128)(2,1)}) custom-call(bf16[4,4,3,48,128]{4,3,2,1,0:T(8,128)(2,1)} %add_convert_fusion.own_ref, bf16[2,4,3,48,128]{4,3,2,1,0:T(8,128)(2,1)} %copy-done.18, ...), custom_call_target="tpu_custom_call" | custom-call | tf_op jit(solution)/shard_map/pallas_call | solution.py:684
  119.1 3.0 %collective-permute-start.25 = (bf16[4,3,48,128]{3,2,1,0:T(8,128)(2,1)}, bf16[4,3,48,128]{3,2,1,0:T(8,128)(2,1)S(1)}, u32[]{:S(2)}, u32[]{:S(2)}) collective-permute-start(bf16[4,3,48,128]{3,2,1,0:T(8,128)(2,1)} %get-tuple-element.126), channel_id=1, source_target_pairs={{0,3},{1,2},{2,1},{3,0},{4,7},{5,6},{6,5},{7,4},{8,11},{9,10},{10,... | collective-permute-start | bytes 442376 | tf_op jit(solution)/shard_map/ppermute | solution.py:626
  122.1 0.5 collective-permute-start.26
  122.6 7.5 %shard_map.161 = (bf16[192,768]{1,0:T(8,128)(2,1)}, bf16[192,384]{1,0:T(8,128)(2,1)}) custom-call(s32[1]{0:T(128)} %bitcast.group_ref, bf16[192,384]{1,0:T(8,128)(2,1)} %single_ref.3, bf16[192,768]{1,0:T(8,128)(2,1)} %bitcast.16, bf16[192,768]{1,0:T(8,128)(2,1)} %bitcast.18, f32[192,768]{1,0:T(8,128)} %get-tuple-element.70.gamma_ref, ...), custom_call_target="tpu_custom_call" | custom-call | tf_op jit(solution)/shard_map/pallas_call | solution.py:768
  130.1 2.2 %collective-permute-done.24.rest_2_ = bf16[4,3,48,128]{3,2,1,0:T(8,128)(2,1)S(1)} collective-permute-done((bf16[4,3,48,128]{3,2,1,0:T(8,128)(2,1)}, bf16[4,3,48,128]{3,2,1,0:T(8,128)(2,1)S(1)}, u32[]{:S(2)}, u32[]{:S(2)}) %collective-permute-start.24) | collective-permute-done | bytes 147488 | tf_op jit(solution)/shard_map/ppermute | solution.py:626
  132.2 1.2 collective-permute-done.26.rest_1_
  133.5 1.6 %collective-permute-done.27 = bf16[192,384]{1,0:T(8,128)(2,1)S(1)} collective-permute-done((bf16[192,384]{1,0:T(8,128)(2,1)}, bf16[192,384]{1,0:T(8,128)(2,1)S(1)}, u32[]{:S(2)}, u32[]{:S(2)}) %collective-permute-start.27) | collective-permute-done | bytes 147488 | tf_op jit(solution)/shard_map/ppermute | solution.py:632
  135.1 1.0 add_convert_fusion.5
  136.0 2.5 %collective-permute-start.30 = (bf16[192,384]{1,0:T(8,128)(2,1)S(1)}, bf16[192,384]{1,0:T(8,128)(2,1)S(1)}, u32[]{:S(2)}, u32[]{:S(2)}) collective-permute-start(bf16[192,384]{1,0:T(8,128)(2,1)S(1)} %add_convert_fusion.5), channel_id=1, source_target_pairs={{0,24},{4,28},{8,16},{12,20},{16,8},{20,12},{24,0},{28,4},{1,25},{... | collective-permute-start | bytes 442376 | tf_op jit(solution)/shard_map/ppermute | solution.py:632
  138.5 0.5 collective-permute-start.29
  139.0 0.5 collective-permute-start.28
  139.6 8.2 %shard_map.162 = bf16[2,48,192,128]{3,2,1,0:T(8,128)(2,1)} custom-call(s32[1]{0:T(128)} %bitcast.group_ref, bf16[2,48,192,128]{3,2,1,0:T(8,128)(2,1)} %bitcast.13, f32[2,48,24,192]{3,2,1,0:T(8,128)} %get-tuple-element.132.stats_ref, bf16[16,128]{1,0:T(8,128)(2,1)} %bitcast.24, bf16[4,3,48,128]{3,2,1,0:T(8,128)(2,1)} %get-tuple-element.133.rest_0_, ...), custom_call_target="tpu_custom_call" | custom-call | tf_op jit(solution)/shard_map/pallas_call | solution.py:326
  147.8 0.8 add_add_fusion
  (72 shorter events, 0.2 us)
Async XLA Ops:
  9.1 15.3 %collective-permute-start = (bf16[4,3,48,128]{3,2,1,0:T(8,128)(2,1)}, bf16[4,3,48,128]{3,2,1,0:T(8,128)(2,1)S(1)}, u32[]{:S(2)}, u32[]{:S(2)}) collective-permute-start(bf16[4,3,48,128]{3,2,1,0:T(8,128)(2,1)} %get-tuple-element.73), channel_id=1, source_target_pairs={{0,2},{1,3},{2,0},{3,1},{4,6},{5,7},{6,4},{7,5},{8,10},{9,11},{10,... | collective-permute-start | bytes 442376 | tf_op jit(solution)/shard_map/ppermute | solution.py:626
  13.1 11.3 %collective-permute-start.1 = (bf16[4,3,48,128]{3,2,1,0:T(8,128)(2,1)}, bf16[4,3,48,128]{3,2,1,0:T(8,128)(2,1)S(1)}, u32[]{:S(2)}, u32[]{:S(2)}) collective-permute-start(bf16[4,3,48,128]{3,2,1,0:T(8,128)(2,1)} %get-tuple-element.74), channel_id=1, source_target_pairs={{0,3},{1,2},{2,1},{3,0},{4,7},{5,6},{6,5},{7,4},{8,11},{9,10},{10,... | collective-permute-start | bytes 442376 | tf_op jit(solution)/shard_map/ppermute | solution.py:626
  14.5 10.4 %collective-permute-start.2 = (bf16[4,3,48,128]{3,2,1,0:T(8,128)(2,1)}, bf16[4,3,48,128]{3,2,1,0:T(8,128)(2,1)S(1)}, u32[]{:S(2)}, u32[]{:S(2)}) collective-permute-start(bf16[4,3,48,128]{3,2,1,0:T(8,128)(2,1)} %get-tuple-element.75), channel_id=1, source_target_pairs={{0,1},{1,0},{2,3},{3,2},{4,5},{5,4},{6,7},{7,6},{8,9},{9,8},{10,11... | collective-permute-start | bytes 442376 | tf_op jit(solution)/shard_map/ppermute | solution.py:626
  14.7 10.2 %copy-start.19 = (bf16[4,3,48,128]{3,2,1,0:T(8,128)(2,1)S(1)}, bf16[4,3,48,128]{3,2,1,0:T(8,128)(2,1)}, u32[]{:S(2)}) copy-start(bf16[4,3,48,128]{3,2,1,0:T(8,128)(2,1)} %get-tuple-element.83) | copy-start | bytes 442372
  21.1 7.0 %copy-start.28 = (bf16[192,768]{1,0:T(8,128)(2,1)S(1)}, bf16[192,768]{1,0:T(8,128)(2,1)}, u32[]{:S(2)}) copy-start(bf16[192,768]{1,0:T(8,128)(2,1)} %get-tuple-element.80) | copy-start | bytes 884740
  21.1 9.6 %copy-start.27 = (bf16[192,768]{1,0:T(8,128)(2,1)S(1)}, bf16[192,768]{1,0:T(8,128)(2,1)}, u32[]{:S(2)}) copy-start(bf16[192,768]{1,0:T(8,128)(2,1)} %get-tuple-element.81) | copy-start | bytes 884740
  21.1 11.5 %copy-start.26 = (bf16[192,768]{1,0:T(8,128)(2,1)S(1)}, bf16[192,768]{1,0:T(8,128)(2,1)}, u32[]{:S(2)}) copy-start(bf16[192,768]{1,0:T(8,128)(2,1)} %get-tuple-element.82) | copy-start | bytes 884740
  25.0 32.9 %copy-start = (bf16[4,4,3,48,128]{4,3,2,1,0:T(8,128)(2,1)}, bf16[4,4,3,48,128]{4,3,2,1,0:T(8,128)(2,1)S(1)}, u32[]{:S(2)}) copy-start(bf16[4,4,3,48,128]{4,3,2,1,0:T(8,128)(2,1)S(1)} %pad_maximum_fusion.rest_0_) | copy-start | bytes 1769476
  25.0 13.3 %collective-permute-start.6 = (bf16[4,4,3,48,128]{4,3,2,1,0:T(8,128)(2,1)S(1)}, bf16[4,4,3,48,128]{4,3,2,1,0:T(8,128)(2,1)S(1)}, u32[]{:S(2)}, u32[]{:S(2)}) collective-permute-start(bf16[4,4,3,48,128]{4,3,2,1,0:T(8,128)(2,1)S(1)} %pad_maximum_fusion.rest_0_), channel_id=1, source_target_pairs={{0,16},{4,20},{8,24},{12,28},{16,0},{20,4},{24,8},{28,12},{1,17},{... | collective-permute-start | bytes 1769480 | tf_op jit(solution)/shard_map/ppermute | solution.py:632
  26.6 13.9 %collective-permute-start.4 = (bf16[4,4,3,48,128]{4,3,2,1,0:T(8,128)(2,1)S(1)}, bf16[4,4,3,48,128]{4,3,2,1,0:T(8,128)(2,1)S(1)}, u32[]{:S(2)}, u32[]{:S(2)}) collective-permute-start(bf16[4,4,3,48,128]{4,3,2,1,0:T(8,128)(2,1)S(1)} %pad_maximum_fusion.rest_0_), channel_id=1, source_target_pairs={{0,8},{4,12},{8,0},{12,4},{16,24},{20,28},{24,16},{28,20},{1,9},{5... | collective-permute-start | bytes 1769480 | tf_op jit(solution)/shard_map/ppermute | solution.py:632
  28.1 15.0 %collective-permute-start.12 = (bf16[192,768]{1,0:T(8,128)(2,1)S(1)}, bf16[192,768]{1,0:T(8,128)(2,1)S(1)}, u32[]{:S(2)}, u32[]{:S(2)}) collective-permute-start(bf16[192,768]{1,0:T(8,128)(2,1)S(1)} %copy-done.28), channel_id=1, source_target_pairs={{0,1},{1,0},{2,3},{3,2},{4,5},{5,4},{6,7},{7,6},{8,9},{9,8},{10,11... | collective-permute-start | bytes 884744 | tf_op jit(solution)/shard_map/ppermute | solution.py:626
  30.7 23.5 %collective-permute-start.10 = (bf16[192,768]{1,0:T(8,128)(2,1)S(1)}, bf16[192,768]{1,0:T(8,128)(2,1)S(1)}, u32[]{:S(2)}, u32[]{:S(2)}) collective-permute-start(bf16[192,768]{1,0:T(8,128)(2,1)S(1)} %copy-done.27), channel_id=1, source_target_pairs={{0,2},{1,3},{2,0},{3,1},{4,6},{5,7},{6,4},{7,5},{8,10},{9,11},{10,... | collective-permute-start | bytes 884744 | tf_op jit(solution)/shard_map/ppermute | solution.py:626
  32.6 21.6 %collective-permute-start.11 = (bf16[192,768]{1,0:T(8,128)(2,1)S(1)}, bf16[192,768]{1,0:T(8,128)(2,1)S(1)}, u32[]{:S(2)}, u32[]{:S(2)}) collective-permute-start(bf16[192,768]{1,0:T(8,128)(2,1)S(1)} %copy-done.26), channel_id=1, source_target_pairs={{0,3},{1,2},{2,1},{3,0},{4,7},{5,6},{6,5},{7,4},{8,11},{9,10},{10,... | collective-permute-start | bytes 884744 | tf_op jit(solution)/shard_map/ppermute | solution.py:626
  38.2 19.7 %copy-start.2 = (bf16[4,4,3,48,128]{4,3,2,1,0:T(8,128)(2,1)}, bf16[4,4,3,48,128]{4,3,2,1,0:T(8,128)(2,1)S(1)}, u32[]{:S(2)}) copy-start(bf16[4,4,3,48,128]{4,3,2,1,0:T(8,128)(2,1)S(1)} %collective-permute-done.6.rest_4_) | copy-start | bytes 1769476
  38.3 16.5 %collective-permute-start.9 = (bf16[2,4,3,48,128]{4,3,2,1,0:T(8,128)(2,1)S(1)}, bf16[2,4,3,48,128]{4,3,2,1,0:T(8,128)(2,1)S(1)}, u32[]{:S(2)}, u32[]{:S(2)}) collective-permute-start(bf16[2,4,3,48,128]{4,3,2,1,0:T(8,128)(2,1)S(1)} %slice.65), channel_id=1, source_target_pairs={{0,8},{4,12},{8,0},{12,4},{16,24},{20,28},{24,16},{28,20},{1,9},{5... | collective-permute-start | bytes 884744 | tf_op jit(solution)/shard_map/ppermute | solution.py:632
  40.5 17.4 %copy-start.3 = (bf16[4,4,3,48,128]{4,3,2,1,0:T(8,128)(2,1)}, bf16[4,4,3,48,128]{4,3,2,1,0:T(8,128)(2,1)S(1)}, u32[]{:S(2)}) copy-start(bf16[4,4,3,48,128]{4,3,2,1,0:T(8,128)(2,1)S(1)} %collective-permute-done.4.rest_2_) | copy-start | bytes 1769476
  40.5 14.2 %collective-permute-start.8 = (bf16[2,4,3,48,128]{4,3,2,1,0:T(8,128)(2,1)S(1)}, bf16[2,4,3,48,128]{4,3,2,1,0:T(8,128)(2,1)S(1)}, u32[]{:S(2)}, u32[]{:S(2)}) collective-permute-start(bf16[2,4,3,48,128]{4,3,2,1,0:T(8,128)(2,1)S(1)} %slice.64), channel_id=1, source_target_pairs={{0,16},{4,20},{8,24},{12,28},{16,0},{20,4},{24,8},{28,12},{1,17},{... | collective-permute-start | bytes 884744 | tf_op jit(solution)/shard_map/ppermute | solution.py:632
  43.1 14.8 %copy-start.7 = (bf16[192,768]{1,0:T(8,128)(2,1)}, bf16[192,768]{1,0:T(8,128)(2,1)S(1)}, u32[]{:S(2)}) copy-start(bf16[192,768]{1,0:T(8,128)(2,1)S(1)} %collective-permute-done.12.rest_11_) | copy-start | bytes 884740
  43.1 12.2 %collective-permute-start.3 = (bf16[4,4,3,48,128]{4,3,2,1,0:T(8,128)(2,1)S(1)}, bf16[4,4,3,48,128]{4,3,2,1,0:T(8,128)(2,1)S(1)}, u32[]{:S(2)}, u32[]{:S(2)}) collective-permute-start(bf16[4,4,3,48,128]{4,3,2,1,0:T(8,128)(2,1)S(1)} %pad_maximum_fusion.rest_0_), channel_id=1, source_target_pairs={{0,4},{4,0},{8,12},{12,8},{16,20},{20,16},{24,28},{28,24},{1,5},{5... | collective-permute-start | bytes 1769480 | tf_op jit(solution)/shard_map/ppermute | solution.py:632
  54.2 3.7 %copy-start.9 = (bf16[192,768]{1,0:T(8,128)(2,1)}, bf16[192,768]{1,0:T(8,128)(2,1)S(1)}, u32[]{:S(2)}) copy-start(bf16[192,768]{1,0:T(8,128)(2,1)S(1)} %collective-permute-done.10.rest_12_) | copy-start | bytes 884740
  54.2 2.0 %collective-permute-start.7 = (bf16[4,4,3,48,128]{4,3,2,1,0:T(8,128)(2,1)S(1)}, bf16[4,4,3,48,128]{4,3,2,1,0:T(8,128)(2,1)S(1)}, u32[]{:S(2)}, u32[]{:S(2)}) collective-permute-start(bf16[4,4,3,48,128]{4,3,2,1,0:T(8,128)(2,1)S(1)} %collective-permute-done.6.rest_4_), channel_id=1, source_target_pairs={{0,4},{4,0},{8,12},{12,8},{16,20},{20,16},{24,28},{28,24},{1,5},{5... | collective-permute-start | bytes 1769480 | tf_op jit(solution)/shard_map/ppermute | solution.py:632
  54.2 3.7 %copy-start.11 = (bf16[192,768]{1,0:T(8,128)(2,1)}, bf16[192,768]{1,0:T(8,128)(2,1)S(1)}, u32[]{:S(2)}) copy-start(bf16[192,768]{1,0:T(8,128)(2,1)S(1)} %collective-permute-done.11.rest_13_) | copy-start | bytes 884740
  54.2 2.8 %collective-permute-start.5 = (bf16[4,4,3,48,128]{4,3,2,1,0:T(8,128)(2,1)S(1)}, bf16[4,4,3,48,128]{4,3,2,1,0:T(8,128)(2,1)S(1)}, u32[]{:S(2)}, u32[]{:S(2)}) collective-permute-start(bf16[4,4,3,48,128]{4,3,2,1,0:T(8,128)(2,1)S(1)} %collective-permute-done.4.rest_2_), channel_id=1, source_target_pairs={{0,4},{4,0},{8,12},{12,8},{16,20},{20,16},{24,28},{28,24},{1,5},{5... | collective-permute-start | bytes 1769480 | tf_op jit(solution)/shard_map/ppermute | solution.py:632
  54.7 3.2 %copy-start.13 = (bf16[2,4,3,48,128]{4,3,2,1,0:T(8,128)(2,1)}, bf16[2,4,3,48,128]{4,3,2,1,0:T(8,128)(2,1)S(1)}, u32[]{:S(2)}) copy-start(bf16[2,4,3,48,128]{4,3,2,1,0:T(8,128)(2,1)S(1)} %collective-permute-done.9.rest_8_) | copy-start | bytes 884740
  54.7 3.2 %copy-start.14 = (bf16[2,4,3,48,128]{4,3,2,1,0:T(8,128)(2,1)}, bf16[2,4,3,48,128]{4,3,2,1,0:T(8,128)(2,1)S(1)}, u32[]{:S(2)}) copy-start(bf16[2,4,3,48,128]{4,3,2,1,0:T(8,128)(2,1)S(1)} %collective-permute-done.8.rest_6_) | copy-start | bytes 884740
  54.7 2.7 %collective-permute-start.13 = (bf16[2,4,3,48,128]{4,3,2,1,0:T(8,128)(2,1)S(1)}, bf16[2,4,3,48,128]{4,3,2,1,0:T(8,128)(2,1)S(1)}, u32[]{:S(2)}, u32[]{:S(2)}) collective-permute-start(bf16[2,4,3,48,128]{4,3,2,1,0:T(8,128)(2,1)S(1)} %collective-permute-done.8.rest_6_), channel_id=1, source_target_pairs={{0,4},{4,0},{8,12},{12,8},{16,20},{20,16},{24,28},{28,24},{1,5},{5... | collective-permute-start | bytes 884744 | tf_op jit(solution)/shard_map/ppermute | solution.py:632
  54.9 3.0 %collective-permute-start.14 = (bf16[2,4,3,48,128]{4,3,2,1,0:T(8,128)(2,1)S(1)}, bf16[2,4,3,48,128]{4,3,2,1,0:T(8,128)(2,1)S(1)}, u32[]{:S(2)}, u32[]{:S(2)}) collective-permute-start(bf16[2,4,3,48,128]{4,3,2,1,0:T(8,128)(2,1)S(1)} %collective-permute-done.9.rest_8_), channel_id=1, source_target_pairs={{0,4},{4,0},{8,12},{12,8},{16,20},{20,16},{24,28},{28,24},{1,5},{5... | collective-permute-start | bytes 884744 | tf_op jit(solution)/shard_map/ppermute | solution.py:632
  55.3 2.6 %copy-start.4 = (bf16[4,4,3,48,128]{4,3,2,1,0:T(8,128)(2,1)}, bf16[4,4,3,48,128]{4,3,2,1,0:T(8,128)(2,1)S(1)}, u32[]{:S(2)}) copy-start(bf16[4,4,3,48,128]{4,3,2,1,0:T(8,128)(2,1)S(1)} %collective-permute-done.3.rest_1_) | copy-start | bytes 1769476
  56.2 1.8 %copy-start.5 = (bf16[4,4,3,48,128]{4,3,2,1,0:T(8,128)(2,1)}, bf16[4,4,3,48,128]{4,3,2,1,0:T(8,128)(2,1)S(1)}, u32[]{:S(2)}) copy-start(bf16[4,4,3,48,128]{4,3,2,1,0:T(8,128)(2,1)S(1)} %collective-permute-done.7.rest_5_) | copy-start | bytes 1769476
  57.0 0.9 copy-start.6
  57.5 0.7 copy-start.15
  58.2 0.7 copy-start.16
  77.0 3.1 %collective-permute-start.15 = (bf16[8,4,3,48,128]{4,3,2,1,0:T(8,128)(2,1)}, bf16[8,4,3,48,128]{4,3,2,1,0:T(8,128)(2,1)S(1)}, u32[]{:S(2)}, u32[]{:S(2)}) collective-permute-start(bf16[8,4,3,48,128]{4,3,2,1,0:T(8,128)(2,1)} %get-tuple-element.97), channel_id=1, source_target_pairs={{0,4},{4,0},{8,12},{12,8},{16,20},{20,16},{24,28},{28,24},{1,5},{5... | collective-permute-start | bytes 3538952 | tf_op jit(solution)/shard_map/ppermute | solution.py:632
  80.1 21.8 %collective-permute-start.16 = (bf16[8,4,3,48,128]{4,3,2,1,0:T(8,128)(2,1)}, bf16[8,4,3,48,128]{4,3,2,1,0:T(8,128)(2,1)S(1)}, u32[]{:S(2)}, u32[]{:S(2)}) collective-permute-start(bf16[8,4,3,48,128]{4,3,2,1,0:T(8,128)(2,1)} %get-tuple-element.99), channel_id=1, source_target_pairs={{0,4},{4,0},{8,12},{12,8},{16,20},{20,16},{24,28},{28,24},{1,5},{5... | collective-permute-start | bytes 3538952 | tf_op jit(solution)/shard_map/ppermute | solution.py:632
  80.2 2.9 %copy-start.25 = (bf16[192,768]{1,0:T(8,128)(2,1)S(1)}, bf16[192,768]{1,0:T(8,128)(2,1)}, u32[]{:S(2)}) copy-start(bf16[192,768]{1,0:T(8,128)(2,1)} %get-tuple-element.102) | copy-start | bytes 884740
  80.2 8.9 %copy-start.24 = (bf16[192,768]{1,0:T(8,128)(2,1)S(1)}, bf16[192,768]{1,0:T(8,128)(2,1)}, u32[]{:S(2)}) copy-start(bf16[192,768]{1,0:T(8,128)(2,1)} %get-tuple-element.103) | copy-start | bytes 884740
  80.2 17.4 %copy-start.23 = (bf16[192,768]{1,0:T(8,128)(2,1)S(1)}, bf16[192,768]{1,0:T(8,128)(2,1)}, u32[]{:S(2)}) copy-start(bf16[192,768]{1,0:T(8,128)(2,1)} %get-tuple-element.104) | copy-start | bytes 884740
  80.2 21.7 %copy-start.1 = (bf16[16,4,3,48,128]{4,3,2,1,0:T(8,128)(2,1)S(1)}, bf16[16,4,3,48,128]{4,3,2,1,0:T(8,128)(2,1)}, u32[]{:S(2)}) copy-start(bf16[16,4,3,48,128]{4,3,2,1,0:T(8,128)(2,1)} %get-tuple-element.96) | copy-start | bytes 7077892
  82.0 15.7 %collective-permute-start.17 = (bf16[4,4,3,48,128]{4,3,2,1,0:T(8,128)(2,1)S(1)}, bf16[4,4,3,48,128]{4,3,2,1,0:T(8,128)(2,1)S(1)}, u32[]{:S(2)}, u32[]{:S(2)}) collective-permute-start(bf16[4,4,3,48,128]{4,3,2,1,0:T(8,128)(2,1)S(1)} %get-tuple-element.139), channel_id=1, source_target_pairs={{0,8},{4,12},{8,0},{12,4},{16,24},{20,28},{24,16},{28,20},{1,9},{5... | collective-permute-start | bytes 1769480 | tf_op jit(solution)/shard_map/ppermute | solution.py:632
  82.6 19.3 %collective-permute-start.18 = (bf16[4,4,3,48,128]{4,3,2,1,0:T(8,128)(2,1)S(1)}, bf16[4,4,3,48,128]{4,3,2,1,0:T(8,128)(2,1)S(1)}, u32[]{:S(2)}, u32[]{:S(2)}) collective-permute-start(bf16[4,4,3,48,128]{4,3,2,1,0:T(8,128)(2,1)S(1)} %get-tuple-element.140), channel_id=1, source_target_pairs={{0,16},{4,20},{8,24},{12,28},{16,0},{20,4},{24,8},{28,12},{1,17},{... | collective-permute-start | bytes 1769480 | tf_op jit(solution)/shard_map/ppermute | solution.py:632
  83.1 26.0 %collective-permute-start.21 = (bf16[192,768]{1,0:T(8,128)(2,1)S(1)}, bf16[192,768]{1,0:T(8,128)(2,1)S(1)}, u32[]{:S(2)}, u32[]{:S(2)}) collective-permute-start(bf16[192,768]{1,0:T(8,128)(2,1)S(1)} %copy-done.25), channel_id=1, source_target_pairs={{0,2},{1,3},{2,0},{3,1},{4,6},{5,7},{6,4},{7,5},{8,10},{9,11},{10,... | collective-permute-start | bytes 884744 | tf_op jit(solution)/shard_map/ppermute | solution.py:626
  89.1 20.0 %collective-permute-start.22 = (bf16[192,768]{1,0:T(8,128)(2,1)S(1)}, bf16[192,768]{1,0:T(8,128)(2,1)S(1)}, u32[]{:S(2)}, u32[]{:S(2)}) collective-permute-start(bf16[192,768]{1,0:T(8,128)(2,1)S(1)} %copy-done.24), channel_id=1, source_target_pairs={{0,3},{1,2},{2,1},{3,0},{4,7},{5,6},{6,5},{7,4},{8,11},{9,10},{10,... | collective-permute-start | bytes 884744 | tf_op jit(solution)/shard_map/ppermute | solution.py:626
  97.6 17.4 %collective-permute-start.23 = (bf16[192,768]{1,0:T(8,128)(2,1)S(1)}, bf16[192,768]{1,0:T(8,128)(2,1)S(1)}, u32[]{:S(2)}, u32[]{:S(2)}) collective-permute-start(bf16[192,768]{1,0:T(8,128)(2,1)S(1)} %copy-done.23), channel_id=1, source_target_pairs={{0,1},{1,0},{2,3},{3,2},{4,5},{5,4},{6,7},{7,6},{8,9},{9,8},{10,11... | collective-permute-start | bytes 884744 | tf_op jit(solution)/shard_map/ppermute | solution.py:626
  102.1 14.1 %collective-permute-start.20 = (bf16[2,4,3,48,128]{4,3,2,1,0:T(8,128)(2,1)S(1)}, bf16[2,4,3,48,128]{4,3,2,1,0:T(8,128)(2,1)S(1)}, u32[]{:S(2)}, u32[]{:S(2)}) collective-permute-start(bf16[2,4,3,48,128]{4,3,2,1,0:T(8,128)(2,1)S(1)} %get-tuple-element.137), channel_id=1, source_target_pairs={{0,8},{4,12},{8,0},{12,4},{16,24},{20,28},{24,16},{28,20},{1,9},{5... | collective-permute-start | bytes 884744 | tf_op jit(solution)/shard_map/ppermute | solution.py:632
  102.7 13.5 %collective-permute-start.19 = (bf16[2,4,3,48,128]{4,3,2,1,0:T(8,128)(2,1)S(1)}, bf16[2,4,3,48,128]{4,3,2,1,0:T(8,128)(2,1)S(1)}, u32[]{:S(2)}, u32[]{:S(2)}) collective-permute-start(bf16[2,4,3,48,128]{4,3,2,1,0:T(8,128)(2,1)S(1)} %get-tuple-element.138), channel_id=1, source_target_pairs={{0,16},{4,20},{8,24},{12,28},{16,0},{20,4},{24,8},{28,12},{1,17},{... | collective-permute-start | bytes 884744 | tf_op jit(solution)/shard_map/ppermute | solution.py:632
  109.1 7.0 %copy-start.8 = (bf16[192,768]{1,0:T(8,128)(2,1)}, bf16[192,768]{1,0:T(8,128)(2,1)S(1)}, u32[]{:S(2)}) copy-start(bf16[192,768]{1,0:T(8,128)(2,1)S(1)} %collective-permute-done.21.rest_2_) | copy-start | bytes 884740
  109.1 7.0 %copy-start.10 = (bf16[192,768]{1,0:T(8,128)(2,1)}, bf16[192,768]{1,0:T(8,128)(2,1)S(1)}, u32[]{:S(2)}) copy-start(bf16[192,768]{1,0:T(8,128)(2,1)S(1)} %collective-permute-done.22.rest_3_) | copy-start | bytes 884740
  115.1 1.1 copy-start.12
  116.2 0.7 copy-start.17
  116.2 0.8 copy-start.18
  119.1 13.1 %collective-permute-start.24 = (bf16[4,3,48,128]{3,2,1,0:T(8,128)(2,1)}, bf16[4,3,48,128]{3,2,1,0:T(8,128)(2,1)S(1)}, u32[]{:S(2)}, u32[]{:S(2)}) collective-permute-start(bf16[4,3,48,128]{3,2,1,0:T(8,128)(2,1)} %get-tuple-element.125), channel_id=1, source_target_pairs={{0,2},{1,3},{2,0},{3,1},{4,6},{5,7},{6,4},{7,5},{8,10},{9,11},{10,... | collective-permute-start | bytes 442376 | tf_op jit(solution)/shard_map/ppermute | solution.py:626
  119.1 13.1 %collective-permute-start.25 = (bf16[4,3,48,128]{3,2,1,0:T(8,128)(2,1)}, bf16[4,3,48,128]{3,2,1,0:T(8,128)(2,1)S(1)}, u32[]{:S(2)}, u32[]{:S(2)}) collective-permute-start(bf16[4,3,48,128]{3,2,1,0:T(8,128)(2,1)} %get-tuple-element.126), channel_id=1, source_target_pairs={{0,3},{1,2},{2,1},{3,0},{4,7},{5,6},{6,5},{7,4},{8,11},{9,10},{10,... | collective-permute-start | bytes 442376 | tf_op jit(solution)/shard_map/ppermute | solution.py:626
  122.1 11.4 %collective-permute-start.26 = (bf16[4,3,48,128]{3,2,1,0:T(8,128)(2,1)}, bf16[4,3,48,128]{3,2,1,0:T(8,128)(2,1)S(1)}, u32[]{:S(2)}, u32[]{:S(2)}) collective-permute-start(bf16[4,3,48,128]{3,2,1,0:T(8,128)(2,1)} %get-tuple-element.127), channel_id=1, source_target_pairs={{0,1},{1,0},{2,3},{3,2},{4,5},{5,4},{6,7},{7,6},{8,9},{9,8},{10,11... | collective-permute-start | bytes 442376 | tf_op jit(solution)/shard_map/ppermute | solution.py:626
  132.2 7.3 %copy-start.20 = (bf16[4,3,48,128]{3,2,1,0:T(8,128)(2,1)}, bf16[4,3,48,128]{3,2,1,0:T(8,128)(2,1)S(1)}, u32[]{:S(2)}) copy-start(bf16[4,3,48,128]{3,2,1,0:T(8,128)(2,1)S(1)} %collective-permute-done.24.rest_2_) | copy-start | bytes 442372
  132.2 7.3 %copy-start.21 = (bf16[4,3,48,128]{3,2,1,0:T(8,128)(2,1)}, bf16[4,3,48,128]{3,2,1,0:T(8,128)(2,1)S(1)}, u32[]{:S(2)}) copy-start(bf16[4,3,48,128]{3,2,1,0:T(8,128)(2,1)S(1)} %collective-permute-done.25.rest_3_) | copy-start | bytes 442372
  133.5 6.1 %copy-start.22 = (bf16[4,3,48,128]{3,2,1,0:T(8,128)(2,1)}, bf16[4,3,48,128]{3,2,1,0:T(8,128)(2,1)S(1)}, u32[]{:S(2)}) copy-start(bf16[4,3,48,128]{3,2,1,0:T(8,128)(2,1)S(1)} %collective-permute-done.26.rest_1_) | copy-start | bytes 442372
  133.5 1.6 %collective-permute-start.27 = (bf16[192,384]{1,0:T(8,128)(2,1)}, bf16[192,384]{1,0:T(8,128)(2,1)S(1)}, u32[]{:S(2)}, u32[]{:S(2)}) collective-permute-start(bf16[192,384]{1,0:T(8,128)(2,1)} %get-tuple-element.131), channel_id=1, source_target_pairs={{0,4},{4,0},{8,12},{12,8},{16,20},{20,16},{24,28},{28,24},{1,5},{5... | collective-permute-start | bytes 442376 | tf_op jit(solution)/shard_map/ppermute | solution.py:632
  136.0 11.7 %collective-permute-start.30 = (bf16[192,384]{1,0:T(8,128)(2,1)S(1)}, bf16[192,384]{1,0:T(8,128)(2,1)S(1)}, u32[]{:S(2)}, u32[]{:S(2)}) collective-permute-start(bf16[192,384]{1,0:T(8,128)(2,1)S(1)} %add_convert_fusion.5), channel_id=1, source_target_pairs={{0,24},{4,28},{8,16},{12,20},{16,8},{20,12},{24,0},{28,4},{1,25},{... | collective-permute-start | bytes 442376 | tf_op jit(solution)/shard_map/ppermute | solution.py:632
  138.5 9.2 %collective-permute-start.29 = (bf16[192,384]{1,0:T(8,128)(2,1)S(1)}, bf16[192,384]{1,0:T(8,128)(2,1)S(1)}, u32[]{:S(2)}, u32[]{:S(2)}) collective-permute-start(bf16[192,384]{1,0:T(8,128)(2,1)S(1)} %add_convert_fusion.5), channel_id=1, source_target_pairs={{0,16},{4,20},{8,24},{12,28},{16,0},{20,4},{24,8},{28,12},{1,17},{... | collective-permute-start | bytes 442376 | tf_op jit(solution)/shard_map/ppermute | solution.py:632
  139.0 8.7 %collective-permute-start.28 = (bf16[192,384]{1,0:T(8,128)(2,1)S(1)}, bf16[192,384]{1,0:T(8,128)(2,1)S(1)}, u32[]{:S(2)}, u32[]{:S(2)}) collective-permute-start(bf16[192,384]{1,0:T(8,128)(2,1)S(1)} %add_convert_fusion.5), channel_id=1, source_target_pairs={{0,8},{4,12},{8,0},{12,4},{16,24},{20,28},{24,16},{28,20},{1,9},{5... | collective-permute-start | bytes 442376 | tf_op jit(solution)/shard_map/ppermute | solution.py:632

commit v5 on v4

--- a/solution.py
+++ b/solution.py
@@ -11,6 +11,7 @@
 EPSILON = 1e-05
 BF16 = jnp.bfloat16
 F32 = jnp.float32
+LOG2_E = math.log2(math.e)
 VMEM_LIMIT = 56 * 1024 * 1024
 
 
@@ -69,6 +70,7 @@
     *rest,
     groups,
     calls,
+    head_size,
 ):
     send_refs = rest[:groups]
     gamma_ref, gate_ref, stage_ref = rest[groups:]
@@ -94,7 +96,7 @@
                 lane = (call * 4 + kind) * part
                 stage_ref[slot, :, lane : lane + part] = rounded[:, feature : feature + part]
 
-    put(0, mm(x_b, w_query_ref[...]))
+    put(0, mm(x_b, w_query_ref[...]) * (LOG2_E / math.sqrt(head_size)))
     put(1, mm(x_b, w_key_ref[...]))
     put(2, mm(x_b, w_value_ref[...]))
     grad_update = (cot_ref[...].astype(F32) * out_gate).astype(BF16)
@@ -167,7 +169,7 @@
         here = chain_all[:, group * cols : (group + 1) * cols]
         chain_cols = jnp.where(group_own == group, here, chain_cols)
     for head in range(heads):
-        gains_ref[head : head + 1, :] = jnp.full((1, cols), gain_ref[head], F32)
+        gains_ref[head : head + 1, :] = jnp.full((1, cols), gain_ref[head] * LOG2_E, F32)
 
     for first in range(0, step, batch):
         center = center_rows(pair_ref, first, batch, means)
@@ -190,7 +192,7 @@
                     stats_ref[side, row, heads:, :] = inverse[:8]
                     chain = chains_ref[row_base + side * half + row]
                     same = (chain_cols == chain).astype(F32)
-                    values = projected + gains_ref[...] * same
+                    values = projected * LOG2_E + gains_ref[...] * same
                     for tile, start, end in lane_tiles(cols):
                         piece = lane_pad(values[:, start:end], 0, 128)
                         flat_ref[side, tile, pl.ds(row, heads, stride=step), :] = piece
@@ -360,7 +362,6 @@
     (
         keep_ref,
         give_ref,
-        give_late_ref,
         query_ref,
         keys_ref,
         values_ref,
@@ -368,7 +369,6 @@
         query_t_ref,
         keys_t_ref,
         values_t_ref,
-        grads_t_ref,
         bias_full,
         score_full,
         att_sum,
@@ -387,7 +387,7 @@
     scale = 1.0 / math.sqrt(head_size)
     extra = att_sum.shape[1] - part
     plain = (query_ref, keys_ref, values_ref, grads_ref)
-    turned = (query_t_ref, keys_t_ref, values_t_ref, grads_t_ref)
+    turned = (query_t_ref, keys_t_ref, values_t_ref)
 
     turns = [(slot * cols, slot * 128, 128) for slot in range(groups)]
     turns += [
@@ -407,9 +407,11 @@
                     plain[kind][place : place + count, :] = acts_refs[slot][
                         inside : inside + count, lanes
                     ]
-            turned[kind][...] = plain[kind][...].T
+            if kind < len(turned):
+                turned[kind][...] = plain[kind][...].T
         att_sum[...] = jnp.zeros_like(att_sum)
         gq_sum[...] = jnp.zeros_like(gq_sum)
+        gv_sum[...] = jnp.zeros_like(gv_sum)
 
     def places(row_part):
         first = row_part * (2 * half)
@@ -440,40 +442,34 @@
     )
     feature = pl.multiple_of(head * head_size, head_size)
     query_t = query_t_ref[pl.ds(feature, head_size), :]
-    grads_t = grads_t_ref[pl.ds(feature, head_size), :]
     gk_t = jnp.zeros((head_size, tokens), F32)
-    gv_t = jnp.zeros((head_size, tokens), F32)
+    gv_t = jnp.zeros((part, tokens), F32)
     for top in range(0, tokens, row_block):
         rows = slice(top, top + row_block)
         query = jnp.where(mine, query_ref[rows, :], zero)
         grads = jnp.where(mine, grads_ref[rows, :], zero)
-        scores = mm(query, keys_t_ref[...]) * scale + bias_full[rows, :].astype(F32)
-        weights = jnp.exp(scores)
-        attended = mm(weights.astype(BF16), values_m)
+        weights = jnp.exp2(mm(query, keys_t_ref[...]) + bias_full[rows, :].astype(F32))
+        weights_b = weights.astype(BF16)
+        attended = mm(weights_b, values_m)
         inverse = 1.0 / attended[:, part : part + 1]
         attended = attended[:, :part] * inverse
         att_sum[rows, :part] += attended
+        grads = (grads.astype(F32) * inverse).astype(BF16)
         delta = jnp.sum(attended * grads.astype(F32), axis=-1, keepdims=True)
-        prob = weights * inverse
-        grad_prob = mm(grads, values_t_ref[...])
-        score = (prob * (grad_prob - delta)).astype(BF16)
+        score = (weights * (mm(grads, values_t_ref[...]) - delta)).astype(BF16)
         score_full[rows, :] = score
         gq_sum[rows, :] += mm(score, keys_m)
         gk_t = gk_t + mm(query_t[:, rows], score)
-        gv_t = gv_t + mm(grads_t[:, rows], prob.astype(BF16))
+        gv_t = gv_t + mm_tn(grads, weights_b)
     gk_sum[pl.ds(feature, head_size), :] = gk_t
-    gv_sum[pl.ds(feature, head_size), :] = gv_t
+    gv_sum[...] += gv_t
 
     order = unit_order(heads)
-    early = len(order) // 2
 
     def give_back(some_heads):
         for other in range(row_parts):
             unit = order.index((other // 2, some_heads[0]))
-            dbias_ref = keep_ref
-            if other % 2:
-                dbias_ref = give_ref if unit < early else give_late_ref
-                unit = unit % early
+            dbias_ref = give_ref if other % 2 else keep_ref
             unit = unit + head - some_heads[0]
             scores = [score_full[rows, :] for _, rows in places(row_ref[0] ^ other)]
             blocks = []
@@ -499,7 +495,7 @@
     def _():
         results = (
             gq_sum[...] * scale,
-            (gk_sum[...] * scale).T,
+            (gk_sum[...] * math.log(2.0)).T,
             gv_sum[...].T,
             att_sum[:, :part],
         )
@@ -522,11 +518,10 @@
     tokens = groups * cols
     part = width // 4
     _, heads, _, half, lanes = bias[0].shape
-    row_block = 256 if tokens % 256 == 0 else cols
+    row_block = tokens
     padded = (part // 128 + 1) * 128
     units = (row_parts // 2 * heads, groups, 3, half, lanes)
-    some = (row_parts // 4 * heads, groups, 3, half, lanes)
-    *grads, keep, give, give_late = pl.pallas_call(
+    *grads, keep, give = pl.pallas_call(
         functools.partial(
             attention_kernel,
             groups=groups,
@@ -542,11 +537,11 @@
         ]
         + [pl.BlockSpec((cols, width), lambda h: (0, 0))] * groups,
         out_specs=[pl.BlockSpec((cols, width), lambda h: (0, 0))] * groups
-        + [pl.BlockSpec(shape, lambda h: (0, 0, 0, 0, 0)) for shape in (units, some, some)],
+        + [pl.BlockSpec(shape, lambda h: (0, 0, 0, 0, 0)) for shape in (units, units)],
         out_shape=[jax.ShapeDtypeStruct((cols, width), BF16)] * groups
-        + [jax.ShapeDtypeStruct(shape, BF16) for shape in (units, some, some)],
+        + [jax.ShapeDtypeStruct(shape, BF16) for shape in (units, units)],
         scratch_shapes=[pltpu.VMEM((tokens, part), BF16) for _ in range(4)]
-        + [pltpu.VMEM((part, tokens), BF16) for _ in range(4)]
+        + [pltpu.VMEM((part, tokens), BF16) for _ in range(3)]
         + [
             pltpu.VMEM((tokens, tokens), BF16),
             pltpu.VMEM((tokens, tokens), BF16),
@@ -557,7 +552,7 @@
         ],
         compiler_params=params(),
     )(group_index, row_index, *bias, *acts)
-    return grads, keep, give, give_late
+    return grads, keep, give
 
 
 def finish_kernel(
@@ -624,7 +619,7 @@
     for bits in order:
         perm = [(index, index ^ bits) for index in range(groups)]
         got.append(lax.ppermute(sends[bits], "grp", perm))
-    got = dict(zip(order, lax.optimization_barrier(got)))
+    got = dict(zip(order, got))
     return [sends[0]] + [got[bits] for bits in range(1, groups)]
 
 
@@ -655,18 +650,14 @@
             out_ref[head] = total[slot]
 
 
-def scatter_rows(keep, give, give_late, row_total):
+def scatter_rows(keep, give, row_total):
     got = flip_rows(give, 1, row_total)
-    got, give_late = lax.optimization_barrier((got, give_late))
-    got_late = flip_rows(give_late, 1, row_total)
-    early = got.shape[0]
+    early = keep.shape[0] // 2
     heads = early // 2
     part = heads // 2
 
     def add(first, count, *others):
-        source, place = (got, first) if first < early else (got_late, first - early)
-        total = keep[first : first + count].astype(F32)
-        total += source[place : place + count].astype(F32)
+        total = keep[first : first + count].astype(F32) + got[first : first + count].astype(F32)
         for other in others:
             total += other.astype(F32)
         return total.astype(BF16)
@@ -732,7 +723,9 @@
     noised = noised[0]
     cotangent = cotangent[0]
     *acts_send, cond_gamma, out_gate = pl.pallas_call(
-        functools.partial(project_kernel, groups=groups, calls=calls),
+        functools.partial(
+            project_kernel, groups=groups, calls=calls, head_size=head_size
+        ),
         in_specs=[smem()] + [vmem()] * 10,
         out_shape=[
             jax.ShapeDtypeStruct((cols, 4 * width // groups), BF16) for _ in range(groups)
@@ -759,9 +752,9 @@
     bias_got, _ = lax.optimization_barrier((bias_got, acts_send))
     acts = swap_groups(acts_send)
     bias_all, acts = gather_rows(jnp.stack(bias_got), acts, row_total)
-    grads_send, keep, give, give_late = attention(group_index, row_index, acts, bias_all, head_size)
+    grads_send, keep, give = attention(group_index, row_index, acts, bias_all, head_size)
     grads = swap_groups(grads_send)
-    own, far_two, near_two = scatter_rows(keep, give, give_late, row_total)
+    own, far_two, near_two = scatter_rows(keep, give, row_total)
     far_two, near_two, grads = lax.optimization_barrier((far_two, near_two, grads))
     dbias_own, grads = lax.optimization_barrier((add_last(own, far_two, near_two), grads))
     dbias_back = swap_groups(dbias_own)
@@ -954,7 +947,7 @@
     def on_device(*args):
         pair, noised, w_pair = args[1], args[3], args[11]
         fits = (
-            groups in (2, 4)
+            groups == 4
             and pair.shape[0] % 32 == 0
             and pair.shape[1] % pair.shape[0] == 0
             and row_total == 8

time: 149 us -> 147 us (0.987)
  Pallas kernels: 50.6 us -> 48.9 us
    ppermute x19 -> x18, waiting for transfers between devices: 20.1 us -> 24.2 us  [flip_rows(): lax.ppermute(values, 'rows', [(index, index ^ bits) for index in range(ro...]
    ppermute x12, waiting for transfers between devices: 31.9 us -> 29 us  [swap_groups(): got.append(lax.ppermute(sends[bits], 'grp', perm))]
    ppermute x12, starting transfers between devices: 25.9 us -> 23.9 us  [swap_groups(): got.append(lax.ppermute(sends[bits], 'grp', perm))]
    pallas_call x1, Pallas kernels: 18 us -> 16.3 us  [attention(): pl.pallas_call(functools.partial(attention_kernel, groups=groups, row_par...]
    ppermute x19 -> x18, starting transfers between devices: 12.4 us -> 13 us  [flip_rows(): lax.ppermute(values, 'rows', [(index, index ^ bits) for index in range(ro...]
  transfers between devices with their start and end apart: 31 -> 30, of which waited for: 17 -> 14; matrix products, arithmetic and copies ran while one was open for 2% -> 1% of each run, Pallas kernels for 15% -> 15%
where the time goes in v5:
time: 147 us
  waiting for transfers between devices  53.2 us (36%)
  Pallas kernels  48.9 us (33%)
  starting transfers between devices  36.9 us (25%)
  other arithmetic  4.82 us (3%)
  local copies, waits for them, and re-layouts  1.96 us (1%)
    ppermute x12, waiting for transfers between devices, swap_groups(): got.append(lax.ppermute(sends[bits], 'grp', perm))  29 us
    ppermute x18, waiting for transfers between devices, flip_rows(): lax.ppermute(values, 'rows', [(index, index ^ bits) for index in range(ro...  24.2 us
    ppermute x12, starting transfers between devices, swap_groups(): got.append(lax.ppermute(sends[bits], 'grp', perm))  23.9 us
    pallas_call x1, Pallas kernels, attention(): pl.pallas_call(functools.partial(attention_kernel, groups=groups, row_par...  16.3 us
    ppermute x18, starting transfers between devices, flip_rows(): lax.ppermute(values, 'rows', [(index, index ^ bits) for index in range(ro...  13 us
    pallas_call x1, Pallas kernels, pair_bias(): pl.pallas_call(functools.partial(bias_kernel, groups=groups, batch=4), gr...  8.46 us
    pallas_call x1, Pallas kernels, pair_back(): pl.pallas_call(functools.partial(pair_back_kernel, groups=groups, calls=l...  8.18 us
    pallas_call x1, Pallas kernels, split_heads(): pl.pallas_call(functools.partial(finish_kernel, groups=groups, calls=call...  7.49 us
  transfers between devices with their start and end apart: 30, of which 14 were waited for; matrix products, arithmetic and copies ran while one was open for 1% of the time, Pallas kernels for 15%

profile of v5, /device:TPU:0, one launch (start us, length us, event | category | flops | bytes accessed | tf_op | source)
XLA Modules:
  0.0 146.7 jit_solution(13758237779718930705)
XLA Ops:
  0.6 8.5 %shard_map.158 = (bf16[4,3,48,128]{3,2,1,0:T(8,128)(2,1)}, bf16[4,3,48,128]{3,2,1,0:T(8,128)(2,1)}, bf16[4,3,48,128]{3,2,1,0:T(8,128)(2,1)}, bf16[4,3,48,128]{3,2,1,0:T(8,128)(2,1)}, f32[2,48,24,192]{3,2,1,0:T(8,128)}) custom-call(s32[1]{0:T(128)} %bitcast.group_ref, s32[1]{0:T(128)} %bitcast.3.rows_ref.row_ref, s32[768]{0:T(1024)} %cols_ref.1, f32[16]{0:T(128)} %gain_ref.1, ...), custom_call_target="tpu_custom_call" | custom-call | tf_op jit(solution)/shard_map/pallas_call | solution.py:217
  9.1 3.0 %collective-permute-start = (bf16[4,3,48,128]{3,2,1,0:T(8,128)(2,1)}, bf16[4,3,48,128]{3,2,1,0:T(8,128)(2,1)S(1)}, u32[]{:S(2)}, u32[]{:S(2)}) collective-permute-start(bf16[4,3,48,128]{3,2,1,0:T(8,128)(2,1)} %get-tuple-element.58), channel_id=1, source_target_pairs={{0,1},{1,0},{2,3},{3,2},{4,5},{5,4},{6,7},{7,6},{8,9},{9,8},{10,11... | collective-permute-start | bytes 442376 | tf_op jit(solution)/shard_map/ppermute | solution.py:621
  12.1 2.6 %collective-permute-start.1 = (bf16[4,3,48,128]{3,2,1,0:T(8,128)(2,1)}, bf16[4,3,48,128]{3,2,1,0:T(8,128)(2,1)S(1)}, u32[]{:S(2)}, u32[]{:S(2)}) collective-permute-start(bf16[4,3,48,128]{3,2,1,0:T(8,128)(2,1)} %get-tuple-element.59), channel_id=1, source_target_pairs={{0,2},{1,3},{2,0},{3,1},{4,6},{5,7},{6,4},{7,5},{8,10},{9,11},{10,... | collective-permute-start | bytes 442376 | tf_op jit(solution)/shard_map/ppermute | solution.py:621
  14.7 0.0 collective-permute-start.2
  14.7 6.4 %shard_map.157 = (bf16[192,768]{1,0:T(8,128)(2,1)}, bf16[192,768]{1,0:T(8,128)(2,1)}, bf16[192,768]{1,0:T(8,128)(2,1)}, bf16[192,768]{1,0:T(8,128)(2,1)}, f32[192,768]{1,0:T(8,128)}, /*index=5*/f32[192,768]{1,0:T(8,128)}) custom-call(s32[1]{0:T(128)} %bitcast.group_ref, bf16[192,384]{1,0:T(8,128)(2,1)} %single_ref.3, bf16[192,768]{1,0:T(8,128)(2,1)} %bitcast.15, ...), custom_call_target="tpu_custom_call" | custom-call | tf_op jit(solution)/shard_map/pallas_call | solution.py:725
  21.1 0.0 copy-start.27
  21.1 0.0 collective-permute-done
  21.1 5.2 %collective-permute-done.1 = bf16[4,3,48,128]{3,2,1,0:T(8,128)(2,1)S(1)} collective-permute-done((bf16[4,3,48,128]{3,2,1,0:T(8,128)(2,1)}, bf16[4,3,48,128]{3,2,1,0:T(8,128)(2,1)S(1)}, u32[]{:S(2)}, u32[]{:S(2)}) %collective-permute-start.1) | collective-permute-done | bytes 147488 | tf_op jit(solution)/shard_map/ppermute | solution.py:621
  26.3 0.0 collective-permute-done.2
  26.3 0.1 pad_maximum_fusion.rest_0_
  26.4 1.6 %collective-permute-start.6 = (bf16[4,4,3,48,128]{4,3,2,1,0:T(8,128)(2,1)S(1)}, bf16[4,4,3,48,128]{4,3,2,1,0:T(8,128)(2,1)S(1)}, u32[]{:S(2)}, u32[]{:S(2)}) collective-permute-start(bf16[4,4,3,48,128]{4,3,2,1,0:T(8,128)(2,1)S(1)} %pad_maximum_fusion.rest_0_), channel_id=1, source_target_pairs={{0,16},{4,20},{8,24},{12,28},{16,0},{20,4},{24,8},{28,12},{1,17},{... | collective-permute-start | bytes 1769480 | tf_op jit(solution)/shard_map/ppermute | solution.py:627
  28.0 1.5 %collective-permute-start.4 = (bf16[4,4,3,48,128]{4,3,2,1,0:T(8,128)(2,1)S(1)}, bf16[4,4,3,48,128]{4,3,2,1,0:T(8,128)(2,1)S(1)}, u32[]{:S(2)}, u32[]{:S(2)}) collective-permute-start(bf16[4,4,3,48,128]{4,3,2,1,0:T(8,128)(2,1)S(1)} %pad_maximum_fusion.rest_0_), channel_id=1, source_target_pairs={{0,8},{4,12},{8,0},{12,4},{16,24},{20,28},{24,16},{28,20},{1,9},{5... | collective-permute-start | bytes 1769480 | tf_op jit(solution)/shard_map/ppermute | solution.py:627
  29.5 2.3 %collective-permute-start.10 = (bf16[192,768]{1,0:T(8,128)(2,1)S(1)}, bf16[192,768]{1,0:T(8,128)(2,1)S(1)}, u32[]{:S(2)}, u32[]{:S(2)}) collective-permute-start(bf16[192,768]{1,0:T(8,128)(2,1)S(1)} %copy-done.28), channel_id=1, source_target_pairs={{0,1},{1,0},{2,3},{3,2},{4,5},{5,4},{6,7},{7,6},{8,9},{9,8},{10,11... | collective-permute-start | bytes 884744 | tf_op jit(solution)/shard_map/ppermute | solution.py:621
  31.8 1.1 collective-permute-start.11
  32.9 1.5 collective-permute-start.12
  34.3 4.7 %collective-permute-done.6.rest_4_ = bf16[4,4,3,48,128]{4,3,2,1,0:T(8,128)(2,1)S(1)} collective-permute-done((bf16[4,4,3,48,128]{4,3,2,1,0:T(8,128)(2,1)S(1)}, bf16[4,4,3,48,128]{4,3,2,1,0:T(8,128)(2,1)S(1)}, u32[]{:S(2)}, u32[]{:S(2)}) %collective-permute-start.6) | collective-permute-done | bytes 589856 | tf_op jit(solution)/shard_map/ppermute | solution.py:627
  39.1 1.5 %collective-permute-start.9 = (bf16[2,4,3,48,128]{4,3,2,1,0:T(8,128)(2,1)S(1)}, bf16[2,4,3,48,128]{4,3,2,1,0:T(8,128)(2,1)S(1)}, u32[]{:S(2)}, u32[]{:S(2)}) collective-permute-start(bf16[2,4,3,48,128]{4,3,2,1,0:T(8,128)(2,1)S(1)} %slice.65), channel_id=1, source_target_pairs={{0,8},{4,12},{8,0},{12,4},{16,24},{20,28},{24,16},{28,20},{1,9},{5... | collective-permute-start | bytes 884744 | tf_op jit(solution)/shard_map/ppermute | solution.py:627
  40.7 1.7 %collective-permute-done.4.rest_2_ = bf16[4,4,3,48,128]{4,3,2,1,0:T(8,128)(2,1)S(1)} collective-permute-done((bf16[4,4,3,48,128]{4,3,2,1,0:T(8,128)(2,1)S(1)}, bf16[4,4,3,48,128]{4,3,2,1,0:T(8,128)(2,1)S(1)}, u32[]{:S(2)}, u32[]{:S(2)}) %collective-permute-start.4) | collective-permute-done | bytes 589856 | tf_op jit(solution)/shard_map/ppermute | solution.py:627
  42.4 0.3 collective-permute-start.8
  42.7 12.6 %collective-permute-done.11.rest_12_ = bf16[192,768]{1,0:T(8,128)(2,1)S(1)} collective-permute-done((bf16[192,768]{1,0:T(8,128)(2,1)S(1)}, bf16[192,768]{1,0:T(8,128)(2,1)S(1)}, u32[]{:S(2)}, u32[]{:S(2)}) %collective-permute-start.11) | collective-permute-done | bytes 294944 | tf_op jit(solution)/shard_map/ppermute | solution.py:621
  55.3 0.5 collective-permute-start.5
  55.8 0.0 copy-start.14
  55.8 0.1 collective-permute-start.13
  56.0 0.4 collective-permute-start.14
  56.4 0.9 collective-permute-done.7.rest_5_
  57.3 0.8 collective-permute-done.5.rest_3_
  58.1 0.4 collective-permute-done.13.rest_7_
  58.6 0.4 collective-permute-done.14.rest_9_
  59.1 0.2 copy-done.15
  59.3 0.7 copy-done.16
  60.0 16.3 %shard_map.159 = (bf16[192,768]{1,0:T(8,128)(2,1)}, bf16[192,768]{1,0:T(8,128)(2,1)}, bf16[192,768]{1,0:T(8,128)(2,1)}, bf16[192,768]{1,0:T(8,128)(2,1)}, bf16[1...) custom-call(s32[1]{0:T(128)} %bitcast.group_ref, s32[1]{0:T(128)} %bitcast.3.rows_ref.row_ref, ...), custom_call_target="tpu_custom_call" | custom-call | tf_op jit(solution)/shard_map/pallas_call | solution.py:524
  76.3 0.2 collective-permute-start.15
  76.5 4.6 %collective-permute-done.15 = bf16[16,4,3,48,128]{4,3,2,1,0:T(8,128)(2,1)S(1)} collective-permute-done((bf16[16,4,3,48,128]{4,3,2,1,0:T(8,128)(2,1)}, bf16[16,4,3,48,128]{4,3,2,1,0:T(8,128)(2,1)S(1)}, u32[]{:S(2)}, u32[]{:S(2)}) %collective-permute-start.15) | collective-permute-done | bytes 2359328 | tf_op jit(solution)/shard_map/ppermute | solution.py:627
  81.1 1.7 %add_convert_fusion.2 = (bf16[4,4,3,48,128]{4,3,2,1,0:T(8,128)(2,1)S(1)}, bf16[4,4,3,48,128]{4,3,2,1,0:T(8,128)(2,1)S(1)}) fusion(bf16[16,4,3,48,128]{4,3,2,1,0:T(8,128)(2,1)S(1)} %collective-permute-done.15, bf16[16,4,3,48,128]{4,3,2,1,0:T(8,128)(2,1)} %get-tuple-element.75), kind=kLoop, calls=%fused_computation.2 | loop fusion | flops 2359296 | bytes 3538944 | tf_op jit(solution)/shard_map/convert_element_type | solution.py:663
  82.9 0.6 collective-permute-start.16
  83.5 0.5 collective-permute-start.17
  84.0 2.9 %collective-permute-start.20 = (bf16[192,768]{1,0:T(8,128)(2,1)S(1)}, bf16[192,768]{1,0:T(8,128)(2,1)S(1)}, u32[]{:S(2)}, u32[]{:S(2)}) collective-permute-start(bf16[192,768]{1,0:T(8,128)(2,1)S(1)} %copy-done.25), channel_id=1, source_target_pairs={{0,1},{1,0},{2,3},{3,2},{4,5},{5,4},{6,7},{7,6},{8,9},{9,8},{10,11... | collective-permute-start | bytes 884744 | tf_op jit(solution)/shard_map/ppermute | solution.py:621
  86.9 1.2 collective-permute-start.21
  88.1 1.5 collective-permute-start.22
  89.6 8.7 %collective-permute-done.16 = bf16[4,4,3,48,128]{4,3,2,1,0:T(8,128)(2,1)S(1)} collective-permute-done((bf16[4,4,3,48,128]{4,3,2,1,0:T(8,128)(2,1)S(1)}, bf16[4,4,3,48,128]{4,3,2,1,0:T(8,128)(2,1)S(1)}, u32[]{:S(2)}, u32[]{:S(2)}) %collective-permute-start.16) | collective-permute-done | bytes 589856 | tf_op jit(solution)/shard_map/ppermute | solution.py:627
  98.3 0.2 collective-permute-done.17
  98.6 0.2 add_convert_fusion.3
  98.8 1.6 %collective-permute-start.19 = (bf16[2,4,3,48,128]{4,3,2,1,0:T(8,128)(2,1)S(1)}, bf16[2,4,3,48,128]{4,3,2,1,0:T(8,128)(2,1)S(1)}, u32[]{:S(2)}, u32[]{:S(2)}) collective-permute-start(bf16[2,4,3,48,128]{4,3,2,1,0:T(8,128)(2,1)S(1)} %get-tuple-element.107), channel_id=1, source_target_pairs={{0,8},{4,12},{8,0},{12,4},{16,24},{20,28},{24,16},{28,20},{1,9},{5... | collective-permute-start | bytes 884744 | tf_op jit(solution)/shard_map/ppermute | solution.py:627
  100.4 0.5 collective-permute-start.18
  100.9 1.0 add_convert_fusion.own_ref
  102.0 8.4 %collective-permute-done.21.rest_2_ = bf16[192,768]{1,0:T(8,128)(2,1)S(1)} collective-permute-done((bf16[192,768]{1,0:T(8,128)(2,1)S(1)}, bf16[192,768]{1,0:T(8,128)(2,1)S(1)}, u32[]{:S(2)}, u32[]{:S(2)}) %collective-permute-start.21) | collective-permute-done | bytes 294944 | tf_op jit(solution)/shard_map/ppermute | solution.py:621
  110.4 0.0 copy-start.18
  110.4 0.7 copy-done.17
  111.2 0.1 copy-done.18
  111.3 2.1 %shard_map.160 = (bf16[4,3,48,128]{3,2,1,0:T(8,128)(2,1)}, bf16[4,3,48,128]{3,2,1,0:T(8,128)(2,1)}, bf16[4,3,48,128]{3,2,1,0:T(8,128)(2,1)}, bf16[4,3,48,128]{3,2,1,0:T(8,128)(2,1)}) custom-call(bf16[4,4,3,48,128]{4,3,2,1,0:T(8,128)(2,1)} %add_convert_fusion.own_ref, bf16[2,4,3,48,128]{4,3,2,1,0:T(8,128)(2,1)} %copy-done.18, ...), custom_call_target="tpu_custom_call" | custom-call | tf_op jit(solution)/shard_map/pallas_call | solution.py:675
  113.4 5.2 %collective-permute-start.23 = (bf16[4,3,48,128]{3,2,1,0:T(8,128)(2,1)}, bf16[4,3,48,128]{3,2,1,0:T(8,128)(2,1)S(1)}, u32[]{:S(2)}, u32[]{:S(2)}) collective-permute-start(bf16[4,3,48,128]{3,2,1,0:T(8,128)(2,1)} %get-tuple-element.98), channel_id=1, source_target_pairs={{0,1},{1,0},{2,3},{3,2},{4,5},{5,4},{6,7},{7,6},{8,9},{9,8},{10,11... | collective-permute-start | bytes 442376 | tf_op jit(solution)/shard_map/ppermute | solution.py:621
  118.6 1.2 collective-permute-start.24
  119.8 1.5 collective-permute-start.25
  121.3 7.5 %shard_map.161 = (bf16[192,768]{1,0:T(8,128)(2,1)}, bf16[192,384]{1,0:T(8,128)(2,1)}) custom-call(s32[1]{0:T(128)} %bitcast.group_ref, bf16[192,384]{1,0:T(8,128)(2,1)} %single_ref.3, bf16[192,768]{1,0:T(8,128)(2,1)} %bitcast.16, bf16[192,768]{1,0:T(8,128)(2,1)} %bitcast.18, f32[192,768]{1,0:T(8,128)} %get-tuple-element.55.gamma_ref, ...), custom_call_target="tpu_custom_call" | custom-call | tf_op jit(solution)/shard_map/pallas_call | solution.py:761
  128.8 0.0 copy-start.20
  128.8 2.8 %collective-permute-done.24.rest_2_ = bf16[4,3,48,128]{3,2,1,0:T(8,128)(2,1)S(1)} collective-permute-done((bf16[4,3,48,128]{3,2,1,0:T(8,128)(2,1)}, bf16[4,3,48,128]{3,2,1,0:T(8,128)(2,1)S(1)}, u32[]{:S(2)}, u32[]{:S(2)}) %collective-permute-start.24) | collective-permute-done | bytes 147488 | tf_op jit(solution)/shard_map/ppermute | solution.py:621
  131.5 0.1 collective-permute-start.26
  131.6 1.6 %collective-permute-done.26 = bf16[192,384]{1,0:T(8,128)(2,1)S(1)} collective-permute-done((bf16[192,384]{1,0:T(8,128)(2,1)}, bf16[192,384]{1,0:T(8,128)(2,1)S(1)}, u32[]{:S(2)}, u32[]{:S(2)}) %collective-permute-start.26) | collective-permute-done | bytes 147488 | tf_op jit(solution)/shard_map/ppermute | solution.py:627
  133.2 1.0 add_convert_fusion.5
  134.1 2.5 %collective-permute-start.29 = (bf16[192,384]{1,0:T(8,128)(2,1)S(1)}, bf16[192,384]{1,0:T(8,128)(2,1)S(1)}, u32[]{:S(2)}, u32[]{:S(2)}) collective-permute-start(bf16[192,384]{1,0:T(8,128)(2,1)S(1)} %add_convert_fusion.5), channel_id=1, source_target_pairs={{0,24},{4,28},{8,16},{12,20},{16,8},{20,12},{24,0},{28,4},{1,25},{... | collective-permute-start | bytes 442376 | tf_op jit(solution)/shard_map/ppermute | solution.py:627
  136.7 0.5 collective-permute-start.28
  137.1 0.6 collective-permute-start.27
  137.7 8.2 %shard_map.162 = bf16[2,48,192,128]{3,2,1,0:T(8,128)(2,1)} custom-call(s32[1]{0:T(128)} %bitcast.group_ref, bf16[2,48,192,128]{3,2,1,0:T(8,128)(2,1)} %bitcast.13, f32[2,48,24,192]{3,2,1,0:T(8,128)} %get-tuple-element.102.stats_ref, bf16[16,128]{1,0:T(8,128)(2,1)} %bitcast.24, bf16[4,3,48,128]{3,2,1,0:T(8,128)(2,1)} %get-tuple-element.103.rest_0_, ...), custom_call_target="tpu_custom_call" | custom-call | tf_op jit(solution)/shard_map/pallas_call | solution.py:328
  145.9 0.8 add_add_fusion
  (70 shorter events, 0.2 us)
Async XLA Ops:
  9.1 12.0 %collective-permute-start = (bf16[4,3,48,128]{3,2,1,0:T(8,128)(2,1)}, bf16[4,3,48,128]{3,2,1,0:T(8,128)(2,1)S(1)}, u32[]{:S(2)}, u32[]{:S(2)}) collective-permute-start(bf16[4,3,48,128]{3,2,1,0:T(8,128)(2,1)} %get-tuple-element.58), channel_id=1, source_target_pairs={{0,1},{1,0},{2,3},{3,2},{4,5},{5,4},{6,7},{7,6},{8,9},{9,8},{10,11... | collective-permute-start | bytes 442376 | tf_op jit(solution)/shard_map/ppermute | solution.py:621
  12.1 14.2 %collective-permute-start.1 = (bf16[4,3,48,128]{3,2,1,0:T(8,128)(2,1)}, bf16[4,3,48,128]{3,2,1,0:T(8,128)(2,1)S(1)}, u32[]{:S(2)}, u32[]{:S(2)}) collective-permute-start(bf16[4,3,48,128]{3,2,1,0:T(8,128)(2,1)} %get-tuple-element.59), channel_id=1, source_target_pairs={{0,2},{1,3},{2,0},{3,1},{4,6},{5,7},{6,4},{7,5},{8,10},{9,11},{10,... | collective-permute-start | bytes 442376 | tf_op jit(solution)/shard_map/ppermute | solution.py:621
  14.7 11.6 %collective-permute-start.2 = (bf16[4,3,48,128]{3,2,1,0:T(8,128)(2,1)}, bf16[4,3,48,128]{3,2,1,0:T(8,128)(2,1)S(1)}, u32[]{:S(2)}, u32[]{:S(2)}) collective-permute-start(bf16[4,3,48,128]{3,2,1,0:T(8,128)(2,1)} %get-tuple-element.60), channel_id=1, source_target_pairs={{0,3},{1,2},{2,1},{3,0},{4,7},{5,6},{6,5},{7,4},{8,11},{9,10},{10,... | collective-permute-start | bytes 442376 | tf_op jit(solution)/shard_map/ppermute | solution.py:621
  14.7 11.6 %copy-start.19 = (bf16[4,3,48,128]{3,2,1,0:T(8,128)(2,1)S(1)}, bf16[4,3,48,128]{3,2,1,0:T(8,128)(2,1)}, u32[]{:S(2)}) copy-start(bf16[4,3,48,128]{3,2,1,0:T(8,128)(2,1)} %get-tuple-element.65) | copy-start | bytes 442372
  21.1 8.4 %copy-start.28 = (bf16[192,768]{1,0:T(8,128)(2,1)S(1)}, bf16[192,768]{1,0:T(8,128)(2,1)}, u32[]{:S(2)}) copy-start(bf16[192,768]{1,0:T(8,128)(2,1)} %get-tuple-element.62) | copy-start | bytes 884740
  21.1 10.7 %copy-start.27 = (bf16[192,768]{1,0:T(8,128)(2,1)S(1)}, bf16[192,768]{1,0:T(8,128)(2,1)}, u32[]{:S(2)}) copy-start(bf16[192,768]{1,0:T(8,128)(2,1)} %get-tuple-element.63) | copy-start | bytes 884740
  21.1 11.8 %copy-start.26 = (bf16[192,768]{1,0:T(8,128)(2,1)S(1)}, bf16[192,768]{1,0:T(8,128)(2,1)}, u32[]{:S(2)}) copy-start(bf16[192,768]{1,0:T(8,128)(2,1)} %get-tuple-element.64) | copy-start | bytes 884740
  26.4 32.6 %copy-start = (bf16[4,4,3,48,128]{4,3,2,1,0:T(8,128)(2,1)}, bf16[4,4,3,48,128]{4,3,2,1,0:T(8,128)(2,1)S(1)}, u32[]{:S(2)}) copy-start(bf16[4,4,3,48,128]{4,3,2,1,0:T(8,128)(2,1)S(1)} %pad_maximum_fusion.rest_0_) | copy-start | bytes 1769476
  26.4 12.7 %collective-permute-start.6 = (bf16[4,4,3,48,128]{4,3,2,1,0:T(8,128)(2,1)S(1)}, bf16[4,4,3,48,128]{4,3,2,1,0:T(8,128)(2,1)S(1)}, u32[]{:S(2)}, u32[]{:S(2)}) collective-permute-start(bf16[4,4,3,48,128]{4,3,2,1,0:T(8,128)(2,1)S(1)} %pad_maximum_fusion.rest_0_), channel_id=1, source_target_pairs={{0,16},{4,20},{8,24},{12,28},{16,0},{20,4},{24,8},{28,12},{1,17},{... | collective-permute-start | bytes 1769480 | tf_op jit(solution)/shard_map/ppermute | solution.py:627
  28.0 14.4 %collective-permute-start.4 = (bf16[4,4,3,48,128]{4,3,2,1,0:T(8,128)(2,1)S(1)}, bf16[4,4,3,48,128]{4,3,2,1,0:T(8,128)(2,1)S(1)}, u32[]{:S(2)}, u32[]{:S(2)}) collective-permute-start(bf16[4,4,3,48,128]{4,3,2,1,0:T(8,128)(2,1)S(1)} %pad_maximum_fusion.rest_0_), channel_id=1, source_target_pairs={{0,8},{4,12},{8,0},{12,4},{16,24},{20,28},{24,16},{28,20},{1,9},{5... | collective-permute-start | bytes 1769480 | tf_op jit(solution)/shard_map/ppermute | solution.py:627
  29.5 13.2 %collective-permute-start.10 = (bf16[192,768]{1,0:T(8,128)(2,1)S(1)}, bf16[192,768]{1,0:T(8,128)(2,1)S(1)}, u32[]{:S(2)}, u32[]{:S(2)}) collective-permute-start(bf16[192,768]{1,0:T(8,128)(2,1)S(1)} %copy-done.28), channel_id=1, source_target_pairs={{0,1},{1,0},{2,3},{3,2},{4,5},{5,4},{6,7},{7,6},{8,9},{9,8},{10,11... | collective-permute-start | bytes 884744 | tf_op jit(solution)/shard_map/ppermute | solution.py:621
  31.8 23.5 %collective-permute-start.11 = (bf16[192,768]{1,0:T(8,128)(2,1)S(1)}, bf16[192,768]{1,0:T(8,128)(2,1)S(1)}, u32[]{:S(2)}, u32[]{:S(2)}) collective-permute-start(bf16[192,768]{1,0:T(8,128)(2,1)S(1)} %copy-done.27), channel_id=1, source_target_pairs={{0,2},{1,3},{2,0},{3,1},{4,6},{5,7},{6,4},{7,5},{8,10},{9,11},{10,... | collective-permute-start | bytes 884744 | tf_op jit(solution)/shard_map/ppermute | solution.py:621
  32.9 22.4 %collective-permute-start.12 = (bf16[192,768]{1,0:T(8,128)(2,1)S(1)}, bf16[192,768]{1,0:T(8,128)(2,1)S(1)}, u32[]{:S(2)}, u32[]{:S(2)}) collective-permute-start(bf16[192,768]{1,0:T(8,128)(2,1)S(1)} %copy-done.26), channel_id=1, source_target_pairs={{0,3},{1,2},{2,1},{3,0},{4,7},{5,6},{6,5},{7,4},{8,11},{9,10},{10,... | collective-permute-start | bytes 884744 | tf_op jit(solution)/shard_map/ppermute | solution.py:621
  39.1 19.9 %copy-start.2 = (bf16[4,4,3,48,128]{4,3,2,1,0:T(8,128)(2,1)}, bf16[4,4,3,48,128]{4,3,2,1,0:T(8,128)(2,1)S(1)}, u32[]{:S(2)}) copy-start(bf16[4,4,3,48,128]{4,3,2,1,0:T(8,128)(2,1)S(1)} %collective-permute-done.6.rest_4_) | copy-start | bytes 1769476
  39.1 16.7 %collective-permute-start.9 = (bf16[2,4,3,48,128]{4,3,2,1,0:T(8,128)(2,1)S(1)}, bf16[2,4,3,48,128]{4,3,2,1,0:T(8,128)(2,1)S(1)}, u32[]{:S(2)}, u32[]{:S(2)}) collective-permute-start(bf16[2,4,3,48,128]{4,3,2,1,0:T(8,128)(2,1)S(1)} %slice.65), channel_id=1, source_target_pairs={{0,8},{4,12},{8,0},{12,4},{16,24},{20,28},{24,16},{28,20},{1,9},{5... | collective-permute-start | bytes 884744 | tf_op jit(solution)/shard_map/ppermute | solution.py:627
  42.4 16.6 %copy-start.3 = (bf16[4,4,3,48,128]{4,3,2,1,0:T(8,128)(2,1)}, bf16[4,4,3,48,128]{4,3,2,1,0:T(8,128)(2,1)S(1)}, u32[]{:S(2)}) copy-start(bf16[4,4,3,48,128]{4,3,2,1,0:T(8,128)(2,1)S(1)} %collective-permute-done.4.rest_2_) | copy-start | bytes 1769476
  42.4 13.4 %collective-permute-start.8 = (bf16[2,4,3,48,128]{4,3,2,1,0:T(8,128)(2,1)S(1)}, bf16[2,4,3,48,128]{4,3,2,1,0:T(8,128)(2,1)S(1)}, u32[]{:S(2)}, u32[]{:S(2)}) collective-permute-start(bf16[2,4,3,48,128]{4,3,2,1,0:T(8,128)(2,1)S(1)} %slice.64), channel_id=1, source_target_pairs={{0,16},{4,20},{8,24},{12,28},{16,0},{20,4},{24,8},{28,12},{1,17},{... | collective-permute-start | bytes 884744 | tf_op jit(solution)/shard_map/ppermute | solution.py:627
  42.7 16.3 %copy-start.7 = (bf16[192,768]{1,0:T(8,128)(2,1)}, bf16[192,768]{1,0:T(8,128)(2,1)S(1)}, u32[]{:S(2)}) copy-start(bf16[192,768]{1,0:T(8,128)(2,1)S(1)} %collective-permute-done.10.rest_11_) | copy-start | bytes 884740
  42.7 13.7 %collective-permute-start.3 = (bf16[4,4,3,48,128]{4,3,2,1,0:T(8,128)(2,1)S(1)}, bf16[4,4,3,48,128]{4,3,2,1,0:T(8,128)(2,1)S(1)}, u32[]{:S(2)}, u32[]{:S(2)}) collective-permute-start(bf16[4,4,3,48,128]{4,3,2,1,0:T(8,128)(2,1)S(1)} %pad_maximum_fusion.rest_0_), channel_id=1, source_target_pairs={{0,4},{4,0},{8,12},{12,8},{16,20},{20,16},{24,28},{28,24},{1,5},{5... | collective-permute-start | bytes 1769480 | tf_op jit(solution)/shard_map/ppermute | solution.py:627
  55.3 3.7 %copy-start.8 = (bf16[192,768]{1,0:T(8,128)(2,1)}, bf16[192,768]{1,0:T(8,128)(2,1)S(1)}, u32[]{:S(2)}) copy-start(bf16[192,768]{1,0:T(8,128)(2,1)S(1)} %collective-permute-done.11.rest_12_) | copy-start | bytes 884740
  55.3 2.0 %collective-permute-start.7 = (bf16[4,4,3,48,128]{4,3,2,1,0:T(8,128)(2,1)S(1)}, bf16[4,4,3,48,128]{4,3,2,1,0:T(8,128)(2,1)S(1)}, u32[]{:S(2)}, u32[]{:S(2)}) collective-permute-start(bf16[4,4,3,48,128]{4,3,2,1,0:T(8,128)(2,1)S(1)} %collective-permute-done.6.rest_4_), channel_id=1, source_target_pairs={{0,4},{4,0},{8,12},{12,8},{16,20},{20,16},{24,28},{28,24},{1,5},{5... | collective-permute-start | bytes 1769480 | tf_op jit(solution)/shard_map/ppermute | solution.py:627
  55.3 3.7 %copy-start.10 = (bf16[192,768]{1,0:T(8,128)(2,1)}, bf16[192,768]{1,0:T(8,128)(2,1)S(1)}, u32[]{:S(2)}) copy-start(bf16[192,768]{1,0:T(8,128)(2,1)S(1)} %collective-permute-done.12.rest_13_) | copy-start | bytes 884740
  55.3 2.8 %collective-permute-start.5 = (bf16[4,4,3,48,128]{4,3,2,1,0:T(8,128)(2,1)S(1)}, bf16[4,4,3,48,128]{4,3,2,1,0:T(8,128)(2,1)S(1)}, u32[]{:S(2)}, u32[]{:S(2)}) collective-permute-start(bf16[4,4,3,48,128]{4,3,2,1,0:T(8,128)(2,1)S(1)} %collective-permute-done.4.rest_2_), channel_id=1, source_target_pairs={{0,4},{4,0},{8,12},{12,8},{16,20},{20,16},{24,28},{28,24},{1,5},{5... | collective-permute-start | bytes 1769480 | tf_op jit(solution)/shard_map/ppermute | solution.py:627
  55.8 3.2 %copy-start.13 = (bf16[2,4,3,48,128]{4,3,2,1,0:T(8,128)(2,1)}, bf16[2,4,3,48,128]{4,3,2,1,0:T(8,128)(2,1)S(1)}, u32[]{:S(2)}) copy-start(bf16[2,4,3,48,128]{4,3,2,1,0:T(8,128)(2,1)S(1)} %collective-permute-done.9.rest_8_) | copy-start | bytes 884740
  55.8 3.2 %copy-start.14 = (bf16[2,4,3,48,128]{4,3,2,1,0:T(8,128)(2,1)}, bf16[2,4,3,48,128]{4,3,2,1,0:T(8,128)(2,1)S(1)}, u32[]{:S(2)}) copy-start(bf16[2,4,3,48,128]{4,3,2,1,0:T(8,128)(2,1)S(1)} %collective-permute-done.8.rest_6_) | copy-start | bytes 884740
  55.8 2.7 %collective-permute-start.13 = (bf16[2,4,3,48,128]{4,3,2,1,0:T(8,128)(2,1)S(1)}, bf16[2,4,3,48,128]{4,3,2,1,0:T(8,128)(2,1)S(1)}, u32[]{:S(2)}, u32[]{:S(2)}) collective-permute-start(bf16[2,4,3,48,128]{4,3,2,1,0:T(8,128)(2,1)S(1)} %collective-permute-done.8.rest_6_), channel_id=1, source_target_pairs={{0,4},{4,0},{8,12},{12,8},{16,20},{20,16},{24,28},{28,24},{1,5},{5... | collective-permute-start | bytes 884744 | tf_op jit(solution)/shard_map/ppermute | solution.py:627
  56.0 3.0 %collective-permute-start.14 = (bf16[2,4,3,48,128]{4,3,2,1,0:T(8,128)(2,1)S(1)}, bf16[2,4,3,48,128]{4,3,2,1,0:T(8,128)(2,1)S(1)}, u32[]{:S(2)}, u32[]{:S(2)}) collective-permute-start(bf16[2,4,3,48,128]{4,3,2,1,0:T(8,128)(2,1)S(1)} %collective-permute-done.9.rest_8_), channel_id=1, source_target_pairs={{0,4},{4,0},{8,12},{12,8},{16,20},{20,16},{24,28},{28,24},{1,5},{5... | collective-permute-start | bytes 884744 | tf_op jit(solution)/shard_map/ppermute | solution.py:627
  56.4 2.6 %copy-start.4 = (bf16[4,4,3,48,128]{4,3,2,1,0:T(8,128)(2,1)}, bf16[4,4,3,48,128]{4,3,2,1,0:T(8,128)(2,1)S(1)}, u32[]{:S(2)}) copy-start(bf16[4,4,3,48,128]{4,3,2,1,0:T(8,128)(2,1)S(1)} %collective-permute-done.3.rest_1_) | copy-start | bytes 1769476
  57.3 1.8 %copy-start.5 = (bf16[4,4,3,48,128]{4,3,2,1,0:T(8,128)(2,1)}, bf16[4,4,3,48,128]{4,3,2,1,0:T(8,128)(2,1)S(1)}, u32[]{:S(2)}) copy-start(bf16[4,4,3,48,128]{4,3,2,1,0:T(8,128)(2,1)S(1)} %collective-permute-done.7.rest_5_) | copy-start | bytes 1769476
  58.1 0.9 copy-start.6
  58.6 0.7 copy-start.15
  59.3 0.7 copy-start.16
  76.3 4.8 %collective-permute-start.15 = (bf16[16,4,3,48,128]{4,3,2,1,0:T(8,128)(2,1)}, bf16[16,4,3,48,128]{4,3,2,1,0:T(8,128)(2,1)S(1)}, u32[]{:S(2)}, u32[]{:S(2)}) collective-permute-start(bf16[16,4,3,48,128]{4,3,2,1,0:T(8,128)(2,1)} %get-tuple-element.76), channel_id=1, source_target_pairs={{0,4},{4,0},{8,12},{12,8},{16,20},{20,16},{24,28},{28,24},{1,5},{5... | collective-permute-start | bytes 7077896 | tf_op jit(solution)/shard_map/ppermute | solution.py:627
  81.1 2.8 %copy-start.25 = (bf16[192,768]{1,0:T(8,128)(2,1)S(1)}, bf16[192,768]{1,0:T(8,128)(2,1)}, u32[]{:S(2)}) copy-start(bf16[192,768]{1,0:T(8,128)(2,1)} %get-tuple-element.78) | copy-start | bytes 884740
  81.1 5.8 %copy-start.24 = (bf16[192,768]{1,0:T(8,128)(2,1)S(1)}, bf16[192,768]{1,0:T(8,128)(2,1)}, u32[]{:S(2)}) copy-start(bf16[192,768]{1,0:T(8,128)(2,1)} %get-tuple-element.79) | copy-start | bytes 884740
  81.1 7.0 %copy-start.23 = (bf16[192,768]{1,0:T(8,128)(2,1)S(1)}, bf16[192,768]{1,0:T(8,128)(2,1)}, u32[]{:S(2)}) copy-start(bf16[192,768]{1,0:T(8,128)(2,1)} %get-tuple-element.80) | copy-start | bytes 884740
  81.1 17.4 %copy-start.1 = (bf16[16,4,3,48,128]{4,3,2,1,0:T(8,128)(2,1)S(1)}, bf16[16,4,3,48,128]{4,3,2,1,0:T(8,128)(2,1)}, u32[]{:S(2)}) copy-start(bf16[16,4,3,48,128]{4,3,2,1,0:T(8,128)(2,1)} %get-tuple-element.75) | copy-start | bytes 7077892
  82.9 15.4 %collective-permute-start.16 = (bf16[4,4,3,48,128]{4,3,2,1,0:T(8,128)(2,1)S(1)}, bf16[4,4,3,48,128]{4,3,2,1,0:T(8,128)(2,1)S(1)}, u32[]{:S(2)}, u32[]{:S(2)}) collective-permute-start(bf16[4,4,3,48,128]{4,3,2,1,0:T(8,128)(2,1)S(1)} %get-tuple-element.109), channel_id=1, source_target_pairs={{0,8},{4,12},{8,0},{12,4},{16,24},{20,28},{24,16},{28,20},{1,9},{5... | collective-permute-start | bytes 1769480 | tf_op jit(solution)/shard_map/ppermute | solution.py:627
  83.5 15.1 %collective-permute-start.17 = (bf16[4,4,3,48,128]{4,3,2,1,0:T(8,128)(2,1)S(1)}, bf16[4,4,3,48,128]{4,3,2,1,0:T(8,128)(2,1)S(1)}, u32[]{:S(2)}, u32[]{:S(2)}) collective-permute-start(bf16[4,4,3,48,128]{4,3,2,1,0:T(8,128)(2,1)S(1)} %get-tuple-element.110), channel_id=1, source_target_pairs={{0,16},{4,20},{8,24},{12,28},{16,0},{20,4},{24,8},{28,12},{1,17},{... | collective-permute-start | bytes 1769480 | tf_op jit(solution)/shard_map/ppermute | solution.py:627
  84.0 18.0 %collective-permute-start.20 = (bf16[192,768]{1,0:T(8,128)(2,1)S(1)}, bf16[192,768]{1,0:T(8,128)(2,1)S(1)}, u32[]{:S(2)}, u32[]{:S(2)}) collective-permute-start(bf16[192,768]{1,0:T(8,128)(2,1)S(1)} %copy-done.25), channel_id=1, source_target_pairs={{0,1},{1,0},{2,3},{3,2},{4,5},{5,4},{6,7},{7,6},{8,9},{9,8},{10,11... | collective-permute-start | bytes 884744 | tf_op jit(solution)/shard_map/ppermute | solution.py:621
  86.9 23.5 %collective-permute-start.21 = (bf16[192,768]{1,0:T(8,128)(2,1)S(1)}, bf16[192,768]{1,0:T(8,128)(2,1)S(1)}, u32[]{:S(2)}, u32[]{:S(2)}) collective-permute-start(bf16[192,768]{1,0:T(8,128)(2,1)S(1)} %copy-done.24), channel_id=1, source_target_pairs={{0,2},{1,3},{2,0},{3,1},{4,6},{5,7},{6,4},{7,5},{8,10},{9,11},{10,... | collective-permute-start | bytes 884744 | tf_op jit(solution)/shard_map/ppermute | solution.py:621
  88.1 22.3 %collective-permute-start.22 = (bf16[192,768]{1,0:T(8,128)(2,1)S(1)}, bf16[192,768]{1,0:T(8,128)(2,1)S(1)}, u32[]{:S(2)}, u32[]{:S(2)}) collective-permute-start(bf16[192,768]{1,0:T(8,128)(2,1)S(1)} %copy-done.23), channel_id=1, source_target_pairs={{0,3},{1,2},{2,1},{3,0},{4,7},{5,6},{6,5},{7,4},{8,11},{9,10},{10,... | collective-permute-start | bytes 884744 | tf_op jit(solution)/shard_map/ppermute | solution.py:621
  98.8 11.6 %collective-permute-start.19 = (bf16[2,4,3,48,128]{4,3,2,1,0:T(8,128)(2,1)S(1)}, bf16[2,4,3,48,128]{4,3,2,1,0:T(8,128)(2,1)S(1)}, u32[]{:S(2)}, u32[]{:S(2)}) collective-permute-start(bf16[2,4,3,48,128]{4,3,2,1,0:T(8,128)(2,1)S(1)} %get-tuple-element.107), channel_id=1, source_target_pairs={{0,8},{4,12},{8,0},{12,4},{16,24},{20,28},{24,16},{28,20},{1,9},{5... | collective-permute-start | bytes 884744 | tf_op jit(solution)/shard_map/ppermute | solution.py:627
  100.4 10.0 %collective-permute-start.18 = (bf16[2,4,3,48,128]{4,3,2,1,0:T(8,128)(2,1)S(1)}, bf16[2,4,3,48,128]{4,3,2,1,0:T(8,128)(2,1)S(1)}, u32[]{:S(2)}, u32[]{:S(2)}) collective-permute-start(bf16[2,4,3,48,128]{4,3,2,1,0:T(8,128)(2,1)S(1)} %get-tuple-element.108), channel_id=1, source_target_pairs={{0,16},{4,20},{8,24},{12,28},{16,0},{20,4},{24,8},{28,12},{1,17},{... | collective-permute-start | bytes 884744 | tf_op jit(solution)/shard_map/ppermute | solution.py:627
  102.0 19.3 %copy-start.9 = (bf16[192,768]{1,0:T(8,128)(2,1)}, bf16[192,768]{1,0:T(8,128)(2,1)S(1)}, u32[]{:S(2)}) copy-start(bf16[192,768]{1,0:T(8,128)(2,1)S(1)} %collective-permute-done.20.rest_1_) | copy-start | bytes 884740
  110.4 10.9 %copy-start.11 = (bf16[192,768]{1,0:T(8,128)(2,1)}, bf16[192,768]{1,0:T(8,128)(2,1)S(1)}, u32[]{:S(2)}) copy-start(bf16[192,768]{1,0:T(8,128)(2,1)S(1)} %collective-permute-done.21.rest_2_) | copy-start | bytes 884740
  110.4 10.9 %copy-start.12 = (bf16[192,768]{1,0:T(8,128)(2,1)}, bf16[192,768]{1,0:T(8,128)(2,1)S(1)}, u32[]{:S(2)}) copy-start(bf16[192,768]{1,0:T(8,128)(2,1)S(1)} %collective-permute-done.22.rest_3_) | copy-start | bytes 884740
  110.4 0.8 copy-start.17
  110.4 0.9 copy-start.18
  113.4 15.3 %collective-permute-start.23 = (bf16[4,3,48,128]{3,2,1,0:T(8,128)(2,1)}, bf16[4,3,48,128]{3,2,1,0:T(8,128)(2,1)S(1)}, u32[]{:S(2)}, u32[]{:S(2)}) collective-permute-start(bf16[4,3,48,128]{3,2,1,0:T(8,128)(2,1)} %get-tuple-element.98), channel_id=1, source_target_pairs={{0,1},{1,0},{2,3},{3,2},{4,5},{5,4},{6,7},{7,6},{8,9},{9,8},{10,11... | collective-permute-start | bytes 442376 | tf_op jit(solution)/shard_map/ppermute | solution.py:621
  118.6 12.9 %collective-permute-start.24 = (bf16[4,3,48,128]{3,2,1,0:T(8,128)(2,1)}, bf16[4,3,48,128]{3,2,1,0:T(8,128)(2,1)S(1)}, u32[]{:S(2)}, u32[]{:S(2)}) collective-permute-start(bf16[4,3,48,128]{3,2,1,0:T(8,128)(2,1)} %get-tuple-element.99), channel_id=1, source_target_pairs={{0,2},{1,3},{2,0},{3,1},{4,6},{5,7},{6,4},{7,5},{8,10},{9,11},{10,... | collective-permute-start | bytes 442376 | tf_op jit(solution)/shard_map/ppermute | solution.py:621
  119.8 11.7 %collective-permute-start.25 = (bf16[4,3,48,128]{3,2,1,0:T(8,128)(2,1)}, bf16[4,3,48,128]{3,2,1,0:T(8,128)(2,1)S(1)}, u32[]{:S(2)}, u32[]{:S(2)}) collective-permute-start(bf16[4,3,48,128]{3,2,1,0:T(8,128)(2,1)} %get-tuple-element.100), channel_id=1, source_target_pairs={{0,3},{1,2},{2,1},{3,0},{4,7},{5,6},{6,5},{7,4},{8,11},{9,10},{10,... | collective-permute-start | bytes 442376 | tf_op jit(solution)/shard_map/ppermute | solution.py:621
  128.8 8.9 %copy-start.20 = (bf16[4,3,48,128]{3,2,1,0:T(8,128)(2,1)}, bf16[4,3,48,128]{3,2,1,0:T(8,128)(2,1)S(1)}, u32[]{:S(2)}) copy-start(bf16[4,3,48,128]{3,2,1,0:T(8,128)(2,1)S(1)} %collective-permute-done.23.rest_1_) | copy-start | bytes 442372
  131.5 6.2 %copy-start.21 = (bf16[4,3,48,128]{3,2,1,0:T(8,128)(2,1)}, bf16[4,3,48,128]{3,2,1,0:T(8,128)(2,1)S(1)}, u32[]{:S(2)}) copy-start(bf16[4,3,48,128]{3,2,1,0:T(8,128)(2,1)S(1)} %collective-permute-done.24.rest_2_) | copy-start | bytes 442372
  131.5 6.2 %copy-start.22 = (bf16[4,3,48,128]{3,2,1,0:T(8,128)(2,1)}, bf16[4,3,48,128]{3,2,1,0:T(8,128)(2,1)S(1)}, u32[]{:S(2)}) copy-start(bf16[4,3,48,128]{3,2,1,0:T(8,128)(2,1)S(1)} %collective-permute-done.25.rest_3_) | copy-start | bytes 442372
  131.5 1.6 %collective-permute-start.26 = (bf16[192,384]{1,0:T(8,128)(2,1)}, bf16[192,384]{1,0:T(8,128)(2,1)S(1)}, u32[]{:S(2)}, u32[]{:S(2)}) collective-permute-start(bf16[192,384]{1,0:T(8,128)(2,1)} %get-tuple-element.101), channel_id=1, source_target_pairs={{0,4},{4,0},{8,12},{12,8},{16,20},{20,16},{24,28},{28,24},{1,5},{5... | collective-permute-start | bytes 442376 | tf_op jit(solution)/shard_map/ppermute | solution.py:627
  134.1 11.7 %collective-permute-start.29 = (bf16[192,384]{1,0:T(8,128)(2,1)S(1)}, bf16[192,384]{1,0:T(8,128)(2,1)S(1)}, u32[]{:S(2)}, u32[]{:S(2)}) collective-permute-start(bf16[192,384]{1,0:T(8,128)(2,1)S(1)} %add_convert_fusion.5), channel_id=1, source_target_pairs={{0,24},{4,28},{8,16},{12,20},{16,8},{20,12},{24,0},{28,4},{1,25},{... | collective-permute-start | bytes 442376 | tf_op jit(solution)/shard_map/ppermute | solution.py:627
  136.7 9.2 %collective-permute-start.28 = (bf16[192,384]{1,0:T(8,128)(2,1)S(1)}, bf16[192,384]{1,0:T(8,128)(2,1)S(1)}, u32[]{:S(2)}, u32[]{:S(2)}) collective-permute-start(bf16[192,384]{1,0:T(8,128)(2,1)S(1)} %add_convert_fusion.5), channel_id=1, source_target_pairs={{0,16},{4,20},{8,24},{12,28},{16,0},{20,4},{24,8},{28,12},{1,17},{... | collective-permute-start | bytes 442376 | tf_op jit(solution)/shard_map/ppermute | solution.py:627
  137.1 8.8 %collective-permute-start.27 = (bf16[192,384]{1,0:T(8,128)(2,1)S(1)}, bf16[192,384]{1,0:T(8,128)(2,1)S(1)}, u32[]{:S(2)}, u32[]{:S(2)}) collective-permute-start(bf16[192,384]{1,0:T(8,128)(2,1)S(1)} %add_convert_fusion.5), channel_id=1, source_target_pairs={{0,8},{4,12},{8,0},{12,4},{16,24},{20,28},{24,16},{28,20},{1,9},{5... | collective-permute-start | bytes 442376 | tf_op jit(solution)/shard_map/ppermute | solution.py:627

commit v6 on v5

--- a/solution.py
+++ b/solution.py
@@ -377,7 +377,7 @@
         gv_sum,
     ) = rest[groups:]
     head = pl.program_id(0)
-    heads = keep_ref.shape[0] * 2 // row_parts
+    heads = keep_ref.shape[1] * 2 // row_parts
     group_own = group_ref[0]
     cols, width = acts_refs[0].shape
     tokens = groups * cols
@@ -481,7 +481,8 @@
                         [score[:, start : start + rest_lanes] for score in scores], axis=1
                     )
                 )
-            dbias_ref[unit] = jnp.stack(blocks).reshape(dbias_ref.shape[1:])
+            for column in range(groups):
+                dbias_ref[column, unit] = jnp.stack(blocks[3 * column : 3 * column + 3])
 
     @pl.when(head < heads // 2)
     def _():
@@ -520,7 +521,7 @@
     _, heads, _, half, lanes = bias[0].shape
     row_block = tokens
     padded = (part // 128 + 1) * 128
-    units = (row_parts // 2 * heads, groups, 3, half, lanes)
+    units = (groups, row_parts // 2 * heads, 3, half, lanes)
     *grads, keep, give = pl.pallas_call(
         functools.partial(
             attention_kernel,
@@ -619,7 +620,7 @@
     for bits in order:
         perm = [(index, index ^ bits) for index in range(groups)]
         got.append(lax.ppermute(sends[bits], "grp", perm))
-    got = dict(zip(order, got))
+    got = dict(zip(order, lax.optimization_barrier(got)))
     return [sends[0]] + [got[bits] for bits in range(1, groups)]
 
 
@@ -633,52 +634,40 @@
     far = flip_rows(own, 4, row_total)
     first = flip_rows(near[:half], 4, row_total)
     second = flip_rows(far[half:], 2, row_total)
-    first, second, acts = lax.optimization_barrier((first, second, acts))
+    acts[2], acts[3], acts[1], first, second = lax.optimization_barrier(
+        (acts[2], acts[3], acts[1], first, second)
+    )
     blocks = []
     for block in (own, near, far, first, second):
         blocks += [block, flip_rows(block, 1, row_total)]
     return blocks, acts
 
 
-def add_last_kernel(own_ref, far_ref, near_ref, *out_refs):
-    heads = own_ref.shape[0]
-    half = heads // 2
-    for head in range(heads):
-        other = far_ref[head] if head < half else near_ref[head - half]
-        total = (own_ref[head].astype(F32) + other.astype(F32)).astype(BF16)
-        for slot, out_ref in enumerate(out_refs):
-            out_ref[head] = total[slot]
-
-
 def scatter_rows(keep, give, row_total):
     got = flip_rows(give, 1, row_total)
-    early = keep.shape[0] // 2
+    early = keep.shape[1] // 2
     heads = early // 2
     part = heads // 2
 
     def add(first, count, *others):
-        total = keep[first : first + count].astype(F32) + got[first : first + count].astype(F32)
+        total = keep[:, first : first + count].astype(F32)
+        total += got[:, first : first + count].astype(F32)
         for other in others:
             total += other.astype(F32)
         return total.astype(BF16)
 
     near = flip_rows(add(0, heads), 2, row_total)
     far = flip_rows(add(heads, heads), 4, row_total)
-    far_two = flip_rows(add(early + heads, part, near[part:]), 4, row_total)
-    near_two = flip_rows(add(early + heads + part, part, far[part:]), 2, row_total)
-    own = add(early, heads, jnp.concatenate([near[:part], far[:part]]))
+    far_two = flip_rows(add(early + heads, part, near[:, part:]), 4, row_total)
+    near_two = flip_rows(add(early + heads + part, part, far[:, part:]), 2, row_total)
+    own = add(early, heads, jnp.concatenate([near[:, :part], far[:, :part]], axis=1))
     return own, far_two, near_two
 
 
 def add_last(own, far_two, near_two):
-    heads, groups = own.shape[:2]
-    return pl.pallas_call(
-        add_last_kernel,
-        in_specs=[vmem()] * 3,
-        out_specs=[vmem()] * groups,
-        out_shape=[jax.ShapeDtypeStruct((heads,) + own.shape[2:], BF16)] * groups,
-        compiler_params=params(),
-    )(own, far_two, near_two)
+    last = jnp.concatenate([far_two, near_two], axis=1)
+    total = (own.astype(F32) + last.astype(F32)).astype(BF16)
+    return [total[slot] for slot in range(total.shape[0])]
 
 
 def sum_cores(mine, row_total):

time: 147 us -> 143 us (0.973)
  waiting for transfers between devices: 53.2 us -> 49.3 us
  starting transfers between devices: 36.9 us -> 39.6 us
  Pallas kernels: 48.9 us -> 46.8 us
    ppermute x18, waiting for transfers between devices: 24.2 us -> 21.7 us  [flip_rows(): lax.ppermute(values, 'rows', [(index, index ^ bits) for index in range(ro...]
    ppermute x12, starting transfers between devices: 23.9 us -> 26.3 us  [swap_groups(): got.append(lax.ppermute(sends[bits], 'grp', perm))]
    pallas_call x1 -> x0, Pallas kernels: 2.13 us -> none  [add_last(): pl.pallas_call(add_last_kernel, in_specs=[vmem()] * 3, out_specs=[vmem()]...]
    convert_element_type x3 -> x2, other arithmetic: 3 us -> 1.96 us  [add(): return total.astype(BF16)]
  transfers between devices with their start and end apart: 30 -> 30, of which waited for: 14 -> 18; matrix products, arithmetic and copies ran while one was open for 1% -> 0% of each run, Pallas kernels for 15% -> 15%
where the time goes in v6:
time: 143 us
  waiting for transfers between devices  49.3 us (34%)
  Pallas kernels  46.8 us (33%)
  starting transfers between devices  39.6 us (28%)
  other arithmetic  4.09 us (3%)
  local copies, waits for them, and re-layouts  2.1 us (1%)
    ppermute x12, waiting for transfers between devices, swap_groups(): got.append(lax.ppermute(sends[bits], 'grp', perm))  27.6 us
    ppermute x12, starting transfers between devices, swap_groups(): got.append(lax.ppermute(sends[bits], 'grp', perm))  26.3 us
    ppermute x18, waiting for transfers between devices, flip_rows(): lax.ppermute(values, 'rows', [(index, index ^ bits) for index in range(ro...  21.7 us
    pallas_call x1, Pallas kernels, attention(): pl.pallas_call(functools.partial(attention_kernel, groups=groups, row_par...  16.3 us
    ppermute x18, starting transfers between devices, flip_rows(): lax.ppermute(values, 'rows', [(index, index ^ bits) for index in range(ro...  13.4 us
    pallas_call x1, Pallas kernels, pair_bias(): pl.pallas_call(functools.partial(bias_kernel, groups=groups, batch=4), gr...  8.47 us
    pallas_call x1, Pallas kernels, pair_back(): pl.pallas_call(functools.partial(pair_back_kernel, groups=groups, calls=l...  8.18 us
    pallas_call x1, Pallas kernels, split_heads(): pl.pallas_call(functools.partial(finish_kernel, groups=groups, calls=call...  7.47 us
  transfers between devices with their start and end apart: 30, of which 18 were waited for; matrix products, arithmetic and copies ran while one was open for 0% of the time, Pallas kernels for 15%

profile of v6, /device:TPU:0, one launch (start us, length us, event | category | flops | bytes accessed | tf_op | source)
XLA Modules:
  0.0 142.8 jit_solution(16644974513179144189)
XLA Ops:
  0.6 8.5 %shard_map.158 = (bf16[4,3,48,128]{3,2,1,0:T(8,128)(2,1)}, bf16[4,3,48,128]{3,2,1,0:T(8,128)(2,1)}, bf16[4,3,48,128]{3,2,1,0:T(8,128)(2,1)}, bf16[4,3,48,128]{3,2,1,0:T(8,128)(2,1)}, f32[2,48,24,192]{3,2,1,0:T(8,128)}) custom-call(s32[1]{0:T(128)} %bitcast.group_ref, s32[1]{0:T(128)} %bitcast.3.rows_ref.row_ref, s32[768]{0:T(1024)} %cols_ref.1, f32[16]{0:T(128)} %gain_ref.1, ...), custom_call_target="tpu_custom_call" | custom-call | tf_op jit(solution)/shard_map/pallas_call | solution.py:217
  9.1 4.0 %collective-permute-start = (bf16[4,3,48,128]{3,2,1,0:T(8,128)(2,1)}, bf16[4,3,48,128]{3,2,1,0:T(8,128)(2,1)S(1)}, u32[]{:S(2)}, u32[]{:S(2)}) collective-permute-start(bf16[4,3,48,128]{3,2,1,0:T(8,128)(2,1)} %get-tuple-element.65), channel_id=1, source_target_pairs={{0,2},{1,3},{2,0},{3,1},{4,6},{5,7},{6,4},{7,5},{8,10},{9,11},{10,... | collective-permute-start | bytes 442376 | tf_op jit(solution)/shard_map/ppermute | solution.py:622
  13.1 1.3 collective-permute-start.1
  14.5 0.2 collective-permute-start.2
  14.7 6.4 %shard_map.157 = (bf16[192,768]{1,0:T(8,128)(2,1)}, bf16[192,768]{1,0:T(8,128)(2,1)}, bf16[192,768]{1,0:T(8,128)(2,1)}, bf16[192,768]{1,0:T(8,128)(2,1)}, f32[192,768]{1,0:T(8,128)}, /*index=5*/f32[192,768]{1,0:T(8,128)}) custom-call(s32[1]{0:T(128)} %bitcast.group_ref, bf16[192,384]{1,0:T(8,128)(2,1)} %single_ref.3, bf16[192,768]{1,0:T(8,128)(2,1)} %bitcast.23, ...), custom_call_target="tpu_custom_call" | custom-call | tf_op jit(solution)/shard_map/pallas_call | solution.py:714
  21.1 0.0 copy-start.25
  21.1 3.3 %collective-permute-done = bf16[4,3,48,128]{3,2,1,0:T(8,128)(2,1)S(1)} collective-permute-done((bf16[4,3,48,128]{3,2,1,0:T(8,128)(2,1)}, bf16[4,3,48,128]{3,2,1,0:T(8,128)(2,1)S(1)}, u32[]{:S(2)}, u32[]{:S(2)}) %collective-permute-start) | collective-permute-done | bytes 147488 | tf_op jit(solution)/shard_map/ppermute | solution.py:622
  24.4 0.5 collective-permute-done.2
  24.9 0.1 pad_maximum_fusion.rest_0_
  25.0 1.6 %collective-permute-start.6 = (bf16[4,4,3,48,128]{4,3,2,1,0:T(8,128)(2,1)S(1)}, bf16[4,4,3,48,128]{4,3,2,1,0:T(8,128)(2,1)S(1)}, u32[]{:S(2)}, u32[]{:S(2)}) collective-permute-start(bf16[4,4,3,48,128]{4,3,2,1,0:T(8,128)(2,1)S(1)} %pad_maximum_fusion.rest_0_), channel_id=1, source_target_pairs={{0,16},{4,20},{8,24},{12,28},{16,0},{20,4},{24,8},{28,12},{1,17},{... | collective-permute-start | bytes 1769480 | tf_op jit(solution)/shard_map/ppermute | solution.py:628
  26.6 1.5 %collective-permute-start.4 = (bf16[4,4,3,48,128]{4,3,2,1,0:T(8,128)(2,1)S(1)}, bf16[4,4,3,48,128]{4,3,2,1,0:T(8,128)(2,1)S(1)}, u32[]{:S(2)}, u32[]{:S(2)}) collective-permute-start(bf16[4,4,3,48,128]{4,3,2,1,0:T(8,128)(2,1)S(1)} %pad_maximum_fusion.rest_0_), channel_id=1, source_target_pairs={{0,8},{4,12},{8,0},{12,4},{16,24},{20,28},{24,16},{28,20},{1,9},{5... | collective-permute-start | bytes 1769480 | tf_op jit(solution)/shard_map/ppermute | solution.py:628
  28.1 2.6 %collective-permute-start.10 = (bf16[192,768]{1,0:T(8,128)(2,1)S(1)}, bf16[192,768]{1,0:T(8,128)(2,1)S(1)}, u32[]{:S(2)}, u32[]{:S(2)}) collective-permute-start(bf16[192,768]{1,0:T(8,128)(2,1)S(1)} %copy-done.26), channel_id=1, source_target_pairs={{0,1},{1,0},{2,3},{3,2},{4,5},{5,4},{6,7},{7,6},{8,9},{9,8},{10,11... | collective-permute-start | bytes 884744 | tf_op jit(solution)/shard_map/ppermute | solution.py:622
  30.7 1.9 %collective-permute-start.8 = (bf16[192,768]{1,0:T(8,128)(2,1)S(1)}, bf16[192,768]{1,0:T(8,128)(2,1)S(1)}, u32[]{:S(2)}, u32[]{:S(2)}) collective-permute-start(bf16[192,768]{1,0:T(8,128)(2,1)S(1)} %copy-done.25), channel_id=1, source_target_pairs={{0,2},{1,3},{2,0},{3,1},{4,6},{5,7},{6,4},{7,5},{8,10},{9,11},{10,... | collective-permute-start | bytes 884744 | tf_op jit(solution)/shard_map/ppermute | solution.py:622
  32.6 1.5 %collective-permute-start.9 = (bf16[192,768]{1,0:T(8,128)(2,1)S(1)}, bf16[192,768]{1,0:T(8,128)(2,1)S(1)}, u32[]{:S(2)}, u32[]{:S(2)}) collective-permute-start(bf16[192,768]{1,0:T(8,128)(2,1)S(1)} %copy-done.23), channel_id=1, source_target_pairs={{0,3},{1,2},{2,1},{3,0},{4,7},{5,6},{6,5},{7,4},{8,11},{9,10},{10,... | collective-permute-start | bytes 884744 | tf_op jit(solution)/shard_map/ppermute | solution.py:622
  34.1 4.2 %collective-permute-done.6.rest_4_ = bf16[4,4,3,48,128]{4,3,2,1,0:T(8,128)(2,1)S(1)} collective-permute-done((bf16[4,4,3,48,128]{4,3,2,1,0:T(8,128)(2,1)S(1)}, bf16[4,4,3,48,128]{4,3,2,1,0:T(8,128)(2,1)S(1)}, u32[]{:S(2)}, u32[]{:S(2)}) %collective-permute-start.6) | collective-permute-done | bytes 589856 | tf_op jit(solution)/shard_map/ppermute | solution.py:628
  38.3 1.3 collective-permute-start.12
  39.6 0.9 collective-permute-done.4.rest_2_
  40.5 0.9 collective-permute-start.11
  41.4 1.7 %collective-permute-done.10.rest_11_ = bf16[192,768]{1,0:T(8,128)(2,1)S(1)} collective-permute-done((bf16[192,768]{1,0:T(8,128)(2,1)S(1)}, bf16[192,768]{1,0:T(8,128)(2,1)S(1)}, u32[]{:S(2)}, u32[]{:S(2)}) %collective-permute-start.10) | collective-permute-done | bytes 294944 | tf_op jit(solution)/shard_map/ppermute | solution.py:622
  43.1 11.1 %collective-permute-done.8.rest_12_ = bf16[192,768]{1,0:T(8,128)(2,1)S(1)} collective-permute-done((bf16[192,768]{1,0:T(8,128)(2,1)S(1)}, bf16[192,768]{1,0:T(8,128)(2,1)S(1)}, u32[]{:S(2)}, u32[]{:S(2)}) %collective-permute-start.8) | collective-permute-done | bytes 294944 | tf_op jit(solution)/shard_map/ppermute | solution.py:622
  54.2 0.0 collective-permute-start.7
  54.2 0.0 collective-permute-done.9.rest_13_
  54.2 0.5 collective-permute-start.5
  54.7 0.0 collective-permute-done.12.rest_8_
  54.7 0.0 copy-start.14
  54.7 0.1 collective-permute-start.13
  54.9 0.4 collective-permute-start.14
  55.3 0.9 collective-permute-done.7.rest_5_
  56.2 0.8 collective-permute-done.5.rest_3_
  57.1 0.4 collective-permute-done.13.rest_7_
  57.5 0.4 collective-permute-done.14.rest_9_
  58.0 0.2 copy-done.15
  58.2 0.7 copy-done.16
  58.9 16.3 %shard_map.159 = (bf16[192,768]{1,0:T(8,128)(2,1)}, bf16[192,768]{1,0:T(8,128)(2,1)}, bf16[192,768]{1,0:T(8,128)(2,1)}, bf16[192,768]{1,0:T(8,128)(2,1)}, bf16[4...) custom-call(s32[1]{0:T(128)} %bitcast.group_ref, s32[1]{0:T(128)} %bitcast.3.rows_ref.row_ref, ...), custom_call_target="tpu_custom_call" | custom-call | tf_op jit(solution)/shard_map/pallas_call | solution.py:525
  75.2 0.2 collective-permute-start.15
  75.4 4.6 %collective-permute-done.15 = bf16[4,16,3,48,128]{4,3,2,1,0:T(8,128)(2,1)S(1)} collective-permute-done((bf16[4,16,3,48,128]{4,3,2,1,0:T(8,128)(2,1)}, bf16[4,16,3,48,128]{4,3,2,1,0:T(8,128)(2,1)S(1)}, u32[]{:S(2)}, u32[]{:S(2)}) %collective-permute-start.15) | collective-permute-done | bytes 2359328 | tf_op jit(solution)/shard_map/ppermute | solution.py:628
  80.1 1.7 %add_convert_fusion.3 = (bf16[4,4,3,48,128]{4,3,2,1,0:T(8,128)(2,1)S(1)}, bf16[4,4,3,48,128]{4,3,2,1,0:T(8,128)(2,1)S(1)}) fusion(bf16[4,16,3,48,128]{4,3,2,1,0:T(8,128)(2,1)S(1)} %collective-permute-done.15, bf16[4,16,3,48,128]{4,3,2,1,0:T(8,128)(2,1)} %get-tuple-element.87), kind=kLoop, calls=%fused_computation.3 | loop fusion | flops 2359296 | bytes 3538944 | tf_op jit(solution)/shard_map/convert_element_type | solution.py:657
  81.8 0.6 collective-permute-start.16
  82.4 0.5 collective-permute-start.17
  82.9 6.0 %collective-permute-start.20 = (bf16[192,768]{1,0:T(8,128)(2,1)S(1)}, bf16[192,768]{1,0:T(8,128)(2,1)S(1)}, u32[]{:S(2)}, u32[]{:S(2)}) collective-permute-start(bf16[192,768]{1,0:T(8,128)(2,1)S(1)} %copy-done.24), channel_id=1, source_target_pairs={{0,2},{1,3},{2,0},{3,1},{4,6},{5,7},{6,4},{7,5},{8,10},{9,11},{10,... | collective-permute-start | bytes 884744 | tf_op jit(solution)/shard_map/ppermute | solution.py:622
  89.0 0.6 collective-permute-start.21
  89.5 0.1 collective-permute-start.22
  89.6 7.6 %collective-permute-done.16 = bf16[4,4,3,48,128]{4,3,2,1,0:T(8,128)(2,1)S(1)} collective-permute-done((bf16[4,4,3,48,128]{4,3,2,1,0:T(8,128)(2,1)S(1)}, bf16[4,4,3,48,128]{4,3,2,1,0:T(8,128)(2,1)S(1)}, u32[]{:S(2)}, u32[]{:S(2)}) %collective-permute-start.16) | collective-permute-done | bytes 589856 | tf_op jit(solution)/shard_map/ppermute | solution.py:628
  97.2 0.3 collective-permute-done.17
  97.5 0.2 add_convert_fusion.4
  97.7 1.5 %collective-permute-start.19 = (bf16[4,2,3,48,128]{4,3,2,1,0:T(8,128)(2,1)S(1)}, bf16[4,2,3,48,128]{4,3,2,1,0:T(8,128)(2,1)S(1)}, u32[]{:S(2)}, u32[]{:S(2)}) collective-permute-start(bf16[4,2,3,48,128]{4,3,2,1,0:T(8,128)(2,1)S(1)} %get-tuple-element.121), channel_id=1, source_target_pairs={{0,8},{4,12},{8,0},{12,4},{16,24},{20,28},{24,16},{28,20},{1,9},{5... | collective-permute-start | bytes 884744 | tf_op jit(solution)/shard_map/ppermute | solution.py:628
  99.3 0.5 collective-permute-start.18
  99.8 9.0 %collective-permute-done.20.rest_2_ = bf16[192,768]{1,0:T(8,128)(2,1)S(1)} collective-permute-done((bf16[192,768]{1,0:T(8,128)(2,1)S(1)}, bf16[192,768]{1,0:T(8,128)(2,1)S(1)}, u32[]{:S(2)}, u32[]{:S(2)}) %collective-permute-start.20) | collective-permute-done | bytes 294944 | tf_op jit(solution)/shard_map/ppermute | solution.py:622
  108.8 0.9 collective-permute-done.22.rest_1_
  109.8 0.3 add_convert_fusion
  110.1 0.3 copy-done.12
  110.4 0.7 slice_bitcast_fusion
  111.1 4.7 %collective-permute-start.23 = (bf16[4,3,48,128]{3,2,1,0:T(8,128)(2,1)S(1)}, bf16[4,3,48,128]{3,2,1,0:T(8,128)(2,1)S(1)}, u32[]{:S(2)}, u32[]{:S(2)}) collective-permute-start(bf16[4,3,48,128]{3,2,1,0:T(8,128)(2,1)S(1)} %get-tuple-element.109), channel_id=1, source_target_pairs={{0,2},{1,3},{2,0},{3,1},{4,6},{5,7},{6,4},{7,5},{8,10},{9,11},{10,... | collective-permute-start | bytes 442376 | tf_op jit(solution)/shard_map/ppermute | solution.py:622
  115.9 3.3 %collective-permute-start.24 = (bf16[4,3,48,128]{3,2,1,0:T(8,128)(2,1)S(1)}, bf16[4,3,48,128]{3,2,1,0:T(8,128)(2,1)S(1)}, u32[]{:S(2)}, u32[]{:S(2)}) collective-permute-start(bf16[4,3,48,128]{3,2,1,0:T(8,128)(2,1)S(1)} %get-tuple-element.110), channel_id=1, source_target_pairs={{0,3},{1,2},{2,1},{3,0},{4,7},{5,6},{6,5},{7,4},{8,11},{9,10},{10,... | collective-permute-start | bytes 442376 | tf_op jit(solution)/shard_map/ppermute | solution.py:622
  119.2 7.5 %shard_map.160 = (bf16[192,768]{1,0:T(8,128)(2,1)}, bf16[192,384]{1,0:T(8,128)(2,1)}) custom-call(s32[1]{0:T(128)} %bitcast.group_ref, bf16[192,384]{1,0:T(8,128)(2,1)} %single_ref.3, bf16[192,768]{1,0:T(8,128)(2,1)} %bitcast.24, bf16[192,768]{1,0:T(8,128)(2,1)} %bitcast.26, f32[192,768]{1,0:T(8,128)} %get-tuple-element.62.gamma_ref, ...), custom_call_target="tpu_custom_call" | custom-call | tf_op jit(solution)/shard_map/pallas_call | solution.py:750
  126.6 0.4 collective-permute-done.24.rest_3_
  127.0 0.6 collective-permute-done.25.rest_1_
  127.7 1.6 %collective-permute-done.26 = bf16[192,384]{1,0:T(8,128)(2,1)S(1)} collective-permute-done((bf16[192,384]{1,0:T(8,128)(2,1)}, bf16[192,384]{1,0:T(8,128)(2,1)S(1)}, u32[]{:S(2)}, u32[]{:S(2)}) %collective-permute-start.26) | collective-permute-done | bytes 147488 | tf_op jit(solution)/shard_map/ppermute | solution.py:628
  129.3 1.0 add_convert_fusion.6
  130.2 2.5 %collective-permute-start.29 = (bf16[192,384]{1,0:T(8,128)(2,1)S(1)}, bf16[192,384]{1,0:T(8,128)(2,1)S(1)}, u32[]{:S(2)}, u32[]{:S(2)}) collective-permute-start(bf16[192,384]{1,0:T(8,128)(2,1)S(1)} %add_convert_fusion.6), channel_id=1, source_target_pairs={{0,24},{4,28},{8,16},{12,20},{16,8},{20,12},{24,0},{28,4},{1,25},{... | collective-permute-start | bytes 442376 | tf_op jit(solution)/shard_map/ppermute | solution.py:628
  132.7 0.5 collective-permute-start.28
  133.2 0.6 collective-permute-start.27
  133.8 8.2 %shard_map.161 = bf16[2,48,192,128]{3,2,1,0:T(8,128)(2,1)} custom-call(s32[1]{0:T(128)} %bitcast.group_ref, bf16[2,48,192,128]{3,2,1,0:T(8,128)(2,1)} %bitcast.21, f32[2,48,24,192]{3,2,1,0:T(8,128)} %get-tuple-element.116.stats_ref, bf16[16,128]{1,0:T(8,128)(2,1)} %bitcast.32, bf16[4,3,48,128]{3,2,1,0:T(8,128)(2,1)} %get-tuple-element.117.rest_0_, ...), custom_call_target="tpu_custom_call" | custom-call | tf_op jit(solution)/shard_map/pallas_call | solution.py:328
  142.0 0.8 add_add_fusion
  (66 shorter events, 0.2 us)
Async XLA Ops:
  9.1 15.3 %collective-permute-start = (bf16[4,3,48,128]{3,2,1,0:T(8,128)(2,1)}, bf16[4,3,48,128]{3,2,1,0:T(8,128)(2,1)S(1)}, u32[]{:S(2)}, u32[]{:S(2)}) collective-permute-start(bf16[4,3,48,128]{3,2,1,0:T(8,128)(2,1)} %get-tuple-element.65), channel_id=1, source_target_pairs={{0,2},{1,3},{2,0},{3,1},{4,6},{5,7},{6,4},{7,5},{8,10},{9,11},{10,... | collective-permute-start | bytes 442376 | tf_op jit(solution)/shard_map/ppermute | solution.py:622
  13.1 11.3 %collective-permute-start.1 = (bf16[4,3,48,128]{3,2,1,0:T(8,128)(2,1)}, bf16[4,3,48,128]{3,2,1,0:T(8,128)(2,1)S(1)}, u32[]{:S(2)}, u32[]{:S(2)}) collective-permute-start(bf16[4,3,48,128]{3,2,1,0:T(8,128)(2,1)} %get-tuple-element.66), channel_id=1, source_target_pairs={{0,3},{1,2},{2,1},{3,0},{4,7},{5,6},{6,5},{7,4},{8,11},{9,10},{10,... | collective-permute-start | bytes 442376 | tf_op jit(solution)/shard_map/ppermute | solution.py:622
  14.5 10.4 %collective-permute-start.2 = (bf16[4,3,48,128]{3,2,1,0:T(8,128)(2,1)}, bf16[4,3,48,128]{3,2,1,0:T(8,128)(2,1)S(1)}, u32[]{:S(2)}, u32[]{:S(2)}) collective-permute-start(bf16[4,3,48,128]{3,2,1,0:T(8,128)(2,1)} %get-tuple-element.67), channel_id=1, source_target_pairs={{0,1},{1,0},{2,3},{3,2},{4,5},{5,4},{6,7},{7,6},{8,9},{9,8},{10,11... | collective-permute-start | bytes 442376 | tf_op jit(solution)/shard_map/ppermute | solution.py:622
  14.7 10.2 %copy-start.17 = (bf16[4,3,48,128]{3,2,1,0:T(8,128)(2,1)S(1)}, bf16[4,3,48,128]{3,2,1,0:T(8,128)(2,1)}, u32[]{:S(2)}) copy-start(bf16[4,3,48,128]{3,2,1,0:T(8,128)(2,1)} %get-tuple-element.75) | copy-start | bytes 442372
  21.1 7.0 %copy-start.26 = (bf16[192,768]{1,0:T(8,128)(2,1)S(1)}, bf16[192,768]{1,0:T(8,128)(2,1)}, u32[]{:S(2)}) copy-start(bf16[192,768]{1,0:T(8,128)(2,1)} %get-tuple-element.72) | copy-start | bytes 884740
  21.1 9.6 %copy-start.25 = (bf16[192,768]{1,0:T(8,128)(2,1)S(1)}, bf16[192,768]{1,0:T(8,128)(2,1)}, u32[]{:S(2)}) copy-start(bf16[192,768]{1,0:T(8,128)(2,1)} %get-tuple-element.73) | copy-start | bytes 884740
  21.1 11.5 %copy-start.23 = (bf16[192,768]{1,0:T(8,128)(2,1)S(1)}, bf16[192,768]{1,0:T(8,128)(2,1)}, u32[]{:S(2)}) copy-start(bf16[192,768]{1,0:T(8,128)(2,1)} %get-tuple-element.74) | copy-start | bytes 884740
  25.0 32.9 %copy-start = (bf16[4,4,3,48,128]{4,3,2,1,0:T(8,128)(2,1)}, bf16[4,4,3,48,128]{4,3,2,1,0:T(8,128)(2,1)S(1)}, u32[]{:S(2)}) copy-start(bf16[4,4,3,48,128]{4,3,2,1,0:T(8,128)(2,1)S(1)} %pad_maximum_fusion.rest_0_) | copy-start | bytes 1769476
  25.0 13.3 %collective-permute-start.6 = (bf16[4,4,3,48,128]{4,3,2,1,0:T(8,128)(2,1)S(1)}, bf16[4,4,3,48,128]{4,3,2,1,0:T(8,128)(2,1)S(1)}, u32[]{:S(2)}, u32[]{:S(2)}) collective-permute-start(bf16[4,4,3,48,128]{4,3,2,1,0:T(8,128)(2,1)S(1)} %pad_maximum_fusion.rest_0_), channel_id=1, source_target_pairs={{0,16},{4,20},{8,24},{12,28},{16,0},{20,4},{24,8},{28,12},{1,17},{... | collective-permute-start | bytes 1769480 | tf_op jit(solution)/shard_map/ppermute | solution.py:628
  26.6 13.8 %collective-permute-start.4 = (bf16[4,4,3,48,128]{4,3,2,1,0:T(8,128)(2,1)S(1)}, bf16[4,4,3,48,128]{4,3,2,1,0:T(8,128)(2,1)S(1)}, u32[]{:S(2)}, u32[]{:S(2)}) collective-permute-start(bf16[4,4,3,48,128]{4,3,2,1,0:T(8,128)(2,1)S(1)} %pad_maximum_fusion.rest_0_), channel_id=1, source_target_pairs={{0,8},{4,12},{8,0},{12,4},{16,24},{20,28},{24,16},{28,20},{1,9},{5... | collective-permute-start | bytes 1769480 | tf_op jit(solution)/shard_map/ppermute | solution.py:628
  28.1 15.0 %collective-permute-start.10 = (bf16[192,768]{1,0:T(8,128)(2,1)S(1)}, bf16[192,768]{1,0:T(8,128)(2,1)S(1)}, u32[]{:S(2)}, u32[]{:S(2)}) collective-permute-start(bf16[192,768]{1,0:T(8,128)(2,1)S(1)} %copy-done.26), channel_id=1, source_target_pairs={{0,1},{1,0},{2,3},{3,2},{4,5},{5,4},{6,7},{7,6},{8,9},{9,8},{10,11... | collective-permute-start | bytes 884744 | tf_op jit(solution)/shard_map/ppermute | solution.py:622
  30.7 23.5 %collective-permute-start.8 = (bf16[192,768]{1,0:T(8,128)(2,1)S(1)}, bf16[192,768]{1,0:T(8,128)(2,1)S(1)}, u32[]{:S(2)}, u32[]{:S(2)}) collective-permute-start(bf16[192,768]{1,0:T(8,128)(2,1)S(1)} %copy-done.25), channel_id=1, source_target_pairs={{0,2},{1,3},{2,0},{3,1},{4,6},{5,7},{6,4},{7,5},{8,10},{9,11},{10,... | collective-permute-start | bytes 884744 | tf_op jit(solution)/shard_map/ppermute | solution.py:622
  32.6 21.6 %collective-permute-start.9 = (bf16[192,768]{1,0:T(8,128)(2,1)S(1)}, bf16[192,768]{1,0:T(8,128)(2,1)S(1)}, u32[]{:S(2)}, u32[]{:S(2)}) collective-permute-start(bf16[192,768]{1,0:T(8,128)(2,1)S(1)} %copy-done.23), channel_id=1, source_target_pairs={{0,3},{1,2},{2,1},{3,0},{4,7},{5,6},{6,5},{7,4},{8,11},{9,10},{10,... | collective-permute-start | bytes 884744 | tf_op jit(solution)/shard_map/ppermute | solution.py:622
  38.2 19.7 %copy-start.2 = (bf16[4,4,3,48,128]{4,3,2,1,0:T(8,128)(2,1)}, bf16[4,4,3,48,128]{4,3,2,1,0:T(8,128)(2,1)S(1)}, u32[]{:S(2)}) copy-start(bf16[4,4,3,48,128]{4,3,2,1,0:T(8,128)(2,1)S(1)} %collective-permute-done.6.rest_4_) | copy-start | bytes 1769476
  38.3 16.5 %collective-permute-start.12 = (bf16[2,4,3,48,128]{4,3,2,1,0:T(8,128)(2,1)S(1)}, bf16[2,4,3,48,128]{4,3,2,1,0:T(8,128)(2,1)S(1)}, u32[]{:S(2)}, u32[]{:S(2)}) collective-permute-start(bf16[2,4,3,48,128]{4,3,2,1,0:T(8,128)(2,1)S(1)} %slice.81), channel_id=1, source_target_pairs={{0,8},{4,12},{8,0},{12,4},{16,24},{20,28},{24,16},{28,20},{1,9},{5... | collective-permute-start | bytes 884744 | tf_op jit(solution)/shard_map/ppermute | solution.py:628
  40.4 17.5 %copy-start.3 = (bf16[4,4,3,48,128]{4,3,2,1,0:T(8,128)(2,1)}, bf16[4,4,3,48,128]{4,3,2,1,0:T(8,128)(2,1)S(1)}, u32[]{:S(2)}) copy-start(bf16[4,4,3,48,128]{4,3,2,1,0:T(8,128)(2,1)S(1)} %collective-permute-done.4.rest_2_) | copy-start | bytes 1769476
  40.5 14.3 %collective-permute-start.11 = (bf16[2,4,3,48,128]{4,3,2,1,0:T(8,128)(2,1)S(1)}, bf16[2,4,3,48,128]{4,3,2,1,0:T(8,128)(2,1)S(1)}, u32[]{:S(2)}, u32[]{:S(2)}) collective-permute-start(bf16[2,4,3,48,128]{4,3,2,1,0:T(8,128)(2,1)S(1)} %slice.80), channel_id=1, source_target_pairs={{0,16},{4,20},{8,24},{12,28},{16,0},{20,4},{24,8},{28,12},{1,17},{... | collective-permute-start | bytes 884744 | tf_op jit(solution)/shard_map/ppermute | solution.py:628
  43.1 14.8 %copy-start.7 = (bf16[192,768]{1,0:T(8,128)(2,1)}, bf16[192,768]{1,0:T(8,128)(2,1)S(1)}, u32[]{:S(2)}) copy-start(bf16[192,768]{1,0:T(8,128)(2,1)S(1)} %collective-permute-done.10.rest_11_) | copy-start | bytes 884740
  43.1 12.2 %collective-permute-start.3 = (bf16[4,4,3,48,128]{4,3,2,1,0:T(8,128)(2,1)S(1)}, bf16[4,4,3,48,128]{4,3,2,1,0:T(8,128)(2,1)S(1)}, u32[]{:S(2)}, u32[]{:S(2)}) collective-permute-start(bf16[4,4,3,48,128]{4,3,2,1,0:T(8,128)(2,1)S(1)} %pad_maximum_fusion.rest_0_), channel_id=1, source_target_pairs={{0,4},{4,0},{8,12},{12,8},{16,20},{20,16},{24,28},{28,24},{1,5},{5... | collective-permute-start | bytes 1769480 | tf_op jit(solution)/shard_map/ppermute | solution.py:628
  54.2 3.7 %copy-start.8 = (bf16[192,768]{1,0:T(8,128)(2,1)}, bf16[192,768]{1,0:T(8,128)(2,1)S(1)}, u32[]{:S(2)}) copy-start(bf16[192,768]{1,0:T(8,128)(2,1)S(1)} %collective-permute-done.8.rest_12_) | copy-start | bytes 884740
  54.2 2.0 %collective-permute-start.7 = (bf16[4,4,3,48,128]{4,3,2,1,0:T(8,128)(2,1)S(1)}, bf16[4,4,3,48,128]{4,3,2,1,0:T(8,128)(2,1)S(1)}, u32[]{:S(2)}, u32[]{:S(2)}) collective-permute-start(bf16[4,4,3,48,128]{4,3,2,1,0:T(8,128)(2,1)S(1)} %collective-permute-done.6.rest_4_), channel_id=1, source_target_pairs={{0,4},{4,0},{8,12},{12,8},{16,20},{20,16},{24,28},{28,24},{1,5},{5... | collective-permute-start | bytes 1769480 | tf_op jit(solution)/shard_map/ppermute | solution.py:628
  54.2 3.7 %copy-start.10 = (bf16[192,768]{1,0:T(8,128)(2,1)}, bf16[192,768]{1,0:T(8,128)(2,1)S(1)}, u32[]{:S(2)}) copy-start(bf16[192,768]{1,0:T(8,128)(2,1)S(1)} %collective-permute-done.9.rest_13_) | copy-start | bytes 884740
  54.2 2.8 %collective-permute-start.5 = (bf16[4,4,3,48,128]{4,3,2,1,0:T(8,128)(2,1)S(1)}, bf16[4,4,3,48,128]{4,3,2,1,0:T(8,128)(2,1)S(1)}, u32[]{:S(2)}, u32[]{:S(2)}) collective-permute-start(bf16[4,4,3,48,128]{4,3,2,1,0:T(8,128)(2,1)S(1)} %collective-permute-done.4.rest_2_), channel_id=1, source_target_pairs={{0,4},{4,0},{8,12},{12,8},{16,20},{20,16},{24,28},{28,24},{1,5},{5... | collective-permute-start | bytes 1769480 | tf_op jit(solution)/shard_map/ppermute | solution.py:628
  54.7 3.2 %copy-start.13 = (bf16[2,4,3,48,128]{4,3,2,1,0:T(8,128)(2,1)}, bf16[2,4,3,48,128]{4,3,2,1,0:T(8,128)(2,1)S(1)}, u32[]{:S(2)}) copy-start(bf16[2,4,3,48,128]{4,3,2,1,0:T(8,128)(2,1)S(1)} %collective-permute-done.12.rest_8_) | copy-start | bytes 884740
  54.7 3.2 %copy-start.14 = (bf16[2,4,3,48,128]{4,3,2,1,0:T(8,128)(2,1)}, bf16[2,4,3,48,128]{4,3,2,1,0:T(8,128)(2,1)S(1)}, u32[]{:S(2)}) copy-start(bf16[2,4,3,48,128]{4,3,2,1,0:T(8,128)(2,1)S(1)} %collective-permute-done.11.rest_6_) | copy-start | bytes 884740
  54.7 2.7 %collective-permute-start.13 = (bf16[2,4,3,48,128]{4,3,2,1,0:T(8,128)(2,1)S(1)}, bf16[2,4,3,48,128]{4,3,2,1,0:T(8,128)(2,1)S(1)}, u32[]{:S(2)}, u32[]{:S(2)}) collective-permute-start(bf16[2,4,3,48,128]{4,3,2,1,0:T(8,128)(2,1)S(1)} %collective-permute-done.11.rest_6_), channel_id=1, source_target_pairs={{0,4},{4,0},{8,12},{12,8},{16,20},{20,16},{24,28},{28,24},{1,5},{5... | collective-permute-start | bytes 884744 | tf_op jit(solution)/shard_map/ppermute | solution.py:628
  54.9 3.0 %collective-permute-start.14 = (bf16[2,4,3,48,128]{4,3,2,1,0:T(8,128)(2,1)S(1)}, bf16[2,4,3,48,128]{4,3,2,1,0:T(8,128)(2,1)S(1)}, u32[]{:S(2)}, u32[]{:S(2)}) collective-permute-start(bf16[2,4,3,48,128]{4,3,2,1,0:T(8,128)(2,1)S(1)} %collective-permute-done.12.rest_8_), channel_id=1, source_target_pairs={{0,4},{4,0},{8,12},{12,8},{16,20},{20,16},{24,28},{28,24},{1,5},{5... | collective-permute-start | bytes 884744 | tf_op jit(solution)/shard_map/ppermute | solution.py:628
  55.3 2.6 %copy-start.4 = (bf16[4,4,3,48,128]{4,3,2,1,0:T(8,128)(2,1)}, bf16[4,4,3,48,128]{4,3,2,1,0:T(8,128)(2,1)S(1)}, u32[]{:S(2)}) copy-start(bf16[4,4,3,48,128]{4,3,2,1,0:T(8,128)(2,1)S(1)} %collective-permute-done.3.rest_1_) | copy-start | bytes 1769476
  56.2 1.8 %copy-start.5 = (bf16[4,4,3,48,128]{4,3,2,1,0:T(8,128)(2,1)}, bf16[4,4,3,48,128]{4,3,2,1,0:T(8,128)(2,1)S(1)}, u32[]{:S(2)}) copy-start(bf16[4,4,3,48,128]{4,3,2,1,0:T(8,128)(2,1)S(1)} %collective-permute-done.7.rest_5_) | copy-start | bytes 1769476
  57.1 0.9 copy-start.6
  57.5 0.7 copy-start.15
  58.2 0.7 copy-start.16
  75.2 4.8 %collective-permute-start.15 = (bf16[4,16,3,48,128]{4,3,2,1,0:T(8,128)(2,1)}, bf16[4,16,3,48,128]{4,3,2,1,0:T(8,128)(2,1)S(1)}, u32[]{:S(2)}, u32[]{:S(2)}) collective-permute-start(bf16[4,16,3,48,128]{4,3,2,1,0:T(8,128)(2,1)} %get-tuple-element.88), channel_id=1, source_target_pairs={{0,4},{4,0},{8,12},{12,8},{16,20},{20,16},{24,28},{28,24},{1,5},{5... | collective-permute-start | bytes 7077896 | tf_op jit(solution)/shard_map/ppermute | solution.py:628
  80.1 2.9 %copy-start.24 = (bf16[192,768]{1,0:T(8,128)(2,1)S(1)}, bf16[192,768]{1,0:T(8,128)(2,1)}, u32[]{:S(2)}) copy-start(bf16[192,768]{1,0:T(8,128)(2,1)} %get-tuple-element.90) | copy-start | bytes 884740
  80.1 8.9 %copy-start.22 = (bf16[192,768]{1,0:T(8,128)(2,1)S(1)}, bf16[192,768]{1,0:T(8,128)(2,1)}, u32[]{:S(2)}) copy-start(bf16[192,768]{1,0:T(8,128)(2,1)} %get-tuple-element.91) | copy-start | bytes 884740
  80.1 9.5 %copy-start.21 = (bf16[192,768]{1,0:T(8,128)(2,1)S(1)}, bf16[192,768]{1,0:T(8,128)(2,1)}, u32[]{:S(2)}) copy-start(bf16[192,768]{1,0:T(8,128)(2,1)} %get-tuple-element.92) | copy-start | bytes 884740
  80.1 17.4 %copy-start.1 = (bf16[4,16,3,48,128]{4,3,2,1,0:T(8,128)(2,1)S(1)}, bf16[4,16,3,48,128]{4,3,2,1,0:T(8,128)(2,1)}, u32[]{:S(2)}) copy-start(bf16[4,16,3,48,128]{4,3,2,1,0:T(8,128)(2,1)} %get-tuple-element.87) | copy-start | bytes 7077892
  81.8 15.4 %collective-permute-start.16 = (bf16[4,4,3,48,128]{4,3,2,1,0:T(8,128)(2,1)S(1)}, bf16[4,4,3,48,128]{4,3,2,1,0:T(8,128)(2,1)S(1)}, u32[]{:S(2)}, u32[]{:S(2)}) collective-permute-start(bf16[4,4,3,48,128]{4,3,2,1,0:T(8,128)(2,1)S(1)} %get-tuple-element.123), channel_id=1, source_target_pairs={{0,8},{4,12},{8,0},{12,4},{16,24},{20,28},{24,16},{28,20},{1,9},{5... | collective-permute-start | bytes 1769480 | tf_op jit(solution)/shard_map/ppermute | solution.py:628
  82.4 15.1 %collective-permute-start.17 = (bf16[4,4,3,48,128]{4,3,2,1,0:T(8,128)(2,1)S(1)}, bf16[4,4,3,48,128]{4,3,2,1,0:T(8,128)(2,1)S(1)}, u32[]{:S(2)}, u32[]{:S(2)}) collective-permute-start(bf16[4,4,3,48,128]{4,3,2,1,0:T(8,128)(2,1)S(1)} %get-tuple-element.124), channel_id=1, source_target_pairs={{0,16},{4,20},{8,24},{12,28},{16,0},{20,4},{24,8},{28,12},{1,17},{... | collective-permute-start | bytes 1769480 | tf_op jit(solution)/shard_map/ppermute | solution.py:628
  82.9 25.9 %collective-permute-start.20 = (bf16[192,768]{1,0:T(8,128)(2,1)S(1)}, bf16[192,768]{1,0:T(8,128)(2,1)S(1)}, u32[]{:S(2)}, u32[]{:S(2)}) collective-permute-start(bf16[192,768]{1,0:T(8,128)(2,1)S(1)} %copy-done.24), channel_id=1, source_target_pairs={{0,2},{1,3},{2,0},{3,1},{4,6},{5,7},{6,4},{7,5},{8,10},{9,11},{10,... | collective-permute-start | bytes 884744 | tf_op jit(solution)/shard_map/ppermute | solution.py:622
  89.0 19.8 %collective-permute-start.21 = (bf16[192,768]{1,0:T(8,128)(2,1)S(1)}, bf16[192,768]{1,0:T(8,128)(2,1)S(1)}, u32[]{:S(2)}, u32[]{:S(2)}) collective-permute-start(bf16[192,768]{1,0:T(8,128)(2,1)S(1)} %copy-done.22), channel_id=1, source_target_pairs={{0,3},{1,2},{2,1},{3,0},{4,7},{5,6},{6,5},{7,4},{8,11},{9,10},{10,... | collective-permute-start | bytes 884744 | tf_op jit(solution)/shard_map/ppermute | solution.py:622
  89.5 20.2 %collective-permute-start.22 = (bf16[192,768]{1,0:T(8,128)(2,1)S(1)}, bf16[192,768]{1,0:T(8,128)(2,1)S(1)}, u32[]{:S(2)}, u32[]{:S(2)}) collective-permute-start(bf16[192,768]{1,0:T(8,128)(2,1)S(1)} %copy-done.21), channel_id=1, source_target_pairs={{0,1},{1,0},{2,3},{3,2},{4,5},{5,4},{6,7},{7,6},{8,9},{9,8},{10,11... | collective-permute-start | bytes 884744 | tf_op jit(solution)/shard_map/ppermute | solution.py:622
  97.7 12.0 %collective-permute-start.19 = (bf16[4,2,3,48,128]{4,3,2,1,0:T(8,128)(2,1)S(1)}, bf16[4,2,3,48,128]{4,3,2,1,0:T(8,128)(2,1)S(1)}, u32[]{:S(2)}, u32[]{:S(2)}) collective-permute-start(bf16[4,2,3,48,128]{4,3,2,1,0:T(8,128)(2,1)S(1)} %get-tuple-element.121), channel_id=1, source_target_pairs={{0,8},{4,12},{8,0},{12,4},{16,24},{20,28},{24,16},{28,20},{1,9},{5... | collective-permute-start | bytes 884744 | tf_op jit(solution)/shard_map/ppermute | solution.py:628
  99.3 10.5 %collective-permute-start.18 = (bf16[4,2,3,48,128]{4,3,2,1,0:T(8,128)(2,1)S(1)}, bf16[4,2,3,48,128]{4,3,2,1,0:T(8,128)(2,1)S(1)}, u32[]{:S(2)}, u32[]{:S(2)}) collective-permute-start(bf16[4,2,3,48,128]{4,3,2,1,0:T(8,128)(2,1)S(1)} %get-tuple-element.122), channel_id=1, source_target_pairs={{0,16},{4,20},{8,24},{12,28},{16,0},{20,4},{24,8},{28,12},{1,17},{... | collective-permute-start | bytes 884744 | tf_op jit(solution)/shard_map/ppermute | solution.py:628
  108.8 1.3 copy-start.9
  108.8 1.4 copy-start.11
  109.7 0.7 copy-start.12
  111.1 15.5 %collective-permute-start.23 = (bf16[4,3,48,128]{3,2,1,0:T(8,128)(2,1)S(1)}, bf16[4,3,48,128]{3,2,1,0:T(8,128)(2,1)S(1)}, u32[]{:S(2)}, u32[]{:S(2)}) collective-permute-start(bf16[4,3,48,128]{3,2,1,0:T(8,128)(2,1)S(1)} %get-tuple-element.109), channel_id=1, source_target_pairs={{0,2},{1,3},{2,0},{3,1},{4,6},{5,7},{6,4},{7,5},{8,10},{9,11},{10,... | collective-permute-start | bytes 442376 | tf_op jit(solution)/shard_map/ppermute | solution.py:622
  115.9 11.2 %collective-permute-start.24 = (bf16[4,3,48,128]{3,2,1,0:T(8,128)(2,1)S(1)}, bf16[4,3,48,128]{3,2,1,0:T(8,128)(2,1)S(1)}, u32[]{:S(2)}, u32[]{:S(2)}) collective-permute-start(bf16[4,3,48,128]{3,2,1,0:T(8,128)(2,1)S(1)} %get-tuple-element.110), channel_id=1, source_target_pairs={{0,3},{1,2},{2,1},{3,0},{4,7},{5,6},{6,5},{7,4},{8,11},{9,10},{10,... | collective-permute-start | bytes 442376 | tf_op jit(solution)/shard_map/ppermute | solution.py:622
  119.2 8.5 %collective-permute-start.25 = (bf16[4,3,48,128]{3,2,1,0:T(8,128)(2,1)S(1)}, bf16[4,3,48,128]{3,2,1,0:T(8,128)(2,1)S(1)}, u32[]{:S(2)}, u32[]{:S(2)}) collective-permute-start(bf16[4,3,48,128]{3,2,1,0:T(8,128)(2,1)S(1)} %get-tuple-element.111), channel_id=1, source_target_pairs={{0,1},{1,0},{2,3},{3,2},{4,5},{5,4},{6,7},{7,6},{8,9},{9,8},{10,11... | collective-permute-start | bytes 442376 | tf_op jit(solution)/shard_map/ppermute | solution.py:622
  126.6 7.2 %copy-start.18 = (bf16[4,3,48,128]{3,2,1,0:T(8,128)(2,1)}, bf16[4,3,48,128]{3,2,1,0:T(8,128)(2,1)S(1)}, u32[]{:S(2)}) copy-start(bf16[4,3,48,128]{3,2,1,0:T(8,128)(2,1)S(1)} %collective-permute-done.23.rest_2_) | copy-start | bytes 442372
  127.0 6.8 %copy-start.19 = (bf16[4,3,48,128]{3,2,1,0:T(8,128)(2,1)}, bf16[4,3,48,128]{3,2,1,0:T(8,128)(2,1)S(1)}, u32[]{:S(2)}) copy-start(bf16[4,3,48,128]{3,2,1,0:T(8,128)(2,1)S(1)} %collective-permute-done.24.rest_3_) | copy-start | bytes 442372
  127.7 6.1 %copy-start.20 = (bf16[4,3,48,128]{3,2,1,0:T(8,128)(2,1)}, bf16[4,3,48,128]{3,2,1,0:T(8,128)(2,1)S(1)}, u32[]{:S(2)}) copy-start(bf16[4,3,48,128]{3,2,1,0:T(8,128)(2,1)S(1)} %collective-permute-done.25.rest_1_) | copy-start | bytes 442372
  127.7 1.6 %collective-permute-start.26 = (bf16[192,384]{1,0:T(8,128)(2,1)}, bf16[192,384]{1,0:T(8,128)(2,1)S(1)}, u32[]{:S(2)}, u32[]{:S(2)}) collective-permute-start(bf16[192,384]{1,0:T(8,128)(2,1)} %get-tuple-element.115), channel_id=1, source_target_pairs={{0,4},{4,0},{8,12},{12,8},{16,20},{20,16},{24,28},{28,24},{1,5},{5... | collective-permute-start | bytes 442376 | tf_op jit(solution)/shard_map/ppermute | solution.py:628
  130.2 11.7 %collective-permute-start.29 = (bf16[192,384]{1,0:T(8,128)(2,1)S(1)}, bf16[192,384]{1,0:T(8,128)(2,1)S(1)}, u32[]{:S(2)}, u32[]{:S(2)}) collective-permute-start(bf16[192,384]{1,0:T(8,128)(2,1)S(1)} %add_convert_fusion.6), channel_id=1, source_target_pairs={{0,24},{4,28},{8,16},{12,20},{16,8},{20,12},{24,0},{28,4},{1,25},{... | collective-permute-start | bytes 442376 | tf_op jit(solution)/shard_map/ppermute | solution.py:628
  132.7 9.2 %collective-permute-start.28 = (bf16[192,384]{1,0:T(8,128)(2,1)S(1)}, bf16[192,384]{1,0:T(8,128)(2,1)S(1)}, u32[]{:S(2)}, u32[]{:S(2)}) collective-permute-start(bf16[192,384]{1,0:T(8,128)(2,1)S(1)} %add_convert_fusion.6), channel_id=1, source_target_pairs={{0,16},{4,20},{8,24},{12,28},{16,0},{20,4},{24,8},{28,12},{1,17},{... | collective-permute-start | bytes 442376 | tf_op jit(solution)/shard_map/ppermute | solution.py:628
  133.2 8.8 %collective-permute-start.27 = (bf16[192,384]{1,0:T(8,128)(2,1)S(1)}, bf16[192,384]{1,0:T(8,128)(2,1)S(1)}, u32[]{:S(2)}, u32[]{:S(2)}) collective-permute-start(bf16[192,384]{1,0:T(8,128)(2,1)S(1)} %add_convert_fusion.6), channel_id=1, source_target_pairs={{0,8},{4,12},{8,0},{12,4},{16,24},{20,28},{24,16},{28,20},{1,9},{5... | collective-permute-start | bytes 442376 | tf_op jit(solution)/shard_map/ppermute | solution.py:628

commit v7 on v6

--- a/solution.py
+++ b/solution.py
@@ -12,6 +12,7 @@
 BF16 = jnp.bfloat16
 F32 = jnp.float32
 LOG2_E = math.log2(math.e)
+SLOT_ORDER = (0, 2, 3, 1)
 VMEM_LIMIT = 56 * 1024 * 1024
 
 
@@ -102,7 +103,7 @@
     grad_update = (cot_ref[...].astype(F32) * out_gate).astype(BF16)
     put(3, mm_nt(grad_update, w_out_ref[...]))
     for slot in range(groups):
-        send_refs[slot][...] = stage_ref[slot]
+        send_refs[SLOT_ORDER.index(slot)][...] = stage_ref[slot]
 
 
 def lane_tiles(cols):
@@ -215,7 +216,7 @@
     step = 16
     tiles = -(-cols // 128)
     *sends, stats = pl.pallas_call(
-        functools.partial(bias_kernel, groups=groups, batch=4),
+        functools.partial(bias_kernel, groups=groups, batch=2),
         grid=(half // step,),
         in_specs=[
             smem(),
@@ -327,7 +328,7 @@
     tiles = -(-cols // 128)
     out = pl.pallas_call(
         functools.partial(
-            pair_back_kernel, groups=groups, calls=len(grads) // groups, factor=factor, batch=4
+            pair_back_kernel, groups=groups, calls=len(grads) // groups, factor=factor, batch=2
         ),
         grid=(half // step,),
         in_specs=[
@@ -357,6 +358,7 @@
 def attention_kernel(group_ref, row_ref, *rest, groups, row_parts, head_size, row_block):
     bias_refs = rest[: row_parts + 2]
     acts_refs = rest[row_parts + 2 : row_parts + 2 + groups]
+    acts_refs = acts_refs[:1] + acts_refs[-1:] + acts_refs[1:-1]
     rest = rest[row_parts + 2 + groups :]
     out_refs = rest[:groups]
     (
@@ -552,7 +554,7 @@
             pltpu.VMEM((part, tokens), F32),
         ],
         compiler_params=params(),
-    )(group_index, row_index, *bias, *acts)
+    )(group_index, row_index, *bias, acts[0], *acts[2:], acts[1])
     return grads, keep, give
 
 
@@ -615,7 +617,7 @@
 
 def swap_groups(sends):
     groups = len(sends)
-    order = (*range(2, groups), 1)
+    order = SLOT_ORDER[1:]
     got = []
     for bits in order:
         perm = [(index, index ^ bits) for index in range(groups)]
@@ -670,13 +672,12 @@
     return [total[slot] for slot in range(total.shape[0])]
 
 
-def sum_cores(mine, row_total):
-    return (mine.astype(F32) + flip_rows(mine, 1, row_total).astype(F32)).astype(BF16)
-
-
-def sum_chips(both, row_total):
-    near, far, last = (flip_rows(both, bits, row_total).astype(F32) for bits in (2, 4, 6))
-    return (both.astype(F32) + near) + (far + last)
+def sum_rows(mine, d_pair, row_total):
+    parts = [flip_rows(mine, bits, row_total) for bits in (2, 4, 6)]
+    parts, d_pair = lax.optimization_barrier((parts, d_pair))
+    near, far, last = (part.astype(F32) for part in parts)
+    chips = ((mine.astype(F32) + near) + (far + last)).astype(BF16)
+    return chips.astype(F32) + flip_rows(chips, 1, row_total).astype(F32), d_pair
 
 
 def split_heads(
@@ -739,6 +740,7 @@
         w_out,
     )
     bias_got, _ = lax.optimization_barrier((bias_got, acts_send))
+    acts_send = [acts_send[SLOT_ORDER.index(slot)] for slot in range(groups)]
     acts = swap_groups(acts_send)
     bias_all, acts = gather_rows(jnp.stack(bias_got), acts, row_total)
     grads_send, keep, give = attention(group_index, row_index, acts, bias_all, head_size)
@@ -772,10 +774,8 @@
         w_out,
         *grads,
     )
-    d_part, dbias_back = lax.optimization_barrier((d_part, dbias_back))
-    d_both = sum_cores(d_part, row_total)
-    d_single = sum_chips(d_both, row_total)
     d_pair = pair_back(pair, stats, dbias_back, w_pair, group_index, groups, float(tokens))
+    d_single, d_pair = sum_rows(d_part, d_pair, row_total)
     return (updated[None], d_single, d_pair)
 
 

time: 143 us -> 140 us (0.979)
  waiting for transfers between devices: 49.3 us -> 45.3 us
    ppermute x12, waiting for transfers between devices: 27.6 us -> 23.8 us  [swap_groups(): got.append(lax.ppermute(sends[bits], 'grp', perm))]
  transfers between devices with their start and end apart: 30 -> 30, of which waited for: 18 -> 17; matrix products, arithmetic and copies ran while one was open for 0% -> 0% of each run, Pallas kernels for 15% -> 16%
where the time goes in v7:
time: 140 us
  Pallas kernels  47.9 us (34%)
  waiting for transfers between devices  45.3 us (32%)
  starting transfers between devices  40.3 us (29%)
  other arithmetic  3.17 us (2%)
  local copies, waits for them, and re-layouts  2.78 us (2%)
    ppermute x12, starting transfers between devices, swap_groups(): got.append(lax.ppermute(sends[bits], 'grp', perm))  26.7 us
    ppermute x12, waiting for transfers between devices, swap_groups(): got.append(lax.ppermute(sends[bits], 'grp', perm))  23.8 us
    ppermute x18, waiting for transfers between devices, flip_rows(): lax.ppermute(values, 'rows', [(index, index ^ bits) for index in range(ro...  21.5 us
    pallas_call x1, Pallas kernels, attention(): pl.pallas_call(functools.partial(attention_kernel, groups=groups, row_par...  16.3 us
    ppermute x18, starting transfers between devices, flip_rows(): lax.ppermute(values, 'rows', [(index, index ^ bits) for index in range(ro...  13.6 us
    pallas_call x1, Pallas kernels, pair_bias(): pl.pallas_call(functools.partial(bias_kernel, groups=groups, batch=2), gr...  9.45 us
    pallas_call x1, Pallas kernels, pair_back(): pl.pallas_call(functools.partial(pair_back_kernel, groups=groups, calls=l...  8.28 us
    pallas_call x1, Pallas kernels, split_heads(): pl.pallas_call(functools.partial(finish_kernel, groups=groups, calls=call...  7.48 us
  transfers between devices with their start and end apart: 30, of which 17 were waited for; matrix products, arithmetic and copies ran while one was open for 0% of the time, Pallas kernels for 16%

profile of v7, /device:TPU:0, one launch (start us, length us, event | category | flops | bytes accessed | tf_op | source)
XLA Modules:
  0.0 140.3 jit_solution(3900609997403274370)
XLA Ops:
  0.6 9.4 %shard_map.158 = (bf16[4,3,48,128]{3,2,1,0:T(8,128)(2,1)}, bf16[4,3,48,128]{3,2,1,0:T(8,128)(2,1)}, bf16[4,3,48,128]{3,2,1,0:T(8,128)(2,1)}, bf16[4,3,48,128]{3,2,1,0:T(8,128)(2,1)}, f32[2,48,24,192]{3,2,1,0:T(8,128)}) custom-call(s32[1]{0:T(128)} %bitcast.group_ref, s32[1]{0:T(128)} %bitcast.3.rows_ref.row_ref, s32[768]{0:T(1024)} %cols_ref.1, f32[16]{0:T(128)} %gain_ref.1, ...), custom_call_target="tpu_custom_call" | custom-call | tf_op jit(solution)/shard_map/pallas_call | solution.py:218
  10.1 4.0 %collective-permute-start = (bf16[4,3,48,128]{3,2,1,0:T(8,128)(2,1)}, bf16[4,3,48,128]{3,2,1,0:T(8,128)(2,1)S(1)}, u32[]{:S(2)}, u32[]{:S(2)}) collective-permute-start(bf16[4,3,48,128]{3,2,1,0:T(8,128)(2,1)} %get-tuple-element.64), channel_id=1, source_target_pairs={{0,2},{1,3},{2,0},{3,1},{4,6},{5,7},{6,4},{7,5},{8,10},{9,11},{10,... | collective-permute-start | bytes 442376 | tf_op jit(solution)/shard_map/ppermute | solution.py:624
  14.1 1.3 collective-permute-start.1
  15.5 0.2 collective-permute-start.2
  15.7 6.4 %shard_map.157 = (bf16[192,768]{1,0:T(8,128)(2,1)}, bf16[192,768]{1,0:T(8,128)(2,1)}, bf16[192,768]{1,0:T(8,128)(2,1)}, bf16[192,768]{1,0:T(8,128)(2,1)}, f32[192,768]{1,0:T(8,128)}, /*index=5*/f32[192,768]{1,0:T(8,128)}) custom-call(s32[1]{0:T(128)} %bitcast.group_ref, bf16[192,384]{1,0:T(8,128)(2,1)} %single_ref.3, bf16[192,768]{1,0:T(8,128)(2,1)} %bitcast.23, ...), custom_call_target="tpu_custom_call" | custom-call | tf_op jit(solution)/shard_map/pallas_call | solution.py:715
  22.1 0.0 copy-start.26
  22.1 3.3 %collective-permute-done = bf16[4,3,48,128]{3,2,1,0:T(8,128)(2,1)S(1)} collective-permute-done((bf16[4,3,48,128]{3,2,1,0:T(8,128)(2,1)}, bf16[4,3,48,128]{3,2,1,0:T(8,128)(2,1)S(1)}, u32[]{:S(2)}, u32[]{:S(2)}) %collective-permute-start) | collective-permute-done | bytes 147488 | tf_op jit(solution)/shard_map/ppermute | solution.py:624
  25.4 0.5 collective-permute-done.2
  25.9 0.1 pad_maximum_fusion.rest_0_
  26.0 1.6 %collective-permute-start.6 = (bf16[4,4,3,48,128]{4,3,2,1,0:T(8,128)(2,1)S(1)}, bf16[4,4,3,48,128]{4,3,2,1,0:T(8,128)(2,1)S(1)}, u32[]{:S(2)}, u32[]{:S(2)}) collective-permute-start(bf16[4,4,3,48,128]{4,3,2,1,0:T(8,128)(2,1)S(1)} %pad_maximum_fusion.rest_0_), channel_id=1, source_target_pairs={{0,16},{4,20},{8,24},{12,28},{16,0},{20,4},{24,8},{28,12},{1,17},{... | collective-permute-start | bytes 1769480 | tf_op jit(solution)/shard_map/ppermute | solution.py:630
  27.6 1.5 %collective-permute-start.4 = (bf16[4,4,3,48,128]{4,3,2,1,0:T(8,128)(2,1)S(1)}, bf16[4,4,3,48,128]{4,3,2,1,0:T(8,128)(2,1)S(1)}, u32[]{:S(2)}, u32[]{:S(2)}) collective-permute-start(bf16[4,4,3,48,128]{4,3,2,1,0:T(8,128)(2,1)S(1)} %pad_maximum_fusion.rest_0_), channel_id=1, source_target_pairs={{0,8},{4,12},{8,0},{12,4},{16,24},{20,28},{24,16},{28,20},{1,9},{5... | collective-permute-start | bytes 1769480 | tf_op jit(solution)/shard_map/ppermute | solution.py:630
  29.1 4.4 %collective-permute-start.8 = (bf16[192,768]{1,0:T(8,128)(2,1)S(1)}, bf16[192,768]{1,0:T(8,128)(2,1)S(1)}, u32[]{:S(2)}, u32[]{:S(2)}) collective-permute-start(bf16[192,768]{1,0:T(8,128)(2,1)S(1)} %copy-done.27), channel_id=1, source_target_pairs={{0,2},{1,3},{2,0},{3,1},{4,6},{5,7},{6,4},{7,5},{8,10},{9,11},{10,... | collective-permute-start | bytes 884744 | tf_op jit(solution)/shard_map/ppermute | solution.py:624
  33.5 0.5 collective-permute-start.9
  34.1 0.1 collective-permute-start.10
  34.2 5.1 %collective-permute-done.6.rest_4_ = bf16[4,4,3,48,128]{4,3,2,1,0:T(8,128)(2,1)S(1)} collective-permute-done((bf16[4,4,3,48,128]{4,3,2,1,0:T(8,128)(2,1)S(1)}, bf16[4,4,3,48,128]{4,3,2,1,0:T(8,128)(2,1)S(1)}, u32[]{:S(2)}, u32[]{:S(2)}) %collective-permute-start.6) | collective-permute-done | bytes 589856 | tf_op jit(solution)/shard_map/ppermute | solution.py:630
  39.3 1.4 collective-permute-start.12
  40.7 0.9 collective-permute-done.4.rest_2_
  41.6 0.7 collective-permute-start.11
  42.2 11.0 %collective-permute-done.8.rest_11_ = bf16[192,768]{1,0:T(8,128)(2,1)S(1)} collective-permute-done((bf16[192,768]{1,0:T(8,128)(2,1)S(1)}, bf16[192,768]{1,0:T(8,128)(2,1)S(1)}, u32[]{:S(2)}, u32[]{:S(2)}) %collective-permute-start.8) | collective-permute-done | bytes 294944 | tf_op jit(solution)/shard_map/ppermute | solution.py:624
  53.3 0.5 collective-permute-start.7
  53.8 0.4 collective-permute-done.10.rest_13_
  54.2 0.6 collective-permute-start.13
  54.8 0.1 collective-permute-start.14
  54.8 0.4 collective-permute-done.3.rest_1_
  55.2 0.8 collective-permute-done.7.rest_5_
  56.1 0.8 collective-permute-done.5.rest_3_
  56.9 0.4 collective-permute-done.13.rest_7_
  57.4 0.4 collective-permute-done.14.rest_9_
  57.9 0.2 copy-done.15
  58.1 0.7 copy-done.16
  58.8 16.3 %shard_map.159 = (bf16[192,768]{1,0:T(8,128)(2,1)}, bf16[192,768]{1,0:T(8,128)(2,1)}, bf16[192,768]{1,0:T(8,128)(2,1)}, bf16[192,768]{1,0:T(8,128)(2,1)}, bf16[4...) custom-call(s32[1]{0:T(128)} %bitcast.group_ref, s32[1]{0:T(128)} %bitcast.3.rows_ref.row_ref, ...), custom_call_target="tpu_custom_call" | custom-call | tf_op jit(solution)/shard_map/pallas_call | solution.py:527
  75.1 0.2 collective-permute-start.15
  75.3 4.6 %collective-permute-done.15 = bf16[4,16,3,48,128]{4,3,2,1,0:T(8,128)(2,1)S(1)} collective-permute-done((bf16[4,16,3,48,128]{4,3,2,1,0:T(8,128)(2,1)}, bf16[4,16,3,48,128]{4,3,2,1,0:T(8,128)(2,1)S(1)}, u32[]{:S(2)}, u32[]{:S(2)}) %collective-permute-start.15) | collective-permute-done | bytes 2359328 | tf_op jit(solution)/shard_map/ppermute | solution.py:630
  79.9 1.7 %add_convert_fusion.3 = (bf16[4,4,3,48,128]{4,3,2,1,0:T(8,128)(2,1)S(1)}, bf16[4,4,3,48,128]{4,3,2,1,0:T(8,128)(2,1)S(1)}) fusion(bf16[4,16,3,48,128]{4,3,2,1,0:T(8,128)(2,1)S(1)} %collective-permute-done.15, bf16[4,16,3,48,128]{4,3,2,1,0:T(8,128)(2,1)} %get-tuple-element.86), kind=kLoop, calls=%fused_computation.3 | loop fusion | flops 2359296 | bytes 3538944 | tf_op jit(solution)/shard_map/convert_element_type | solution.py:659
  81.7 0.6 collective-permute-start.16
  82.3 0.5 collective-permute-start.17
  82.8 4.7 %collective-permute-start.20 = (bf16[192,768]{1,0:T(8,128)(2,1)S(1)}, bf16[192,768]{1,0:T(8,128)(2,1)S(1)}, u32[]{:S(2)}, u32[]{:S(2)}) collective-permute-start(bf16[192,768]{1,0:T(8,128)(2,1)S(1)} %copy-done.25), channel_id=1, source_target_pairs={{0,2},{1,3},{2,0},{3,1},{4,6},{5,7},{6,4},{7,5},{8,10},{9,11},{10,... | collective-permute-start | bytes 884744 | tf_op jit(solution)/shard_map/ppermute | solution.py:624
  87.5 3.3 %collective-permute-start.21 = (bf16[192,768]{1,0:T(8,128)(2,1)S(1)}, bf16[192,768]{1,0:T(8,128)(2,1)S(1)}, u32[]{:S(2)}, u32[]{:S(2)}) collective-permute-start(bf16[192,768]{1,0:T(8,128)(2,1)S(1)} %copy-done.23), channel_id=1, source_target_pairs={{0,3},{1,2},{2,1},{3,0},{4,7},{5,6},{6,5},{7,4},{8,11},{9,10},{10,... | collective-permute-start | bytes 884744 | tf_op jit(solution)/shard_map/ppermute | solution.py:624
  90.8 6.3 %collective-permute-done.16 = bf16[4,4,3,48,128]{4,3,2,1,0:T(8,128)(2,1)S(1)} collective-permute-done((bf16[4,4,3,48,128]{4,3,2,1,0:T(8,128)(2,1)S(1)}, bf16[4,4,3,48,128]{4,3,2,1,0:T(8,128)(2,1)S(1)}, u32[]{:S(2)}, u32[]{:S(2)}) %collective-permute-start.16) | collective-permute-done | bytes 589856 | tf_op jit(solution)/shard_map/ppermute | solution.py:630
  97.1 0.2 collective-permute-done.17
  97.4 0.2 add_convert_fusion.4
  97.6 1.6 %collective-permute-start.19 = (bf16[4,2,3,48,128]{4,3,2,1,0:T(8,128)(2,1)S(1)}, bf16[4,2,3,48,128]{4,3,2,1,0:T(8,128)(2,1)S(1)}, u32[]{:S(2)}, u32[]{:S(2)}) collective-permute-start(bf16[4,2,3,48,128]{4,3,2,1,0:T(8,128)(2,1)S(1)} %get-tuple-element.119), channel_id=1, source_target_pairs={{0,8},{4,12},{8,0},{12,4},{16,24},{20,28},{24,16},{28,20},{1,9},{5... | collective-permute-start | bytes 884744 | tf_op jit(solution)/shard_map/ppermute | solution.py:630
  99.2 0.5 collective-permute-start.18
  99.7 8.4 %collective-permute-done.20.rest_2_ = bf16[192,768]{1,0:T(8,128)(2,1)S(1)} collective-permute-done((bf16[192,768]{1,0:T(8,128)(2,1)S(1)}, bf16[192,768]{1,0:T(8,128)(2,1)S(1)}, u32[]{:S(2)}, u32[]{:S(2)}) %collective-permute-start.20) | collective-permute-done | bytes 294944 | tf_op jit(solution)/shard_map/ppermute | solution.py:624
  108.1 0.2 collective-permute-done.22.rest_1_
  108.4 0.3 add_convert_fusion
  108.7 0.1 copy-done.9
  108.8 0.1 copy-done.11
  108.9 0.1 copy-done.12
  109.0 0.7 slice_bitcast_fusion
  109.7 7.5 %collective-permute-start.26 = (bf16[4,3,48,128]{3,2,1,0:T(8,128)(2,1)S(1)}, bf16[4,3,48,128]{3,2,1,0:T(8,128)(2,1)S(1)}, u32[]{:S(2)}, u32[]{:S(2)}) collective-permute-start(bf16[4,3,48,128]{3,2,1,0:T(8,128)(2,1)S(1)} %get-tuple-element.109), channel_id=1, source_target_pairs={{0,2},{1,3},{2,0},{3,1},{4,6},{5,7},{6,4},{7,5},{8,10},{9,11},{10,... | collective-permute-start | bytes 442376 | tf_op jit(solution)/shard_map/ppermute | solution.py:624
  117.1 0.6 collective-permute-start.27
  117.7 0.0 collective-permute-start.28
  117.7 7.5 %shard_map.160 = (bf16[192,768]{1,0:T(8,128)(2,1)}, bf16[192,384]{1,0:T(8,128)(2,1)}) custom-call(s32[1]{0:T(128)} %bitcast.group_ref, bf16[192,384]{1,0:T(8,128)(2,1)} %single_ref.3, bf16[192,768]{1,0:T(8,128)(2,1)} %bitcast.24, bf16[192,768]{1,0:T(8,128)(2,1)} %bitcast.26, f32[192,768]{1,0:T(8,128)} %get-tuple-element.61.gamma_ref, ...), custom_call_target="tpu_custom_call" | custom-call | tf_op jit(solution)/shard_map/pallas_call | solution.py:752
  125.2 2.5 %collective-permute-start.25 = (bf16[192,384]{1,0:T(8,128)(2,1)}, bf16[192,384]{1,0:T(8,128)(2,1)S(1)}, u32[]{:S(2)}, u32[]{:S(2)}) collective-permute-start(bf16[192,384]{1,0:T(8,128)(2,1)} %get-tuple-element.106), channel_id=1, source_target_pairs={{0,24},{4,28},{8,16},{12,20},{16,8},{20,12},{24,0},{28,4},{1,25},{... | collective-permute-start | bytes 442376 | tf_op jit(solution)/shard_map/ppermute | solution.py:630
  127.6 0.5 collective-permute-start.24
  128.2 0.9 collective-permute-start.23
  129.1 0.6 copy-done.20
  129.7 0.1 copy-done.21
  129.7 8.3 %shard_map.161 = bf16[2,48,192,128]{3,2,1,0:T(8,128)(2,1)} custom-call(s32[1]{0:T(128)} %bitcast.group_ref, bf16[2,48,192,128]{3,2,1,0:T(8,128)(2,1)} %bitcast.21, f32[2,48,24,192]{3,2,1,0:T(8,128)} %get-tuple-element.107.stats_ref, bf16[16,128]{1,0:T(8,128)(2,1)} %bitcast.32, bf16[4,3,48,128]{3,2,1,0:T(8,128)(2,1)} %get-tuple-element.108.rest_0_, ...), custom_call_target="tpu_custom_call" | custom-call | tf_op jit(solution)/shard_map/pallas_call | solution.py:329
  138.0 0.1 add_convert_fusion.6
  138.1 0.1 collective-permute-start.29
  138.2 1.4 collective-permute-done.29
  139.6 0.7 convert_add_fusion
  (68 shorter events, 0.2 us)
Async XLA Ops:
  10.1 15.3 %collective-permute-start = (bf16[4,3,48,128]{3,2,1,0:T(8,128)(2,1)}, bf16[4,3,48,128]{3,2,1,0:T(8,128)(2,1)S(1)}, u32[]{:S(2)}, u32[]{:S(2)}) collective-permute-start(bf16[4,3,48,128]{3,2,1,0:T(8,128)(2,1)} %get-tuple-element.64), channel_id=1, source_target_pairs={{0,2},{1,3},{2,0},{3,1},{4,6},{5,7},{6,4},{7,5},{8,10},{9,11},{10,... | collective-permute-start | bytes 442376 | tf_op jit(solution)/shard_map/ppermute | solution.py:624
  14.1 11.3 %collective-permute-start.1 = (bf16[4,3,48,128]{3,2,1,0:T(8,128)(2,1)}, bf16[4,3,48,128]{3,2,1,0:T(8,128)(2,1)S(1)}, u32[]{:S(2)}, u32[]{:S(2)}) collective-permute-start(bf16[4,3,48,128]{3,2,1,0:T(8,128)(2,1)} %get-tuple-element.65), channel_id=1, source_target_pairs={{0,3},{1,2},{2,1},{3,0},{4,7},{5,6},{6,5},{7,4},{8,11},{9,10},{10,... | collective-permute-start | bytes 442376 | tf_op jit(solution)/shard_map/ppermute | solution.py:624
  15.5 10.4 %collective-permute-start.2 = (bf16[4,3,48,128]{3,2,1,0:T(8,128)(2,1)}, bf16[4,3,48,128]{3,2,1,0:T(8,128)(2,1)S(1)}, u32[]{:S(2)}, u32[]{:S(2)}) collective-permute-start(bf16[4,3,48,128]{3,2,1,0:T(8,128)(2,1)} %get-tuple-element.66), channel_id=1, source_target_pairs={{0,1},{1,0},{2,3},{3,2},{4,5},{5,4},{6,7},{7,6},{8,9},{9,8},{10,11... | collective-permute-start | bytes 442376 | tf_op jit(solution)/shard_map/ppermute | solution.py:624
  15.7 10.2 %copy-start.17 = (bf16[4,3,48,128]{3,2,1,0:T(8,128)(2,1)S(1)}, bf16[4,3,48,128]{3,2,1,0:T(8,128)(2,1)}, u32[]{:S(2)}) copy-start(bf16[4,3,48,128]{3,2,1,0:T(8,128)(2,1)} %get-tuple-element.74) | copy-start | bytes 442372
  22.1 7.0 %copy-start.27 = (bf16[192,768]{1,0:T(8,128)(2,1)S(1)}, bf16[192,768]{1,0:T(8,128)(2,1)}, u32[]{:S(2)}) copy-start(bf16[192,768]{1,0:T(8,128)(2,1)} %get-tuple-element.71) | copy-start | bytes 884740
  22.1 11.4 %copy-start.26 = (bf16[192,768]{1,0:T(8,128)(2,1)S(1)}, bf16[192,768]{1,0:T(8,128)(2,1)}, u32[]{:S(2)}) copy-start(bf16[192,768]{1,0:T(8,128)(2,1)} %get-tuple-element.72) | copy-start | bytes 884740
  22.1 12.0 %copy-start.24 = (bf16[192,768]{1,0:T(8,128)(2,1)S(1)}, bf16[192,768]{1,0:T(8,128)(2,1)}, u32[]{:S(2)}) copy-start(bf16[192,768]{1,0:T(8,128)(2,1)} %get-tuple-element.73) | copy-start | bytes 884740
  26.0 31.8 %copy-start = (bf16[4,4,3,48,128]{4,3,2,1,0:T(8,128)(2,1)}, bf16[4,4,3,48,128]{4,3,2,1,0:T(8,128)(2,1)S(1)}, u32[]{:S(2)}) copy-start(bf16[4,4,3,48,128]{4,3,2,1,0:T(8,128)(2,1)S(1)} %pad_maximum_fusion.rest_0_) | copy-start | bytes 1769476
  26.0 13.3 %collective-permute-start.6 = (bf16[4,4,3,48,128]{4,3,2,1,0:T(8,128)(2,1)S(1)}, bf16[4,4,3,48,128]{4,3,2,1,0:T(8,128)(2,1)S(1)}, u32[]{:S(2)}, u32[]{:S(2)}) collective-permute-start(bf16[4,4,3,48,128]{4,3,2,1,0:T(8,128)(2,1)S(1)} %pad_maximum_fusion.rest_0_), channel_id=1, source_target_pairs={{0,16},{4,20},{8,24},{12,28},{16,0},{20,4},{24,8},{28,12},{1,17},{... | collective-permute-start | bytes 1769480 | tf_op jit(solution)/shard_map/ppermute | solution.py:630
  27.6 13.9 %collective-permute-start.4 = (bf16[4,4,3,48,128]{4,3,2,1,0:T(8,128)(2,1)S(1)}, bf16[4,4,3,48,128]{4,3,2,1,0:T(8,128)(2,1)S(1)}, u32[]{:S(2)}, u32[]{:S(2)}) collective-permute-start(bf16[4,4,3,48,128]{4,3,2,1,0:T(8,128)(2,1)S(1)} %pad_maximum_fusion.rest_0_), channel_id=1, source_target_pairs={{0,8},{4,12},{8,0},{12,4},{16,24},{20,28},{24,16},{28,20},{1,9},{5... | collective-permute-start | bytes 1769480 | tf_op jit(solution)/shard_map/ppermute | solution.py:630
  29.1 24.1 %collective-permute-start.8 = (bf16[192,768]{1,0:T(8,128)(2,1)S(1)}, bf16[192,768]{1,0:T(8,128)(2,1)S(1)}, u32[]{:S(2)}, u32[]{:S(2)}) collective-permute-start(bf16[192,768]{1,0:T(8,128)(2,1)S(1)} %copy-done.27), channel_id=1, source_target_pairs={{0,2},{1,3},{2,0},{3,1},{4,6},{5,7},{6,4},{7,5},{8,10},{9,11},{10,... | collective-permute-start | bytes 884744 | tf_op jit(solution)/shard_map/ppermute | solution.py:624
  33.5 19.7 %collective-permute-start.9 = (bf16[192,768]{1,0:T(8,128)(2,1)S(1)}, bf16[192,768]{1,0:T(8,128)(2,1)S(1)}, u32[]{:S(2)}, u32[]{:S(2)}) collective-permute-start(bf16[192,768]{1,0:T(8,128)(2,1)S(1)} %copy-done.26), channel_id=1, source_target_pairs={{0,3},{1,2},{2,1},{3,0},{4,7},{5,6},{6,5},{7,4},{8,11},{9,10},{10,... | collective-permute-start | bytes 884744 | tf_op jit(solution)/shard_map/ppermute | solution.py:624
  34.1 20.1 %collective-permute-start.10 = (bf16[192,768]{1,0:T(8,128)(2,1)S(1)}, bf16[192,768]{1,0:T(8,128)(2,1)S(1)}, u32[]{:S(2)}, u32[]{:S(2)}) collective-permute-start(bf16[192,768]{1,0:T(8,128)(2,1)S(1)} %copy-done.24), channel_id=1, source_target_pairs={{0,1},{1,0},{2,3},{3,2},{4,5},{5,4},{6,7},{7,6},{8,9},{9,8},{10,11... | collective-permute-start | bytes 884744 | tf_op jit(solution)/shard_map/ppermute | solution.py:624
  39.3 18.5 %copy-start.2 = (bf16[4,4,3,48,128]{4,3,2,1,0:T(8,128)(2,1)}, bf16[4,4,3,48,128]{4,3,2,1,0:T(8,128)(2,1)S(1)}, u32[]{:S(2)}) copy-start(bf16[4,4,3,48,128]{4,3,2,1,0:T(8,128)(2,1)S(1)} %collective-permute-done.6.rest_4_) | copy-start | bytes 1769476
  39.3 14.9 %collective-permute-start.12 = (bf16[2,4,3,48,128]{4,3,2,1,0:T(8,128)(2,1)S(1)}, bf16[2,4,3,48,128]{4,3,2,1,0:T(8,128)(2,1)S(1)}, u32[]{:S(2)}, u32[]{:S(2)}) collective-permute-start(bf16[2,4,3,48,128]{4,3,2,1,0:T(8,128)(2,1)S(1)} %slice.81), channel_id=1, source_target_pairs={{0,8},{4,12},{8,0},{12,4},{16,24},{20,28},{24,16},{28,20},{1,9},{5... | collective-permute-start | bytes 884744 | tf_op jit(solution)/shard_map/ppermute | solution.py:630
  41.5 16.2 %copy-start.3 = (bf16[4,4,3,48,128]{4,3,2,1,0:T(8,128)(2,1)}, bf16[4,4,3,48,128]{4,3,2,1,0:T(8,128)(2,1)S(1)}, u32[]{:S(2)}) copy-start(bf16[4,4,3,48,128]{4,3,2,1,0:T(8,128)(2,1)S(1)} %collective-permute-done.4.rest_2_) | copy-start | bytes 1769476
  41.6 12.6 %collective-permute-start.11 = (bf16[2,4,3,48,128]{4,3,2,1,0:T(8,128)(2,1)S(1)}, bf16[2,4,3,48,128]{4,3,2,1,0:T(8,128)(2,1)S(1)}, u32[]{:S(2)}, u32[]{:S(2)}) collective-permute-start(bf16[2,4,3,48,128]{4,3,2,1,0:T(8,128)(2,1)S(1)} %slice.80), channel_id=1, source_target_pairs={{0,16},{4,20},{8,24},{12,28},{16,0},{20,4},{24,8},{28,12},{1,17},{... | collective-permute-start | bytes 884744 | tf_op jit(solution)/shard_map/ppermute | solution.py:630
  53.2 4.6 %copy-start.7 = (bf16[192,768]{1,0:T(8,128)(2,1)}, bf16[192,768]{1,0:T(8,128)(2,1)S(1)}, u32[]{:S(2)}) copy-start(bf16[192,768]{1,0:T(8,128)(2,1)S(1)} %collective-permute-done.8.rest_11_) | copy-start | bytes 884740
  53.2 2.0 %collective-permute-start.3 = (bf16[4,4,3,48,128]{4,3,2,1,0:T(8,128)(2,1)S(1)}, bf16[4,4,3,48,128]{4,3,2,1,0:T(8,128)(2,1)S(1)}, u32[]{:S(2)}, u32[]{:S(2)}) collective-permute-start(bf16[4,4,3,48,128]{4,3,2,1,0:T(8,128)(2,1)S(1)} %pad_maximum_fusion.rest_0_), channel_id=1, source_target_pairs={{0,4},{4,0},{8,12},{12,8},{16,20},{20,16},{24,28},{28,24},{1,5},{5... | collective-permute-start | bytes 1769480 | tf_op jit(solution)/shard_map/ppermute | solution.py:630
  53.2 4.5 %copy-start.8 = (bf16[192,768]{1,0:T(8,128)(2,1)}, bf16[192,768]{1,0:T(8,128)(2,1)S(1)}, u32[]{:S(2)}) copy-start(bf16[192,768]{1,0:T(8,128)(2,1)S(1)} %collective-permute-done.9.rest_12_) | copy-start | bytes 884740
  53.3 2.8 %collective-permute-start.7 = (bf16[4,4,3,48,128]{4,3,2,1,0:T(8,128)(2,1)S(1)}, bf16[4,4,3,48,128]{4,3,2,1,0:T(8,128)(2,1)S(1)}, u32[]{:S(2)}, u32[]{:S(2)}) collective-permute-start(bf16[4,4,3,48,128]{4,3,2,1,0:T(8,128)(2,1)S(1)} %collective-permute-done.6.rest_4_), channel_id=1, source_target_pairs={{0,4},{4,0},{8,12},{12,8},{16,20},{20,16},{24,28},{28,24},{1,5},{5... | collective-permute-start | bytes 1769480 | tf_op jit(solution)/shard_map/ppermute | solution.py:630
  54.2 3.6 %copy-start.10 = (bf16[192,768]{1,0:T(8,128)(2,1)}, bf16[192,768]{1,0:T(8,128)(2,1)S(1)}, u32[]{:S(2)}) copy-start(bf16[192,768]{1,0:T(8,128)(2,1)S(1)} %collective-permute-done.10.rest_13_) | copy-start | bytes 884740
  54.2 2.8 %collective-permute-start.5 = (bf16[4,4,3,48,128]{4,3,2,1,0:T(8,128)(2,1)S(1)}, bf16[4,4,3,48,128]{4,3,2,1,0:T(8,128)(2,1)S(1)}, u32[]{:S(2)}, u32[]{:S(2)}) collective-permute-start(bf16[4,4,3,48,128]{4,3,2,1,0:T(8,128)(2,1)S(1)} %collective-permute-done.4.rest_2_), channel_id=1, source_target_pairs={{0,4},{4,0},{8,12},{12,8},{16,20},{20,16},{24,28},{28,24},{1,5},{5... | collective-permute-start | bytes 1769480 | tf_op jit(solution)/shard_map/ppermute | solution.py:630
  54.2 3.6 %copy-start.13 = (bf16[2,4,3,48,128]{4,3,2,1,0:T(8,128)(2,1)}, bf16[2,4,3,48,128]{4,3,2,1,0:T(8,128)(2,1)S(1)}, u32[]{:S(2)}) copy-start(bf16[2,4,3,48,128]{4,3,2,1,0:T(8,128)(2,1)S(1)} %collective-permute-done.12.rest_8_) | copy-start | bytes 884740
  54.2 3.6 %copy-start.14 = (bf16[2,4,3,48,128]{4,3,2,1,0:T(8,128)(2,1)}, bf16[2,4,3,48,128]{4,3,2,1,0:T(8,128)(2,1)S(1)}, u32[]{:S(2)}) copy-start(bf16[2,4,3,48,128]{4,3,2,1,0:T(8,128)(2,1)S(1)} %collective-permute-done.11.rest_6_) | copy-start | bytes 884740
  54.2 3.1 %collective-permute-start.13 = (bf16[2,4,3,48,128]{4,3,2,1,0:T(8,128)(2,1)S(1)}, bf16[2,4,3,48,128]{4,3,2,1,0:T(8,128)(2,1)S(1)}, u32[]{:S(2)}, u32[]{:S(2)}) collective-permute-start(bf16[2,4,3,48,128]{4,3,2,1,0:T(8,128)(2,1)S(1)} %collective-permute-done.11.rest_6_), channel_id=1, source_target_pairs={{0,4},{4,0},{8,12},{12,8},{16,20},{20,16},{24,28},{28,24},{1,5},{5... | collective-permute-start | bytes 884744 | tf_op jit(solution)/shard_map/ppermute | solution.py:630
  54.8 3.0 %collective-permute-start.14 = (bf16[2,4,3,48,128]{4,3,2,1,0:T(8,128)(2,1)S(1)}, bf16[2,4,3,48,128]{4,3,2,1,0:T(8,128)(2,1)S(1)}, u32[]{:S(2)}, u32[]{:S(2)}) collective-permute-start(bf16[2,4,3,48,128]{4,3,2,1,0:T(8,128)(2,1)S(1)} %collective-permute-done.12.rest_8_), channel_id=1, source_target_pairs={{0,4},{4,0},{8,12},{12,8},{16,20},{20,16},{24,28},{28,24},{1,5},{5... | collective-permute-start | bytes 884744 | tf_op jit(solution)/shard_map/ppermute | solution.py:630
  55.2 2.6 %copy-start.4 = (bf16[4,4,3,48,128]{4,3,2,1,0:T(8,128)(2,1)}, bf16[4,4,3,48,128]{4,3,2,1,0:T(8,128)(2,1)S(1)}, u32[]{:S(2)}) copy-start(bf16[4,4,3,48,128]{4,3,2,1,0:T(8,128)(2,1)S(1)} %collective-permute-done.3.rest_1_) | copy-start | bytes 1769476
  56.1 1.8 %copy-start.5 = (bf16[4,4,3,48,128]{4,3,2,1,0:T(8,128)(2,1)}, bf16[4,4,3,48,128]{4,3,2,1,0:T(8,128)(2,1)S(1)}, u32[]{:S(2)}) copy-start(bf16[4,4,3,48,128]{4,3,2,1,0:T(8,128)(2,1)S(1)} %collective-permute-done.7.rest_5_) | copy-start | bytes 1769476
  56.9 0.9 copy-start.6
  57.3 0.7 copy-start.15
  58.1 0.7 copy-start.16
  75.1 4.8 %collective-permute-start.15 = (bf16[4,16,3,48,128]{4,3,2,1,0:T(8,128)(2,1)}, bf16[4,16,3,48,128]{4,3,2,1,0:T(8,128)(2,1)S(1)}, u32[]{:S(2)}, u32[]{:S(2)}) collective-permute-start(bf16[4,16,3,48,128]{4,3,2,1,0:T(8,128)(2,1)} %get-tuple-element.87), channel_id=1, source_target_pairs={{0,4},{4,0},{8,12},{12,8},{16,20},{20,16},{24,28},{28,24},{1,5},{5... | collective-permute-start | bytes 7077896 | tf_op jit(solution)/shard_map/ppermute | solution.py:630
  79.9 2.9 %copy-start.25 = (bf16[192,768]{1,0:T(8,128)(2,1)S(1)}, bf16[192,768]{1,0:T(8,128)(2,1)}, u32[]{:S(2)}) copy-start(bf16[192,768]{1,0:T(8,128)(2,1)} %get-tuple-element.89) | copy-start | bytes 884740
  79.9 7.6 %copy-start.23 = (bf16[192,768]{1,0:T(8,128)(2,1)S(1)}, bf16[192,768]{1,0:T(8,128)(2,1)}, u32[]{:S(2)}) copy-start(bf16[192,768]{1,0:T(8,128)(2,1)} %get-tuple-element.90) | copy-start | bytes 884740
  79.9 10.9 %copy-start.22 = (bf16[192,768]{1,0:T(8,128)(2,1)S(1)}, bf16[192,768]{1,0:T(8,128)(2,1)}, u32[]{:S(2)}) copy-start(bf16[192,768]{1,0:T(8,128)(2,1)} %get-tuple-element.91) | copy-start | bytes 884740
  79.9 17.4 %copy-start.1 = (bf16[4,16,3,48,128]{4,3,2,1,0:T(8,128)(2,1)S(1)}, bf16[4,16,3,48,128]{4,3,2,1,0:T(8,128)(2,1)}, u32[]{:S(2)}) copy-start(bf16[4,16,3,48,128]{4,3,2,1,0:T(8,128)(2,1)} %get-tuple-element.86) | copy-start | bytes 7077892
  81.7 15.4 %collective-permute-start.16 = (bf16[4,4,3,48,128]{4,3,2,1,0:T(8,128)(2,1)S(1)}, bf16[4,4,3,48,128]{4,3,2,1,0:T(8,128)(2,1)S(1)}, u32[]{:S(2)}, u32[]{:S(2)}) collective-permute-start(bf16[4,4,3,48,128]{4,3,2,1,0:T(8,128)(2,1)S(1)} %get-tuple-element.121), channel_id=1, source_target_pairs={{0,8},{4,12},{8,0},{12,4},{16,24},{20,28},{24,16},{28,20},{1,9},{5... | collective-permute-start | bytes 1769480 | tf_op jit(solution)/shard_map/ppermute | solution.py:630
  82.3 15.1 %collective-permute-start.17 = (bf16[4,4,3,48,128]{4,3,2,1,0:T(8,128)(2,1)S(1)}, bf16[4,4,3,48,128]{4,3,2,1,0:T(8,128)(2,1)S(1)}, u32[]{:S(2)}, u32[]{:S(2)}) collective-permute-start(bf16[4,4,3,48,128]{4,3,2,1,0:T(8,128)(2,1)S(1)} %get-tuple-element.122), channel_id=1, source_target_pairs={{0,16},{4,20},{8,24},{12,28},{16,0},{20,4},{24,8},{28,12},{1,17},{... | collective-permute-start | bytes 1769480 | tf_op jit(solution)/shard_map/ppermute | solution.py:630
  82.8 25.3 %collective-permute-start.20 = (bf16[192,768]{1,0:T(8,128)(2,1)S(1)}, bf16[192,768]{1,0:T(8,128)(2,1)S(1)}, u32[]{:S(2)}, u32[]{:S(2)}) collective-permute-start(bf16[192,768]{1,0:T(8,128)(2,1)S(1)} %copy-done.25), channel_id=1, source_target_pairs={{0,2},{1,3},{2,0},{3,1},{4,6},{5,7},{6,4},{7,5},{8,10},{9,11},{10,... | collective-permute-start | bytes 884744 | tf_op jit(solution)/shard_map/ppermute | solution.py:624
  87.5 20.6 %collective-permute-start.21 = (bf16[192,768]{1,0:T(8,128)(2,1)S(1)}, bf16[192,768]{1,0:T(8,128)(2,1)S(1)}, u32[]{:S(2)}, u32[]{:S(2)}) collective-permute-start(bf16[192,768]{1,0:T(8,128)(2,1)S(1)} %copy-done.23), channel_id=1, source_target_pairs={{0,3},{1,2},{2,1},{3,0},{4,7},{5,6},{6,5},{7,4},{8,11},{9,10},{10,... | collective-permute-start | bytes 884744 | tf_op jit(solution)/shard_map/ppermute | solution.py:624
  90.8 17.5 %collective-permute-start.22 = (bf16[192,768]{1,0:T(8,128)(2,1)S(1)}, bf16[192,768]{1,0:T(8,128)(2,1)S(1)}, u32[]{:S(2)}, u32[]{:S(2)}) collective-permute-start(bf16[192,768]{1,0:T(8,128)(2,1)S(1)} %copy-done.22), channel_id=1, source_target_pairs={{0,1},{1,0},{2,3},{3,2},{4,5},{5,4},{6,7},{7,6},{8,9},{9,8},{10,11... | collective-permute-start | bytes 884744 | tf_op jit(solution)/shard_map/ppermute | solution.py:624
  97.6 10.7 %collective-permute-start.19 = (bf16[4,2,3,48,128]{4,3,2,1,0:T(8,128)(2,1)S(1)}, bf16[4,2,3,48,128]{4,3,2,1,0:T(8,128)(2,1)S(1)}, u32[]{:S(2)}, u32[]{:S(2)}) collective-permute-start(bf16[4,2,3,48,128]{4,3,2,1,0:T(8,128)(2,1)S(1)} %get-tuple-element.119), channel_id=1, source_target_pairs={{0,8},{4,12},{8,0},{12,4},{16,24},{20,28},{24,16},{28,20},{1,9},{5... | collective-permute-start | bytes 884744 | tf_op jit(solution)/shard_map/ppermute | solution.py:630
  99.2 9.2 %collective-permute-start.18 = (bf16[4,2,3,48,128]{4,3,2,1,0:T(8,128)(2,1)S(1)}, bf16[4,2,3,48,128]{4,3,2,1,0:T(8,128)(2,1)S(1)}, u32[]{:S(2)}, u32[]{:S(2)}) collective-permute-start(bf16[4,2,3,48,128]{4,3,2,1,0:T(8,128)(2,1)S(1)} %get-tuple-element.120), channel_id=1, source_target_pairs={{0,16},{4,20},{8,24},{12,28},{16,0},{20,4},{24,8},{28,12},{1,17},{... | collective-permute-start | bytes 884744 | tf_op jit(solution)/shard_map/ppermute | solution.py:630
  108.1 0.7 copy-start.9
  108.1 0.8 copy-start.11
  108.3 0.7 copy-start.12
  109.7 18.5 %collective-permute-start.26 = (bf16[4,3,48,128]{3,2,1,0:T(8,128)(2,1)S(1)}, bf16[4,3,48,128]{3,2,1,0:T(8,128)(2,1)S(1)}, u32[]{:S(2)}, u32[]{:S(2)}) collective-permute-start(bf16[4,3,48,128]{3,2,1,0:T(8,128)(2,1)S(1)} %get-tuple-element.109), channel_id=1, source_target_pairs={{0,2},{1,3},{2,0},{3,1},{4,6},{5,7},{6,4},{7,5},{8,10},{9,11},{10,... | collective-permute-start | bytes 442376 | tf_op jit(solution)/shard_map/ppermute | solution.py:624
  117.1 11.9 %collective-permute-start.27 = (bf16[4,3,48,128]{3,2,1,0:T(8,128)(2,1)S(1)}, bf16[4,3,48,128]{3,2,1,0:T(8,128)(2,1)S(1)}, u32[]{:S(2)}, u32[]{:S(2)}) collective-permute-start(bf16[4,3,48,128]{3,2,1,0:T(8,128)(2,1)S(1)} %get-tuple-element.110), channel_id=1, source_target_pairs={{0,3},{1,2},{2,1},{3,0},{4,7},{5,6},{6,5},{7,4},{8,11},{9,10},{10,... | collective-permute-start | bytes 442376 | tf_op jit(solution)/shard_map/ppermute | solution.py:624
  117.7 11.3 %collective-permute-start.28 = (bf16[4,3,48,128]{3,2,1,0:T(8,128)(2,1)S(1)}, bf16[4,3,48,128]{3,2,1,0:T(8,128)(2,1)S(1)}, u32[]{:S(2)}, u32[]{:S(2)}) collective-permute-start(bf16[4,3,48,128]{3,2,1,0:T(8,128)(2,1)S(1)} %get-tuple-element.111), channel_id=1, source_target_pairs={{0,1},{1,0},{2,3},{3,2},{4,5},{5,4},{6,7},{7,6},{8,9},{9,8},{10,11... | collective-permute-start | bytes 442376 | tf_op jit(solution)/shard_map/ppermute | solution.py:624
  125.2 12.8 %collective-permute-start.25 = (bf16[192,384]{1,0:T(8,128)(2,1)}, bf16[192,384]{1,0:T(8,128)(2,1)S(1)}, u32[]{:S(2)}, u32[]{:S(2)}) collective-permute-start(bf16[192,384]{1,0:T(8,128)(2,1)} %get-tuple-element.106), channel_id=1, source_target_pairs={{0,24},{4,28},{8,16},{12,20},{16,8},{20,12},{24,0},{28,4},{1,25},{... | collective-permute-start | bytes 442376 | tf_op jit(solution)/shard_map/ppermute | solution.py:630
  127.6 10.4 %collective-permute-start.24 = (bf16[192,384]{1,0:T(8,128)(2,1)}, bf16[192,384]{1,0:T(8,128)(2,1)S(1)}, u32[]{:S(2)}, u32[]{:S(2)}) collective-permute-start(bf16[192,384]{1,0:T(8,128)(2,1)} %get-tuple-element.106), channel_id=1, source_target_pairs={{0,16},{4,20},{8,24},{12,28},{16,0},{20,4},{24,8},{28,12},{1,17},{... | collective-permute-start | bytes 442376 | tf_op jit(solution)/shard_map/ppermute | solution.py:630
  128.2 0.9 copy-start.19
  128.2 9.9 %collective-permute-start.23 = (bf16[192,384]{1,0:T(8,128)(2,1)}, bf16[192,384]{1,0:T(8,128)(2,1)S(1)}, u32[]{:S(2)}, u32[]{:S(2)}) collective-permute-start(bf16[192,384]{1,0:T(8,128)(2,1)} %get-tuple-element.106), channel_id=1, source_target_pairs={{0,8},{4,12},{8,0},{12,4},{16,24},{20,28},{24,16},{28,20},{1,9},{5... | collective-permute-start | bytes 442376 | tf_op jit(solution)/shard_map/ppermute | solution.py:630
  129.0 0.7 copy-start.20
  129.0 0.7 copy-start.21
  129.7 8.3 %copy-start.18 = (bf16[192,384]{1,0:T(8,128)(2,1)S(1)}, bf16[192,384]{1,0:T(8,128)(2,1)}, u32[]{:S(2)}) copy-start(bf16[192,384]{1,0:T(8,128)(2,1)} %get-tuple-element.106) | copy-start | bytes 442372
  138.1 1.4 %collective-permute-start.29 = (bf16[192,384]{1,0:T(8,128)(2,1)S(1)}, bf16[192,384]{1,0:T(8,128)(2,1)S(1)}, u32[]{:S(2)}, u32[]{:S(2)}) collective-permute-start(bf16[192,384]{1,0:T(8,128)(2,1)S(1)} %add_convert_fusion.6), channel_id=1, source_target_pairs={{0,4},{4,0},{8,12},{12,8},{16,20},{20,16},{24,28},{28,24},{1,5},{5... | collective-permute-start | bytes 442376 | tf_op jit(solution)/shard_map/ppermute | solution.py:630

commit v8 on v7

--- a/solution.py
+++ b/solution.py
@@ -216,7 +216,7 @@
     step = 16
     tiles = -(-cols // 128)
     *sends, stats = pl.pallas_call(
-        functools.partial(bias_kernel, groups=groups, batch=2),
+        functools.partial(bias_kernel, groups=groups, batch=16),
         grid=(half // step,),
         in_specs=[
             smem(),
@@ -328,7 +328,7 @@
     tiles = -(-cols // 128)
     out = pl.pallas_call(
         functools.partial(
-            pair_back_kernel, groups=groups, calls=len(grads) // groups, factor=factor, batch=2
+            pair_back_kernel, groups=groups, calls=len(grads) // groups, factor=factor, batch=8
         ),
         grid=(half // step,),
         in_specs=[
@@ -355,7 +355,7 @@
     return order
 
 
-def attention_kernel(group_ref, row_ref, *rest, groups, row_parts, head_size, row_block):
+def attention_kernel(group_ref, row_ref, *rest, groups, row_parts, head_size):
     bias_refs = rest[: row_parts + 2]
     acts_refs = rest[row_parts + 2 : row_parts + 2 + groups]
     acts_refs = acts_refs[:1] + acts_refs[-1:] + acts_refs[1:-1]
@@ -378,7 +378,6 @@
         gk_sum,
         gv_sum,
     ) = rest[groups:]
-    head = pl.program_id(0)
     heads = keep_ref.shape[1] * 2 // row_parts
     group_own = group_ref[0]
     cols, width = acts_refs[0].shape
@@ -387,7 +386,7 @@
     half = bias_refs[0].shape[3]
     rest_lanes = cols - 128
     scale = 1.0 / math.sqrt(head_size)
-    extra = att_sum.shape[1] - part
+    extra = 128 - part % 128
     plain = (query_ref, keys_ref, values_ref, grads_ref)
     turned = (query_t_ref, keys_t_ref, values_t_ref)
 
@@ -395,25 +394,19 @@
     turns += [
         (slot * cols + 128, groups * 128 + slot * rest_lanes, rest_lanes) for slot in range(groups)
     ]
-
-    @pl.when(head == 0)
-    def _():
-        for kind in range(4):
-            lanes = slice(kind * part, (kind + 1) * part)
-            if kind in (0, 3):
-                for slot in range(groups):
-                    plain[kind][slot * cols : (slot + 1) * cols, :] = acts_refs[slot][:, lanes]
-            else:
-                for token, place, count in turns:
-                    slot, inside = divmod(token, cols)
-                    plain[kind][place : place + count, :] = acts_refs[slot][
-                        inside : inside + count, lanes
-                    ]
-            if kind < len(turned):
-                turned[kind][...] = plain[kind][...].T
-        att_sum[...] = jnp.zeros_like(att_sum)
-        gq_sum[...] = jnp.zeros_like(gq_sum)
-        gv_sum[...] = jnp.zeros_like(gv_sum)
+    for kind in range(4):
+        lanes = slice(kind * part, (kind + 1) * part)
+        if kind in (0, 3):
+            for slot in range(groups):
+                plain[kind][slot * cols : (slot + 1) * cols, :] = acts_refs[slot][:, lanes]
+        else:
+            for token, place, count in turns:
+                slot, inside = divmod(token, cols)
+                plain[kind][place : place + count, :] = acts_refs[slot][
+                    inside : inside + count, lanes
+                ]
+        if kind < len(turned):
+            turned[kind][...] = plain[kind][...].T
 
     def places(row_part):
         first = row_part * (2 * half)
@@ -422,96 +415,82 @@
             top = slot * cols + lax.rem(first, cols) + side * half
             yield side, pl.ds(pl.multiple_of(top, 16), half)
 
-    for other in range(row_parts):
-
-        def block(column, which, other=other):
-            if other >= row_parts - 2 and column >= groups // 2:
-                return bias_refs[other + 2][column - groups // 2, 0, which]
-            return bias_refs[other][column, 0, which]
-
-        for side, rows in places(row_ref[0] ^ other):
-            lanes = slice(side * rest_lanes, (side + 1) * rest_lanes)
-            tiles = [block(column, side) for column in range(groups)]
-            tiles += [block(column, 2)[:, lanes] for column in range(groups)]
-            bias_full[rows, :] = jnp.concatenate(tiles, axis=1)
+    def block(other, column, head, which):
+        if other >= row_parts - 2 and column >= groups // 2:
+            return bias_refs[other + 2][column - groups // 2, head, which]
+        return bias_refs[other][column, head, which]
 
     lane = lax.broadcasted_iota(jnp.int32, (1, part), 1)
-    mine = (lane >= head * head_size) & (lane < (head + 1) * head_size)
     zero = jnp.zeros((), BF16)
-    keys_m = jnp.where(mine, keys_ref[...], zero)
-    values_m = jnp.concatenate(
-        [jnp.where(mine, values_ref[...], zero), jnp.ones((tokens, extra), BF16)], axis=1
-    )
-    feature = pl.multiple_of(head * head_size, head_size)
-    query_t = query_t_ref[pl.ds(feature, head_size), :]
-    gk_t = jnp.zeros((head_size, tokens), F32)
-    gv_t = jnp.zeros((part, tokens), F32)
-    for top in range(0, tokens, row_block):
-        rows = slice(top, top + row_block)
-        query = jnp.where(mine, query_ref[rows, :], zero)
-        grads = jnp.where(mine, grads_ref[rows, :], zero)
-        weights = jnp.exp2(mm(query, keys_t_ref[...]) + bias_full[rows, :].astype(F32))
+    order = unit_order(heads)
+    for head in range(heads):
+        bias_head, score_head = bias_full.at[head % 2], score_full.at[head % 2]
+        for other in range(row_parts):
+            for side, rows in places(row_ref[0] ^ other):
+                lanes = slice(side * rest_lanes, (side + 1) * rest_lanes)
+                tiles = [block(other, column, head, side) for column in range(groups)]
+                tiles += [block(other, column, head, 2)[:, lanes] for column in range(groups)]
+                bias_head[rows, :] = jnp.concatenate(tiles, axis=1)
+
+        features = slice(head * head_size, (head + 1) * head_size)
+        mine = (lane >= features.start) & (lane < features.stop)
+        query = jnp.where(mine, query_ref[...], zero)
+        grads = jnp.where(mine, grads_ref[...], zero)
+        keys_m = jnp.where(mine, keys_ref[...], zero)
+        values_m = jnp.concatenate(
+            [jnp.where(mine, values_ref[...], zero), jnp.ones((tokens, extra), BF16)], axis=1
+        )
+        weights = jnp.exp2(mm(query, keys_t_ref[...]) + bias_head[...].astype(F32))
         weights_b = weights.astype(BF16)
         attended = mm(weights_b, values_m)
         inverse = 1.0 / attended[:, part : part + 1]
         attended = attended[:, :part] * inverse
-        att_sum[rows, :part] += attended
         grads = (grads.astype(F32) * inverse).astype(BF16)
         delta = jnp.sum(attended * grads.astype(F32), axis=-1, keepdims=True)
         score = (weights * (mm(grads, values_t_ref[...]) - delta)).astype(BF16)
-        score_full[rows, :] = score
-        gq_sum[rows, :] += mm(score, keys_m)
-        gk_t = gk_t + mm(query_t[:, rows], score)
-        gv_t = gv_t + mm_tn(grads, weights_b)
-    gk_sum[pl.ds(feature, head_size), :] = gk_t
-    gv_sum[...] += gv_t
-
-    order = unit_order(heads)
-
-    def give_back(some_heads):
+        score_head[...] = score
+        grad_query = mm(score, keys_m)
+        grad_value = mm_tn(grads, weights_b)
+        if head == 0:
+            att_sum[...] = attended
+            gq_sum[...] = grad_query
+            gv_sum[...] = grad_value
+        else:
+            att_sum[...] += attended
+            gq_sum[...] += grad_query
+            gv_sum[...] += grad_value
+        gk_sum[features, :] = mm(query_t_ref[features, :], score)
+
         for other in range(row_parts):
-            unit = order.index((other // 2, some_heads[0]))
+            unit = order.index((other // 2, head))
             dbias_ref = give_ref if other % 2 else keep_ref
-            unit = unit + head - some_heads[0]
-            scores = [score_full[rows, :] for _, rows in places(row_ref[0] ^ other)]
-            blocks = []
+            scores = [score_head[rows, :] for _, rows in places(row_ref[0] ^ other)]
             for column in range(groups):
                 start = groups * 128 + column * rest_lanes
-                blocks += [score[:, column * 128 : (column + 1) * 128] for score in scores]
+                blocks = [score[:, column * 128 : (column + 1) * 128] for score in scores]
                 blocks.append(
                     jnp.concatenate(
                         [score[:, start : start + rest_lanes] for score in scores], axis=1
                     )
                 )
-            for column in range(groups):
-                dbias_ref[column, unit] = jnp.stack(blocks[3 * column : 3 * column + 3])
-
-    @pl.when(head < heads // 2)
-    def _():
-        give_back(range(heads // 2))
-
-    @pl.when(head >= heads // 2)
-    def _():
-        give_back(range(heads // 2, heads))
-
-    @pl.when(head == heads - 1)
-    def _():
-        results = (
-            gq_sum[...] * scale,
-            (gk_sum[...] * math.log(2.0)).T,
-            gv_sum[...].T,
-            att_sum[:, :part],
-        )
-        for kind, values in enumerate(results):
-            rounded = values.astype(BF16)
-            lanes = slice(kind * part, (kind + 1) * part)
-            if kind in (0, 3):
-                for slot in range(groups):
-                    out_refs[slot][:, lanes] = rounded[slot * cols : (slot + 1) * cols]
-            else:
-                for token, place, count in turns:
-                    slot, inside = divmod(token, cols)
-                    out_refs[slot][inside : inside + count, lanes] = rounded[place : place + count]
+                dbias_ref[column, unit] = jnp.stack(blocks)
+
+    results = (
+        gq_sum[...] * scale,
+        (gk_sum[...] * math.log(2.0)).T,
+        gv_sum[...].T,
+        att_sum[...],
+    )
+    for kind, values in enumerate(results):
+        rounded = values.astype(BF16)
+        lanes = slice(kind * part, (kind + 1) * part)
+        if kind in (0, 3):
+            for slot in range(groups):
+                out_refs[slot][:, lanes] = rounded[slot * cols : (slot + 1) * cols]
+        else:
+            for token, place, count in turns:
+                slot, inside = divmod(token, cols)
+                out_refs[slot][inside : inside + count, lanes] = rounded[place : place + count]
 
 
 def attention(group_index, row_index, acts, bias, head_size):
@@ -520,35 +499,21 @@
     cols, width = acts[0].shape
     tokens = groups * cols
     part = width // 4
-    _, heads, _, half, lanes = bias[0].shape
-    row_block = tokens
-    padded = (part // 128 + 1) * 128
-    units = (groups, row_parts // 2 * heads, 3, half, lanes)
+    _, heads, _, half, _ = bias[0].shape
+    units = (groups, row_parts // 2 * heads, 3, half, 128)
     *grads, keep, give = pl.pallas_call(
         functools.partial(
-            attention_kernel,
-            groups=groups,
-            row_parts=row_parts,
-            head_size=head_size,
-            row_block=row_block,
+            attention_kernel, groups=groups, row_parts=row_parts, head_size=head_size
         ),
-        grid=(heads,),
-        in_specs=[smem(), smem()]
-        + [
-            pl.BlockSpec((block.shape[0], 1, 3, half, lanes), lambda h: (0, h, 0, 0, 0))
-            for block in bias
-        ]
-        + [pl.BlockSpec((cols, width), lambda h: (0, 0))] * groups,
-        out_specs=[pl.BlockSpec((cols, width), lambda h: (0, 0))] * groups
-        + [pl.BlockSpec(shape, lambda h: (0, 0, 0, 0, 0)) for shape in (units, units)],
+        in_specs=[smem(), smem()] + [vmem()] * (len(bias) + groups),
         out_shape=[jax.ShapeDtypeStruct((cols, width), BF16)] * groups
-        + [jax.ShapeDtypeStruct(shape, BF16) for shape in (units, units)],
+        + [jax.ShapeDtypeStruct(units, BF16)] * 2,
         scratch_shapes=[pltpu.VMEM((tokens, part), BF16) for _ in range(4)]
         + [pltpu.VMEM((part, tokens), BF16) for _ in range(3)]
         + [
-            pltpu.VMEM((tokens, tokens), BF16),
-            pltpu.VMEM((tokens, tokens), BF16),
-            pltpu.VMEM((tokens, padded), F32),
+            pltpu.VMEM((2, tokens, tokens), BF16),
+            pltpu.VMEM((2, tokens, tokens), BF16),
+            pltpu.VMEM((tokens, part), F32),
             pltpu.VMEM((tokens, part), F32),
             pltpu.VMEM((part, tokens), F32),
             pltpu.VMEM((part, tokens), F32),
@@ -577,7 +542,27 @@
     calls,
 ):
     got_refs = rest[: groups * calls]
-    updated_ref, d_single_ref, stage_ref = rest[groups * calls :]
+    updated_ref, d_single_ref, stage_ref, *held_refs, copied = rest[groups * calls :]
+    sources = (
+        w_out_ref,
+        w_query_ref,
+        w_key_ref,
+        w_value_ref,
+        w_gamma_ref,
+        w_beta_ref,
+        w_outgate_ref,
+    )
+    copies = [
+        pltpu.make_async_copy(source, held, copied.at[number])
+        for number, (source, held) in enumerate(zip(sources, held_refs))
+    ]
+    for copy in copies:
+        copy.start()
+
+    def weight(number):
+        copies[number].wait()
+        return held_refs[number][...]
+
     width = stage_ref.shape[3]
     part = width // 4
     for slot in range(groups):
@@ -598,19 +583,19 @@
 
     out_gate = gate_ref[...]
     cond_gamma = gamma_ref[...]
-    block_update = mm(take(3), w_out_ref[...])
+    block_update = mm(take(3), weight(0))
     noised = noised_ref[...].astype(F32)
     updated_ref[...] = (noised + out_gate * block_update).astype(BF16)
     gate_part = cot_ref[...].astype(F32) * block_update
     pre_gate = (gate_part * out_gate * (1.0 - out_gate)).astype(BF16)
-    grad_input = mm_nt(take(0), w_query_ref[...])
-    grad_input += mm_nt(take(1), w_key_ref[...])
-    grad_input += mm_nt(take(2), w_value_ref[...])
+    grad_input = mm_nt(take(0), weight(1))
+    grad_input += mm_nt(take(1), weight(2))
+    grad_input += mm_nt(take(2), weight(3))
     noised_norm, _ = norm_rows(noised)
     pre_gamma = (grad_input * noised_norm * cond_gamma * (1.0 - cond_gamma)).astype(BF16)
-    grad_snorm = mm_nt(pre_gamma, w_gamma_ref[...])
-    grad_snorm += mm_nt(grad_input.astype(BF16), w_beta_ref[...])
-    grad_snorm += mm_nt(pre_gate, w_outgate_ref[...])
+    grad_snorm = mm_nt(pre_gamma, weight(4))
+    grad_snorm += mm_nt(grad_input.astype(BF16), weight(5))
+    grad_snorm += mm_nt(pre_gate, weight(6))
     single_norm, single_inv = norm_rows(single_ref[...].astype(F32))
     d_single_ref[...] = norm_back(grad_snorm, single_norm, single_inv).astype(BF16)
 
@@ -751,12 +736,20 @@
     dbias_back = swap_groups(dbias_own)
     updated, d_part = pl.pallas_call(
         functools.partial(finish_kernel, groups=groups, calls=calls),
-        in_specs=[smem()] + [vmem()] * (12 + groups * calls),
+        in_specs=[smem()]
+        + [vmem()] * 5
+        + [pl.BlockSpec(memory_space=pl.ANY)] * 7
+        + [vmem()] * (groups * calls),
         out_shape=[
             jax.ShapeDtypeStruct((cols, width), BF16),
             jax.ShapeDtypeStruct(single.shape, BF16),
         ],
-        scratch_shapes=[pltpu.VMEM((groups, calls, cols, 4 * width // (groups * calls)), BF16)],
+        scratch_shapes=[pltpu.VMEM((groups, calls, cols, 4 * width // (groups * calls)), BF16)]
+        + [
+            pltpu.VMEM(weight.shape, BF16)
+            for weight in (w_out, w_query, w_key, w_value, w_gamma, w_beta, w_outgate)
+        ]
+        + [pltpu.SemaphoreType.DMA((7,))],
         compiler_params=params(),
     )(
         group_index,

time: 140 us -> 138 us (0.986)
  Pallas kernels: 47.9 us -> 45.6 us
    pallas_call x1, Pallas kernels: 9.45 us -> 8 us  [pair_bias(): pl.pallas_call(functools.partial(bias_kernel, groups=groups, batch=16), g...]
where the time goes in v8:
time: 138 us
  Pallas kernels  45.6 us (33%)
  waiting for transfers between devices  45.4 us (33%)
  starting transfers between devices  39.9 us (29%)
  other arithmetic  3.17 us (2%)
  local copies, waits for them, and re-layouts  2.78 us (2%)
    ppermute x12, starting transfers between devices, swap_groups(): got.append(lax.ppermute(sends[bits], 'grp', perm))  26.7 us
    ppermute x12, waiting for transfers between devices, swap_groups(): got.append(lax.ppermute(sends[bits], 'grp', perm))  23.9 us
    ppermute x18, waiting for transfers between devices, flip_rows(): lax.ppermute(values, 'rows', [(index, index ^ bits) for index in range(ro...  21.5 us
    pallas_call x1, Pallas kernels, attention(): pl.pallas_call(functools.partial(attention_kernel, groups=groups, row_par...  15.2 us
    ppermute x18, starting transfers between devices, flip_rows(): lax.ppermute(values, 'rows', [(index, index ^ bits) for index in range(ro...  13.2 us
    pallas_call x1, Pallas kernels, pair_back(): pl.pallas_call(functools.partial(pair_back_kernel, groups=groups, calls=l...  8.21 us
    pallas_call x1, Pallas kernels, pair_bias(): pl.pallas_call(functools.partial(bias_kernel, groups=groups, batch=16), g...  8 us
    pallas_call x1, Pallas kernels, split_heads(): pl.pallas_call(functools.partial(finish_kernel, groups=groups, calls=call...  7.78 us
  transfers between devices with their start and end apart: 30, of which 17 were waited for; matrix products, arithmetic and copies ran while one was open for 0% of the time, Pallas kernels for 16%

profile of v8, /device:TPU:0, one launch (start us, length us, event | category | flops | bytes accessed | tf_op | source)
XLA Modules:
  0.0 137.7 jit_solution(7156575737376747691)
XLA Ops:
  0.6 8.0 %shard_map.158 = (bf16[4,3,48,128]{3,2,1,0:T(8,128)(2,1)}, bf16[4,3,48,128]{3,2,1,0:T(8,128)(2,1)}, bf16[4,3,48,128]{3,2,1,0:T(8,128)(2,1)}, bf16[4,3,48,128]{3,2,1,0:T(8,128)(2,1)}, f32[2,48,24,192]{3,2,1,0:T(8,128)}) custom-call(s32[1]{0:T(128)} %bitcast.group_ref, s32[1]{0:T(128)} %bitcast.3.rows_ref.row_ref, s32[768]{0:T(1024)} %cols_ref.1, f32[16]{0:T(128)} %gain_ref.1, ...), custom_call_target="tpu_custom_call" | custom-call | tf_op jit(solution)/shard_map/pallas_call | solution.py:218
  8.6 4.0 %collective-permute-start = (bf16[4,3,48,128]{3,2,1,0:T(8,128)(2,1)}, bf16[4,3,48,128]{3,2,1,0:T(8,128)(2,1)S(1)}, u32[]{:S(2)}, u32[]{:S(2)}) collective-permute-start(bf16[4,3,48,128]{3,2,1,0:T(8,128)(2,1)} %get-tuple-element.64), channel_id=1, source_target_pairs={{0,2},{1,3},{2,0},{3,1},{4,6},{5,7},{6,4},{7,5},{8,10},{9,11},{10,... | collective-permute-start | bytes 442376 | tf_op jit(solution)/shard_map/ppermute | solution.py:609
  12.7 1.3 collective-permute-start.1
  14.0 0.2 collective-permute-start.2
  14.3 6.4 %shard_map.157 = (bf16[192,768]{1,0:T(8,128)(2,1)}, bf16[192,768]{1,0:T(8,128)(2,1)}, bf16[192,768]{1,0:T(8,128)(2,1)}, bf16[192,768]{1,0:T(8,128)(2,1)}, f32[192,768]{1,0:T(8,128)}, /*index=5*/f32[192,768]{1,0:T(8,128)}) custom-call(s32[1]{0:T(128)} %bitcast.group_ref, bf16[192,384]{1,0:T(8,128)(2,1)} %single_ref.3, bf16[192,768]{1,0:T(8,128)(2,1)} %bitcast.23, ...), custom_call_target="tpu_custom_call" | custom-call | tf_op jit(solution)/shard_map/pallas_call | solution.py:700
  20.6 3.3 %collective-permute-done = bf16[4,3,48,128]{3,2,1,0:T(8,128)(2,1)S(1)} collective-permute-done((bf16[4,3,48,128]{3,2,1,0:T(8,128)(2,1)}, bf16[4,3,48,128]{3,2,1,0:T(8,128)(2,1)S(1)}, u32[]{:S(2)}, u32[]{:S(2)}) %collective-permute-start) | collective-permute-done | bytes 147488 | tf_op jit(solution)/shard_map/ppermute | solution.py:609
  23.9 0.5 collective-permute-done.2
  24.4 0.1 pad_maximum_fusion.rest_0_
  24.5 1.6 %collective-permute-start.6 = (bf16[4,4,3,48,128]{4,3,2,1,0:T(8,128)(2,1)S(1)}, bf16[4,4,3,48,128]{4,3,2,1,0:T(8,128)(2,1)S(1)}, u32[]{:S(2)}, u32[]{:S(2)}) collective-permute-start(bf16[4,4,3,48,128]{4,3,2,1,0:T(8,128)(2,1)S(1)} %pad_maximum_fusion.rest_0_), channel_id=1, source_target_pairs={{0,16},{4,20},{8,24},{12,28},{16,0},{20,4},{24,8},{28,12},{1,17},{... | collective-permute-start | bytes 1769480 | tf_op jit(solution)/shard_map/ppermute | solution.py:615
  26.2 1.5 %collective-permute-start.4 = (bf16[4,4,3,48,128]{4,3,2,1,0:T(8,128)(2,1)S(1)}, bf16[4,4,3,48,128]{4,3,2,1,0:T(8,128)(2,1)S(1)}, u32[]{:S(2)}, u32[]{:S(2)}) collective-permute-start(bf16[4,4,3,48,128]{4,3,2,1,0:T(8,128)(2,1)S(1)} %pad_maximum_fusion.rest_0_), channel_id=1, source_target_pairs={{0,8},{4,12},{8,0},{12,4},{16,24},{20,28},{24,16},{28,20},{1,9},{5... | collective-permute-start | bytes 1769480 | tf_op jit(solution)/shard_map/ppermute | solution.py:615
  27.7 4.4 %collective-permute-start.8 = (bf16[192,768]{1,0:T(8,128)(2,1)S(1)}, bf16[192,768]{1,0:T(8,128)(2,1)S(1)}, u32[]{:S(2)}, u32[]{:S(2)}) collective-permute-start(bf16[192,768]{1,0:T(8,128)(2,1)S(1)} %copy-done.27), channel_id=1, source_target_pairs={{0,2},{1,3},{2,0},{3,1},{4,6},{5,7},{6,4},{7,5},{8,10},{9,11},{10,... | collective-permute-start | bytes 884744 | tf_op jit(solution)/shard_map/ppermute | solution.py:609
  32.1 0.5 collective-permute-start.9
  32.6 0.1 collective-permute-start.10
  32.7 5.1 %collective-permute-done.6.rest_4_ = bf16[4,4,3,48,128]{4,3,2,1,0:T(8,128)(2,1)S(1)} collective-permute-done((bf16[4,4,3,48,128]{4,3,2,1,0:T(8,128)(2,1)S(1)}, bf16[4,4,3,48,128]{4,3,2,1,0:T(8,128)(2,1)S(1)}, u32[]{:S(2)}, u32[]{:S(2)}) %collective-permute-start.6) | collective-permute-done | bytes 589856 | tf_op jit(solution)/shard_map/ppermute | solution.py:615
  37.9 1.3 collective-permute-start.12
  39.2 0.9 collective-permute-done.4.rest_2_
  40.1 0.6 collective-permute-start.11
  40.7 11.0 %collective-permute-done.8.rest_11_ = bf16[192,768]{1,0:T(8,128)(2,1)S(1)} collective-permute-done((bf16[192,768]{1,0:T(8,128)(2,1)S(1)}, bf16[192,768]{1,0:T(8,128)(2,1)S(1)}, u32[]{:S(2)}, u32[]{:S(2)}) %collective-permute-start.8) | collective-permute-done | bytes 294944 | tf_op jit(solution)/shard_map/ppermute | solution.py:609
  51.8 0.5 collective-permute-start.7
  52.3 0.4 collective-permute-done.10.rest_13_
  52.8 0.6 collective-permute-start.13
  53.3 0.1 collective-permute-start.14
  53.4 0.4 collective-permute-done.3.rest_1_
  53.8 0.8 collective-permute-done.7.rest_5_
  54.6 0.8 collective-permute-done.5.rest_3_
  55.5 0.4 collective-permute-done.13.rest_7_
  55.9 0.4 collective-permute-done.14.rest_9_
  56.4 0.2 copy-done.15
  56.6 0.7 copy-done.16
  57.3 15.2 %shard_map.159 = (bf16[192,768]{1,0:T(8,128)(2,1)}, bf16[192,768]{1,0:T(8,128)(2,1)}, bf16[192,768]{1,0:T(8,128)(2,1)}, bf16[192,768]{1,0:T(8,128)(2,1)}, bf16[4...) custom-call(s32[1]{0:T(128)} %bitcast.group_ref, s32[1]{0:T(128)} %bitcast.3.rows_ref.row_ref, ...), custom_call_target="tpu_custom_call" | custom-call | tf_op jit(solution)/shard_map/pallas_call | solution.py:504
  72.5 0.2 collective-permute-start.15
  72.7 4.6 %collective-permute-done.15 = bf16[4,16,3,48,128]{4,3,2,1,0:T(8,128)(2,1)S(1)} collective-permute-done((bf16[4,16,3,48,128]{4,3,2,1,0:T(8,128)(2,1)}, bf16[4,16,3,48,128]{4,3,2,1,0:T(8,128)(2,1)S(1)}, u32[]{:S(2)}, u32[]{:S(2)}) %collective-permute-start.15) | collective-permute-done | bytes 2359328 | tf_op jit(solution)/shard_map/ppermute | solution.py:615
  77.4 1.7 %add_convert_fusion.3 = (bf16[4,4,3,48,128]{4,3,2,1,0:T(8,128)(2,1)S(1)}, bf16[4,4,3,48,128]{4,3,2,1,0:T(8,128)(2,1)S(1)}) fusion(bf16[4,16,3,48,128]{4,3,2,1,0:T(8,128)(2,1)S(1)} %collective-permute-done.15, bf16[4,16,3,48,128]{4,3,2,1,0:T(8,128)(2,1)} %get-tuple-element.86), kind=kLoop, calls=%fused_computation.3 | loop fusion | flops 2359296 | bytes 3538944 | tf_op jit(solution)/shard_map/convert_element_type | solution.py:644
  79.1 0.6 collective-permute-start.16
  79.7 0.5 collective-permute-start.17
  80.2 4.7 %collective-permute-start.20 = (bf16[192,768]{1,0:T(8,128)(2,1)S(1)}, bf16[192,768]{1,0:T(8,128)(2,1)S(1)}, u32[]{:S(2)}, u32[]{:S(2)}) collective-permute-start(bf16[192,768]{1,0:T(8,128)(2,1)S(1)} %copy-done.25), channel_id=1, source_target_pairs={{0,2},{1,3},{2,0},{3,1},{4,6},{5,7},{6,4},{7,5},{8,10},{9,11},{10,... | collective-permute-start | bytes 884744 | tf_op jit(solution)/shard_map/ppermute | solution.py:609
  84.9 3.3 %collective-permute-start.21 = (bf16[192,768]{1,0:T(8,128)(2,1)S(1)}, bf16[192,768]{1,0:T(8,128)(2,1)S(1)}, u32[]{:S(2)}, u32[]{:S(2)}) collective-permute-start(bf16[192,768]{1,0:T(8,128)(2,1)S(1)} %copy-done.23), channel_id=1, source_target_pairs={{0,3},{1,2},{2,1},{3,0},{4,7},{5,6},{6,5},{7,4},{8,11},{9,10},{10,... | collective-permute-start | bytes 884744 | tf_op jit(solution)/shard_map/ppermute | solution.py:609
  88.2 6.3 %collective-permute-done.16 = bf16[4,4,3,48,128]{4,3,2,1,0:T(8,128)(2,1)S(1)} collective-permute-done((bf16[4,4,3,48,128]{4,3,2,1,0:T(8,128)(2,1)S(1)}, bf16[4,4,3,48,128]{4,3,2,1,0:T(8,128)(2,1)S(1)}, u32[]{:S(2)}, u32[]{:S(2)}) %collective-permute-start.16) | collective-permute-done | bytes 589856 | tf_op jit(solution)/shard_map/ppermute | solution.py:615
  94.5 0.2 collective-permute-done.17
  94.8 0.2 add_convert_fusion.4
  95.0 1.6 %collective-permute-start.19 = (bf16[4,2,3,48,128]{4,3,2,1,0:T(8,128)(2,1)S(1)}, bf16[4,2,3,48,128]{4,3,2,1,0:T(8,128)(2,1)S(1)}, u32[]{:S(2)}, u32[]{:S(2)}) collective-permute-start(bf16[4,2,3,48,128]{4,3,2,1,0:T(8,128)(2,1)S(1)} %get-tuple-element.119), channel_id=1, source_target_pairs={{0,8},{4,12},{8,0},{12,4},{16,24},{20,28},{24,16},{28,20},{1,9},{5... | collective-permute-start | bytes 884744 | tf_op jit(solution)/shard_map/ppermute | solution.py:615
  96.6 0.5 collective-permute-start.18
  97.1 8.4 %collective-permute-done.20.rest_2_ = bf16[192,768]{1,0:T(8,128)(2,1)S(1)} collective-permute-done((bf16[192,768]{1,0:T(8,128)(2,1)S(1)}, bf16[192,768]{1,0:T(8,128)(2,1)S(1)}, u32[]{:S(2)}, u32[]{:S(2)}) %collective-permute-start.20) | collective-permute-done | bytes 294944 | tf_op jit(solution)/shard_map/ppermute | solution.py:609
  105.5 0.2 collective-permute-done.22.rest_1_
  105.8 0.3 add_convert_fusion
  106.1 0.1 copy-done.9
  106.2 0.1 copy-done.11
  106.3 0.1 copy-done.12
  106.4 0.7 slice_bitcast_fusion
  107.1 7.5 %collective-permute-start.26 = (bf16[4,3,48,128]{3,2,1,0:T(8,128)(2,1)S(1)}, bf16[4,3,48,128]{3,2,1,0:T(8,128)(2,1)S(1)}, u32[]{:S(2)}, u32[]{:S(2)}) collective-permute-start(bf16[4,3,48,128]{3,2,1,0:T(8,128)(2,1)S(1)} %get-tuple-element.109), channel_id=1, source_target_pairs={{0,2},{1,3},{2,0},{3,1},{4,6},{5,7},{6,4},{7,5},{8,10},{9,11},{10,... | collective-permute-start | bytes 442376 | tf_op jit(solution)/shard_map/ppermute | solution.py:609
  114.6 0.6 collective-permute-start.27
  115.1 0.0 collective-permute-start.28
  115.1 7.8 %shard_map.160 = (bf16[192,768]{1,0:T(8,128)(2,1)}, bf16[192,384]{1,0:T(8,128)(2,1)}) custom-call(s32[1]{0:T(128)} %bitcast.group_ref, bf16[192,384]{1,0:T(8,128)(2,1)} %single_ref.3, bf16[192,768]{1,0:T(8,128)(2,1)} %bitcast.24, bf16[192,768]{1,0:T(8,128)(2,1)} %bitcast.26, f32[192,768]{1,0:T(8,128)} %get-tuple-element.61.gamma_ref, ...), custom_call_target="tpu_custom_call" | custom-call | tf_op jit(solution)/shard_map/pallas_call | solution.py:737
  122.9 2.5 %collective-permute-start.25 = (bf16[192,384]{1,0:T(8,128)(2,1)}, bf16[192,384]{1,0:T(8,128)(2,1)S(1)}, u32[]{:S(2)}, u32[]{:S(2)}) collective-permute-start(bf16[192,384]{1,0:T(8,128)(2,1)} %get-tuple-element.106), channel_id=1, source_target_pairs={{0,24},{4,28},{8,16},{12,20},{16,8},{20,12},{24,0},{28,4},{1,25},{... | collective-permute-start | bytes 442376 | tf_op jit(solution)/shard_map/ppermute | solution.py:615
  125.4 0.5 collective-permute-start.24
  125.9 0.5 collective-permute-start.23
  126.5 0.1 copy-done.19
  126.6 0.5 copy-done.20
  127.1 0.1 copy-done.21
  127.2 8.2 %shard_map.161 = bf16[2,48,192,128]{3,2,1,0:T(8,128)(2,1)} custom-call(s32[1]{0:T(128)} %bitcast.group_ref, bf16[2,48,192,128]{3,2,1,0:T(8,128)(2,1)} %bitcast.21, f32[2,48,24,192]{3,2,1,0:T(8,128)} %get-tuple-element.107.stats_ref, bf16[16,128]{1,0:T(8,128)(2,1)} %bitcast.32, bf16[4,3,48,128]{3,2,1,0:T(8,128)(2,1)} %get-tuple-element.108.rest_0_, ...), custom_call_target="tpu_custom_call" | custom-call | tf_op jit(solution)/shard_map/pallas_call | solution.py:329
  135.4 0.1 add_convert_fusion.6
  135.5 0.1 collective-permute-start.29
  135.6 1.4 collective-permute-done.29
  137.0 0.7 convert_add_fusion
  (68 shorter events, 0.2 us)
Async XLA Ops:
  8.6 15.3 %collective-permute-start = (bf16[4,3,48,128]{3,2,1,0:T(8,128)(2,1)}, bf16[4,3,48,128]{3,2,1,0:T(8,128)(2,1)S(1)}, u32[]{:S(2)}, u32[]{:S(2)}) collective-permute-start(bf16[4,3,48,128]{3,2,1,0:T(8,128)(2,1)} %get-tuple-element.64), channel_id=1, source_target_pairs={{0,2},{1,3},{2,0},{3,1},{4,6},{5,7},{6,4},{7,5},{8,10},{9,11},{10,... | collective-permute-start | bytes 442376 | tf_op jit(solution)/shard_map/ppermute | solution.py:609
  12.7 11.3 %collective-permute-start.1 = (bf16[4,3,48,128]{3,2,1,0:T(8,128)(2,1)}, bf16[4,3,48,128]{3,2,1,0:T(8,128)(2,1)S(1)}, u32[]{:S(2)}, u32[]{:S(2)}) collective-permute-start(bf16[4,3,48,128]{3,2,1,0:T(8,128)(2,1)} %get-tuple-element.65), channel_id=1, source_target_pairs={{0,3},{1,2},{2,1},{3,0},{4,7},{5,6},{6,5},{7,4},{8,11},{9,10},{10,... | collective-permute-start | bytes 442376 | tf_op jit(solution)/shard_map/ppermute | solution.py:609
  14.0 10.4 %collective-permute-start.2 = (bf16[4,3,48,128]{3,2,1,0:T(8,128)(2,1)}, bf16[4,3,48,128]{3,2,1,0:T(8,128)(2,1)S(1)}, u32[]{:S(2)}, u32[]{:S(2)}) collective-permute-start(bf16[4,3,48,128]{3,2,1,0:T(8,128)(2,1)} %get-tuple-element.66), channel_id=1, source_target_pairs={{0,1},{1,0},{2,3},{3,2},{4,5},{5,4},{6,7},{7,6},{8,9},{9,8},{10,11... | collective-permute-start | bytes 442376 | tf_op jit(solution)/shard_map/ppermute | solution.py:609
  14.3 10.2 %copy-start.17 = (bf16[4,3,48,128]{3,2,1,0:T(8,128)(2,1)S(1)}, bf16[4,3,48,128]{3,2,1,0:T(8,128)(2,1)}, u32[]{:S(2)}) copy-start(bf16[4,3,48,128]{3,2,1,0:T(8,128)(2,1)} %get-tuple-element.74) | copy-start | bytes 442372
  20.6 7.0 %copy-start.27 = (bf16[192,768]{1,0:T(8,128)(2,1)S(1)}, bf16[192,768]{1,0:T(8,128)(2,1)}, u32[]{:S(2)}) copy-start(bf16[192,768]{1,0:T(8,128)(2,1)} %get-tuple-element.71) | copy-start | bytes 884740
  20.6 11.5 %copy-start.26 = (bf16[192,768]{1,0:T(8,128)(2,1)S(1)}, bf16[192,768]{1,0:T(8,128)(2,1)}, u32[]{:S(2)}) copy-start(bf16[192,768]{1,0:T(8,128)(2,1)} %get-tuple-element.72) | copy-start | bytes 884740
  20.6 12.0 %copy-start.24 = (bf16[192,768]{1,0:T(8,128)(2,1)S(1)}, bf16[192,768]{1,0:T(8,128)(2,1)}, u32[]{:S(2)}) copy-start(bf16[192,768]{1,0:T(8,128)(2,1)} %get-tuple-element.73) | copy-start | bytes 884740
  24.5 31.8 %copy-start = (bf16[4,4,3,48,128]{4,3,2,1,0:T(8,128)(2,1)}, bf16[4,4,3,48,128]{4,3,2,1,0:T(8,128)(2,1)S(1)}, u32[]{:S(2)}) copy-start(bf16[4,4,3,48,128]{4,3,2,1,0:T(8,128)(2,1)S(1)} %pad_maximum_fusion.rest_0_) | copy-start | bytes 1769476
  24.5 13.3 %collective-permute-start.6 = (bf16[4,4,3,48,128]{4,3,2,1,0:T(8,128)(2,1)S(1)}, bf16[4,4,3,48,128]{4,3,2,1,0:T(8,128)(2,1)S(1)}, u32[]{:S(2)}, u32[]{:S(2)}) collective-permute-start(bf16[4,4,3,48,128]{4,3,2,1,0:T(8,128)(2,1)S(1)} %pad_maximum_fusion.rest_0_), channel_id=1, source_target_pairs={{0,16},{4,20},{8,24},{12,28},{16,0},{20,4},{24,8},{28,12},{1,17},{... | collective-permute-start | bytes 1769480 | tf_op jit(solution)/shard_map/ppermute | solution.py:615
  26.2 13.9 %collective-permute-start.4 = (bf16[4,4,3,48,128]{4,3,2,1,0:T(8,128)(2,1)S(1)}, bf16[4,4,3,48,128]{4,3,2,1,0:T(8,128)(2,1)S(1)}, u32[]{:S(2)}, u32[]{:S(2)}) collective-permute-start(bf16[4,4,3,48,128]{4,3,2,1,0:T(8,128)(2,1)S(1)} %pad_maximum_fusion.rest_0_), channel_id=1, source_target_pairs={{0,8},{4,12},{8,0},{12,4},{16,24},{20,28},{24,16},{28,20},{1,9},{5... | collective-permute-start | bytes 1769480 | tf_op jit(solution)/shard_map/ppermute | solution.py:615
  27.7 24.1 %collective-permute-start.8 = (bf16[192,768]{1,0:T(8,128)(2,1)S(1)}, bf16[192,768]{1,0:T(8,128)(2,1)S(1)}, u32[]{:S(2)}, u32[]{:S(2)}) collective-permute-start(bf16[192,768]{1,0:T(8,128)(2,1)S(1)} %copy-done.27), channel_id=1, source_target_pairs={{0,2},{1,3},{2,0},{3,1},{4,6},{5,7},{6,4},{7,5},{8,10},{9,11},{10,... | collective-permute-start | bytes 884744 | tf_op jit(solution)/shard_map/ppermute | solution.py:609
  32.1 19.7 %collective-permute-start.9 = (bf16[192,768]{1,0:T(8,128)(2,1)S(1)}, bf16[192,768]{1,0:T(8,128)(2,1)S(1)}, u32[]{:S(2)}, u32[]{:S(2)}) collective-permute-start(bf16[192,768]{1,0:T(8,128)(2,1)S(1)} %copy-done.26), channel_id=1, source_target_pairs={{0,3},{1,2},{2,1},{3,0},{4,7},{5,6},{6,5},{7,4},{8,11},{9,10},{10,... | collective-permute-start | bytes 884744 | tf_op jit(solution)/shard_map/ppermute | solution.py:609
  32.6 20.1 %collective-permute-start.10 = (bf16[192,768]{1,0:T(8,128)(2,1)S(1)}, bf16[192,768]{1,0:T(8,128)(2,1)S(1)}, u32[]{:S(2)}, u32[]{:S(2)}) collective-permute-start(bf16[192,768]{1,0:T(8,128)(2,1)S(1)} %copy-done.24), channel_id=1, source_target_pairs={{0,1},{1,0},{2,3},{3,2},{4,5},{5,4},{6,7},{7,6},{8,9},{9,8},{10,11... | collective-permute-start | bytes 884744 | tf_op jit(solution)/shard_map/ppermute | solution.py:609
  37.8 18.5 %copy-start.2 = (bf16[4,4,3,48,128]{4,3,2,1,0:T(8,128)(2,1)}, bf16[4,4,3,48,128]{4,3,2,1,0:T(8,128)(2,1)S(1)}, u32[]{:S(2)}) copy-start(bf16[4,4,3,48,128]{4,3,2,1,0:T(8,128)(2,1)S(1)} %collective-permute-done.6.rest_4_) | copy-start | bytes 1769476
  37.9 14.9 %collective-permute-start.12 = (bf16[2,4,3,48,128]{4,3,2,1,0:T(8,128)(2,1)S(1)}, bf16[2,4,3,48,128]{4,3,2,1,0:T(8,128)(2,1)S(1)}, u32[]{:S(2)}, u32[]{:S(2)}) collective-permute-start(bf16[2,4,3,48,128]{4,3,2,1,0:T(8,128)(2,1)S(1)} %slice.81), channel_id=1, source_target_pairs={{0,8},{4,12},{8,0},{12,4},{16,24},{20,28},{24,16},{28,20},{1,9},{5... | collective-permute-start | bytes 884744 | tf_op jit(solution)/shard_map/ppermute | solution.py:615
  40.1 16.2 %copy-start.3 = (bf16[4,4,3,48,128]{4,3,2,1,0:T(8,128)(2,1)}, bf16[4,4,3,48,128]{4,3,2,1,0:T(8,128)(2,1)S(1)}, u32[]{:S(2)}) copy-start(bf16[4,4,3,48,128]{4,3,2,1,0:T(8,128)(2,1)S(1)} %collective-permute-done.4.rest_2_) | copy-start | bytes 1769476
  40.1 12.6 %collective-permute-start.11 = (bf16[2,4,3,48,128]{4,3,2,1,0:T(8,128)(2,1)S(1)}, bf16[2,4,3,48,128]{4,3,2,1,0:T(8,128)(2,1)S(1)}, u32[]{:S(2)}, u32[]{:S(2)}) collective-permute-start(bf16[2,4,3,48,128]{4,3,2,1,0:T(8,128)(2,1)S(1)} %slice.80), channel_id=1, source_target_pairs={{0,16},{4,20},{8,24},{12,28},{16,0},{20,4},{24,8},{28,12},{1,17},{... | collective-permute-start | bytes 884744 | tf_op jit(solution)/shard_map/ppermute | solution.py:615
  51.8 4.6 %copy-start.7 = (bf16[192,768]{1,0:T(8,128)(2,1)}, bf16[192,768]{1,0:T(8,128)(2,1)S(1)}, u32[]{:S(2)}) copy-start(bf16[192,768]{1,0:T(8,128)(2,1)S(1)} %collective-permute-done.8.rest_11_) | copy-start | bytes 884740
  51.8 2.0 %collective-permute-start.3 = (bf16[4,4,3,48,128]{4,3,2,1,0:T(8,128)(2,1)S(1)}, bf16[4,4,3,48,128]{4,3,2,1,0:T(8,128)(2,1)S(1)}, u32[]{:S(2)}, u32[]{:S(2)}) collective-permute-start(bf16[4,4,3,48,128]{4,3,2,1,0:T(8,128)(2,1)S(1)} %pad_maximum_fusion.rest_0_), channel_id=1, source_target_pairs={{0,4},{4,0},{8,12},{12,8},{16,20},{20,16},{24,28},{28,24},{1,5},{5... | collective-permute-start | bytes 1769480 | tf_op jit(solution)/shard_map/ppermute | solution.py:615
  51.8 4.5 %copy-start.8 = (bf16[192,768]{1,0:T(8,128)(2,1)}, bf16[192,768]{1,0:T(8,128)(2,1)S(1)}, u32[]{:S(2)}) copy-start(bf16[192,768]{1,0:T(8,128)(2,1)S(1)} %collective-permute-done.9.rest_12_) | copy-start | bytes 884740
  51.8 2.8 %collective-permute-start.7 = (bf16[4,4,3,48,128]{4,3,2,1,0:T(8,128)(2,1)S(1)}, bf16[4,4,3,48,128]{4,3,2,1,0:T(8,128)(2,1)S(1)}, u32[]{:S(2)}, u32[]{:S(2)}) collective-permute-start(bf16[4,4,3,48,128]{4,3,2,1,0:T(8,128)(2,1)S(1)} %collective-permute-done.6.rest_4_), channel_id=1, source_target_pairs={{0,4},{4,0},{8,12},{12,8},{16,20},{20,16},{24,28},{28,24},{1,5},{5... | collective-permute-start | bytes 1769480 | tf_op jit(solution)/shard_map/ppermute | solution.py:615
  52.7 3.6 %copy-start.10 = (bf16[192,768]{1,0:T(8,128)(2,1)}, bf16[192,768]{1,0:T(8,128)(2,1)S(1)}, u32[]{:S(2)}) copy-start(bf16[192,768]{1,0:T(8,128)(2,1)S(1)} %collective-permute-done.10.rest_13_) | copy-start | bytes 884740
  52.7 2.8 %collective-permute-start.5 = (bf16[4,4,3,48,128]{4,3,2,1,0:T(8,128)(2,1)S(1)}, bf16[4,4,3,48,128]{4,3,2,1,0:T(8,128)(2,1)S(1)}, u32[]{:S(2)}, u32[]{:S(2)}) collective-permute-start(bf16[4,4,3,48,128]{4,3,2,1,0:T(8,128)(2,1)S(1)} %collective-permute-done.4.rest_2_), channel_id=1, source_target_pairs={{0,4},{4,0},{8,12},{12,8},{16,20},{20,16},{24,28},{28,24},{1,5},{5... | collective-permute-start | bytes 1769480 | tf_op jit(solution)/shard_map/ppermute | solution.py:615
  52.7 3.6 %copy-start.13 = (bf16[2,4,3,48,128]{4,3,2,1,0:T(8,128)(2,1)}, bf16[2,4,3,48,128]{4,3,2,1,0:T(8,128)(2,1)S(1)}, u32[]{:S(2)}) copy-start(bf16[2,4,3,48,128]{4,3,2,1,0:T(8,128)(2,1)S(1)} %collective-permute-done.12.rest_8_) | copy-start | bytes 884740
  52.7 3.6 %copy-start.14 = (bf16[2,4,3,48,128]{4,3,2,1,0:T(8,128)(2,1)}, bf16[2,4,3,48,128]{4,3,2,1,0:T(8,128)(2,1)S(1)}, u32[]{:S(2)}) copy-start(bf16[2,4,3,48,128]{4,3,2,1,0:T(8,128)(2,1)S(1)} %collective-permute-done.11.rest_6_) | copy-start | bytes 884740
  52.8 3.1 %collective-permute-start.13 = (bf16[2,4,3,48,128]{4,3,2,1,0:T(8,128)(2,1)S(1)}, bf16[2,4,3,48,128]{4,3,2,1,0:T(8,128)(2,1)S(1)}, u32[]{:S(2)}, u32[]{:S(2)}) collective-permute-start(bf16[2,4,3,48,128]{4,3,2,1,0:T(8,128)(2,1)S(1)} %collective-permute-done.11.rest_6_), channel_id=1, source_target_pairs={{0,4},{4,0},{8,12},{12,8},{16,20},{20,16},{24,28},{28,24},{1,5},{5... | collective-permute-start | bytes 884744 | tf_op jit(solution)/shard_map/ppermute | solution.py:615
  53.3 3.0 %collective-permute-start.14 = (bf16[2,4,3,48,128]{4,3,2,1,0:T(8,128)(2,1)S(1)}, bf16[2,4,3,48,128]{4,3,2,1,0:T(8,128)(2,1)S(1)}, u32[]{:S(2)}, u32[]{:S(2)}) collective-permute-start(bf16[2,4,3,48,128]{4,3,2,1,0:T(8,128)(2,1)S(1)} %collective-permute-done.12.rest_8_), channel_id=1, source_target_pairs={{0,4},{4,0},{8,12},{12,8},{16,20},{20,16},{24,28},{28,24},{1,5},{5... | collective-permute-start | bytes 884744 | tf_op jit(solution)/shard_map/ppermute | solution.py:615
  53.8 2.6 %copy-start.4 = (bf16[4,4,3,48,128]{4,3,2,1,0:T(8,128)(2,1)}, bf16[4,4,3,48,128]{4,3,2,1,0:T(8,128)(2,1)S(1)}, u32[]{:S(2)}) copy-start(bf16[4,4,3,48,128]{4,3,2,1,0:T(8,128)(2,1)S(1)} %collective-permute-done.3.rest_1_) | copy-start | bytes 1769476
  54.6 1.8 %copy-start.5 = (bf16[4,4,3,48,128]{4,3,2,1,0:T(8,128)(2,1)}, bf16[4,4,3,48,128]{4,3,2,1,0:T(8,128)(2,1)S(1)}, u32[]{:S(2)}) copy-start(bf16[4,4,3,48,128]{4,3,2,1,0:T(8,128)(2,1)S(1)} %collective-permute-done.7.rest_5_) | copy-start | bytes 1769476
  55.5 0.9 copy-start.6
  55.9 0.7 copy-start.15
  56.6 0.7 copy-start.16
  72.5 4.8 %collective-permute-start.15 = (bf16[4,16,3,48,128]{4,3,2,1,0:T(8,128)(2,1)}, bf16[4,16,3,48,128]{4,3,2,1,0:T(8,128)(2,1)S(1)}, u32[]{:S(2)}, u32[]{:S(2)}) collective-permute-start(bf16[4,16,3,48,128]{4,3,2,1,0:T(8,128)(2,1)} %get-tuple-element.87), channel_id=1, source_target_pairs={{0,4},{4,0},{8,12},{12,8},{16,20},{20,16},{24,28},{28,24},{1,5},{5... | collective-permute-start | bytes 7077896 | tf_op jit(solution)/shard_map/ppermute | solution.py:615
  77.3 2.9 %copy-start.25 = (bf16[192,768]{1,0:T(8,128)(2,1)S(1)}, bf16[192,768]{1,0:T(8,128)(2,1)}, u32[]{:S(2)}) copy-start(bf16[192,768]{1,0:T(8,128)(2,1)} %get-tuple-element.89) | copy-start | bytes 884740
  77.4 7.6 %copy-start.23 = (bf16[192,768]{1,0:T(8,128)(2,1)S(1)}, bf16[192,768]{1,0:T(8,128)(2,1)}, u32[]{:S(2)}) copy-start(bf16[192,768]{1,0:T(8,128)(2,1)} %get-tuple-element.90) | copy-start | bytes 884740
  77.4 10.9 %copy-start.22 = (bf16[192,768]{1,0:T(8,128)(2,1)S(1)}, bf16[192,768]{1,0:T(8,128)(2,1)}, u32[]{:S(2)}) copy-start(bf16[192,768]{1,0:T(8,128)(2,1)} %get-tuple-element.91) | copy-start | bytes 884740
  77.4 17.4 %copy-start.1 = (bf16[4,16,3,48,128]{4,3,2,1,0:T(8,128)(2,1)S(1)}, bf16[4,16,3,48,128]{4,3,2,1,0:T(8,128)(2,1)}, u32[]{:S(2)}) copy-start(bf16[4,16,3,48,128]{4,3,2,1,0:T(8,128)(2,1)} %get-tuple-element.86) | copy-start | bytes 7077892
  79.1 15.4 %collective-permute-start.16 = (bf16[4,4,3,48,128]{4,3,2,1,0:T(8,128)(2,1)S(1)}, bf16[4,4,3,48,128]{4,3,2,1,0:T(8,128)(2,1)S(1)}, u32[]{:S(2)}, u32[]{:S(2)}) collective-permute-start(bf16[4,4,3,48,128]{4,3,2,1,0:T(8,128)(2,1)S(1)} %get-tuple-element.121), channel_id=1, source_target_pairs={{0,8},{4,12},{8,0},{12,4},{16,24},{20,28},{24,16},{28,20},{1,9},{5... | collective-permute-start | bytes 1769480 | tf_op jit(solution)/shard_map/ppermute | solution.py:615
  79.7 15.1 %collective-permute-start.17 = (bf16[4,4,3,48,128]{4,3,2,1,0:T(8,128)(2,1)S(1)}, bf16[4,4,3,48,128]{4,3,2,1,0:T(8,128)(2,1)S(1)}, u32[]{:S(2)}, u32[]{:S(2)}) collective-permute-start(bf16[4,4,3,48,128]{4,3,2,1,0:T(8,128)(2,1)S(1)} %get-tuple-element.122), channel_id=1, source_target_pairs={{0,16},{4,20},{8,24},{12,28},{16,0},{20,4},{24,8},{28,12},{1,17},{... | collective-permute-start | bytes 1769480 | tf_op jit(solution)/shard_map/ppermute | solution.py:615
  80.2 25.3 %collective-permute-start.20 = (bf16[192,768]{1,0:T(8,128)(2,1)S(1)}, bf16[192,768]{1,0:T(8,128)(2,1)S(1)}, u32[]{:S(2)}, u32[]{:S(2)}) collective-permute-start(bf16[192,768]{1,0:T(8,128)(2,1)S(1)} %copy-done.25), channel_id=1, source_target_pairs={{0,2},{1,3},{2,0},{3,1},{4,6},{5,7},{6,4},{7,5},{8,10},{9,11},{10,... | collective-permute-start | bytes 884744 | tf_op jit(solution)/shard_map/ppermute | solution.py:609
  84.9 20.6 %collective-permute-start.21 = (bf16[192,768]{1,0:T(8,128)(2,1)S(1)}, bf16[192,768]{1,0:T(8,128)(2,1)S(1)}, u32[]{:S(2)}, u32[]{:S(2)}) collective-permute-start(bf16[192,768]{1,0:T(8,128)(2,1)S(1)} %copy-done.23), channel_id=1, source_target_pairs={{0,3},{1,2},{2,1},{3,0},{4,7},{5,6},{6,5},{7,4},{8,11},{9,10},{10,... | collective-permute-start | bytes 884744 | tf_op jit(solution)/shard_map/ppermute | solution.py:609
  88.2 17.5 %collective-permute-start.22 = (bf16[192,768]{1,0:T(8,128)(2,1)S(1)}, bf16[192,768]{1,0:T(8,128)(2,1)S(1)}, u32[]{:S(2)}, u32[]{:S(2)}) collective-permute-start(bf16[192,768]{1,0:T(8,128)(2,1)S(1)} %copy-done.22), channel_id=1, source_target_pairs={{0,1},{1,0},{2,3},{3,2},{4,5},{5,4},{6,7},{7,6},{8,9},{9,8},{10,11... | collective-permute-start | bytes 884744 | tf_op jit(solution)/shard_map/ppermute | solution.py:609
  95.0 10.7 %collective-permute-start.19 = (bf16[4,2,3,48,128]{4,3,2,1,0:T(8,128)(2,1)S(1)}, bf16[4,2,3,48,128]{4,3,2,1,0:T(8,128)(2,1)S(1)}, u32[]{:S(2)}, u32[]{:S(2)}) collective-permute-start(bf16[4,2,3,48,128]{4,3,2,1,0:T(8,128)(2,1)S(1)} %get-tuple-element.119), channel_id=1, source_target_pairs={{0,8},{4,12},{8,0},{12,4},{16,24},{20,28},{24,16},{28,20},{1,9},{5... | collective-permute-start | bytes 884744 | tf_op jit(solution)/shard_map/ppermute | solution.py:615
  96.6 9.2 %collective-permute-start.18 = (bf16[4,2,3,48,128]{4,3,2,1,0:T(8,128)(2,1)S(1)}, bf16[4,2,3,48,128]{4,3,2,1,0:T(8,128)(2,1)S(1)}, u32[]{:S(2)}, u32[]{:S(2)}) collective-permute-start(bf16[4,2,3,48,128]{4,3,2,1,0:T(8,128)(2,1)S(1)} %get-tuple-element.120), channel_id=1, source_target_pairs={{0,16},{4,20},{8,24},{12,28},{16,0},{20,4},{24,8},{28,12},{1,17},{... | collective-permute-start | bytes 884744 | tf_op jit(solution)/shard_map/ppermute | solution.py:615
  105.5 0.7 copy-start.9
  105.5 0.8 copy-start.11
  105.7 0.7 copy-start.12
  107.1 18.8 %collective-permute-start.26 = (bf16[4,3,48,128]{3,2,1,0:T(8,128)(2,1)S(1)}, bf16[4,3,48,128]{3,2,1,0:T(8,128)(2,1)S(1)}, u32[]{:S(2)}, u32[]{:S(2)}) collective-permute-start(bf16[4,3,48,128]{3,2,1,0:T(8,128)(2,1)S(1)} %get-tuple-element.109), channel_id=1, source_target_pairs={{0,2},{1,3},{2,0},{3,1},{4,6},{5,7},{6,4},{7,5},{8,10},{9,11},{10,... | collective-permute-start | bytes 442376 | tf_op jit(solution)/shard_map/ppermute | solution.py:609
  114.6 11.9 %collective-permute-start.27 = (bf16[4,3,48,128]{3,2,1,0:T(8,128)(2,1)S(1)}, bf16[4,3,48,128]{3,2,1,0:T(8,128)(2,1)S(1)}, u32[]{:S(2)}, u32[]{:S(2)}) collective-permute-start(bf16[4,3,48,128]{3,2,1,0:T(8,128)(2,1)S(1)} %get-tuple-element.110), channel_id=1, source_target_pairs={{0,3},{1,2},{2,1},{3,0},{4,7},{5,6},{6,5},{7,4},{8,11},{9,10},{10,... | collective-permute-start | bytes 442376 | tf_op jit(solution)/shard_map/ppermute | solution.py:609
  115.1 11.4 %collective-permute-start.28 = (bf16[4,3,48,128]{3,2,1,0:T(8,128)(2,1)S(1)}, bf16[4,3,48,128]{3,2,1,0:T(8,128)(2,1)S(1)}, u32[]{:S(2)}, u32[]{:S(2)}) collective-permute-start(bf16[4,3,48,128]{3,2,1,0:T(8,128)(2,1)S(1)} %get-tuple-element.111), channel_id=1, source_target_pairs={{0,1},{1,0},{2,3},{3,2},{4,5},{5,4},{6,7},{7,6},{8,9},{9,8},{10,11... | collective-permute-start | bytes 442376 | tf_op jit(solution)/shard_map/ppermute | solution.py:609
  122.9 12.5 %collective-permute-start.25 = (bf16[192,384]{1,0:T(8,128)(2,1)}, bf16[192,384]{1,0:T(8,128)(2,1)S(1)}, u32[]{:S(2)}, u32[]{:S(2)}) collective-permute-start(bf16[192,384]{1,0:T(8,128)(2,1)} %get-tuple-element.106), channel_id=1, source_target_pairs={{0,24},{4,28},{8,16},{12,20},{16,8},{20,12},{24,0},{28,4},{1,25},{... | collective-permute-start | bytes 442376 | tf_op jit(solution)/shard_map/ppermute | solution.py:615
  125.4 10.0 %collective-permute-start.24 = (bf16[192,384]{1,0:T(8,128)(2,1)}, bf16[192,384]{1,0:T(8,128)(2,1)S(1)}, u32[]{:S(2)}, u32[]{:S(2)}) collective-permute-start(bf16[192,384]{1,0:T(8,128)(2,1)} %get-tuple-element.106), channel_id=1, source_target_pairs={{0,16},{4,20},{8,24},{12,28},{16,0},{20,4},{24,8},{28,12},{1,17},{... | collective-permute-start | bytes 442376 | tf_op jit(solution)/shard_map/ppermute | solution.py:615
  125.9 0.7 copy-start.19
  125.9 9.5 %collective-permute-start.23 = (bf16[192,384]{1,0:T(8,128)(2,1)}, bf16[192,384]{1,0:T(8,128)(2,1)S(1)}, u32[]{:S(2)}, u32[]{:S(2)}) collective-permute-start(bf16[192,384]{1,0:T(8,128)(2,1)} %get-tuple-element.106), channel_id=1, source_target_pairs={{0,8},{4,12},{8,0},{12,4},{16,24},{20,28},{24,16},{28,20},{1,9},{5... | collective-permute-start | bytes 442376 | tf_op jit(solution)/shard_map/ppermute | solution.py:615
  126.5 0.7 copy-start.20
  126.5 0.7 copy-start.21
  127.2 8.2 %copy-start.18 = (bf16[192,384]{1,0:T(8,128)(2,1)S(1)}, bf16[192,384]{1,0:T(8,128)(2,1)}, u32[]{:S(2)}) copy-start(bf16[192,384]{1,0:T(8,128)(2,1)} %get-tuple-element.106) | copy-start | bytes 442372
  135.5 1.4 %collective-permute-start.29 = (bf16[192,384]{1,0:T(8,128)(2,1)S(1)}, bf16[192,384]{1,0:T(8,128)(2,1)S(1)}, u32[]{:S(2)}, u32[]{:S(2)}) collective-permute-start(bf16[192,384]{1,0:T(8,128)(2,1)S(1)} %add_convert_fusion.6), channel_id=1, source_target_pairs={{0,4},{4,0},{8,12},{12,8},{16,20},{20,16},{24,28},{28,24},{1,5},{5... | collective-permute-start | bytes 442376 | tf_op jit(solution)/shard_map/ppermute | solution.py:615

commit v9 on v8

--- a/solution.py
+++ b/solution.py
@@ -356,12 +356,16 @@
 
 
 def attention_kernel(group_ref, row_ref, *rest, groups, row_parts, head_size):
-    bias_refs = rest[: row_parts + 2]
+    bias_sources = rest[: row_parts + 2]
     acts_refs = rest[row_parts + 2 : row_parts + 2 + groups]
     acts_refs = acts_refs[:1] + acts_refs[-1:] + acts_refs[1:-1]
     rest = rest[row_parts + 2 + groups :]
     out_refs = rest[:groups]
+    bias_refs = rest[-row_parts - 4 : -2]
+    bias_done, back_done = rest[-2:]
     (
+        keep_out,
+        give_out,
         keep_ref,
         give_ref,
         query_ref,
@@ -377,8 +381,21 @@
         gq_sum,
         gk_sum,
         gv_sum,
-    ) = rest[groups:]
+    ) = rest[groups : -row_parts - 4]
     heads = keep_ref.shape[1] * 2 // row_parts
+    coming = [
+        [
+            pltpu.make_async_copy(
+                source.at[:, head], bias_refs[number].at[:, head], bias_done.at[head, number]
+            )
+            for number, source in enumerate(bias_sources)
+        ]
+        for head in range(heads)
+    ]
+    for head_copies in coming:
+        for copy in head_copies:
+            copy.start()
+    going = []
     group_own = group_ref[0]
     cols, width = acts_refs[0].shape
     tokens = groups * cols
@@ -425,6 +442,8 @@
     order = unit_order(heads)
     for head in range(heads):
         bias_head, score_head = bias_full.at[head % 2], score_full.at[head % 2]
+        for copy in coming[head]:
+            copy.wait()
         for other in range(row_parts):
             for side, rows in places(row_ref[0] ^ other):
                 lanes = slice(side * rest_lanes, (side + 1) * rest_lanes)
@@ -474,6 +493,12 @@
                     )
                 )
                 dbias_ref[column, unit] = jnp.stack(blocks)
+            target = give_out if other % 2 else keep_out
+            copy = pltpu.make_async_copy(
+                dbias_ref.at[:, unit], target.at[:, unit], back_done.at[head, other]
+            )
+            copy.start()
+            going.append(copy)
 
     results = (
         gq_sum[...] * scale,
@@ -491,6 +516,8 @@
             for token, place, count in turns:
                 slot, inside = divmod(token, cols)
                 out_refs[slot][inside : inside + count, lanes] = rounded[place : place + count]
+    for copy in going:
+        copy.wait()
 
 
 def attention(group_index, row_index, acts, bias, head_size):
@@ -501,14 +528,17 @@
     part = width // 4
     _, heads, _, half, _ = bias[0].shape
     units = (groups, row_parts // 2 * heads, 3, half, 128)
+    anywhere = pl.BlockSpec(memory_space=pl.ANY)
     *grads, keep, give = pl.pallas_call(
         functools.partial(
             attention_kernel, groups=groups, row_parts=row_parts, head_size=head_size
         ),
-        in_specs=[smem(), smem()] + [vmem()] * (len(bias) + groups),
+        in_specs=[smem(), smem()] + [anywhere] * len(bias) + [vmem()] * groups,
+        out_specs=[vmem()] * groups + [anywhere] * 2,
         out_shape=[jax.ShapeDtypeStruct((cols, width), BF16)] * groups
         + [jax.ShapeDtypeStruct(units, BF16)] * 2,
-        scratch_shapes=[pltpu.VMEM((tokens, part), BF16) for _ in range(4)]
+        scratch_shapes=[pltpu.VMEM(units, BF16) for _ in range(2)]
+        + [pltpu.VMEM((tokens, part), BF16) for _ in range(4)]
         + [pltpu.VMEM((part, tokens), BF16) for _ in range(3)]
         + [
             pltpu.VMEM((2, tokens, tokens), BF16),
@@ -517,6 +547,11 @@
             pltpu.VMEM((tokens, part), F32),
             pltpu.VMEM((part, tokens), F32),
             pltpu.VMEM((part, tokens), F32),
+        ]
+        + [pltpu.VMEM(block.shape, BF16) for block in bias]
+        + [
+            pltpu.SemaphoreType.DMA((heads, len(bias))),
+            pltpu.SemaphoreType.DMA((heads, row_parts)),
         ],
         compiler_params=params(),
     )(group_index, row_index, *bias, acts[0], *acts[2:], acts[1])
@@ -542,27 +577,7 @@
     calls,
 ):
     got_refs = rest[: groups * calls]
-    updated_ref, d_single_ref, stage_ref, *held_refs, copied = rest[groups * calls :]
-    sources = (
-        w_out_ref,
-        w_query_ref,
-        w_key_ref,
-        w_value_ref,
-        w_gamma_ref,
-        w_beta_ref,
-        w_outgate_ref,
-    )
-    copies = [
-        pltpu.make_async_copy(source, held, copied.at[number])
-        for number, (source, held) in enumerate(zip(sources, held_refs))
-    ]
-    for copy in copies:
-        copy.start()
-
-    def weight(number):
-        copies[number].wait()
-        return held_refs[number][...]
-
+    updated_ref, d_single_ref, stage_ref = rest[groups * calls :]
     width = stage_ref.shape[3]
     part = width // 4
     for slot in range(groups):
@@ -583,19 +598,19 @@
 
     out_gate = gate_ref[...]
     cond_gamma = gamma_ref[...]
-    block_update = mm(take(3), weight(0))
+    block_update = mm(take(3), w_out_ref[...])
     noised = noised_ref[...].astype(F32)
     updated_ref[...] = (noised + out_gate * block_update).astype(BF16)
     gate_part = cot_ref[...].astype(F32) * block_update
     pre_gate = (gate_part * out_gate * (1.0 - out_gate)).astype(BF16)
-    grad_input = mm_nt(take(0), weight(1))
-    grad_input += mm_nt(take(1), weight(2))
-    grad_input += mm_nt(take(2), weight(3))
+    grad_input = mm_nt(take(0), w_query_ref[...])
+    grad_input += mm_nt(take(1), w_key_ref[...])
+    grad_input += mm_nt(take(2), w_value_ref[...])
     noised_norm, _ = norm_rows(noised)
     pre_gamma = (grad_input * noised_norm * cond_gamma * (1.0 - cond_gamma)).astype(BF16)
-    grad_snorm = mm_nt(pre_gamma, weight(4))
-    grad_snorm += mm_nt(grad_input.astype(BF16), weight(5))
-    grad_snorm += mm_nt(pre_gate, weight(6))
+    grad_snorm = mm_nt(pre_gamma, w_gamma_ref[...])
+    grad_snorm += mm_nt(grad_input.astype(BF16), w_beta_ref[...])
+    grad_snorm += mm_nt(pre_gate, w_outgate_ref[...])
     single_norm, single_inv = norm_rows(single_ref[...].astype(F32))
     d_single_ref[...] = norm_back(grad_snorm, single_norm, single_inv).astype(BF16)
 
@@ -736,20 +751,12 @@
     dbias_back = swap_groups(dbias_own)
     updated, d_part = pl.pallas_call(
         functools.partial(finish_kernel, groups=groups, calls=calls),
-        in_specs=[smem()]
-        + [vmem()] * 5
-        + [pl.BlockSpec(memory_space=pl.ANY)] * 7
-        + [vmem()] * (groups * calls),
+        in_specs=[smem()] + [vmem()] * (12 + groups * calls),
         out_shape=[
             jax.ShapeDtypeStruct((cols, width), BF16),
             jax.ShapeDtypeStruct(single.shape, BF16),
         ],
-        scratch_shapes=[pltpu.VMEM((groups, calls, cols, 4 * width // (groups * calls)), BF16)]
-        + [
-            pltpu.VMEM(weight.shape, BF16)
-            for weight in (w_out, w_query, w_key, w_value, w_gamma, w_beta, w_outgate)
-        ]
-        + [pltpu.SemaphoreType.DMA((7,))],
+        scratch_shapes=[pltpu.VMEM((groups, calls, cols, 4 * width // (groups * calls)), BF16)],
         compiler_params=params(),
     )(
         group_index,

time: 138 us -> 139 us (level)
  no operation moved by 1% of the time
where the time goes in v9:
time: 139 us; the launch traced here: 138 us
  Pallas kernels  45.9 us (33%)
  waiting for transfers between devices  45.4 us (33%)
  starting transfers between devices  40.1 us (29%)
  other arithmetic  3.17 us (2%)
  local copies, waits for them, and re-layouts  2.78 us (2%)
    ppermute x12, starting transfers between devices, swap_groups(): got.append(lax.ppermute(sends[bits], 'grp', perm))  26.7 us
    ppermute x12, waiting for transfers between devices, swap_groups(): got.append(lax.ppermute(sends[bits], 'grp', perm))  23.9 us
    ppermute x18, waiting for transfers between devices, flip_rows(): lax.ppermute(values, 'rows', [(index, index ^ bits) for index in range(ro...  21.5 us
    pallas_call x1, Pallas kernels, attention(): pl.pallas_call(functools.partial(attention_kernel, groups=groups, row_par...  15.9 us
    ppermute x18, starting transfers between devices, flip_rows(): lax.ppermute(values, 'rows', [(index, index ^ bits) for index in range(ro...  13.4 us
    pallas_call x1, Pallas kernels, pair_back(): pl.pallas_call(functools.partial(pair_back_kernel, groups=groups, calls=l...  8.21 us
    pallas_call x1, Pallas kernels, pair_bias(): pl.pallas_call(functools.partial(bias_kernel, groups=groups, batch=16), g...  8 us
    pallas_call x1, Pallas kernels, split_heads(): pl.pallas_call(functools.partial(finish_kernel, groups=groups, calls=call...  7.48 us
  transfers between devices with their start and end apart: 30, of which 17 were waited for; matrix products, arithmetic and copies ran while one was open for 0% of the time, Pallas kernels for 16%

profile of v9, /device:TPU:0, one launch (start us, length us, event | category | flops | bytes accessed | tf_op | source)
XLA Modules:
  0.0 138.3 jit_solution(11020287600736963618)
XLA Ops:
  0.6 8.0 %shard_map.158 = (bf16[4,3,48,128]{3,2,1,0:T(8,128)(2,1)}, bf16[4,3,48,128]{3,2,1,0:T(8,128)(2,1)}, bf16[4,3,48,128]{3,2,1,0:T(8,128)(2,1)}, bf16[4,3,48,128]{3,2,1,0:T(8,128)(2,1)}, f32[2,48,24,192]{3,2,1,0:T(8,128)}) custom-call(s32[1]{0:T(128)} %bitcast.group_ref, s32[1]{0:T(128)} %bitcast.3.rows_ref.row_ref, s32[768]{0:T(1024)} %cols_ref.1, f32[16]{0:T(128)} %gain_ref.1, ...), custom_call_target="tpu_custom_call" | custom-call | tf_op jit(solution)/shard_map/pallas_call | solution.py:218
  8.6 4.0 %collective-permute-start = (bf16[4,3,48,128]{3,2,1,0:T(8,128)(2,1)}, bf16[4,3,48,128]{3,2,1,0:T(8,128)(2,1)S(1)}, u32[]{:S(2)}, u32[]{:S(2)}) collective-permute-start(bf16[4,3,48,128]{3,2,1,0:T(8,128)(2,1)} %get-tuple-element.64), channel_id=1, source_target_pairs={{0,2},{1,3},{2,0},{3,1},{4,6},{5,7},{6,4},{7,5},{8,10},{9,11},{10,... | collective-permute-start | bytes 442376 | tf_op jit(solution)/shard_map/ppermute | solution.py:624
  12.7 1.3 collective-permute-start.1
  14.0 0.2 collective-permute-start.2
  14.3 6.4 %shard_map.157 = (bf16[192,768]{1,0:T(8,128)(2,1)}, bf16[192,768]{1,0:T(8,128)(2,1)}, bf16[192,768]{1,0:T(8,128)(2,1)}, bf16[192,768]{1,0:T(8,128)(2,1)}, f32[192,768]{1,0:T(8,128)}, /*index=5*/f32[192,768]{1,0:T(8,128)}) custom-call(s32[1]{0:T(128)} %bitcast.group_ref, bf16[192,384]{1,0:T(8,128)(2,1)} %single_ref.3, bf16[192,768]{1,0:T(8,128)(2,1)} %bitcast.23, ...), custom_call_target="tpu_custom_call" | custom-call | tf_op jit(solution)/shard_map/pallas_call | solution.py:715
  20.6 0.0 copy-start.26
  20.6 3.3 %collective-permute-done = bf16[4,3,48,128]{3,2,1,0:T(8,128)(2,1)S(1)} collective-permute-done((bf16[4,3,48,128]{3,2,1,0:T(8,128)(2,1)}, bf16[4,3,48,128]{3,2,1,0:T(8,128)(2,1)S(1)}, u32[]{:S(2)}, u32[]{:S(2)}) %collective-permute-start) | collective-permute-done | bytes 147488 | tf_op jit(solution)/shard_map/ppermute | solution.py:624
  23.9 0.5 collective-permute-done.2
  24.4 0.1 pad_maximum_fusion.rest_0_
  24.5 1.6 %collective-permute-start.6 = (bf16[4,4,3,48,128]{4,3,2,1,0:T(8,128)(2,1)S(1)}, bf16[4,4,3,48,128]{4,3,2,1,0:T(8,128)(2,1)S(1)}, u32[]{:S(2)}, u32[]{:S(2)}) collective-permute-start(bf16[4,4,3,48,128]{4,3,2,1,0:T(8,128)(2,1)S(1)} %pad_maximum_fusion.rest_0_), channel_id=1, source_target_pairs={{0,16},{4,20},{8,24},{12,28},{16,0},{20,4},{24,8},{28,12},{1,17},{... | collective-permute-start | bytes 1769480 | tf_op jit(solution)/shard_map/ppermute | solution.py:630
  26.2 1.5 %collective-permute-start.4 = (bf16[4,4,3,48,128]{4,3,2,1,0:T(8,128)(2,1)S(1)}, bf16[4,4,3,48,128]{4,3,2,1,0:T(8,128)(2,1)S(1)}, u32[]{:S(2)}, u32[]{:S(2)}) collective-permute-start(bf16[4,4,3,48,128]{4,3,2,1,0:T(8,128)(2,1)S(1)} %pad_maximum_fusion.rest_0_), channel_id=1, source_target_pairs={{0,8},{4,12},{8,0},{12,4},{16,24},{20,28},{24,16},{28,20},{1,9},{5... | collective-permute-start | bytes 1769480 | tf_op jit(solution)/shard_map/ppermute | solution.py:630
  27.7 4.4 %collective-permute-start.8 = (bf16[192,768]{1,0:T(8,128)(2,1)S(1)}, bf16[192,768]{1,0:T(8,128)(2,1)S(1)}, u32[]{:S(2)}, u32[]{:S(2)}) collective-permute-start(bf16[192,768]{1,0:T(8,128)(2,1)S(1)} %copy-done.27), channel_id=1, source_target_pairs={{0,2},{1,3},{2,0},{3,1},{4,6},{5,7},{6,4},{7,5},{8,10},{9,11},{10,... | collective-permute-start | bytes 884744 | tf_op jit(solution)/shard_map/ppermute | solution.py:624
  32.1 0.5 collective-permute-start.9
  32.6 0.1 collective-permute-start.10
  32.7 5.1 %collective-permute-done.6.rest_4_ = bf16[4,4,3,48,128]{4,3,2,1,0:T(8,128)(2,1)S(1)} collective-permute-done((bf16[4,4,3,48,128]{4,3,2,1,0:T(8,128)(2,1)S(1)}, bf16[4,4,3,48,128]{4,3,2,1,0:T(8,128)(2,1)S(1)}, u32[]{:S(2)}, u32[]{:S(2)}) %collective-permute-start.6) | collective-permute-done | bytes 589856 | tf_op jit(solution)/shard_map/ppermute | solution.py:630
  37.9 1.3 collective-permute-start.12
  39.2 0.9 collective-permute-done.4.rest_2_
  40.1 0.6 collective-permute-start.11
  40.7 11.0 %collective-permute-done.8.rest_11_ = bf16[192,768]{1,0:T(8,128)(2,1)S(1)} collective-permute-done((bf16[192,768]{1,0:T(8,128)(2,1)S(1)}, bf16[192,768]{1,0:T(8,128)(2,1)S(1)}, u32[]{:S(2)}, u32[]{:S(2)}) %collective-permute-start.8) | collective-permute-done | bytes 294944 | tf_op jit(solution)/shard_map/ppermute | solution.py:624
  51.8 0.5 collective-permute-start.7
  52.3 0.4 collective-permute-done.10.rest_13_
  52.8 0.6 collective-permute-start.13
  53.3 0.1 collective-permute-start.14
  53.4 0.4 collective-permute-done.3.rest_1_
  53.8 0.8 collective-permute-done.7.rest_5_
  54.6 0.8 collective-permute-done.5.rest_3_
  55.5 0.4 collective-permute-done.13.rest_7_
  55.9 0.4 collective-permute-done.14.rest_9_
  56.4 0.2 copy-done.15
  56.6 0.7 copy-done.16
  57.3 15.9 %shard_map.159 = (bf16[192,768]{1,0:T(8,128)(2,1)}, bf16[192,768]{1,0:T(8,128)(2,1)}, bf16[192,768]{1,0:T(8,128)(2,1)}, bf16[192,768]{1,0:T(8,128)(2,1)}, bf16[4...) custom-call(s32[1]{0:T(128)} %bitcast.group_ref, s32[1]{0:T(128)} %bitcast.3.rows_ref.row_ref, ...), custom_call_target="tpu_custom_call" | custom-call | tf_op jit(solution)/shard_map/pallas_call | solution.py:532
  73.2 0.2 collective-permute-start.15
  73.4 4.6 %collective-permute-done.15 = bf16[4,16,3,48,128]{4,3,2,1,0:T(8,128)(2,1)S(1)} collective-permute-done((bf16[4,16,3,48,128]{4,3,2,1,0:T(8,128)(2,1)}, bf16[4,16,3,48,128]{4,3,2,1,0:T(8,128)(2,1)S(1)}, u32[]{:S(2)}, u32[]{:S(2)}) %collective-permute-start.15) | collective-permute-done | bytes 2359328 | tf_op jit(solution)/shard_map/ppermute | solution.py:630
  78.0 1.7 %add_convert_fusion.3 = (bf16[4,4,3,48,128]{4,3,2,1,0:T(8,128)(2,1)S(1)}, bf16[4,4,3,48,128]{4,3,2,1,0:T(8,128)(2,1)S(1)}) fusion(bf16[4,16,3,48,128]{4,3,2,1,0:T(8,128)(2,1)S(1)} %collective-permute-done.15, bf16[4,16,3,48,128]{4,3,2,1,0:T(8,128)(2,1)} %get-tuple-element.86), kind=kLoop, calls=%fused_computation.3 | loop fusion | flops 2359296 | bytes 3538944 | tf_op jit(solution)/shard_map/convert_element_type | solution.py:659
  79.8 0.6 collective-permute-start.16
  80.4 0.5 collective-permute-start.17
  80.9 4.7 %collective-permute-start.20 = (bf16[192,768]{1,0:T(8,128)(2,1)S(1)}, bf16[192,768]{1,0:T(8,128)(2,1)S(1)}, u32[]{:S(2)}, u32[]{:S(2)}) collective-permute-start(bf16[192,768]{1,0:T(8,128)(2,1)S(1)} %copy-done.25), channel_id=1, source_target_pairs={{0,2},{1,3},{2,0},{3,1},{4,6},{5,7},{6,4},{7,5},{8,10},{9,11},{10,... | collective-permute-start | bytes 884744 | tf_op jit(solution)/shard_map/ppermute | solution.py:624
  85.6 3.3 %collective-permute-start.21 = (bf16[192,768]{1,0:T(8,128)(2,1)S(1)}, bf16[192,768]{1,0:T(8,128)(2,1)S(1)}, u32[]{:S(2)}, u32[]{:S(2)}) collective-permute-start(bf16[192,768]{1,0:T(8,128)(2,1)S(1)} %copy-done.23), channel_id=1, source_target_pairs={{0,3},{1,2},{2,1},{3,0},{4,7},{5,6},{6,5},{7,4},{8,11},{9,10},{10,... | collective-permute-start | bytes 884744 | tf_op jit(solution)/shard_map/ppermute | solution.py:624
  88.9 6.3 %collective-permute-done.16 = bf16[4,4,3,48,128]{4,3,2,1,0:T(8,128)(2,1)S(1)} collective-permute-done((bf16[4,4,3,48,128]{4,3,2,1,0:T(8,128)(2,1)S(1)}, bf16[4,4,3,48,128]{4,3,2,1,0:T(8,128)(2,1)S(1)}, u32[]{:S(2)}, u32[]{:S(2)}) %collective-permute-start.16) | collective-permute-done | bytes 589856 | tf_op jit(solution)/shard_map/ppermute | solution.py:630
  95.2 0.3 collective-permute-done.17
  95.5 0.2 add_convert_fusion.4
  95.7 1.6 %collective-permute-start.19 = (bf16[4,2,3,48,128]{4,3,2,1,0:T(8,128)(2,1)S(1)}, bf16[4,2,3,48,128]{4,3,2,1,0:T(8,128)(2,1)S(1)}, u32[]{:S(2)}, u32[]{:S(2)}) collective-permute-start(bf16[4,2,3,48,128]{4,3,2,1,0:T(8,128)(2,1)S(1)} %get-tuple-element.119), channel_id=1, source_target_pairs={{0,8},{4,12},{8,0},{12,4},{16,24},{20,28},{24,16},{28,20},{1,9},{5... | collective-permute-start | bytes 884744 | tf_op jit(solution)/shard_map/ppermute | solution.py:630
  97.3 0.5 collective-permute-start.18
  97.8 8.4 %collective-permute-done.20.rest_2_ = bf16[192,768]{1,0:T(8,128)(2,1)S(1)} collective-permute-done((bf16[192,768]{1,0:T(8,128)(2,1)S(1)}, bf16[192,768]{1,0:T(8,128)(2,1)S(1)}, u32[]{:S(2)}, u32[]{:S(2)}) %collective-permute-start.20) | collective-permute-done | bytes 294944 | tf_op jit(solution)/shard_map/ppermute | solution.py:624
  106.2 0.2 collective-permute-done.22.rest_1_
  106.4 0.3 add_convert_fusion
  106.8 0.1 copy-done.9
  106.9 0.1 copy-done.11
  107.0 0.1 copy-done.12
  107.1 0.7 slice_bitcast_fusion
  107.8 7.5 %collective-permute-start.26 = (bf16[4,3,48,128]{3,2,1,0:T(8,128)(2,1)S(1)}, bf16[4,3,48,128]{3,2,1,0:T(8,128)(2,1)S(1)}, u32[]{:S(2)}, u32[]{:S(2)}) collective-permute-start(bf16[4,3,48,128]{3,2,1,0:T(8,128)(2,1)S(1)} %get-tuple-element.109), channel_id=1, source_target_pairs={{0,2},{1,3},{2,0},{3,1},{4,6},{5,7},{6,4},{7,5},{8,10},{9,11},{10,... | collective-permute-start | bytes 442376 | tf_op jit(solution)/shard_map/ppermute | solution.py:624
  115.2 0.5 collective-permute-start.27
  115.8 0.0 collective-permute-start.28
  115.8 7.5 %shard_map.160 = (bf16[192,768]{1,0:T(8,128)(2,1)}, bf16[192,384]{1,0:T(8,128)(2,1)}) custom-call(s32[1]{0:T(128)} %bitcast.group_ref, bf16[192,384]{1,0:T(8,128)(2,1)} %single_ref.3, bf16[192,768]{1,0:T(8,128)(2,1)} %bitcast.24, bf16[192,768]{1,0:T(8,128)(2,1)} %bitcast.26, f32[192,768]{1,0:T(8,128)} %get-tuple-element.61.gamma_ref, ...), custom_call_target="tpu_custom_call" | custom-call | tf_op jit(solution)/shard_map/pallas_call | solution.py:752
  123.3 2.4 %collective-permute-start.25 = (bf16[192,384]{1,0:T(8,128)(2,1)}, bf16[192,384]{1,0:T(8,128)(2,1)S(1)}, u32[]{:S(2)}, u32[]{:S(2)}) collective-permute-start(bf16[192,384]{1,0:T(8,128)(2,1)} %get-tuple-element.106), channel_id=1, source_target_pairs={{0,24},{4,28},{8,16},{12,20},{16,8},{20,12},{24,0},{28,4},{1,25},{... | collective-permute-start | bytes 442376 | tf_op jit(solution)/shard_map/ppermute | solution.py:630
  125.7 0.5 collective-permute-start.24
  126.3 0.9 collective-permute-start.23
  127.1 0.6 copy-done.20
  127.8 0.1 copy-done.21
  127.8 8.2 %shard_map.161 = bf16[2,48,192,128]{3,2,1,0:T(8,128)(2,1)} custom-call(s32[1]{0:T(128)} %bitcast.group_ref, bf16[2,48,192,128]{3,2,1,0:T(8,128)(2,1)} %bitcast.21, f32[2,48,24,192]{3,2,1,0:T(8,128)} %get-tuple-element.107.stats_ref, bf16[16,128]{1,0:T(8,128)(2,1)} %bitcast.32, bf16[4,3,48,128]{3,2,1,0:T(8,128)(2,1)} %get-tuple-element.108.rest_0_, ...), custom_call_target="tpu_custom_call" | custom-call | tf_op jit(solution)/shard_map/pallas_call | solution.py:329
  136.1 0.1 add_convert_fusion.6
  136.2 0.1 collective-permute-start.29
  136.2 1.4 collective-permute-done.29
  137.6 0.7 convert_add_fusion
  (68 shorter events, 0.2 us)
Async XLA Ops:
  8.6 15.3 %collective-permute-start = (bf16[4,3,48,128]{3,2,1,0:T(8,128)(2,1)}, bf16[4,3,48,128]{3,2,1,0:T(8,128)(2,1)S(1)}, u32[]{:S(2)}, u32[]{:S(2)}) collective-permute-start(bf16[4,3,48,128]{3,2,1,0:T(8,128)(2,1)} %get-tuple-element.64), channel_id=1, source_target_pairs={{0,2},{1,3},{2,0},{3,1},{4,6},{5,7},{6,4},{7,5},{8,10},{9,11},{10,... | collective-permute-start | bytes 442376 | tf_op jit(solution)/shard_map/ppermute | solution.py:624
  12.7 11.3 %collective-permute-start.1 = (bf16[4,3,48,128]{3,2,1,0:T(8,128)(2,1)}, bf16[4,3,48,128]{3,2,1,0:T(8,128)(2,1)S(1)}, u32[]{:S(2)}, u32[]{:S(2)}) collective-permute-start(bf16[4,3,48,128]{3,2,1,0:T(8,128)(2,1)} %get-tuple-element.65), channel_id=1, source_target_pairs={{0,3},{1,2},{2,1},{3,0},{4,7},{5,6},{6,5},{7,4},{8,11},{9,10},{10,... | collective-permute-start | bytes 442376 | tf_op jit(solution)/shard_map/ppermute | solution.py:624
  14.0 10.4 %collective-permute-start.2 = (bf16[4,3,48,128]{3,2,1,0:T(8,128)(2,1)}, bf16[4,3,48,128]{3,2,1,0:T(8,128)(2,1)S(1)}, u32[]{:S(2)}, u32[]{:S(2)}) collective-permute-start(bf16[4,3,48,128]{3,2,1,0:T(8,128)(2,1)} %get-tuple-element.66), channel_id=1, source_target_pairs={{0,1},{1,0},{2,3},{3,2},{4,5},{5,4},{6,7},{7,6},{8,9},{9,8},{10,11... | collective-permute-start | bytes 442376 | tf_op jit(solution)/shard_map/ppermute | solution.py:624
  14.3 10.2 %copy-start.17 = (bf16[4,3,48,128]{3,2,1,0:T(8,128)(2,1)S(1)}, bf16[4,3,48,128]{3,2,1,0:T(8,128)(2,1)}, u32[]{:S(2)}) copy-start(bf16[4,3,48,128]{3,2,1,0:T(8,128)(2,1)} %get-tuple-element.74) | copy-start | bytes 442372
  20.6 7.0 %copy-start.27 = (bf16[192,768]{1,0:T(8,128)(2,1)S(1)}, bf16[192,768]{1,0:T(8,128)(2,1)}, u32[]{:S(2)}) copy-start(bf16[192,768]{1,0:T(8,128)(2,1)} %get-tuple-element.71) | copy-start | bytes 884740
  20.6 11.5 %copy-start.26 = (bf16[192,768]{1,0:T(8,128)(2,1)S(1)}, bf16[192,768]{1,0:T(8,128)(2,1)}, u32[]{:S(2)}) copy-start(bf16[192,768]{1,0:T(8,128)(2,1)} %get-tuple-element.72) | copy-start | bytes 884740
  20.6 12.0 %copy-start.24 = (bf16[192,768]{1,0:T(8,128)(2,1)S(1)}, bf16[192,768]{1,0:T(8,128)(2,1)}, u32[]{:S(2)}) copy-start(bf16[192,768]{1,0:T(8,128)(2,1)} %get-tuple-element.73) | copy-start | bytes 884740
  24.5 31.8 %copy-start = (bf16[4,4,3,48,128]{4,3,2,1,0:T(8,128)(2,1)}, bf16[4,4,3,48,128]{4,3,2,1,0:T(8,128)(2,1)S(1)}, u32[]{:S(2)}) copy-start(bf16[4,4,3,48,128]{4,3,2,1,0:T(8,128)(2,1)S(1)} %pad_maximum_fusion.rest_0_) | copy-start | bytes 1769476
  24.5 13.3 %collective-permute-start.6 = (bf16[4,4,3,48,128]{4,3,2,1,0:T(8,128)(2,1)S(1)}, bf16[4,4,3,48,128]{4,3,2,1,0:T(8,128)(2,1)S(1)}, u32[]{:S(2)}, u32[]{:S(2)}) collective-permute-start(bf16[4,4,3,48,128]{4,3,2,1,0:T(8,128)(2,1)S(1)} %pad_maximum_fusion.rest_0_), channel_id=1, source_target_pairs={{0,16},{4,20},{8,24},{12,28},{16,0},{20,4},{24,8},{28,12},{1,17},{... | collective-permute-start | bytes 1769480 | tf_op jit(solution)/shard_map/ppermute | solution.py:630
  26.2 13.9 %collective-permute-start.4 = (bf16[4,4,3,48,128]{4,3,2,1,0:T(8,128)(2,1)S(1)}, bf16[4,4,3,48,128]{4,3,2,1,0:T(8,128)(2,1)S(1)}, u32[]{:S(2)}, u32[]{:S(2)}) collective-permute-start(bf16[4,4,3,48,128]{4,3,2,1,0:T(8,128)(2,1)S(1)} %pad_maximum_fusion.rest_0_), channel_id=1, source_target_pairs={{0,8},{4,12},{8,0},{12,4},{16,24},{20,28},{24,16},{28,20},{1,9},{5... | collective-permute-start | bytes 1769480 | tf_op jit(solution)/shard_map/ppermute | solution.py:630
  27.7 24.1 %collective-permute-start.8 = (bf16[192,768]{1,0:T(8,128)(2,1)S(1)}, bf16[192,768]{1,0:T(8,128)(2,1)S(1)}, u32[]{:S(2)}, u32[]{:S(2)}) collective-permute-start(bf16[192,768]{1,0:T(8,128)(2,1)S(1)} %copy-done.27), channel_id=1, source_target_pairs={{0,2},{1,3},{2,0},{3,1},{4,6},{5,7},{6,4},{7,5},{8,10},{9,11},{10,... | collective-permute-start | bytes 884744 | tf_op jit(solution)/shard_map/ppermute | solution.py:624
  32.1 19.7 %collective-permute-start.9 = (bf16[192,768]{1,0:T(8,128)(2,1)S(1)}, bf16[192,768]{1,0:T(8,128)(2,1)S(1)}, u32[]{:S(2)}, u32[]{:S(2)}) collective-permute-start(bf16[192,768]{1,0:T(8,128)(2,1)S(1)} %copy-done.26), channel_id=1, source_target_pairs={{0,3},{1,2},{2,1},{3,0},{4,7},{5,6},{6,5},{7,4},{8,11},{9,10},{10,... | collective-permute-start | bytes 884744 | tf_op jit(solution)/shard_map/ppermute | solution.py:624
  32.6 20.1 %collective-permute-start.10 = (bf16[192,768]{1,0:T(8,128)(2,1)S(1)}, bf16[192,768]{1,0:T(8,128)(2,1)S(1)}, u32[]{:S(2)}, u32[]{:S(2)}) collective-permute-start(bf16[192,768]{1,0:T(8,128)(2,1)S(1)} %copy-done.24), channel_id=1, source_target_pairs={{0,1},{1,0},{2,3},{3,2},{4,5},{5,4},{6,7},{7,6},{8,9},{9,8},{10,11... | collective-permute-start | bytes 884744 | tf_op jit(solution)/shard_map/ppermute | solution.py:624
  37.8 18.5 %copy-start.2 = (bf16[4,4,3,48,128]{4,3,2,1,0:T(8,128)(2,1)}, bf16[4,4,3,48,128]{4,3,2,1,0:T(8,128)(2,1)S(1)}, u32[]{:S(2)}) copy-start(bf16[4,4,3,48,128]{4,3,2,1,0:T(8,128)(2,1)S(1)} %collective-permute-done.6.rest_4_) | copy-start | bytes 1769476
  37.9 14.9 %collective-permute-start.12 = (bf16[2,4,3,48,128]{4,3,2,1,0:T(8,128)(2,1)S(1)}, bf16[2,4,3,48,128]{4,3,2,1,0:T(8,128)(2,1)S(1)}, u32[]{:S(2)}, u32[]{:S(2)}) collective-permute-start(bf16[2,4,3,48,128]{4,3,2,1,0:T(8,128)(2,1)S(1)} %slice.81), channel_id=1, source_target_pairs={{0,8},{4,12},{8,0},{12,4},{16,24},{20,28},{24,16},{28,20},{1,9},{5... | collective-permute-start | bytes 884744 | tf_op jit(solution)/shard_map/ppermute | solution.py:630
  40.1 16.2 %copy-start.3 = (bf16[4,4,3,48,128]{4,3,2,1,0:T(8,128)(2,1)}, bf16[4,4,3,48,128]{4,3,2,1,0:T(8,128)(2,1)S(1)}, u32[]{:S(2)}) copy-start(bf16[4,4,3,48,128]{4,3,2,1,0:T(8,128)(2,1)S(1)} %collective-permute-done.4.rest_2_) | copy-start | bytes 1769476
  40.1 12.6 %collective-permute-start.11 = (bf16[2,4,3,48,128]{4,3,2,1,0:T(8,128)(2,1)S(1)}, bf16[2,4,3,48,128]{4,3,2,1,0:T(8,128)(2,1)S(1)}, u32[]{:S(2)}, u32[]{:S(2)}) collective-permute-start(bf16[2,4,3,48,128]{4,3,2,1,0:T(8,128)(2,1)S(1)} %slice.80), channel_id=1, source_target_pairs={{0,16},{4,20},{8,24},{12,28},{16,0},{20,4},{24,8},{28,12},{1,17},{... | collective-permute-start | bytes 884744 | tf_op jit(solution)/shard_map/ppermute | solution.py:630
  51.8 4.6 %copy-start.7 = (bf16[192,768]{1,0:T(8,128)(2,1)}, bf16[192,768]{1,0:T(8,128)(2,1)S(1)}, u32[]{:S(2)}) copy-start(bf16[192,768]{1,0:T(8,128)(2,1)S(1)} %collective-permute-done.8.rest_11_) | copy-start | bytes 884740
  51.8 2.0 %collective-permute-start.3 = (bf16[4,4,3,48,128]{4,3,2,1,0:T(8,128)(2,1)S(1)}, bf16[4,4,3,48,128]{4,3,2,1,0:T(8,128)(2,1)S(1)}, u32[]{:S(2)}, u32[]{:S(2)}) collective-permute-start(bf16[4,4,3,48,128]{4,3,2,1,0:T(8,128)(2,1)S(1)} %pad_maximum_fusion.rest_0_), channel_id=1, source_target_pairs={{0,4},{4,0},{8,12},{12,8},{16,20},{20,16},{24,28},{28,24},{1,5},{5... | collective-permute-start | bytes 1769480 | tf_op jit(solution)/shard_map/ppermute | solution.py:630
  51.8 4.5 %copy-start.8 = (bf16[192,768]{1,0:T(8,128)(2,1)}, bf16[192,768]{1,0:T(8,128)(2,1)S(1)}, u32[]{:S(2)}) copy-start(bf16[192,768]{1,0:T(8,128)(2,1)S(1)} %collective-permute-done.9.rest_12_) | copy-start | bytes 884740
  51.8 2.8 %collective-permute-start.7 = (bf16[4,4,3,48,128]{4,3,2,1,0:T(8,128)(2,1)S(1)}, bf16[4,4,3,48,128]{4,3,2,1,0:T(8,128)(2,1)S(1)}, u32[]{:S(2)}, u32[]{:S(2)}) collective-permute-start(bf16[4,4,3,48,128]{4,3,2,1,0:T(8,128)(2,1)S(1)} %collective-permute-done.6.rest_4_), channel_id=1, source_target_pairs={{0,4},{4,0},{8,12},{12,8},{16,20},{20,16},{24,28},{28,24},{1,5},{5... | collective-permute-start | bytes 1769480 | tf_op jit(solution)/shard_map/ppermute | solution.py:630
  52.7 3.6 %copy-start.10 = (bf16[192,768]{1,0:T(8,128)(2,1)}, bf16[192,768]{1,0:T(8,128)(2,1)S(1)}, u32[]{:S(2)}) copy-start(bf16[192,768]{1,0:T(8,128)(2,1)S(1)} %collective-permute-done.10.rest_13_) | copy-start | bytes 884740
  52.7 2.8 %collective-permute-start.5 = (bf16[4,4,3,48,128]{4,3,2,1,0:T(8,128)(2,1)S(1)}, bf16[4,4,3,48,128]{4,3,2,1,0:T(8,128)(2,1)S(1)}, u32[]{:S(2)}, u32[]{:S(2)}) collective-permute-start(bf16[4,4,3,48,128]{4,3,2,1,0:T(8,128)(2,1)S(1)} %collective-permute-done.4.rest_2_), channel_id=1, source_target_pairs={{0,4},{4,0},{8,12},{12,8},{16,20},{20,16},{24,28},{28,24},{1,5},{5... | collective-permute-start | bytes 1769480 | tf_op jit(solution)/shard_map/ppermute | solution.py:630
  52.7 3.6 %copy-start.13 = (bf16[2,4,3,48,128]{4,3,2,1,0:T(8,128)(2,1)}, bf16[2,4,3,48,128]{4,3,2,1,0:T(8,128)(2,1)S(1)}, u32[]{:S(2)}) copy-start(bf16[2,4,3,48,128]{4,3,2,1,0:T(8,128)(2,1)S(1)} %collective-permute-done.12.rest_8_) | copy-start | bytes 884740
  52.7 3.6 %copy-start.14 = (bf16[2,4,3,48,128]{4,3,2,1,0:T(8,128)(2,1)}, bf16[2,4,3,48,128]{4,3,2,1,0:T(8,128)(2,1)S(1)}, u32[]{:S(2)}) copy-start(bf16[2,4,3,48,128]{4,3,2,1,0:T(8,128)(2,1)S(1)} %collective-permute-done.11.rest_6_) | copy-start | bytes 884740
  52.8 3.1 %collective-permute-start.13 = (bf16[2,4,3,48,128]{4,3,2,1,0:T(8,128)(2,1)S(1)}, bf16[2,4,3,48,128]{4,3,2,1,0:T(8,128)(2,1)S(1)}, u32[]{:S(2)}, u32[]{:S(2)}) collective-permute-start(bf16[2,4,3,48,128]{4,3,2,1,0:T(8,128)(2,1)S(1)} %collective-permute-done.11.rest_6_), channel_id=1, source_target_pairs={{0,4},{4,0},{8,12},{12,8},{16,20},{20,16},{24,28},{28,24},{1,5},{5... | collective-permute-start | bytes 884744 | tf_op jit(solution)/shard_map/ppermute | solution.py:630
  53.3 3.0 %collective-permute-start.14 = (bf16[2,4,3,48,128]{4,3,2,1,0:T(8,128)(2,1)S(1)}, bf16[2,4,3,48,128]{4,3,2,1,0:T(8,128)(2,1)S(1)}, u32[]{:S(2)}, u32[]{:S(2)}) collective-permute-start(bf16[2,4,3,48,128]{4,3,2,1,0:T(8,128)(2,1)S(1)} %collective-permute-done.12.rest_8_), channel_id=1, source_target_pairs={{0,4},{4,0},{8,12},{12,8},{16,20},{20,16},{24,28},{28,24},{1,5},{5... | collective-permute-start | bytes 884744 | tf_op jit(solution)/shard_map/ppermute | solution.py:630
  53.8 2.6 %copy-start.4 = (bf16[4,4,3,48,128]{4,3,2,1,0:T(8,128)(2,1)}, bf16[4,4,3,48,128]{4,3,2,1,0:T(8,128)(2,1)S(1)}, u32[]{:S(2)}) copy-start(bf16[4,4,3,48,128]{4,3,2,1,0:T(8,128)(2,1)S(1)} %collective-permute-done.3.rest_1_) | copy-start | bytes 1769476
  54.6 1.8 %copy-start.5 = (bf16[4,4,3,48,128]{4,3,2,1,0:T(8,128)(2,1)}, bf16[4,4,3,48,128]{4,3,2,1,0:T(8,128)(2,1)S(1)}, u32[]{:S(2)}) copy-start(bf16[4,4,3,48,128]{4,3,2,1,0:T(8,128)(2,1)S(1)} %collective-permute-done.7.rest_5_) | copy-start | bytes 1769476
  55.5 0.9 copy-start.6
  55.9 0.7 copy-start.15
  56.6 0.7 copy-start.16
  73.2 4.8 %collective-permute-start.15 = (bf16[4,16,3,48,128]{4,3,2,1,0:T(8,128)(2,1)}, bf16[4,16,3,48,128]{4,3,2,1,0:T(8,128)(2,1)S(1)}, u32[]{:S(2)}, u32[]{:S(2)}) collective-permute-start(bf16[4,16,3,48,128]{4,3,2,1,0:T(8,128)(2,1)} %get-tuple-element.87), channel_id=1, source_target_pairs={{0,4},{4,0},{8,12},{12,8},{16,20},{20,16},{24,28},{28,24},{1,5},{5... | collective-permute-start | bytes 7077896 | tf_op jit(solution)/shard_map/ppermute | solution.py:630
  78.0 2.9 %copy-start.25 = (bf16[192,768]{1,0:T(8,128)(2,1)S(1)}, bf16[192,768]{1,0:T(8,128)(2,1)}, u32[]{:S(2)}) copy-start(bf16[192,768]{1,0:T(8,128)(2,1)} %get-tuple-element.89) | copy-start | bytes 884740
  78.0 7.6 %copy-start.23 = (bf16[192,768]{1,0:T(8,128)(2,1)S(1)}, bf16[192,768]{1,0:T(8,128)(2,1)}, u32[]{:S(2)}) copy-start(bf16[192,768]{1,0:T(8,128)(2,1)} %get-tuple-element.90) | copy-start | bytes 884740
  78.0 10.9 %copy-start.22 = (bf16[192,768]{1,0:T(8,128)(2,1)S(1)}, bf16[192,768]{1,0:T(8,128)(2,1)}, u32[]{:S(2)}) copy-start(bf16[192,768]{1,0:T(8,128)(2,1)} %get-tuple-element.91) | copy-start | bytes 884740
  78.0 17.4 %copy-start.1 = (bf16[4,16,3,48,128]{4,3,2,1,0:T(8,128)(2,1)S(1)}, bf16[4,16,3,48,128]{4,3,2,1,0:T(8,128)(2,1)}, u32[]{:S(2)}) copy-start(bf16[4,16,3,48,128]{4,3,2,1,0:T(8,128)(2,1)} %get-tuple-element.86) | copy-start | bytes 7077892
  79.8 15.4 %collective-permute-start.16 = (bf16[4,4,3,48,128]{4,3,2,1,0:T(8,128)(2,1)S(1)}, bf16[4,4,3,48,128]{4,3,2,1,0:T(8,128)(2,1)S(1)}, u32[]{:S(2)}, u32[]{:S(2)}) collective-permute-start(bf16[4,4,3,48,128]{4,3,2,1,0:T(8,128)(2,1)S(1)} %get-tuple-element.121), channel_id=1, source_target_pairs={{0,8},{4,12},{8,0},{12,4},{16,24},{20,28},{24,16},{28,20},{1,9},{5... | collective-permute-start | bytes 1769480 | tf_op jit(solution)/shard_map/ppermute | solution.py:630
  80.4 15.1 %collective-permute-start.17 = (bf16[4,4,3,48,128]{4,3,2,1,0:T(8,128)(2,1)S(1)}, bf16[4,4,3,48,128]{4,3,2,1,0:T(8,128)(2,1)S(1)}, u32[]{:S(2)}, u32[]{:S(2)}) collective-permute-start(bf16[4,4,3,48,128]{4,3,2,1,0:T(8,128)(2,1)S(1)} %get-tuple-element.122), channel_id=1, source_target_pairs={{0,16},{4,20},{8,24},{12,28},{16,0},{20,4},{24,8},{28,12},{1,17},{... | collective-permute-start | bytes 1769480 | tf_op jit(solution)/shard_map/ppermute | solution.py:630
  80.9 25.3 %collective-permute-start.20 = (bf16[192,768]{1,0:T(8,128)(2,1)S(1)}, bf16[192,768]{1,0:T(8,128)(2,1)S(1)}, u32[]{:S(2)}, u32[]{:S(2)}) collective-permute-start(bf16[192,768]{1,0:T(8,128)(2,1)S(1)} %copy-done.25), channel_id=1, source_target_pairs={{0,2},{1,3},{2,0},{3,1},{4,6},{5,7},{6,4},{7,5},{8,10},{9,11},{10,... | collective-permute-start | bytes 884744 | tf_op jit(solution)/shard_map/ppermute | solution.py:624
  85.6 20.6 %collective-permute-start.21 = (bf16[192,768]{1,0:T(8,128)(2,1)S(1)}, bf16[192,768]{1,0:T(8,128)(2,1)S(1)}, u32[]{:S(2)}, u32[]{:S(2)}) collective-permute-start(bf16[192,768]{1,0:T(8,128)(2,1)S(1)} %copy-done.23), channel_id=1, source_target_pairs={{0,3},{1,2},{2,1},{3,0},{4,7},{5,6},{6,5},{7,4},{8,11},{9,10},{10,... | collective-permute-start | bytes 884744 | tf_op jit(solution)/shard_map/ppermute | solution.py:624
  88.9 17.5 %collective-permute-start.22 = (bf16[192,768]{1,0:T(8,128)(2,1)S(1)}, bf16[192,768]{1,0:T(8,128)(2,1)S(1)}, u32[]{:S(2)}, u32[]{:S(2)}) collective-permute-start(bf16[192,768]{1,0:T(8,128)(2,1)S(1)} %copy-done.22), channel_id=1, source_target_pairs={{0,1},{1,0},{2,3},{3,2},{4,5},{5,4},{6,7},{7,6},{8,9},{9,8},{10,11... | collective-permute-start | bytes 884744 | tf_op jit(solution)/shard_map/ppermute | solution.py:624
  95.7 10.7 %collective-permute-start.19 = (bf16[4,2,3,48,128]{4,3,2,1,0:T(8,128)(2,1)S(1)}, bf16[4,2,3,48,128]{4,3,2,1,0:T(8,128)(2,1)S(1)}, u32[]{:S(2)}, u32[]{:S(2)}) collective-permute-start(bf16[4,2,3,48,128]{4,3,2,1,0:T(8,128)(2,1)S(1)} %get-tuple-element.119), channel_id=1, source_target_pairs={{0,8},{4,12},{8,0},{12,4},{16,24},{20,28},{24,16},{28,20},{1,9},{5... | collective-permute-start | bytes 884744 | tf_op jit(solution)/shard_map/ppermute | solution.py:630
  97.3 9.2 %collective-permute-start.18 = (bf16[4,2,3,48,128]{4,3,2,1,0:T(8,128)(2,1)S(1)}, bf16[4,2,3,48,128]{4,3,2,1,0:T(8,128)(2,1)S(1)}, u32[]{:S(2)}, u32[]{:S(2)}) collective-permute-start(bf16[4,2,3,48,128]{4,3,2,1,0:T(8,128)(2,1)S(1)} %get-tuple-element.120), channel_id=1, source_target_pairs={{0,16},{4,20},{8,24},{12,28},{16,0},{20,4},{24,8},{28,12},{1,17},{... | collective-permute-start | bytes 884744 | tf_op jit(solution)/shard_map/ppermute | solution.py:630
  106.2 0.7 copy-start.9
  106.2 0.8 copy-start.11
  106.4 0.7 copy-start.12
  107.8 18.5 %collective-permute-start.26 = (bf16[4,3,48,128]{3,2,1,0:T(8,128)(2,1)S(1)}, bf16[4,3,48,128]{3,2,1,0:T(8,128)(2,1)S(1)}, u32[]{:S(2)}, u32[]{:S(2)}) collective-permute-start(bf16[4,3,48,128]{3,2,1,0:T(8,128)(2,1)S(1)} %get-tuple-element.109), channel_id=1, source_target_pairs={{0,2},{1,3},{2,0},{3,1},{4,6},{5,7},{6,4},{7,5},{8,10},{9,11},{10,... | collective-permute-start | bytes 442376 | tf_op jit(solution)/shard_map/ppermute | solution.py:624
  115.2 11.9 %collective-permute-start.27 = (bf16[4,3,48,128]{3,2,1,0:T(8,128)(2,1)S(1)}, bf16[4,3,48,128]{3,2,1,0:T(8,128)(2,1)S(1)}, u32[]{:S(2)}, u32[]{:S(2)}) collective-permute-start(bf16[4,3,48,128]{3,2,1,0:T(8,128)(2,1)S(1)} %get-tuple-element.110), channel_id=1, source_target_pairs={{0,3},{1,2},{2,1},{3,0},{4,7},{5,6},{6,5},{7,4},{8,11},{9,10},{10,... | collective-permute-start | bytes 442376 | tf_op jit(solution)/shard_map/ppermute | solution.py:624
  115.8 11.3 %collective-permute-start.28 = (bf16[4,3,48,128]{3,2,1,0:T(8,128)(2,1)S(1)}, bf16[4,3,48,128]{3,2,1,0:T(8,128)(2,1)S(1)}, u32[]{:S(2)}, u32[]{:S(2)}) collective-permute-start(bf16[4,3,48,128]{3,2,1,0:T(8,128)(2,1)S(1)} %get-tuple-element.111), channel_id=1, source_target_pairs={{0,1},{1,0},{2,3},{3,2},{4,5},{5,4},{6,7},{7,6},{8,9},{9,8},{10,11... | collective-permute-start | bytes 442376 | tf_op jit(solution)/shard_map/ppermute | solution.py:624
  123.3 12.7 %collective-permute-start.25 = (bf16[192,384]{1,0:T(8,128)(2,1)}, bf16[192,384]{1,0:T(8,128)(2,1)S(1)}, u32[]{:S(2)}, u32[]{:S(2)}) collective-permute-start(bf16[192,384]{1,0:T(8,128)(2,1)} %get-tuple-element.106), channel_id=1, source_target_pairs={{0,24},{4,28},{8,16},{12,20},{16,8},{20,12},{24,0},{28,4},{1,25},{... | collective-permute-start | bytes 442376 | tf_op jit(solution)/shard_map/ppermute | solution.py:630
  125.7 10.3 %collective-permute-start.24 = (bf16[192,384]{1,0:T(8,128)(2,1)}, bf16[192,384]{1,0:T(8,128)(2,1)S(1)}, u32[]{:S(2)}, u32[]{:S(2)}) collective-permute-start(bf16[192,384]{1,0:T(8,128)(2,1)} %get-tuple-element.106), channel_id=1, source_target_pairs={{0,16},{4,20},{8,24},{12,28},{16,0},{20,4},{24,8},{28,12},{1,17},{... | collective-permute-start | bytes 442376 | tf_op jit(solution)/shard_map/ppermute | solution.py:630
  126.3 0.9 copy-start.19
  126.3 9.8 %collective-permute-start.23 = (bf16[192,384]{1,0:T(8,128)(2,1)}, bf16[192,384]{1,0:T(8,128)(2,1)S(1)}, u32[]{:S(2)}, u32[]{:S(2)}) collective-permute-start(bf16[192,384]{1,0:T(8,128)(2,1)} %get-tuple-element.106), channel_id=1, source_target_pairs={{0,8},{4,12},{8,0},{12,4},{16,24},{20,28},{24,16},{28,20},{1,9},{5... | collective-permute-start | bytes 442376 | tf_op jit(solution)/shard_map/ppermute | solution.py:630
  127.1 0.7 copy-start.20
  127.1 0.7 copy-start.21
  127.8 8.2 %copy-start.18 = (bf16[192,384]{1,0:T(8,128)(2,1)S(1)}, bf16[192,384]{1,0:T(8,128)(2,1)}, u32[]{:S(2)}) copy-start(bf16[192,384]{1,0:T(8,128)(2,1)} %get-tuple-element.106) | copy-start | bytes 442372
  136.2 1.4 %collective-permute-start.29 = (bf16[192,384]{1,0:T(8,128)(2,1)S(1)}, bf16[192,384]{1,0:T(8,128)(2,1)S(1)}, u32[]{:S(2)}, u32[]{:S(2)}) collective-permute-start(bf16[192,384]{1,0:T(8,128)(2,1)S(1)} %add_convert_fusion.6), channel_id=1, source_target_pairs={{0,4},{4,0},{8,12},{12,8},{16,20},{20,16},{24,28},{28,24},{1,5},{5... | collective-permute-start | bytes 442376 | tf_op jit(solution)/shard_map/ppermute | solution.py:630

commit v10 on v9

--- a/solution.py
+++ b/solution.py
@@ -110,19 +110,13 @@
     return [(tile, tile * 128, min(cols, tile * 128 + 128)) for tile in range(-(-cols // 128))]
 
 
-def mean_matrix(channels):
-    first = lax.broadcasted_iota(jnp.int32, (2 * channels, 2 * channels), 0) >= channels
-    second = lax.broadcasted_iota(jnp.int32, (2 * channels, 2 * channels), 1) >= channels
-    return jnp.where(first == second, 1.0 / channels, 0.0).astype(BF16)
-
-
-def center_rows(pair_ref, first, batch, means):
+def center_rows(pair_ref, first, batch):
     _, _, cols, channels = pair_ref.shape
-    both = jnp.concatenate(
-        [pair_ref[side, first : first + batch].reshape(batch * cols, channels) for side in range(2)],
-        axis=1,
-    )
-    return both.astype(F32) - mm(both, means)
+    halves = []
+    for side in range(2):
+        rows = pair_ref[side, first : first + batch].reshape(batch * cols, channels).astype(F32)
+        halves.append(rows - jnp.sum(rows, axis=-1, keepdims=True) * (1.0 / channels))
+    return jnp.concatenate(halves, axis=1)
 
 
 def lane_pad(block, before, total):
@@ -155,7 +149,6 @@
     half = step * pl.num_programs(0)
     group_own = group_ref[0]
     row_base = rows_ref[0] * 2 * half + pl.program_id(0) * step
-    means = mean_matrix(channels)
     weight = w_pair_ref[...].astype(F32).T.astype(BF16)
     mean_part = jnp.full((channels, heads), 1.0 / channels, BF16)
     mixed = []
@@ -173,7 +166,7 @@
         gains_ref[head : head + 1, :] = jnp.full((1, cols), gain_ref[head] * LOG2_E, F32)
 
     for first in range(0, step, batch):
-        center = center_rows(pair_ref, first, batch, means)
+        center = center_rows(pair_ref, first, batch)
         center_b = center.astype(BF16)
         square = (center * center).astype(BF16)
         for base in range(0, batch, 2):
@@ -262,7 +255,6 @@
     per_call = grad_refs[0].shape[0]
     heads = groups * calls * per_call
     group_own = group_ref[0]
-    means = mean_matrix(channels)
     weight = w_pair_ref[...].astype(F32)
     weight = (weight - jnp.mean(weight, axis=-1, keepdims=True)).astype(BF16)
     spread = lax.broadcasted_iota(jnp.int32, (heads, channels), 0)
@@ -287,7 +279,7 @@
                 ]
 
     for first in range(0, step, batch):
-        center = center_rows(pair_ref, first, batch, means)
+        center = center_rows(pair_ref, first, batch)
         for base in range(0, batch, 2):
             places = [(base + inner, side) for inner in range(2) for side in range(2)]
             left = []
@@ -356,16 +348,12 @@
 
 
 def attention_kernel(group_ref, row_ref, *rest, groups, row_parts, head_size):
-    bias_sources = rest[: row_parts + 2]
+    bias_refs = rest[: row_parts + 2]
     acts_refs = rest[row_parts + 2 : row_parts + 2 + groups]
     acts_refs = acts_refs[:1] + acts_refs[-1:] + acts_refs[1:-1]
     rest = rest[row_parts + 2 + groups :]
     out_refs = rest[:groups]
-    bias_refs = rest[-row_parts - 4 : -2]
-    bias_done, back_done = rest[-2:]
     (
-        keep_out,
-        give_out,
         keep_ref,
         give_ref,
         query_ref,
@@ -381,21 +369,8 @@
         gq_sum,
         gk_sum,
         gv_sum,
-    ) = rest[groups : -row_parts - 4]
+    ) = rest[groups:]
     heads = keep_ref.shape[1] * 2 // row_parts
-    coming = [
-        [
-            pltpu.make_async_copy(
-                source.at[:, head], bias_refs[number].at[:, head], bias_done.at[head, number]
-            )
-            for number, source in enumerate(bias_sources)
-        ]
-        for head in range(heads)
-    ]
-    for head_copies in coming:
-        for copy in head_copies:
-            copy.start()
-    going = []
     group_own = group_ref[0]
     cols, width = acts_refs[0].shape
     tokens = groups * cols
@@ -442,8 +417,6 @@
     order = unit_order(heads)
     for head in range(heads):
         bias_head, score_head = bias_full.at[head % 2], score_full.at[head % 2]
-        for copy in coming[head]:
-            copy.wait()
         for other in range(row_parts):
             for side, rows in places(row_ref[0] ^ other):
                 lanes = slice(side * rest_lanes, (side + 1) * rest_lanes)
@@ -493,12 +466,6 @@
                     )
                 )
                 dbias_ref[column, unit] = jnp.stack(blocks)
-            target = give_out if other % 2 else keep_out
-            copy = pltpu.make_async_copy(
-                dbias_ref.at[:, unit], target.at[:, unit], back_done.at[head, other]
-            )
-            copy.start()
-            going.append(copy)
 
     results = (
         gq_sum[...] * scale,
@@ -516,8 +483,6 @@
             for token, place, count in turns:
                 slot, inside = divmod(token, cols)
                 out_refs[slot][inside : inside + count, lanes] = rounded[place : place + count]
-    for copy in going:
-        copy.wait()
 
 
 def attention(group_index, row_index, acts, bias, head_size):
@@ -528,17 +493,14 @@
     part = width // 4
     _, heads, _, half, _ = bias[0].shape
     units = (groups, row_parts // 2 * heads, 3, half, 128)
-    anywhere = pl.BlockSpec(memory_space=pl.ANY)
     *grads, keep, give = pl.pallas_call(
         functools.partial(
             attention_kernel, groups=groups, row_parts=row_parts, head_size=head_size
         ),
-        in_specs=[smem(), smem()] + [anywhere] * len(bias) + [vmem()] * groups,
-        out_specs=[vmem()] * groups + [anywhere] * 2,
+        in_specs=[smem(), smem()] + [vmem()] * (len(bias) + groups),
         out_shape=[jax.ShapeDtypeStruct((cols, width), BF16)] * groups
         + [jax.ShapeDtypeStruct(units, BF16)] * 2,
-        scratch_shapes=[pltpu.VMEM(units, BF16) for _ in range(2)]
-        + [pltpu.VMEM((tokens, part), BF16) for _ in range(4)]
+        scratch_shapes=[pltpu.VMEM((tokens, part), BF16) for _ in range(4)]
         + [pltpu.VMEM((part, tokens), BF16) for _ in range(3)]
         + [
             pltpu.VMEM((2, tokens, tokens), BF16),
@@ -547,11 +509,6 @@
             pltpu.VMEM((tokens, part), F32),
             pltpu.VMEM((part, tokens), F32),
             pltpu.VMEM((part, tokens), F32),
-        ]
-        + [pltpu.VMEM(block.shape, BF16) for block in bias]
-        + [
-            pltpu.SemaphoreType.DMA((heads, len(bias))),
-            pltpu.SemaphoreType.DMA((heads, row_parts)),
         ],
         compiler_params=params(),
     )(group_index, row_index, *bias, acts[0], *acts[2:], acts[1])

time: 139 us -> 137 us (0.986)
  Pallas kernels: 45.9 us -> 44.4 us
where the time goes in v10:
time: 137 us
  waiting for transfers between devices  45.1 us (33%)
  Pallas kernels  44.4 us (32%)
  starting transfers between devices  40.4 us (29%)
  other arithmetic  3.17 us (2%)
  local copies, waits for them, and re-layouts  2.78 us (2%)
    ppermute x12, starting transfers between devices, swap_groups(): got.append(lax.ppermute(sends[bits], 'grp', perm))  26.7 us
    ppermute x12, waiting for transfers between devices, swap_groups(): got.append(lax.ppermute(sends[bits], 'grp', perm))  23.7 us
    ppermute x18, waiting for transfers between devices, flip_rows(): lax.ppermute(values, 'rows', [(index, index ^ bits) for index in range(ro...  21.4 us
    pallas_call x1, Pallas kernels, attention(): pl.pallas_call(functools.partial(attention_kernel, groups=groups, row_par...  15.2 us
    ppermute x18, starting transfers between devices, flip_rows(): lax.ppermute(values, 'rows', [(index, index ^ bits) for index in range(ro...  13.7 us
    pallas_call x1, Pallas kernels, pair_back(): pl.pallas_call(functools.partial(pair_back_kernel, groups=groups, calls=l...  7.8 us
    pallas_call x1, Pallas kernels, pair_bias(): pl.pallas_call(functools.partial(bias_kernel, groups=groups, batch=16), g...  7.53 us
    pallas_call x1, Pallas kernels, split_heads(): pl.pallas_call(functools.partial(finish_kernel, groups=groups, calls=call...  7.48 us
  transfers between devices with their start and end apart: 30, of which 17 were waited for; matrix products, arithmetic and copies ran while one was open for 0% of the time, Pallas kernels for 16%

profile of v10, /device:TPU:0, one launch (start us, length us, event | category | flops | bytes accessed | tf_op | source)
XLA Modules:
  0.0 136.8 jit_solution(11520587745305730574)
XLA Ops:
  0.6 7.5 %shard_map.158 = (bf16[4,3,48,128]{3,2,1,0:T(8,128)(2,1)}, bf16[4,3,48,128]{3,2,1,0:T(8,128)(2,1)}, bf16[4,3,48,128]{3,2,1,0:T(8,128)(2,1)}, bf16[4,3,48,128]{3,2,1,0:T(8,128)(2,1)}, f32[2,48,24,192]{3,2,1,0:T(8,128)}) custom-call(s32[1]{0:T(128)} %bitcast.group_ref, s32[1]{0:T(128)} %bitcast.3.rows_ref.row_ref, s32[768]{0:T(1024)} %cols_ref.1, f32[16]{0:T(128)} %gain_ref.1, ...), custom_call_target="tpu_custom_call" | custom-call | tf_op jit(solution)/shard_map/pallas_call | solution.py:211
  8.2 4.0 %collective-permute-start = (bf16[4,3,48,128]{3,2,1,0:T(8,128)(2,1)}, bf16[4,3,48,128]{3,2,1,0:T(8,128)(2,1)S(1)}, u32[]{:S(2)}, u32[]{:S(2)}) collective-permute-start(bf16[4,3,48,128]{3,2,1,0:T(8,128)(2,1)} %get-tuple-element.64), channel_id=1, source_target_pairs={{0,2},{1,3},{2,0},{3,1},{4,6},{5,7},{6,4},{7,5},{8,10},{9,11},{10,... | collective-permute-start | bytes 442376 | tf_op jit(solution)/shard_map/ppermute | solution.py:581
  12.2 1.4 collective-permute-start.1
  13.5 0.2 collective-permute-start.2
  13.8 6.4 %shard_map.157 = (bf16[192,768]{1,0:T(8,128)(2,1)}, bf16[192,768]{1,0:T(8,128)(2,1)}, bf16[192,768]{1,0:T(8,128)(2,1)}, bf16[192,768]{1,0:T(8,128)(2,1)}, f32[192,768]{1,0:T(8,128)}, /*index=5*/f32[192,768]{1,0:T(8,128)}) custom-call(s32[1]{0:T(128)} %bitcast.group_ref, bf16[192,384]{1,0:T(8,128)(2,1)} %single_ref.3, bf16[192,768]{1,0:T(8,128)(2,1)} %bitcast.23, ...), custom_call_target="tpu_custom_call" | custom-call | tf_op jit(solution)/shard_map/pallas_call | solution.py:672
  20.2 3.3 %collective-permute-done = bf16[4,3,48,128]{3,2,1,0:T(8,128)(2,1)S(1)} collective-permute-done((bf16[4,3,48,128]{3,2,1,0:T(8,128)(2,1)}, bf16[4,3,48,128]{3,2,1,0:T(8,128)(2,1)S(1)}, u32[]{:S(2)}, u32[]{:S(2)}) %collective-permute-start) | collective-permute-done | bytes 147488 | tf_op jit(solution)/shard_map/ppermute | solution.py:581
  23.5 0.5 collective-permute-done.2
  24.0 0.1 pad_maximum_fusion.rest_0_
  24.1 1.6 %collective-permute-start.6 = (bf16[4,4,3,48,128]{4,3,2,1,0:T(8,128)(2,1)S(1)}, bf16[4,4,3,48,128]{4,3,2,1,0:T(8,128)(2,1)S(1)}, u32[]{:S(2)}, u32[]{:S(2)}) collective-permute-start(bf16[4,4,3,48,128]{4,3,2,1,0:T(8,128)(2,1)S(1)} %pad_maximum_fusion.rest_0_), channel_id=1, source_target_pairs={{0,16},{4,20},{8,24},{12,28},{16,0},{20,4},{24,8},{28,12},{1,17},{... | collective-permute-start | bytes 1769480 | tf_op jit(solution)/shard_map/ppermute | solution.py:587
  25.7 1.5 %collective-permute-start.4 = (bf16[4,4,3,48,128]{4,3,2,1,0:T(8,128)(2,1)S(1)}, bf16[4,4,3,48,128]{4,3,2,1,0:T(8,128)(2,1)S(1)}, u32[]{:S(2)}, u32[]{:S(2)}) collective-permute-start(bf16[4,4,3,48,128]{4,3,2,1,0:T(8,128)(2,1)S(1)} %pad_maximum_fusion.rest_0_), channel_id=1, source_target_pairs={{0,8},{4,12},{8,0},{12,4},{16,24},{20,28},{24,16},{28,20},{1,9},{5... | collective-permute-start | bytes 1769480 | tf_op jit(solution)/shard_map/ppermute | solution.py:587
  27.2 4.4 %collective-permute-start.8 = (bf16[192,768]{1,0:T(8,128)(2,1)S(1)}, bf16[192,768]{1,0:T(8,128)(2,1)S(1)}, u32[]{:S(2)}, u32[]{:S(2)}) collective-permute-start(bf16[192,768]{1,0:T(8,128)(2,1)S(1)} %copy-done.27), channel_id=1, source_target_pairs={{0,2},{1,3},{2,0},{3,1},{4,6},{5,7},{6,4},{7,5},{8,10},{9,11},{10,... | collective-permute-start | bytes 884744 | tf_op jit(solution)/shard_map/ppermute | solution.py:581
  31.6 0.5 collective-permute-start.9
  32.2 0.1 collective-permute-start.10
  32.2 5.1 %collective-permute-done.6.rest_4_ = bf16[4,4,3,48,128]{4,3,2,1,0:T(8,128)(2,1)S(1)} collective-permute-done((bf16[4,4,3,48,128]{4,3,2,1,0:T(8,128)(2,1)S(1)}, bf16[4,4,3,48,128]{4,3,2,1,0:T(8,128)(2,1)S(1)}, u32[]{:S(2)}, u32[]{:S(2)}) %collective-permute-start.6) | collective-permute-done | bytes 589856 | tf_op jit(solution)/shard_map/ppermute | solution.py:587
  37.4 1.3 collective-permute-start.12
  38.7 0.8 collective-permute-done.4.rest_2_
  39.5 0.9 collective-permute-start.11
  40.4 10.9 %collective-permute-done.8.rest_11_ = bf16[192,768]{1,0:T(8,128)(2,1)S(1)} collective-permute-done((bf16[192,768]{1,0:T(8,128)(2,1)S(1)}, bf16[192,768]{1,0:T(8,128)(2,1)S(1)}, u32[]{:S(2)}, u32[]{:S(2)}) %collective-permute-start.8) | collective-permute-done | bytes 294944 | tf_op jit(solution)/shard_map/ppermute | solution.py:581
  51.3 0.5 collective-permute-start.7
  51.8 0.4 collective-permute-done.10.rest_13_
  52.3 0.0 copy-start.14
  52.3 0.6 collective-permute-start.13
  52.8 0.1 collective-permute-start.14
  52.9 0.4 collective-permute-done.3.rest_1_
  53.3 0.8 collective-permute-done.7.rest_5_
  54.2 0.8 collective-permute-done.5.rest_3_
  55.0 0.4 collective-permute-done.13.rest_7_
  55.4 0.4 collective-permute-done.14.rest_9_
  55.9 0.2 copy-done.15
  56.1 0.7 copy-done.16
  56.9 15.2 %shard_map.159 = (bf16[192,768]{1,0:T(8,128)(2,1)}, bf16[192,768]{1,0:T(8,128)(2,1)}, bf16[192,768]{1,0:T(8,128)(2,1)}, bf16[192,768]{1,0:T(8,128)(2,1)}, bf16[4...) custom-call(s32[1]{0:T(128)} %bitcast.group_ref, s32[1]{0:T(128)} %bitcast.3.rows_ref.row_ref, ...), custom_call_target="tpu_custom_call" | custom-call | tf_op jit(solution)/shard_map/pallas_call | solution.py:496
  72.1 0.2 collective-permute-start.15
  72.3 4.6 %collective-permute-done.15 = bf16[4,16,3,48,128]{4,3,2,1,0:T(8,128)(2,1)S(1)} collective-permute-done((bf16[4,16,3,48,128]{4,3,2,1,0:T(8,128)(2,1)}, bf16[4,16,3,48,128]{4,3,2,1,0:T(8,128)(2,1)S(1)}, u32[]{:S(2)}, u32[]{:S(2)}) %collective-permute-start.15) | collective-permute-done | bytes 2359328 | tf_op jit(solution)/shard_map/ppermute | solution.py:587
  76.9 1.7 %add_convert_fusion.3 = (bf16[4,4,3,48,128]{4,3,2,1,0:T(8,128)(2,1)S(1)}, bf16[4,4,3,48,128]{4,3,2,1,0:T(8,128)(2,1)S(1)}) fusion(bf16[4,16,3,48,128]{4,3,2,1,0:T(8,128)(2,1)S(1)} %collective-permute-done.15, bf16[4,16,3,48,128]{4,3,2,1,0:T(8,128)(2,1)} %get-tuple-element.86), kind=kLoop, calls=%fused_computation.3 | loop fusion | flops 2359296 | bytes 3538944 | tf_op jit(solution)/shard_map/convert_element_type | solution.py:616
  78.6 0.6 collective-permute-start.16
  79.2 0.5 collective-permute-start.17
  79.7 4.7 %collective-permute-start.20 = (bf16[192,768]{1,0:T(8,128)(2,1)S(1)}, bf16[192,768]{1,0:T(8,128)(2,1)S(1)}, u32[]{:S(2)}, u32[]{:S(2)}) collective-permute-start(bf16[192,768]{1,0:T(8,128)(2,1)S(1)} %copy-done.25), channel_id=1, source_target_pairs={{0,2},{1,3},{2,0},{3,1},{4,6},{5,7},{6,4},{7,5},{8,10},{9,11},{10,... | collective-permute-start | bytes 884744 | tf_op jit(solution)/shard_map/ppermute | solution.py:581
  84.5 3.3 %collective-permute-start.21 = (bf16[192,768]{1,0:T(8,128)(2,1)S(1)}, bf16[192,768]{1,0:T(8,128)(2,1)S(1)}, u32[]{:S(2)}, u32[]{:S(2)}) collective-permute-start(bf16[192,768]{1,0:T(8,128)(2,1)S(1)} %copy-done.23), channel_id=1, source_target_pairs={{0,3},{1,2},{2,1},{3,0},{4,7},{5,6},{6,5},{7,4},{8,11},{9,10},{10,... | collective-permute-start | bytes 884744 | tf_op jit(solution)/shard_map/ppermute | solution.py:581
  87.8 6.3 %collective-permute-done.16 = bf16[4,4,3,48,128]{4,3,2,1,0:T(8,128)(2,1)S(1)} collective-permute-done((bf16[4,4,3,48,128]{4,3,2,1,0:T(8,128)(2,1)S(1)}, bf16[4,4,3,48,128]{4,3,2,1,0:T(8,128)(2,1)S(1)}, u32[]{:S(2)}, u32[]{:S(2)}) %collective-permute-start.16) | collective-permute-done | bytes 589856 | tf_op jit(solution)/shard_map/ppermute | solution.py:587
  94.1 0.3 collective-permute-done.17
  94.3 0.2 add_convert_fusion.4
  94.6 1.5 %collective-permute-start.19 = (bf16[4,2,3,48,128]{4,3,2,1,0:T(8,128)(2,1)S(1)}, bf16[4,2,3,48,128]{4,3,2,1,0:T(8,128)(2,1)S(1)}, u32[]{:S(2)}, u32[]{:S(2)}) collective-permute-start(bf16[4,2,3,48,128]{4,3,2,1,0:T(8,128)(2,1)S(1)} %get-tuple-element.119), channel_id=1, source_target_pairs={{0,8},{4,12},{8,0},{12,4},{16,24},{20,28},{24,16},{28,20},{1,9},{5... | collective-permute-start | bytes 884744 | tf_op jit(solution)/shard_map/ppermute | solution.py:587
  96.1 0.5 collective-permute-start.18
  96.6 8.4 %collective-permute-done.20.rest_2_ = bf16[192,768]{1,0:T(8,128)(2,1)S(1)} collective-permute-done((bf16[192,768]{1,0:T(8,128)(2,1)S(1)}, bf16[192,768]{1,0:T(8,128)(2,1)S(1)}, u32[]{:S(2)}, u32[]{:S(2)}) %collective-permute-start.20) | collective-permute-done | bytes 294944 | tf_op jit(solution)/shard_map/ppermute | solution.py:581
  105.0 0.2 collective-permute-done.22.rest_1_
  105.3 0.3 add_convert_fusion
  105.6 0.1 copy-done.9
  105.7 0.1 copy-done.11
  105.9 0.1 copy-done.12
  105.9 0.7 slice_bitcast_fusion
  106.6 7.5 %collective-permute-start.26 = (bf16[4,3,48,128]{3,2,1,0:T(8,128)(2,1)S(1)}, bf16[4,3,48,128]{3,2,1,0:T(8,128)(2,1)S(1)}, u32[]{:S(2)}, u32[]{:S(2)}) collective-permute-start(bf16[4,3,48,128]{3,2,1,0:T(8,128)(2,1)S(1)} %get-tuple-element.109), channel_id=1, source_target_pairs={{0,2},{1,3},{2,0},{3,1},{4,6},{5,7},{6,4},{7,5},{8,10},{9,11},{10,... | collective-permute-start | bytes 442376 | tf_op jit(solution)/shard_map/ppermute | solution.py:581
  114.1 0.5 collective-permute-start.27
  114.6 0.0 collective-permute-start.28
  114.7 7.5 %shard_map.160 = (bf16[192,768]{1,0:T(8,128)(2,1)}, bf16[192,384]{1,0:T(8,128)(2,1)}) custom-call(s32[1]{0:T(128)} %bitcast.group_ref, bf16[192,384]{1,0:T(8,128)(2,1)} %single_ref.3, bf16[192,768]{1,0:T(8,128)(2,1)} %bitcast.24, bf16[192,768]{1,0:T(8,128)(2,1)} %bitcast.26, f32[192,768]{1,0:T(8,128)} %get-tuple-element.61.gamma_ref, ...), custom_call_target="tpu_custom_call" | custom-call | tf_op jit(solution)/shard_map/pallas_call | solution.py:709
  122.1 2.4 %collective-permute-start.25 = (bf16[192,384]{1,0:T(8,128)(2,1)}, bf16[192,384]{1,0:T(8,128)(2,1)S(1)}, u32[]{:S(2)}, u32[]{:S(2)}) collective-permute-start(bf16[192,384]{1,0:T(8,128)(2,1)} %get-tuple-element.106), channel_id=1, source_target_pairs={{0,24},{4,28},{8,16},{12,20},{16,8},{20,12},{24,0},{28,4},{1,25},{... | collective-permute-start | bytes 442376 | tf_op jit(solution)/shard_map/ppermute | solution.py:587
  124.6 0.5 collective-permute-start.24
  125.1 0.8 collective-permute-start.23
  126.0 0.6 copy-done.20
  126.6 0.1 copy-done.21
  126.7 7.8 %shard_map.161 = bf16[2,48,192,128]{3,2,1,0:T(8,128)(2,1)} custom-call(s32[1]{0:T(128)} %bitcast.group_ref, bf16[2,48,192,128]{3,2,1,0:T(8,128)(2,1)} %bitcast.21, f32[2,48,24,192]{3,2,1,0:T(8,128)} %get-tuple-element.107.stats_ref, bf16[16,128]{1,0:T(8,128)(2,1)} %bitcast.32, bf16[4,3,48,128]{3,2,1,0:T(8,128)(2,1)} %get-tuple-element.108.rest_0_, ...), custom_call_target="tpu_custom_call" | custom-call | tf_op jit(solution)/shard_map/pallas_call | solution.py:321
  134.5 0.1 add_convert_fusion.6
  134.6 0.1 collective-permute-start.29
  134.7 1.4 collective-permute-done.29
  136.0 0.7 convert_add_fusion
  (68 shorter events, 0.2 us)
Async XLA Ops:
  8.2 15.3 %collective-permute-start = (bf16[4,3,48,128]{3,2,1,0:T(8,128)(2,1)}, bf16[4,3,48,128]{3,2,1,0:T(8,128)(2,1)S(1)}, u32[]{:S(2)}, u32[]{:S(2)}) collective-permute-start(bf16[4,3,48,128]{3,2,1,0:T(8,128)(2,1)} %get-tuple-element.64), channel_id=1, source_target_pairs={{0,2},{1,3},{2,0},{3,1},{4,6},{5,7},{6,4},{7,5},{8,10},{9,11},{10,... | collective-permute-start | bytes 442376 | tf_op jit(solution)/shard_map/ppermute | solution.py:581
  12.2 11.3 %collective-permute-start.1 = (bf16[4,3,48,128]{3,2,1,0:T(8,128)(2,1)}, bf16[4,3,48,128]{3,2,1,0:T(8,128)(2,1)S(1)}, u32[]{:S(2)}, u32[]{:S(2)}) collective-permute-start(bf16[4,3,48,128]{3,2,1,0:T(8,128)(2,1)} %get-tuple-element.65), channel_id=1, source_target_pairs={{0,3},{1,2},{2,1},{3,0},{4,7},{5,6},{6,5},{7,4},{8,11},{9,10},{10,... | collective-permute-start | bytes 442376 | tf_op jit(solution)/shard_map/ppermute | solution.py:581
  13.5 10.4 %collective-permute-start.2 = (bf16[4,3,48,128]{3,2,1,0:T(8,128)(2,1)}, bf16[4,3,48,128]{3,2,1,0:T(8,128)(2,1)S(1)}, u32[]{:S(2)}, u32[]{:S(2)}) collective-permute-start(bf16[4,3,48,128]{3,2,1,0:T(8,128)(2,1)} %get-tuple-element.66), channel_id=1, source_target_pairs={{0,1},{1,0},{2,3},{3,2},{4,5},{5,4},{6,7},{7,6},{8,9},{9,8},{10,11... | collective-permute-start | bytes 442376 | tf_op jit(solution)/shard_map/ppermute | solution.py:581
  13.8 10.2 %copy-start.17 = (bf16[4,3,48,128]{3,2,1,0:T(8,128)(2,1)S(1)}, bf16[4,3,48,128]{3,2,1,0:T(8,128)(2,1)}, u32[]{:S(2)}) copy-start(bf16[4,3,48,128]{3,2,1,0:T(8,128)(2,1)} %get-tuple-element.74) | copy-start | bytes 442372
  20.1 7.0 %copy-start.27 = (bf16[192,768]{1,0:T(8,128)(2,1)S(1)}, bf16[192,768]{1,0:T(8,128)(2,1)}, u32[]{:S(2)}) copy-start(bf16[192,768]{1,0:T(8,128)(2,1)} %get-tuple-element.71) | copy-start | bytes 884740
  20.1 11.5 %copy-start.26 = (bf16[192,768]{1,0:T(8,128)(2,1)S(1)}, bf16[192,768]{1,0:T(8,128)(2,1)}, u32[]{:S(2)}) copy-start(bf16[192,768]{1,0:T(8,128)(2,1)} %get-tuple-element.72) | copy-start | bytes 884740
  20.2 12.0 %copy-start.24 = (bf16[192,768]{1,0:T(8,128)(2,1)S(1)}, bf16[192,768]{1,0:T(8,128)(2,1)}, u32[]{:S(2)}) copy-start(bf16[192,768]{1,0:T(8,128)(2,1)} %get-tuple-element.73) | copy-start | bytes 884740
  24.0 31.8 %copy-start = (bf16[4,4,3,48,128]{4,3,2,1,0:T(8,128)(2,1)}, bf16[4,4,3,48,128]{4,3,2,1,0:T(8,128)(2,1)S(1)}, u32[]{:S(2)}) copy-start(bf16[4,4,3,48,128]{4,3,2,1,0:T(8,128)(2,1)S(1)} %pad_maximum_fusion.rest_0_) | copy-start | bytes 1769476
  24.1 13.3 %collective-permute-start.6 = (bf16[4,4,3,48,128]{4,3,2,1,0:T(8,128)(2,1)S(1)}, bf16[4,4,3,48,128]{4,3,2,1,0:T(8,128)(2,1)S(1)}, u32[]{:S(2)}, u32[]{:S(2)}) collective-permute-start(bf16[4,4,3,48,128]{4,3,2,1,0:T(8,128)(2,1)S(1)} %pad_maximum_fusion.rest_0_), channel_id=1, source_target_pairs={{0,16},{4,20},{8,24},{12,28},{16,0},{20,4},{24,8},{28,12},{1,17},{... | collective-permute-start | bytes 1769480 | tf_op jit(solution)/shard_map/ppermute | solution.py:587
  25.7 13.8 %collective-permute-start.4 = (bf16[4,4,3,48,128]{4,3,2,1,0:T(8,128)(2,1)S(1)}, bf16[4,4,3,48,128]{4,3,2,1,0:T(8,128)(2,1)S(1)}, u32[]{:S(2)}, u32[]{:S(2)}) collective-permute-start(bf16[4,4,3,48,128]{4,3,2,1,0:T(8,128)(2,1)S(1)} %pad_maximum_fusion.rest_0_), channel_id=1, source_target_pairs={{0,8},{4,12},{8,0},{12,4},{16,24},{20,28},{24,16},{28,20},{1,9},{5... | collective-permute-start | bytes 1769480 | tf_op jit(solution)/shard_map/ppermute | solution.py:587
  27.2 24.1 %collective-permute-start.8 = (bf16[192,768]{1,0:T(8,128)(2,1)S(1)}, bf16[192,768]{1,0:T(8,128)(2,1)S(1)}, u32[]{:S(2)}, u32[]{:S(2)}) collective-permute-start(bf16[192,768]{1,0:T(8,128)(2,1)S(1)} %copy-done.27), channel_id=1, source_target_pairs={{0,2},{1,3},{2,0},{3,1},{4,6},{5,7},{6,4},{7,5},{8,10},{9,11},{10,... | collective-permute-start | bytes 884744 | tf_op jit(solution)/shard_map/ppermute | solution.py:581
  31.6 19.7 %collective-permute-start.9 = (bf16[192,768]{1,0:T(8,128)(2,1)S(1)}, bf16[192,768]{1,0:T(8,128)(2,1)S(1)}, u32[]{:S(2)}, u32[]{:S(2)}) collective-permute-start(bf16[192,768]{1,0:T(8,128)(2,1)S(1)} %copy-done.26), channel_id=1, source_target_pairs={{0,3},{1,2},{2,1},{3,0},{4,7},{5,6},{6,5},{7,4},{8,11},{9,10},{10,... | collective-permute-start | bytes 884744 | tf_op jit(solution)/shard_map/ppermute | solution.py:581
  32.2 20.1 %collective-permute-start.10 = (bf16[192,768]{1,0:T(8,128)(2,1)S(1)}, bf16[192,768]{1,0:T(8,128)(2,1)S(1)}, u32[]{:S(2)}, u32[]{:S(2)}) collective-permute-start(bf16[192,768]{1,0:T(8,128)(2,1)S(1)} %copy-done.24), channel_id=1, source_target_pairs={{0,1},{1,0},{2,3},{3,2},{4,5},{5,4},{6,7},{7,6},{8,9},{9,8},{10,11... | collective-permute-start | bytes 884744 | tf_op jit(solution)/shard_map/ppermute | solution.py:581
  37.4 18.5 %copy-start.2 = (bf16[4,4,3,48,128]{4,3,2,1,0:T(8,128)(2,1)}, bf16[4,4,3,48,128]{4,3,2,1,0:T(8,128)(2,1)S(1)}, u32[]{:S(2)}) copy-start(bf16[4,4,3,48,128]{4,3,2,1,0:T(8,128)(2,1)S(1)} %collective-permute-done.6.rest_4_) | copy-start | bytes 1769476
  37.4 14.9 %collective-permute-start.12 = (bf16[2,4,3,48,128]{4,3,2,1,0:T(8,128)(2,1)S(1)}, bf16[2,4,3,48,128]{4,3,2,1,0:T(8,128)(2,1)S(1)}, u32[]{:S(2)}, u32[]{:S(2)}) collective-permute-start(bf16[2,4,3,48,128]{4,3,2,1,0:T(8,128)(2,1)S(1)} %slice.81), channel_id=1, source_target_pairs={{0,8},{4,12},{8,0},{12,4},{16,24},{20,28},{24,16},{28,20},{1,9},{5... | collective-permute-start | bytes 884744 | tf_op jit(solution)/shard_map/ppermute | solution.py:587
  39.5 16.3 %copy-start.3 = (bf16[4,4,3,48,128]{4,3,2,1,0:T(8,128)(2,1)}, bf16[4,4,3,48,128]{4,3,2,1,0:T(8,128)(2,1)S(1)}, u32[]{:S(2)}) copy-start(bf16[4,4,3,48,128]{4,3,2,1,0:T(8,128)(2,1)S(1)} %collective-permute-done.4.rest_2_) | copy-start | bytes 1769476
  39.5 12.7 %collective-permute-start.11 = (bf16[2,4,3,48,128]{4,3,2,1,0:T(8,128)(2,1)S(1)}, bf16[2,4,3,48,128]{4,3,2,1,0:T(8,128)(2,1)S(1)}, u32[]{:S(2)}, u32[]{:S(2)}) collective-permute-start(bf16[2,4,3,48,128]{4,3,2,1,0:T(8,128)(2,1)S(1)} %slice.80), channel_id=1, source_target_pairs={{0,16},{4,20},{8,24},{12,28},{16,0},{20,4},{24,8},{28,12},{1,17},{... | collective-permute-start | bytes 884744 | tf_op jit(solution)/shard_map/ppermute | solution.py:587
  51.3 4.6 %copy-start.7 = (bf16[192,768]{1,0:T(8,128)(2,1)}, bf16[192,768]{1,0:T(8,128)(2,1)S(1)}, u32[]{:S(2)}) copy-start(bf16[192,768]{1,0:T(8,128)(2,1)S(1)} %collective-permute-done.8.rest_11_) | copy-start | bytes 884740
  51.3 2.0 %collective-permute-start.3 = (bf16[4,4,3,48,128]{4,3,2,1,0:T(8,128)(2,1)S(1)}, bf16[4,4,3,48,128]{4,3,2,1,0:T(8,128)(2,1)S(1)}, u32[]{:S(2)}, u32[]{:S(2)}) collective-permute-start(bf16[4,4,3,48,128]{4,3,2,1,0:T(8,128)(2,1)S(1)} %pad_maximum_fusion.rest_0_), channel_id=1, source_target_pairs={{0,4},{4,0},{8,12},{12,8},{16,20},{20,16},{24,28},{28,24},{1,5},{5... | collective-permute-start | bytes 1769480 | tf_op jit(solution)/shard_map/ppermute | solution.py:587
  51.3 4.5 %copy-start.8 = (bf16[192,768]{1,0:T(8,128)(2,1)}, bf16[192,768]{1,0:T(8,128)(2,1)S(1)}, u32[]{:S(2)}) copy-start(bf16[192,768]{1,0:T(8,128)(2,1)S(1)} %collective-permute-done.9.rest_12_) | copy-start | bytes 884740
  51.3 2.8 %collective-permute-start.7 = (bf16[4,4,3,48,128]{4,3,2,1,0:T(8,128)(2,1)S(1)}, bf16[4,4,3,48,128]{4,3,2,1,0:T(8,128)(2,1)S(1)}, u32[]{:S(2)}, u32[]{:S(2)}) collective-permute-start(bf16[4,4,3,48,128]{4,3,2,1,0:T(8,128)(2,1)S(1)} %collective-permute-done.6.rest_4_), channel_id=1, source_target_pairs={{0,4},{4,0},{8,12},{12,8},{16,20},{20,16},{24,28},{28,24},{1,5},{5... | collective-permute-start | bytes 1769480 | tf_op jit(solution)/shard_map/ppermute | solution.py:587
  52.2 3.6 %copy-start.10 = (bf16[192,768]{1,0:T(8,128)(2,1)}, bf16[192,768]{1,0:T(8,128)(2,1)S(1)}, u32[]{:S(2)}) copy-start(bf16[192,768]{1,0:T(8,128)(2,1)S(1)} %collective-permute-done.10.rest_13_) | copy-start | bytes 884740
  52.2 2.8 %collective-permute-start.5 = (bf16[4,4,3,48,128]{4,3,2,1,0:T(8,128)(2,1)S(1)}, bf16[4,4,3,48,128]{4,3,2,1,0:T(8,128)(2,1)S(1)}, u32[]{:S(2)}, u32[]{:S(2)}) collective-permute-start(bf16[4,4,3,48,128]{4,3,2,1,0:T(8,128)(2,1)S(1)} %collective-permute-done.4.rest_2_), channel_id=1, source_target_pairs={{0,4},{4,0},{8,12},{12,8},{16,20},{20,16},{24,28},{28,24},{1,5},{5... | collective-permute-start | bytes 1769480 | tf_op jit(solution)/shard_map/ppermute | solution.py:587
  52.2 3.6 %copy-start.13 = (bf16[2,4,3,48,128]{4,3,2,1,0:T(8,128)(2,1)}, bf16[2,4,3,48,128]{4,3,2,1,0:T(8,128)(2,1)S(1)}, u32[]{:S(2)}) copy-start(bf16[2,4,3,48,128]{4,3,2,1,0:T(8,128)(2,1)S(1)} %collective-permute-done.12.rest_8_) | copy-start | bytes 884740
  52.3 3.6 %copy-start.14 = (bf16[2,4,3,48,128]{4,3,2,1,0:T(8,128)(2,1)}, bf16[2,4,3,48,128]{4,3,2,1,0:T(8,128)(2,1)S(1)}, u32[]{:S(2)}) copy-start(bf16[2,4,3,48,128]{4,3,2,1,0:T(8,128)(2,1)S(1)} %collective-permute-done.11.rest_6_) | copy-start | bytes 884740
  52.3 3.1 %collective-permute-start.13 = (bf16[2,4,3,48,128]{4,3,2,1,0:T(8,128)(2,1)S(1)}, bf16[2,4,3,48,128]{4,3,2,1,0:T(8,128)(2,1)S(1)}, u32[]{:S(2)}, u32[]{:S(2)}) collective-permute-start(bf16[2,4,3,48,128]{4,3,2,1,0:T(8,128)(2,1)S(1)} %collective-permute-done.11.rest_6_), channel_id=1, source_target_pairs={{0,4},{4,0},{8,12},{12,8},{16,20},{20,16},{24,28},{28,24},{1,5},{5... | collective-permute-start | bytes 884744 | tf_op jit(solution)/shard_map/ppermute | solution.py:587
  52.8 3.0 %collective-permute-start.14 = (bf16[2,4,3,48,128]{4,3,2,1,0:T(8,128)(2,1)S(1)}, bf16[2,4,3,48,128]{4,3,2,1,0:T(8,128)(2,1)S(1)}, u32[]{:S(2)}, u32[]{:S(2)}) collective-permute-start(bf16[2,4,3,48,128]{4,3,2,1,0:T(8,128)(2,1)S(1)} %collective-permute-done.12.rest_8_), channel_id=1, source_target_pairs={{0,4},{4,0},{8,12},{12,8},{16,20},{20,16},{24,28},{28,24},{1,5},{5... | collective-permute-start | bytes 884744 | tf_op jit(solution)/shard_map/ppermute | solution.py:587
  53.3 2.6 %copy-start.4 = (bf16[4,4,3,48,128]{4,3,2,1,0:T(8,128)(2,1)}, bf16[4,4,3,48,128]{4,3,2,1,0:T(8,128)(2,1)S(1)}, u32[]{:S(2)}) copy-start(bf16[4,4,3,48,128]{4,3,2,1,0:T(8,128)(2,1)S(1)} %collective-permute-done.3.rest_1_) | copy-start | bytes 1769476
  54.2 1.8 %copy-start.5 = (bf16[4,4,3,48,128]{4,3,2,1,0:T(8,128)(2,1)}, bf16[4,4,3,48,128]{4,3,2,1,0:T(8,128)(2,1)S(1)}, u32[]{:S(2)}) copy-start(bf16[4,4,3,48,128]{4,3,2,1,0:T(8,128)(2,1)S(1)} %collective-permute-done.7.rest_5_) | copy-start | bytes 1769476
  55.0 0.9 copy-start.6
  55.4 0.7 copy-start.15
  56.1 0.7 copy-start.16
  72.1 4.8 %collective-permute-start.15 = (bf16[4,16,3,48,128]{4,3,2,1,0:T(8,128)(2,1)}, bf16[4,16,3,48,128]{4,3,2,1,0:T(8,128)(2,1)S(1)}, u32[]{:S(2)}, u32[]{:S(2)}) collective-permute-start(bf16[4,16,3,48,128]{4,3,2,1,0:T(8,128)(2,1)} %get-tuple-element.87), channel_id=1, source_target_pairs={{0,4},{4,0},{8,12},{12,8},{16,20},{20,16},{24,28},{28,24},{1,5},{5... | collective-permute-start | bytes 7077896 | tf_op jit(solution)/shard_map/ppermute | solution.py:587
  76.9 2.9 %copy-start.25 = (bf16[192,768]{1,0:T(8,128)(2,1)S(1)}, bf16[192,768]{1,0:T(8,128)(2,1)}, u32[]{:S(2)}) copy-start(bf16[192,768]{1,0:T(8,128)(2,1)} %get-tuple-element.89) | copy-start | bytes 884740
  76.9 7.6 %copy-start.23 = (bf16[192,768]{1,0:T(8,128)(2,1)S(1)}, bf16[192,768]{1,0:T(8,128)(2,1)}, u32[]{:S(2)}) copy-start(bf16[192,768]{1,0:T(8,128)(2,1)} %get-tuple-element.90) | copy-start | bytes 884740
  76.9 10.9 %copy-start.22 = (bf16[192,768]{1,0:T(8,128)(2,1)S(1)}, bf16[192,768]{1,0:T(8,128)(2,1)}, u32[]{:S(2)}) copy-start(bf16[192,768]{1,0:T(8,128)(2,1)} %get-tuple-element.91) | copy-start | bytes 884740
  76.9 17.4 %copy-start.1 = (bf16[4,16,3,48,128]{4,3,2,1,0:T(8,128)(2,1)S(1)}, bf16[4,16,3,48,128]{4,3,2,1,0:T(8,128)(2,1)}, u32[]{:S(2)}) copy-start(bf16[4,16,3,48,128]{4,3,2,1,0:T(8,128)(2,1)} %get-tuple-element.86) | copy-start | bytes 7077892
  78.6 15.4 %collective-permute-start.16 = (bf16[4,4,3,48,128]{4,3,2,1,0:T(8,128)(2,1)S(1)}, bf16[4,4,3,48,128]{4,3,2,1,0:T(8,128)(2,1)S(1)}, u32[]{:S(2)}, u32[]{:S(2)}) collective-permute-start(bf16[4,4,3,48,128]{4,3,2,1,0:T(8,128)(2,1)S(1)} %get-tuple-element.121), channel_id=1, source_target_pairs={{0,8},{4,12},{8,0},{12,4},{16,24},{20,28},{24,16},{28,20},{1,9},{5... | collective-permute-start | bytes 1769480 | tf_op jit(solution)/shard_map/ppermute | solution.py:587
  79.2 15.1 %collective-permute-start.17 = (bf16[4,4,3,48,128]{4,3,2,1,0:T(8,128)(2,1)S(1)}, bf16[4,4,3,48,128]{4,3,2,1,0:T(8,128)(2,1)S(1)}, u32[]{:S(2)}, u32[]{:S(2)}) collective-permute-start(bf16[4,4,3,48,128]{4,3,2,1,0:T(8,128)(2,1)S(1)} %get-tuple-element.122), channel_id=1, source_target_pairs={{0,16},{4,20},{8,24},{12,28},{16,0},{20,4},{24,8},{28,12},{1,17},{... | collective-permute-start | bytes 1769480 | tf_op jit(solution)/shard_map/ppermute | solution.py:587
  79.7 25.3 %collective-permute-start.20 = (bf16[192,768]{1,0:T(8,128)(2,1)S(1)}, bf16[192,768]{1,0:T(8,128)(2,1)S(1)}, u32[]{:S(2)}, u32[]{:S(2)}) collective-permute-start(bf16[192,768]{1,0:T(8,128)(2,1)S(1)} %copy-done.25), channel_id=1, source_target_pairs={{0,2},{1,3},{2,0},{3,1},{4,6},{5,7},{6,4},{7,5},{8,10},{9,11},{10,... | collective-permute-start | bytes 884744 | tf_op jit(solution)/shard_map/ppermute | solution.py:581
  84.5 20.6 %collective-permute-start.21 = (bf16[192,768]{1,0:T(8,128)(2,1)S(1)}, bf16[192,768]{1,0:T(8,128)(2,1)S(1)}, u32[]{:S(2)}, u32[]{:S(2)}) collective-permute-start(bf16[192,768]{1,0:T(8,128)(2,1)S(1)} %copy-done.23), channel_id=1, source_target_pairs={{0,3},{1,2},{2,1},{3,0},{4,7},{5,6},{6,5},{7,4},{8,11},{9,10},{10,... | collective-permute-start | bytes 884744 | tf_op jit(solution)/shard_map/ppermute | solution.py:581
  87.8 17.5 %collective-permute-start.22 = (bf16[192,768]{1,0:T(8,128)(2,1)S(1)}, bf16[192,768]{1,0:T(8,128)(2,1)S(1)}, u32[]{:S(2)}, u32[]{:S(2)}) collective-permute-start(bf16[192,768]{1,0:T(8,128)(2,1)S(1)} %copy-done.22), channel_id=1, source_target_pairs={{0,1},{1,0},{2,3},{3,2},{4,5},{5,4},{6,7},{7,6},{8,9},{9,8},{10,11... | collective-permute-start | bytes 884744 | tf_op jit(solution)/shard_map/ppermute | solution.py:581
  94.6 10.7 %collective-permute-start.19 = (bf16[4,2,3,48,128]{4,3,2,1,0:T(8,128)(2,1)S(1)}, bf16[4,2,3,48,128]{4,3,2,1,0:T(8,128)(2,1)S(1)}, u32[]{:S(2)}, u32[]{:S(2)}) collective-permute-start(bf16[4,2,3,48,128]{4,3,2,1,0:T(8,128)(2,1)S(1)} %get-tuple-element.119), channel_id=1, source_target_pairs={{0,8},{4,12},{8,0},{12,4},{16,24},{20,28},{24,16},{28,20},{1,9},{5... | collective-permute-start | bytes 884744 | tf_op jit(solution)/shard_map/ppermute | solution.py:587
  96.1 9.2 %collective-permute-start.18 = (bf16[4,2,3,48,128]{4,3,2,1,0:T(8,128)(2,1)S(1)}, bf16[4,2,3,48,128]{4,3,2,1,0:T(8,128)(2,1)S(1)}, u32[]{:S(2)}, u32[]{:S(2)}) collective-permute-start(bf16[4,2,3,48,128]{4,3,2,1,0:T(8,128)(2,1)S(1)} %get-tuple-element.120), channel_id=1, source_target_pairs={{0,16},{4,20},{8,24},{12,28},{16,0},{20,4},{24,8},{28,12},{1,17},{... | collective-permute-start | bytes 884744 | tf_op jit(solution)/shard_map/ppermute | solution.py:587
  105.0 0.7 copy-start.9
  105.0 0.8 copy-start.11
  105.2 0.7 copy-start.12
  106.6 18.5 %collective-permute-start.26 = (bf16[4,3,48,128]{3,2,1,0:T(8,128)(2,1)S(1)}, bf16[4,3,48,128]{3,2,1,0:T(8,128)(2,1)S(1)}, u32[]{:S(2)}, u32[]{:S(2)}) collective-permute-start(bf16[4,3,48,128]{3,2,1,0:T(8,128)(2,1)S(1)} %get-tuple-element.109), channel_id=1, source_target_pairs={{0,2},{1,3},{2,0},{3,1},{4,6},{5,7},{6,4},{7,5},{8,10},{9,11},{10,... | collective-permute-start | bytes 442376 | tf_op jit(solution)/shard_map/ppermute | solution.py:581
  114.1 11.9 %collective-permute-start.27 = (bf16[4,3,48,128]{3,2,1,0:T(8,128)(2,1)S(1)}, bf16[4,3,48,128]{3,2,1,0:T(8,128)(2,1)S(1)}, u32[]{:S(2)}, u32[]{:S(2)}) collective-permute-start(bf16[4,3,48,128]{3,2,1,0:T(8,128)(2,1)S(1)} %get-tuple-element.110), channel_id=1, source_target_pairs={{0,3},{1,2},{2,1},{3,0},{4,7},{5,6},{6,5},{7,4},{8,11},{9,10},{10,... | collective-permute-start | bytes 442376 | tf_op jit(solution)/shard_map/ppermute | solution.py:581
  114.6 11.3 %collective-permute-start.28 = (bf16[4,3,48,128]{3,2,1,0:T(8,128)(2,1)S(1)}, bf16[4,3,48,128]{3,2,1,0:T(8,128)(2,1)S(1)}, u32[]{:S(2)}, u32[]{:S(2)}) collective-permute-start(bf16[4,3,48,128]{3,2,1,0:T(8,128)(2,1)S(1)} %get-tuple-element.111), channel_id=1, source_target_pairs={{0,1},{1,0},{2,3},{3,2},{4,5},{5,4},{6,7},{7,6},{8,9},{9,8},{10,11... | collective-permute-start | bytes 442376 | tf_op jit(solution)/shard_map/ppermute | solution.py:581
  122.1 12.3 %collective-permute-start.25 = (bf16[192,384]{1,0:T(8,128)(2,1)}, bf16[192,384]{1,0:T(8,128)(2,1)S(1)}, u32[]{:S(2)}, u32[]{:S(2)}) collective-permute-start(bf16[192,384]{1,0:T(8,128)(2,1)} %get-tuple-element.106), channel_id=1, source_target_pairs={{0,24},{4,28},{8,16},{12,20},{16,8},{20,12},{24,0},{28,4},{1,25},{... | collective-permute-start | bytes 442376 | tf_op jit(solution)/shard_map/ppermute | solution.py:587
  124.6 9.9 %collective-permute-start.24 = (bf16[192,384]{1,0:T(8,128)(2,1)}, bf16[192,384]{1,0:T(8,128)(2,1)S(1)}, u32[]{:S(2)}, u32[]{:S(2)}) collective-permute-start(bf16[192,384]{1,0:T(8,128)(2,1)} %get-tuple-element.106), channel_id=1, source_target_pairs={{0,16},{4,20},{8,24},{12,28},{16,0},{20,4},{24,8},{28,12},{1,17},{... | collective-permute-start | bytes 442376 | tf_op jit(solution)/shard_map/ppermute | solution.py:587
  125.1 0.9 copy-start.19
  125.1 9.4 %collective-permute-start.23 = (bf16[192,384]{1,0:T(8,128)(2,1)}, bf16[192,384]{1,0:T(8,128)(2,1)S(1)}, u32[]{:S(2)}, u32[]{:S(2)}) collective-permute-start(bf16[192,384]{1,0:T(8,128)(2,1)} %get-tuple-element.106), channel_id=1, source_target_pairs={{0,8},{4,12},{8,0},{12,4},{16,24},{20,28},{24,16},{28,20},{1,9},{5... | collective-permute-start | bytes 442376 | tf_op jit(solution)/shard_map/ppermute | solution.py:587
  126.0 0.7 copy-start.20
  126.0 0.7 copy-start.21
  126.7 7.8 %copy-start.18 = (bf16[192,384]{1,0:T(8,128)(2,1)S(1)}, bf16[192,384]{1,0:T(8,128)(2,1)}, u32[]{:S(2)}) copy-start(bf16[192,384]{1,0:T(8,128)(2,1)} %get-tuple-element.106) | copy-start | bytes 442372
  134.6 1.4 %collective-permute-start.29 = (bf16[192,384]{1,0:T(8,128)(2,1)S(1)}, bf16[192,384]{1,0:T(8,128)(2,1)S(1)}, u32[]{:S(2)}, u32[]{:S(2)}) collective-permute-start(bf16[192,384]{1,0:T(8,128)(2,1)S(1)} %add_convert_fusion.6), channel_id=1, source_target_pairs={{0,4},{4,0},{8,12},{12,8},{16,20},{20,16},{24,28},{28,24},{1,5},{5... | collective-permute-start | bytes 442376 | tf_op jit(solution)/shard_map/ppermute | solution.py:587

commit v11 on v10

--- a/solution.py
+++ b/solution.py
@@ -356,6 +356,7 @@
     (
         keep_ref,
         give_ref,
+        give_late_ref,
         query_ref,
         keys_ref,
         values_ref,
@@ -455,7 +456,11 @@
 
         for other in range(row_parts):
             unit = order.index((other // 2, head))
-            dbias_ref = give_ref if other % 2 else keep_ref
+            dbias_ref = keep_ref
+            if other % 2:
+                early = len(order) // 2
+                dbias_ref = give_ref if unit < early else give_late_ref
+                unit = unit % early
             scores = [score_head[rows, :] for _, rows in places(row_ref[0] ^ other)]
             for column in range(groups):
                 start = groups * 128 + column * rest_lanes
@@ -493,13 +498,14 @@
     part = width // 4
     _, heads, _, half, _ = bias[0].shape
     units = (groups, row_parts // 2 * heads, 3, half, 128)
-    *grads, keep, give = pl.pallas_call(
+    some = (groups, row_parts // 4 * heads, 3, half, 128)
+    *grads, keep, give, give_late = pl.pallas_call(
         functools.partial(
             attention_kernel, groups=groups, row_parts=row_parts, head_size=head_size
         ),
         in_specs=[smem(), smem()] + [vmem()] * (len(bias) + groups),
         out_shape=[jax.ShapeDtypeStruct((cols, width), BF16)] * groups
-        + [jax.ShapeDtypeStruct(units, BF16)] * 2,
+        + [jax.ShapeDtypeStruct(shape, BF16) for shape in (units, some, some)],
         scratch_shapes=[pltpu.VMEM((tokens, part), BF16) for _ in range(4)]
         + [pltpu.VMEM((part, tokens), BF16) for _ in range(3)]
         + [
@@ -512,7 +518,7 @@
         ],
         compiler_params=params(),
     )(group_index, row_index, *bias, acts[0], *acts[2:], acts[1])
-    return grads, keep, give
+    return grads, keep, give, give_late
 
 
 def finish_kernel(
@@ -602,15 +608,21 @@
     return blocks, acts
 
 
-def scatter_rows(keep, give, row_total):
+def swap_cores(give, give_late, row_total):
     got = flip_rows(give, 1, row_total)
-    early = keep.shape[1] // 2
+    got, give_late = lax.optimization_barrier((got, give_late))
+    return got, flip_rows(give_late, 1, row_total)
+
+
+def scatter_rows(keep, got, got_late, row_total):
+    early = got.shape[1]
     heads = early // 2
     part = heads // 2
 
     def add(first, count, *others):
+        source, place = (got, first) if first < early else (got_late, first - early)
         total = keep[:, first : first + count].astype(F32)
-        total += got[:, first : first + count].astype(F32)
+        total += source[:, place : place + count].astype(F32)
         for other in others:
             total += other.astype(F32)
         return total.astype(BF16)
@@ -700,9 +712,13 @@
     acts_send = [acts_send[SLOT_ORDER.index(slot)] for slot in range(groups)]
     acts = swap_groups(acts_send)
     bias_all, acts = gather_rows(jnp.stack(bias_got), acts, row_total)
-    grads_send, keep, give = attention(group_index, row_index, acts, bias_all, head_size)
+    grads_send, keep, give, give_late = attention(
+        group_index, row_index, acts, bias_all, head_size
+    )
+    got, got_late = swap_cores(give, give_late, row_total)
+    got_late, grads_send[1] = lax.optimization_barrier((got_late, grads_send[1]))
     grads = swap_groups(grads_send)
-    own, far_two, near_two = scatter_rows(keep, give, row_total)
+    own, far_two, near_two = scatter_rows(keep, got, got_late, row_total)
     far_two, near_two, grads = lax.optimization_barrier((far_two, near_two, grads))
     dbias_own, grads = lax.optimization_barrier((add_last(own, far_two, near_two), grads))
     dbias_back = swap_groups(dbias_own)

time: 137 us -> 136 us (level)
  waiting for transfers between devices: 45.1 us -> 43.6 us
    ppermute x18 -> x19, waiting for transfers between devices: 21.4 us -> 19.9 us  [flip_rows(): lax.ppermute(values, 'rows', [(index, index ^ bits) for index in range(ro...]
    ppermute x18 -> x19, starting transfers between devices: 13.7 us -> 13.9 us  [flip_rows(): lax.ppermute(values, 'rows', [(index, index ^ bits) for index in range(ro...]
  transfers between devices with their start and end apart: 30 -> 31, of which waited for: 17 -> 17; matrix products, arithmetic and copies ran while one was open for 0% -> 2% of each run, Pallas kernels for 16% -> 16%
where the time goes in v11:
time: 136 us; the launch traced here: 135 us
  Pallas kernels  44.4 us (33%)
  waiting for transfers between devices  43.6 us (32%)
  starting transfers between devices  40.6 us (30%)
  other arithmetic  3.17 us (2%)
  local copies, waits for them, and re-layouts  2.83 us (2%)
    ppermute x12, starting transfers between devices, swap_groups(): got.append(lax.ppermute(sends[bits], 'grp', perm))  26.7 us
    ppermute x12, waiting for transfers between devices, swap_groups(): got.append(lax.ppermute(sends[bits], 'grp', perm))  23.6 us
    ppermute x19, waiting for transfers between devices, flip_rows(): lax.ppermute(values, 'rows', [(index, index ^ bits) for index in range(ro...  19.9 us
    pallas_call x1, Pallas kernels, attention(): pl.pallas_call(functools.partial(attention_kernel, groups=groups, row_par...  15.2 us
    ppermute x19, starting transfers between devices, flip_rows(): lax.ppermute(values, 'rows', [(index, index ^ bits) for index in range(ro...  13.9 us
    pallas_call x1, Pallas kernels, pair_back(): pl.pallas_call(functools.partial(pair_back_kernel, groups=groups, calls=l...  7.8 us
    pallas_call x1, Pallas kernels, pair_bias(): pl.pallas_call(functools.partial(bias_kernel, groups=groups, batch=16), g...  7.52 us
    pallas_call x1, Pallas kernels, split_heads(): pl.pallas_call(functools.partial(finish_kernel, groups=groups, calls=call...  7.48 us
  transfers between devices with their start and end apart: 31, of which 17 were waited for; matrix products, arithmetic and copies ran while one was open for 2% of the time, Pallas kernels for 16%

profile of v11, /device:TPU:0, one launch (start us, length us, event | category | flops | bytes accessed | tf_op | source)
XLA Modules:
  0.0 135.5 jit_solution(1263863294129863533)
XLA Ops:
  0.6 7.5 %shard_map.158 = (bf16[4,3,48,128]{3,2,1,0:T(8,128)(2,1)}, bf16[4,3,48,128]{3,2,1,0:T(8,128)(2,1)}, bf16[4,3,48,128]{3,2,1,0:T(8,128)(2,1)}, bf16[4,3,48,128]{3,2,1,0:T(8,128)(2,1)}, f32[2,48,24,192]{3,2,1,0:T(8,128)}) custom-call(s32[1]{0:T(128)} %bitcast.group_ref, s32[1]{0:T(128)} %bitcast.3.rows_ref.row_ref, s32[768]{0:T(1024)} %cols_ref.1, f32[16]{0:T(128)} %gain_ref.1, ...), custom_call_target="tpu_custom_call" | custom-call | tf_op jit(solution)/shard_map/pallas_call | solution.py:211
  8.2 4.0 %collective-permute-start = (bf16[4,3,48,128]{3,2,1,0:T(8,128)(2,1)}, bf16[4,3,48,128]{3,2,1,0:T(8,128)(2,1)S(1)}, u32[]{:S(2)}, u32[]{:S(2)}) collective-permute-start(bf16[4,3,48,128]{3,2,1,0:T(8,128)(2,1)} %get-tuple-element.69), channel_id=1, source_target_pairs={{0,2},{1,3},{2,0},{3,1},{4,6},{5,7},{6,4},{7,5},{8,10},{9,11},{10,... | collective-permute-start | bytes 442376 | tf_op jit(solution)/shard_map/ppermute | solution.py:587
  12.2 1.4 collective-permute-start.1
  13.5 0.2 collective-permute-start.2
  13.8 6.4 %shard_map.157 = (bf16[192,768]{1,0:T(8,128)(2,1)}, bf16[192,768]{1,0:T(8,128)(2,1)}, bf16[192,768]{1,0:T(8,128)(2,1)}, bf16[192,768]{1,0:T(8,128)(2,1)}, f32[192,768]{1,0:T(8,128)}, /*index=5*/f32[192,768]{1,0:T(8,128)}) custom-call(s32[1]{0:T(128)} %bitcast.group_ref, bf16[192,384]{1,0:T(8,128)(2,1)} %single_ref.3, bf16[192,768]{1,0:T(8,128)(2,1)} %bitcast.23, ...), custom_call_target="tpu_custom_call" | custom-call | tf_op jit(solution)/shard_map/pallas_call | solution.py:684
  20.2 3.3 %collective-permute-done = bf16[4,3,48,128]{3,2,1,0:T(8,128)(2,1)S(1)} collective-permute-done((bf16[4,3,48,128]{3,2,1,0:T(8,128)(2,1)}, bf16[4,3,48,128]{3,2,1,0:T(8,128)(2,1)S(1)}, u32[]{:S(2)}, u32[]{:S(2)}) %collective-permute-start) | collective-permute-done | bytes 147488 | tf_op jit(solution)/shard_map/ppermute | solution.py:587
  23.4 0.5 collective-permute-done.2
  24.0 0.1 pad_maximum_fusion.rest_0_
  24.0 1.6 %collective-permute-start.6 = (bf16[4,4,3,48,128]{4,3,2,1,0:T(8,128)(2,1)S(1)}, bf16[4,4,3,48,128]{4,3,2,1,0:T(8,128)(2,1)S(1)}, u32[]{:S(2)}, u32[]{:S(2)}) collective-permute-start(bf16[4,4,3,48,128]{4,3,2,1,0:T(8,128)(2,1)S(1)} %pad_maximum_fusion.rest_0_), channel_id=1, source_target_pairs={{0,16},{4,20},{8,24},{12,28},{16,0},{20,4},{24,8},{28,12},{1,17},{... | collective-permute-start | bytes 1769480 | tf_op jit(solution)/shard_map/ppermute | solution.py:593
  25.7 1.5 %collective-permute-start.4 = (bf16[4,4,3,48,128]{4,3,2,1,0:T(8,128)(2,1)S(1)}, bf16[4,4,3,48,128]{4,3,2,1,0:T(8,128)(2,1)S(1)}, u32[]{:S(2)}, u32[]{:S(2)}) collective-permute-start(bf16[4,4,3,48,128]{4,3,2,1,0:T(8,128)(2,1)S(1)} %pad_maximum_fusion.rest_0_), channel_id=1, source_target_pairs={{0,8},{4,12},{8,0},{12,4},{16,24},{20,28},{24,16},{28,20},{1,9},{5... | collective-permute-start | bytes 1769480 | tf_op jit(solution)/shard_map/ppermute | solution.py:593
  27.2 4.4 %collective-permute-start.8 = (bf16[192,768]{1,0:T(8,128)(2,1)S(1)}, bf16[192,768]{1,0:T(8,128)(2,1)S(1)}, u32[]{:S(2)}, u32[]{:S(2)}) collective-permute-start(bf16[192,768]{1,0:T(8,128)(2,1)S(1)} %copy-done.27), channel_id=1, source_target_pairs={{0,2},{1,3},{2,0},{3,1},{4,6},{5,7},{6,4},{7,5},{8,10},{9,11},{10,... | collective-permute-start | bytes 884744 | tf_op jit(solution)/shard_map/ppermute | solution.py:587
  31.6 0.5 collective-permute-start.9
  32.1 0.1 collective-permute-start.10
  32.2 5.1 %collective-permute-done.6.rest_4_ = bf16[4,4,3,48,128]{4,3,2,1,0:T(8,128)(2,1)S(1)} collective-permute-done((bf16[4,4,3,48,128]{4,3,2,1,0:T(8,128)(2,1)S(1)}, bf16[4,4,3,48,128]{4,3,2,1,0:T(8,128)(2,1)S(1)}, u32[]{:S(2)}, u32[]{:S(2)}) %collective-permute-start.6) | collective-permute-done | bytes 589856 | tf_op jit(solution)/shard_map/ppermute | solution.py:593
  37.4 1.3 collective-permute-start.12
  38.7 0.8 collective-permute-done.4.rest_2_
  39.5 0.9 collective-permute-start.11
  40.4 10.9 %collective-permute-done.8.rest_11_ = bf16[192,768]{1,0:T(8,128)(2,1)S(1)} collective-permute-done((bf16[192,768]{1,0:T(8,128)(2,1)S(1)}, bf16[192,768]{1,0:T(8,128)(2,1)S(1)}, u32[]{:S(2)}, u32[]{:S(2)}) %collective-permute-start.8) | collective-permute-done | bytes 294944 | tf_op jit(solution)/shard_map/ppermute | solution.py:587
  51.3 0.5 collective-permute-start.7
  51.8 0.4 collective-permute-done.10.rest_13_
  52.3 0.0 copy-start.14
  52.3 0.6 collective-permute-start.13
  52.8 0.1 collective-permute-start.14
  52.9 0.4 collective-permute-done.3.rest_1_
  53.3 0.8 collective-permute-done.7.rest_5_
  54.2 0.8 collective-permute-done.5.rest_3_
  55.0 0.4 collective-permute-done.13.rest_7_
  55.4 0.4 collective-permute-done.14.rest_9_
  55.9 0.2 copy-done.15
  56.1 0.7 copy-done.16
  56.8 15.2 %shard_map.159 = (bf16[192,768]{1,0:T(8,128)(2,1)}, bf16[192,768]{1,0:T(8,128)(2,1)}, bf16[192,768]{1,0:T(8,128)(2,1)}, bf16[192,768]{1,0:T(8,128)(2,1)}, bf16[4...) custom-call(s32[1]{0:T(128)} %bitcast.group_ref, ...), custom_call_target="tpu_custom_call" | custom-call | tf_op jit(solution)/shard_map/pallas_call | solution.py:502
  72.1 0.2 collective-permute-start.15
  72.3 2.9 %collective-permute-done.15 = bf16[4,8,3,48,128]{4,3,2,1,0:T(8,128)(2,1)S(1)} collective-permute-done((bf16[4,8,3,48,128]{4,3,2,1,0:T(8,128)(2,1)}, bf16[4,8,3,48,128]{4,3,2,1,0:T(8,128)(2,1)S(1)}, u32[]{:S(2)}, u32[]{:S(2)}) %collective-permute-start.15) | collective-permute-done | bytes 1179680 | tf_op jit(solution)/shard_map/ppermute | solution.py:593
  75.2 0.1 collective-permute-start.16
  75.3 1.7 %add_convert_fusion.3 = (bf16[4,4,3,48,128]{4,3,2,1,0:T(8,128)(2,1)S(1)}, bf16[4,4,3,48,128]{4,3,2,1,0:T(8,128)(2,1)S(1)}) fusion(bf16[4,8,3,48,128]{4,3,2,1,0:T(8,128)(2,1)S(1)} %collective-permute-done.15, bf16[4,16,3,48,128]{4,3,2,1,0:T(8,128)(2,1)} %get-tuple-element.91), kind=kLoop, calls=%fused_computation.3 | loop fusion | flops 2359296 | bytes 3538944 | tf_op jit(solution)/shard_map/convert_element_type | solution.py:628
  77.1 0.6 collective-permute-start.17
  77.7 0.5 collective-permute-start.18
  78.2 4.7 %collective-permute-start.21 = (bf16[192,768]{1,0:T(8,128)(2,1)S(1)}, bf16[192,768]{1,0:T(8,128)(2,1)S(1)}, u32[]{:S(2)}, u32[]{:S(2)}) collective-permute-start(bf16[192,768]{1,0:T(8,128)(2,1)S(1)} %copy-done.24), channel_id=1, source_target_pairs={{0,2},{1,3},{2,0},{3,1},{4,6},{5,7},{6,4},{7,5},{8,10},{9,11},{10,... | collective-permute-start | bytes 884744 | tf_op jit(solution)/shard_map/ppermute | solution.py:587
  82.9 3.3 %collective-permute-start.22 = (bf16[192,768]{1,0:T(8,128)(2,1)S(1)}, bf16[192,768]{1,0:T(8,128)(2,1)S(1)}, u32[]{:S(2)}, u32[]{:S(2)}) collective-permute-start(bf16[192,768]{1,0:T(8,128)(2,1)S(1)} %copy-done.23), channel_id=1, source_target_pairs={{0,3},{1,2},{2,1},{3,0},{4,7},{5,6},{6,5},{7,4},{8,11},{9,10},{10,... | collective-permute-start | bytes 884744 | tf_op jit(solution)/shard_map/ppermute | solution.py:587
  86.2 6.5 %collective-permute-done.17 = bf16[4,4,3,48,128]{4,3,2,1,0:T(8,128)(2,1)S(1)} collective-permute-done((bf16[4,4,3,48,128]{4,3,2,1,0:T(8,128)(2,1)S(1)}, bf16[4,4,3,48,128]{4,3,2,1,0:T(8,128)(2,1)S(1)}, u32[]{:S(2)}, u32[]{:S(2)}) %collective-permute-start.17) | collective-permute-done | bytes 589856 | tf_op jit(solution)/shard_map/ppermute | solution.py:593
  92.7 0.3 collective-permute-done.18
  93.0 0.2 add_convert_fusion.4
  93.2 1.6 %collective-permute-start.20 = (bf16[4,2,3,48,128]{4,3,2,1,0:T(8,128)(2,1)S(1)}, bf16[4,2,3,48,128]{4,3,2,1,0:T(8,128)(2,1)S(1)}, u32[]{:S(2)}, u32[]{:S(2)}) collective-permute-start(bf16[4,2,3,48,128]{4,3,2,1,0:T(8,128)(2,1)S(1)} %get-tuple-element.129), channel_id=1, source_target_pairs={{0,8},{4,12},{8,0},{12,4},{16,24},{20,28},{24,16},{28,20},{1,9},{5... | collective-permute-start | bytes 884744 | tf_op jit(solution)/shard_map/ppermute | solution.py:593
  94.8 0.5 collective-permute-start.19
  95.4 8.1 %collective-permute-done.21.rest_2_ = bf16[192,768]{1,0:T(8,128)(2,1)S(1)} collective-permute-done((bf16[192,768]{1,0:T(8,128)(2,1)S(1)}, bf16[192,768]{1,0:T(8,128)(2,1)S(1)}, u32[]{:S(2)}, u32[]{:S(2)}) %collective-permute-start.21) | collective-permute-done | bytes 294944 | tf_op jit(solution)/shard_map/ppermute | solution.py:587
  103.5 0.4 collective-permute-done.23.rest_1_
  103.9 0.3 add_convert_fusion
  104.3 0.0 copy-done.10
  104.3 0.3 copy-done.12
  104.6 0.7 slice_bitcast_fusion
  105.3 7.5 %collective-permute-start.27 = (bf16[4,3,48,128]{3,2,1,0:T(8,128)(2,1)S(1)}, bf16[4,3,48,128]{3,2,1,0:T(8,128)(2,1)S(1)}, u32[]{:S(2)}, u32[]{:S(2)}) collective-permute-start(bf16[4,3,48,128]{3,2,1,0:T(8,128)(2,1)S(1)} %get-tuple-element.119), channel_id=1, source_target_pairs={{0,2},{1,3},{2,0},{3,1},{4,6},{5,7},{6,4},{7,5},{8,10},{9,11},{10,... | collective-permute-start | bytes 442376 | tf_op jit(solution)/shard_map/ppermute | solution.py:587
  112.8 0.5 collective-permute-start.28
  113.3 0.0 collective-permute-start.29
  113.3 7.5 %shard_map.160 = (bf16[192,768]{1,0:T(8,128)(2,1)}, bf16[192,384]{1,0:T(8,128)(2,1)}) custom-call(s32[1]{0:T(128)} %bitcast.group_ref, bf16[192,384]{1,0:T(8,128)(2,1)} %single_ref.3, bf16[192,768]{1,0:T(8,128)(2,1)} %bitcast.24, bf16[192,768]{1,0:T(8,128)(2,1)} %bitcast.26, f32[192,768]{1,0:T(8,128)} %get-tuple-element.66.gamma_ref, ...), custom_call_target="tpu_custom_call" | custom-call | tf_op jit(solution)/shard_map/pallas_call | solution.py:725
  120.8 2.5 %collective-permute-start.26 = (bf16[192,384]{1,0:T(8,128)(2,1)}, bf16[192,384]{1,0:T(8,128)(2,1)S(1)}, u32[]{:S(2)}, u32[]{:S(2)}) collective-permute-start(bf16[192,384]{1,0:T(8,128)(2,1)} %get-tuple-element.116), channel_id=1, source_target_pairs={{0,24},{4,28},{8,16},{12,20},{16,8},{20,12},{24,0},{28,4},{1,25},{... | collective-permute-start | bytes 442376 | tf_op jit(solution)/shard_map/ppermute | solution.py:593
  123.3 0.5 collective-permute-start.25
  123.8 0.9 collective-permute-start.24
  124.7 0.6 copy-done.20
  125.3 0.1 copy-done.21
  125.4 7.8 %shard_map.161 = bf16[2,48,192,128]{3,2,1,0:T(8,128)(2,1)} custom-call(s32[1]{0:T(128)} %bitcast.group_ref, bf16[2,48,192,128]{3,2,1,0:T(8,128)(2,1)} %bitcast.21, f32[2,48,24,192]{3,2,1,0:T(8,128)} %get-tuple-element.117.stats_ref, bf16[16,128]{1,0:T(8,128)(2,1)} %bitcast.32, bf16[4,3,48,128]{3,2,1,0:T(8,128)(2,1)} %get-tuple-element.118.rest_0_, ...), custom_call_target="tpu_custom_call" | custom-call | tf_op jit(solution)/shard_map/pallas_call | solution.py:321
  133.2 0.1 add_convert_fusion.6
  133.3 0.1 collective-permute-start.30
  133.4 1.4 %collective-permute-done.30 = bf16[192,384]{1,0:T(8,128)(2,1)S(1)} collective-permute-done((bf16[192,384]{1,0:T(8,128)(2,1)S(1)}, bf16[192,384]{1,0:T(8,128)(2,1)S(1)}, u32[]{:S(2)}, u32[]{:S(2)}) %collective-permute-start.30) | collective-permute-done | bytes 147488 | tf_op jit(solution)/shard_map/ppermute | solution.py:593
  134.7 0.7 convert_add_fusion
  (70 shorter events, 0.2 us)
Async XLA Ops:
  8.2 15.3 %collective-permute-start = (bf16[4,3,48,128]{3,2,1,0:T(8,128)(2,1)}, bf16[4,3,48,128]{3,2,1,0:T(8,128)(2,1)S(1)}, u32[]{:S(2)}, u32[]{:S(2)}) collective-permute-start(bf16[4,3,48,128]{3,2,1,0:T(8,128)(2,1)} %get-tuple-element.69), channel_id=1, source_target_pairs={{0,2},{1,3},{2,0},{3,1},{4,6},{5,7},{6,4},{7,5},{8,10},{9,11},{10,... | collective-permute-start | bytes 442376 | tf_op jit(solution)/shard_map/ppermute | solution.py:587
  12.2 11.3 %collective-permute-start.1 = (bf16[4,3,48,128]{3,2,1,0:T(8,128)(2,1)}, bf16[4,3,48,128]{3,2,1,0:T(8,128)(2,1)S(1)}, u32[]{:S(2)}, u32[]{:S(2)}) collective-permute-start(bf16[4,3,48,128]{3,2,1,0:T(8,128)(2,1)} %get-tuple-element.70), channel_id=1, source_target_pairs={{0,3},{1,2},{2,1},{3,0},{4,7},{5,6},{6,5},{7,4},{8,11},{9,10},{10,... | collective-permute-start | bytes 442376 | tf_op jit(solution)/shard_map/ppermute | solution.py:587
  13.5 10.4 %collective-permute-start.2 = (bf16[4,3,48,128]{3,2,1,0:T(8,128)(2,1)}, bf16[4,3,48,128]{3,2,1,0:T(8,128)(2,1)S(1)}, u32[]{:S(2)}, u32[]{:S(2)}) collective-permute-start(bf16[4,3,48,128]{3,2,1,0:T(8,128)(2,1)} %get-tuple-element.71), channel_id=1, source_target_pairs={{0,1},{1,0},{2,3},{3,2},{4,5},{5,4},{6,7},{7,6},{8,9},{9,8},{10,11... | collective-permute-start | bytes 442376 | tf_op jit(solution)/shard_map/ppermute | solution.py:587
  13.8 10.2 %copy-start.17 = (bf16[4,3,48,128]{3,2,1,0:T(8,128)(2,1)S(1)}, bf16[4,3,48,128]{3,2,1,0:T(8,128)(2,1)}, u32[]{:S(2)}) copy-start(bf16[4,3,48,128]{3,2,1,0:T(8,128)(2,1)} %get-tuple-element.79) | copy-start | bytes 442372
  20.1 7.0 %copy-start.27 = (bf16[192,768]{1,0:T(8,128)(2,1)S(1)}, bf16[192,768]{1,0:T(8,128)(2,1)}, u32[]{:S(2)}) copy-start(bf16[192,768]{1,0:T(8,128)(2,1)} %get-tuple-element.76) | copy-start | bytes 884740
  20.1 11.4 %copy-start.26 = (bf16[192,768]{1,0:T(8,128)(2,1)S(1)}, bf16[192,768]{1,0:T(8,128)(2,1)}, u32[]{:S(2)}) copy-start(bf16[192,768]{1,0:T(8,128)(2,1)} %get-tuple-element.77) | copy-start | bytes 884740
  20.2 12.0 %copy-start.25 = (bf16[192,768]{1,0:T(8,128)(2,1)S(1)}, bf16[192,768]{1,0:T(8,128)(2,1)}, u32[]{:S(2)}) copy-start(bf16[192,768]{1,0:T(8,128)(2,1)} %get-tuple-element.78) | copy-start | bytes 884740
  24.0 31.8 %copy-start = (bf16[4,4,3,48,128]{4,3,2,1,0:T(8,128)(2,1)}, bf16[4,4,3,48,128]{4,3,2,1,0:T(8,128)(2,1)S(1)}, u32[]{:S(2)}) copy-start(bf16[4,4,3,48,128]{4,3,2,1,0:T(8,128)(2,1)S(1)} %pad_maximum_fusion.rest_0_) | copy-start | bytes 1769476
  24.0 13.3 %collective-permute-start.6 = (bf16[4,4,3,48,128]{4,3,2,1,0:T(8,128)(2,1)S(1)}, bf16[4,4,3,48,128]{4,3,2,1,0:T(8,128)(2,1)S(1)}, u32[]{:S(2)}, u32[]{:S(2)}) collective-permute-start(bf16[4,4,3,48,128]{4,3,2,1,0:T(8,128)(2,1)S(1)} %pad_maximum_fusion.rest_0_), channel_id=1, source_target_pairs={{0,16},{4,20},{8,24},{12,28},{16,0},{20,4},{24,8},{28,12},{1,17},{... | collective-permute-start | bytes 1769480 | tf_op jit(solution)/shard_map/ppermute | solution.py:593
  25.7 13.8 %collective-permute-start.4 = (bf16[4,4,3,48,128]{4,3,2,1,0:T(8,128)(2,1)S(1)}, bf16[4,4,3,48,128]{4,3,2,1,0:T(8,128)(2,1)S(1)}, u32[]{:S(2)}, u32[]{:S(2)}) collective-permute-start(bf16[4,4,3,48,128]{4,3,2,1,0:T(8,128)(2,1)S(1)} %pad_maximum_fusion.rest_0_), channel_id=1, source_target_pairs={{0,8},{4,12},{8,0},{12,4},{16,24},{20,28},{24,16},{28,20},{1,9},{5... | collective-permute-start | bytes 1769480 | tf_op jit(solution)/shard_map/ppermute | solution.py:593
  27.2 24.1 %collective-permute-start.8 = (bf16[192,768]{1,0:T(8,128)(2,1)S(1)}, bf16[192,768]{1,0:T(8,128)(2,1)S(1)}, u32[]{:S(2)}, u32[]{:S(2)}) collective-permute-start(bf16[192,768]{1,0:T(8,128)(2,1)S(1)} %copy-done.27), channel_id=1, source_target_pairs={{0,2},{1,3},{2,0},{3,1},{4,6},{5,7},{6,4},{7,5},{8,10},{9,11},{10,... | collective-permute-start | bytes 884744 | tf_op jit(solution)/shard_map/ppermute | solution.py:587
  31.6 19.7 %collective-permute-start.9 = (bf16[192,768]{1,0:T(8,128)(2,1)S(1)}, bf16[192,768]{1,0:T(8,128)(2,1)S(1)}, u32[]{:S(2)}, u32[]{:S(2)}) collective-permute-start(bf16[192,768]{1,0:T(8,128)(2,1)S(1)} %copy-done.26), channel_id=1, source_target_pairs={{0,3},{1,2},{2,1},{3,0},{4,7},{5,6},{6,5},{7,4},{8,11},{9,10},{10,... | collective-permute-start | bytes 884744 | tf_op jit(solution)/shard_map/ppermute | solution.py:587
  32.1 20.1 %collective-permute-start.10 = (bf16[192,768]{1,0:T(8,128)(2,1)S(1)}, bf16[192,768]{1,0:T(8,128)(2,1)S(1)}, u32[]{:S(2)}, u32[]{:S(2)}) collective-permute-start(bf16[192,768]{1,0:T(8,128)(2,1)S(1)} %copy-done.25), channel_id=1, source_target_pairs={{0,1},{1,0},{2,3},{3,2},{4,5},{5,4},{6,7},{7,6},{8,9},{9,8},{10,11... | collective-permute-start | bytes 884744 | tf_op jit(solution)/shard_map/ppermute | solution.py:587
  37.3 18.5 %copy-start.2 = (bf16[4,4,3,48,128]{4,3,2,1,0:T(8,128)(2,1)}, bf16[4,4,3,48,128]{4,3,2,1,0:T(8,128)(2,1)S(1)}, u32[]{:S(2)}) copy-start(bf16[4,4,3,48,128]{4,3,2,1,0:T(8,128)(2,1)S(1)} %collective-permute-done.6.rest_4_) | copy-start | bytes 1769476
  37.4 14.9 %collective-permute-start.12 = (bf16[2,4,3,48,128]{4,3,2,1,0:T(8,128)(2,1)S(1)}, bf16[2,4,3,48,128]{4,3,2,1,0:T(8,128)(2,1)S(1)}, u32[]{:S(2)}, u32[]{:S(2)}) collective-permute-start(bf16[2,4,3,48,128]{4,3,2,1,0:T(8,128)(2,1)S(1)} %slice.81), channel_id=1, source_target_pairs={{0,8},{4,12},{8,0},{12,4},{16,24},{20,28},{24,16},{28,20},{1,9},{5... | collective-permute-start | bytes 884744 | tf_op jit(solution)/shard_map/ppermute | solution.py:593
  39.5 16.3 %copy-start.3 = (bf16[4,4,3,48,128]{4,3,2,1,0:T(8,128)(2,1)}, bf16[4,4,3,48,128]{4,3,2,1,0:T(8,128)(2,1)S(1)}, u32[]{:S(2)}) copy-start(bf16[4,4,3,48,128]{4,3,2,1,0:T(8,128)(2,1)S(1)} %collective-permute-done.4.rest_2_) | copy-start | bytes 1769476
  39.5 12.7 %collective-permute-start.11 = (bf16[2,4,3,48,128]{4,3,2,1,0:T(8,128)(2,1)S(1)}, bf16[2,4,3,48,128]{4,3,2,1,0:T(8,128)(2,1)S(1)}, u32[]{:S(2)}, u32[]{:S(2)}) collective-permute-start(bf16[2,4,3,48,128]{4,3,2,1,0:T(8,128)(2,1)S(1)} %slice.80), channel_id=1, source_target_pairs={{0,16},{4,20},{8,24},{12,28},{16,0},{20,4},{24,8},{28,12},{1,17},{... | collective-permute-start | bytes 884744 | tf_op jit(solution)/shard_map/ppermute | solution.py:593
  51.3 4.6 %copy-start.7 = (bf16[192,768]{1,0:T(8,128)(2,1)}, bf16[192,768]{1,0:T(8,128)(2,1)S(1)}, u32[]{:S(2)}) copy-start(bf16[192,768]{1,0:T(8,128)(2,1)S(1)} %collective-permute-done.8.rest_11_) | copy-start | bytes 884740
  51.3 2.0 %collective-permute-start.3 = (bf16[4,4,3,48,128]{4,3,2,1,0:T(8,128)(2,1)S(1)}, bf16[4,4,3,48,128]{4,3,2,1,0:T(8,128)(2,1)S(1)}, u32[]{:S(2)}, u32[]{:S(2)}) collective-permute-start(bf16[4,4,3,48,128]{4,3,2,1,0:T(8,128)(2,1)S(1)} %pad_maximum_fusion.rest_0_), channel_id=1, source_target_pairs={{0,4},{4,0},{8,12},{12,8},{16,20},{20,16},{24,28},{28,24},{1,5},{5... | collective-permute-start | bytes 1769480 | tf_op jit(solution)/shard_map/ppermute | solution.py:593
  51.3 4.5 %copy-start.9 = (bf16[192,768]{1,0:T(8,128)(2,1)}, bf16[192,768]{1,0:T(8,128)(2,1)S(1)}, u32[]{:S(2)}) copy-start(bf16[192,768]{1,0:T(8,128)(2,1)S(1)} %collective-permute-done.9.rest_12_) | copy-start | bytes 884740
  51.3 2.8 %collective-permute-start.7 = (bf16[4,4,3,48,128]{4,3,2,1,0:T(8,128)(2,1)S(1)}, bf16[4,4,3,48,128]{4,3,2,1,0:T(8,128)(2,1)S(1)}, u32[]{:S(2)}, u32[]{:S(2)}) collective-permute-start(bf16[4,4,3,48,128]{4,3,2,1,0:T(8,128)(2,1)S(1)} %collective-permute-done.6.rest_4_), channel_id=1, source_target_pairs={{0,4},{4,0},{8,12},{12,8},{16,20},{20,16},{24,28},{28,24},{1,5},{5... | collective-permute-start | bytes 1769480 | tf_op jit(solution)/shard_map/ppermute | solution.py:593
  52.2 3.6 %copy-start.11 = (bf16[192,768]{1,0:T(8,128)(2,1)}, bf16[192,768]{1,0:T(8,128)(2,1)S(1)}, u32[]{:S(2)}) copy-start(bf16[192,768]{1,0:T(8,128)(2,1)S(1)} %collective-permute-done.10.rest_13_) | copy-start | bytes 884740
  52.2 2.8 %collective-permute-start.5 = (bf16[4,4,3,48,128]{4,3,2,1,0:T(8,128)(2,1)S(1)}, bf16[4,4,3,48,128]{4,3,2,1,0:T(8,128)(2,1)S(1)}, u32[]{:S(2)}, u32[]{:S(2)}) collective-permute-start(bf16[4,4,3,48,128]{4,3,2,1,0:T(8,128)(2,1)S(1)} %collective-permute-done.4.rest_2_), channel_id=1, source_target_pairs={{0,4},{4,0},{8,12},{12,8},{16,20},{20,16},{24,28},{28,24},{1,5},{5... | collective-permute-start | bytes 1769480 | tf_op jit(solution)/shard_map/ppermute | solution.py:593
  52.2 3.6 %copy-start.13 = (bf16[2,4,3,48,128]{4,3,2,1,0:T(8,128)(2,1)}, bf16[2,4,3,48,128]{4,3,2,1,0:T(8,128)(2,1)S(1)}, u32[]{:S(2)}) copy-start(bf16[2,4,3,48,128]{4,3,2,1,0:T(8,128)(2,1)S(1)} %collective-permute-done.12.rest_8_) | copy-start | bytes 884740
  52.3 3.6 %copy-start.14 = (bf16[2,4,3,48,128]{4,3,2,1,0:T(8,128)(2,1)}, bf16[2,4,3,48,128]{4,3,2,1,0:T(8,128)(2,1)S(1)}, u32[]{:S(2)}) copy-start(bf16[2,4,3,48,128]{4,3,2,1,0:T(8,128)(2,1)S(1)} %collective-permute-done.11.rest_6_) | copy-start | bytes 884740
  52.3 3.1 %collective-permute-start.13 = (bf16[2,4,3,48,128]{4,3,2,1,0:T(8,128)(2,1)S(1)}, bf16[2,4,3,48,128]{4,3,2,1,0:T(8,128)(2,1)S(1)}, u32[]{:S(2)}, u32[]{:S(2)}) collective-permute-start(bf16[2,4,3,48,128]{4,3,2,1,0:T(8,128)(2,1)S(1)} %collective-permute-done.11.rest_6_), channel_id=1, source_target_pairs={{0,4},{4,0},{8,12},{12,8},{16,20},{20,16},{24,28},{28,24},{1,5},{5... | collective-permute-start | bytes 884744 | tf_op jit(solution)/shard_map/ppermute | solution.py:593
  52.8 3.0 %collective-permute-start.14 = (bf16[2,4,3,48,128]{4,3,2,1,0:T(8,128)(2,1)S(1)}, bf16[2,4,3,48,128]{4,3,2,1,0:T(8,128)(2,1)S(1)}, u32[]{:S(2)}, u32[]{:S(2)}) collective-permute-start(bf16[2,4,3,48,128]{4,3,2,1,0:T(8,128)(2,1)S(1)} %collective-permute-done.12.rest_8_), channel_id=1, source_target_pairs={{0,4},{4,0},{8,12},{12,8},{16,20},{20,16},{24,28},{28,24},{1,5},{5... | collective-permute-start | bytes 884744 | tf_op jit(solution)/shard_map/ppermute | solution.py:593
  53.3 2.6 %copy-start.4 = (bf16[4,4,3,48,128]{4,3,2,1,0:T(8,128)(2,1)}, bf16[4,4,3,48,128]{4,3,2,1,0:T(8,128)(2,1)S(1)}, u32[]{:S(2)}) copy-start(bf16[4,4,3,48,128]{4,3,2,1,0:T(8,128)(2,1)S(1)} %collective-permute-done.3.rest_1_) | copy-start | bytes 1769476
  54.2 1.8 %copy-start.5 = (bf16[4,4,3,48,128]{4,3,2,1,0:T(8,128)(2,1)}, bf16[4,4,3,48,128]{4,3,2,1,0:T(8,128)(2,1)S(1)}, u32[]{:S(2)}) copy-start(bf16[4,4,3,48,128]{4,3,2,1,0:T(8,128)(2,1)S(1)} %collective-permute-done.7.rest_5_) | copy-start | bytes 1769476
  55.0 0.9 copy-start.6
  55.4 0.7 copy-start.15
  56.1 0.7 copy-start.16
  72.1 3.1 %collective-permute-start.15 = (bf16[4,8,3,48,128]{4,3,2,1,0:T(8,128)(2,1)}, bf16[4,8,3,48,128]{4,3,2,1,0:T(8,128)(2,1)S(1)}, u32[]{:S(2)}, u32[]{:S(2)}) collective-permute-start(bf16[4,8,3,48,128]{4,3,2,1,0:T(8,128)(2,1)} %get-tuple-element.92), channel_id=1, source_target_pairs={{0,4},{4,0},{8,12},{12,8},{16,20},{20,16},{24,28},{28,24},{1,5},{5... | collective-permute-start | bytes 3538952 | tf_op jit(solution)/shard_map/ppermute | solution.py:593
  75.2 11.0 %collective-permute-start.16 = (bf16[4,8,3,48,128]{4,3,2,1,0:T(8,128)(2,1)}, bf16[4,8,3,48,128]{4,3,2,1,0:T(8,128)(2,1)S(1)}, u32[]{:S(2)}, u32[]{:S(2)}) collective-permute-start(bf16[4,8,3,48,128]{4,3,2,1,0:T(8,128)(2,1)} %get-tuple-element.94), channel_id=1, source_target_pairs={{0,4},{4,0},{8,12},{12,8},{16,20},{20,16},{24,28},{28,24},{1,5},{5... | collective-permute-start | bytes 3538952 | tf_op jit(solution)/shard_map/ppermute | solution.py:593
  75.3 2.9 %copy-start.24 = (bf16[192,768]{1,0:T(8,128)(2,1)S(1)}, bf16[192,768]{1,0:T(8,128)(2,1)}, u32[]{:S(2)}) copy-start(bf16[192,768]{1,0:T(8,128)(2,1)} %get-tuple-element.99) | copy-start | bytes 884740
  75.3 7.6 %copy-start.23 = (bf16[192,768]{1,0:T(8,128)(2,1)S(1)}, bf16[192,768]{1,0:T(8,128)(2,1)}, u32[]{:S(2)}) copy-start(bf16[192,768]{1,0:T(8,128)(2,1)} %get-tuple-element.100) | copy-start | bytes 884740
  75.3 10.9 %copy-start.22 = (bf16[192,768]{1,0:T(8,128)(2,1)S(1)}, bf16[192,768]{1,0:T(8,128)(2,1)}, u32[]{:S(2)}) copy-start(bf16[192,768]{1,0:T(8,128)(2,1)} %get-tuple-element.101) | copy-start | bytes 884740
  75.3 17.7 %copy-start.1 = (bf16[4,16,3,48,128]{4,3,2,1,0:T(8,128)(2,1)S(1)}, bf16[4,16,3,48,128]{4,3,2,1,0:T(8,128)(2,1)}, u32[]{:S(2)}) copy-start(bf16[4,16,3,48,128]{4,3,2,1,0:T(8,128)(2,1)} %get-tuple-element.91) | copy-start | bytes 7077892
  77.1 15.7 %collective-permute-start.17 = (bf16[4,4,3,48,128]{4,3,2,1,0:T(8,128)(2,1)S(1)}, bf16[4,4,3,48,128]{4,3,2,1,0:T(8,128)(2,1)S(1)}, u32[]{:S(2)}, u32[]{:S(2)}) collective-permute-start(bf16[4,4,3,48,128]{4,3,2,1,0:T(8,128)(2,1)S(1)} %get-tuple-element.131), channel_id=1, source_target_pairs={{0,8},{4,12},{8,0},{12,4},{16,24},{20,28},{24,16},{28,20},{1,9},{5... | collective-permute-start | bytes 1769480 | tf_op jit(solution)/shard_map/ppermute | solution.py:593
  77.7 15.3 %collective-permute-start.18 = (bf16[4,4,3,48,128]{4,3,2,1,0:T(8,128)(2,1)S(1)}, bf16[4,4,3,48,128]{4,3,2,1,0:T(8,128)(2,1)S(1)}, u32[]{:S(2)}, u32[]{:S(2)}) collective-permute-start(bf16[4,4,3,48,128]{4,3,2,1,0:T(8,128)(2,1)S(1)} %get-tuple-element.132), channel_id=1, source_target_pairs={{0,16},{4,20},{8,24},{12,28},{16,0},{20,4},{24,8},{28,12},{1,17},{... | collective-permute-start | bytes 1769480 | tf_op jit(solution)/shard_map/ppermute | solution.py:593
  78.2 25.3 %collective-permute-start.21 = (bf16[192,768]{1,0:T(8,128)(2,1)S(1)}, bf16[192,768]{1,0:T(8,128)(2,1)S(1)}, u32[]{:S(2)}, u32[]{:S(2)}) collective-permute-start(bf16[192,768]{1,0:T(8,128)(2,1)S(1)} %copy-done.24), channel_id=1, source_target_pairs={{0,2},{1,3},{2,0},{3,1},{4,6},{5,7},{6,4},{7,5},{8,10},{9,11},{10,... | collective-permute-start | bytes 884744 | tf_op jit(solution)/shard_map/ppermute | solution.py:587
  82.9 20.5 %collective-permute-start.22 = (bf16[192,768]{1,0:T(8,128)(2,1)S(1)}, bf16[192,768]{1,0:T(8,128)(2,1)S(1)}, u32[]{:S(2)}, u32[]{:S(2)}) collective-permute-start(bf16[192,768]{1,0:T(8,128)(2,1)S(1)} %copy-done.23), channel_id=1, source_target_pairs={{0,3},{1,2},{2,1},{3,0},{4,7},{5,6},{6,5},{7,4},{8,11},{9,10},{10,... | collective-permute-start | bytes 884744 | tf_op jit(solution)/shard_map/ppermute | solution.py:587
  86.2 17.7 %collective-permute-start.23 = (bf16[192,768]{1,0:T(8,128)(2,1)S(1)}, bf16[192,768]{1,0:T(8,128)(2,1)S(1)}, u32[]{:S(2)}, u32[]{:S(2)}) collective-permute-start(bf16[192,768]{1,0:T(8,128)(2,1)S(1)} %copy-done.22), channel_id=1, source_target_pairs={{0,1},{1,0},{2,3},{3,2},{4,5},{5,4},{6,7},{7,6},{8,9},{9,8},{10,11... | collective-permute-start | bytes 884744 | tf_op jit(solution)/shard_map/ppermute | solution.py:587
  93.2 10.7 %collective-permute-start.20 = (bf16[4,2,3,48,128]{4,3,2,1,0:T(8,128)(2,1)S(1)}, bf16[4,2,3,48,128]{4,3,2,1,0:T(8,128)(2,1)S(1)}, u32[]{:S(2)}, u32[]{:S(2)}) collective-permute-start(bf16[4,2,3,48,128]{4,3,2,1,0:T(8,128)(2,1)S(1)} %get-tuple-element.129), channel_id=1, source_target_pairs={{0,8},{4,12},{8,0},{12,4},{16,24},{20,28},{24,16},{28,20},{1,9},{5... | collective-permute-start | bytes 884744 | tf_op jit(solution)/shard_map/ppermute | solution.py:593
  94.8 9.1 %collective-permute-start.19 = (bf16[4,2,3,48,128]{4,3,2,1,0:T(8,128)(2,1)S(1)}, bf16[4,2,3,48,128]{4,3,2,1,0:T(8,128)(2,1)S(1)}, u32[]{:S(2)}, u32[]{:S(2)}) collective-permute-start(bf16[4,2,3,48,128]{4,3,2,1,0:T(8,128)(2,1)S(1)} %get-tuple-element.130), channel_id=1, source_target_pairs={{0,16},{4,20},{8,24},{12,28},{16,0},{20,4},{24,8},{28,12},{1,17},{... | collective-permute-start | bytes 884744 | tf_op jit(solution)/shard_map/ppermute | solution.py:593
  103.5 0.8 copy-start.8
  103.5 0.8 copy-start.10
  103.9 0.7 copy-start.12
  105.3 18.5 %collective-permute-start.27 = (bf16[4,3,48,128]{3,2,1,0:T(8,128)(2,1)S(1)}, bf16[4,3,48,128]{3,2,1,0:T(8,128)(2,1)S(1)}, u32[]{:S(2)}, u32[]{:S(2)}) collective-permute-start(bf16[4,3,48,128]{3,2,1,0:T(8,128)(2,1)S(1)} %get-tuple-element.119), channel_id=1, source_target_pairs={{0,2},{1,3},{2,0},{3,1},{4,6},{5,7},{6,4},{7,5},{8,10},{9,11},{10,... | collective-permute-start | bytes 442376 | tf_op jit(solution)/shard_map/ppermute | solution.py:587
  112.8 11.9 %collective-permute-start.28 = (bf16[4,3,48,128]{3,2,1,0:T(8,128)(2,1)S(1)}, bf16[4,3,48,128]{3,2,1,0:T(8,128)(2,1)S(1)}, u32[]{:S(2)}, u32[]{:S(2)}) collective-permute-start(bf16[4,3,48,128]{3,2,1,0:T(8,128)(2,1)S(1)} %get-tuple-element.120), channel_id=1, source_target_pairs={{0,3},{1,2},{2,1},{3,0},{4,7},{5,6},{6,5},{7,4},{8,11},{9,10},{10,... | collective-permute-start | bytes 442376 | tf_op jit(solution)/shard_map/ppermute | solution.py:587
  113.3 11.3 %collective-permute-start.29 = (bf16[4,3,48,128]{3,2,1,0:T(8,128)(2,1)S(1)}, bf16[4,3,48,128]{3,2,1,0:T(8,128)(2,1)S(1)}, u32[]{:S(2)}, u32[]{:S(2)}) collective-permute-start(bf16[4,3,48,128]{3,2,1,0:T(8,128)(2,1)S(1)} %get-tuple-element.121), channel_id=1, source_target_pairs={{0,1},{1,0},{2,3},{3,2},{4,5},{5,4},{6,7},{7,6},{8,9},{9,8},{10,11... | collective-permute-start | bytes 442376 | tf_op jit(solution)/shard_map/ppermute | solution.py:587
  120.8 12.4 %collective-permute-start.26 = (bf16[192,384]{1,0:T(8,128)(2,1)}, bf16[192,384]{1,0:T(8,128)(2,1)S(1)}, u32[]{:S(2)}, u32[]{:S(2)}) collective-permute-start(bf16[192,384]{1,0:T(8,128)(2,1)} %get-tuple-element.116), channel_id=1, source_target_pairs={{0,24},{4,28},{8,16},{12,20},{16,8},{20,12},{24,0},{28,4},{1,25},{... | collective-permute-start | bytes 442376 | tf_op jit(solution)/shard_map/ppermute | solution.py:593
  123.3 9.9 %collective-permute-start.25 = (bf16[192,384]{1,0:T(8,128)(2,1)}, bf16[192,384]{1,0:T(8,128)(2,1)S(1)}, u32[]{:S(2)}, u32[]{:S(2)}) collective-permute-start(bf16[192,384]{1,0:T(8,128)(2,1)} %get-tuple-element.116), channel_id=1, source_target_pairs={{0,16},{4,20},{8,24},{12,28},{16,0},{20,4},{24,8},{28,12},{1,17},{... | collective-permute-start | bytes 442376 | tf_op jit(solution)/shard_map/ppermute | solution.py:593
  123.8 0.9 copy-start.19
  123.8 9.4 %collective-permute-start.24 = (bf16[192,384]{1,0:T(8,128)(2,1)}, bf16[192,384]{1,0:T(8,128)(2,1)S(1)}, u32[]{:S(2)}, u32[]{:S(2)}) collective-permute-start(bf16[192,384]{1,0:T(8,128)(2,1)} %get-tuple-element.116), channel_id=1, source_target_pairs={{0,8},{4,12},{8,0},{12,4},{16,24},{20,28},{24,16},{28,20},{1,9},{5... | collective-permute-start | bytes 442376 | tf_op jit(solution)/shard_map/ppermute | solution.py:593
  124.7 0.7 copy-start.20
  124.7 0.7 copy-start.21
  125.4 7.8 %copy-start.18 = (bf16[192,384]{1,0:T(8,128)(2,1)S(1)}, bf16[192,384]{1,0:T(8,128)(2,1)}, u32[]{:S(2)}) copy-start(bf16[192,384]{1,0:T(8,128)(2,1)} %get-tuple-element.116) | copy-start | bytes 442372
  133.3 1.4 %collective-permute-start.30 = (bf16[192,384]{1,0:T(8,128)(2,1)S(1)}, bf16[192,384]{1,0:T(8,128)(2,1)S(1)}, u32[]{:S(2)}, u32[]{:S(2)}) collective-permute-start(bf16[192,384]{1,0:T(8,128)(2,1)S(1)} %add_convert_fusion.6), channel_id=1, source_target_pairs={{0,4},{4,0},{8,12},{12,8},{16,20},{20,16},{24,28},{28,24},{1,5},{5... | collective-permute-start | bytes 442376 | tf_op jit(solution)/shard_map/ppermute | solution.py:593

commit v12 on v11

--- a/solution.py
+++ b/solution.py
@@ -209,7 +209,7 @@
     step = 16
     tiles = -(-cols // 128)
     *sends, stats = pl.pallas_call(
-        functools.partial(bias_kernel, groups=groups, batch=16),
+        functools.partial(bias_kernel, groups=groups, batch=2),
         grid=(half // step,),
         in_specs=[
             smem(),
@@ -320,7 +320,7 @@
     tiles = -(-cols // 128)
     out = pl.pallas_call(
         functools.partial(
-            pair_back_kernel, groups=groups, calls=len(grads) // groups, factor=factor, batch=8
+            pair_back_kernel, groups=groups, calls=len(grads) // groups, factor=factor, batch=2
         ),
         grid=(half // step,),
         in_specs=[

time: 136 us -> 136 us (level)
  no operation moved by 1% of the time
where the time goes in v12:
time: 136 us
  Pallas kernels  44.4 us (33%)
  waiting for transfers between devices  43.5 us (32%)
  starting transfers between devices  40.6 us (30%)
  other arithmetic  3.17 us (2%)
  local copies, waits for them, and re-layouts  2.83 us (2%)
    ppermute x12, starting transfers between devices, swap_groups(): got.append(lax.ppermute(sends[bits], 'grp', perm))  26.7 us
    ppermute x12, waiting for transfers between devices, swap_groups(): got.append(lax.ppermute(sends[bits], 'grp', perm))  23.6 us
    ppermute x19, waiting for transfers between devices, flip_rows(): lax.ppermute(values, 'rows', [(index, index ^ bits) for index in range(ro...  19.9 us
    pallas_call x1, Pallas kernels, attention(): pl.pallas_call(functools.partial(attention_kernel, groups=groups, row_par...  15.2 us
    ppermute x19, starting transfers between devices, flip_rows(): lax.ppermute(values, 'rows', [(index, index ^ bits) for index in range(ro...  13.9 us
    pallas_call x1, Pallas kernels, pair_back(): pl.pallas_call(functools.partial(pair_back_kernel, groups=groups, calls=l...  7.71 us
    pallas_call x1, Pallas kernels, pair_bias(): pl.pallas_call(functools.partial(bias_kernel, groups=groups, batch=2), gr...  7.63 us
    pallas_call x1, Pallas kernels, split_heads(): pl.pallas_call(functools.partial(finish_kernel, groups=groups, calls=call...  7.48 us
  transfers between devices with their start and end apart: 31, of which 17 were waited for; matrix products, arithmetic and copies ran while one was open for 2% of the time, Pallas kernels for 16%

profile of v12, /device:TPU:0, one launch (start us, length us, event | category | flops | bytes accessed | tf_op | source)
XLA Modules:
  0.0 135.5 jit_solution(13566222685039608760)
XLA Ops:
  0.6 7.6 %shard_map.158 = (bf16[4,3,48,128]{3,2,1,0:T(8,128)(2,1)}, bf16[4,3,48,128]{3,2,1,0:T(8,128)(2,1)}, bf16[4,3,48,128]{3,2,1,0:T(8,128)(2,1)}, bf16[4,3,48,128]{3,2,1,0:T(8,128)(2,1)}, f32[2,48,24,192]{3,2,1,0:T(8,128)}) custom-call(s32[1]{0:T(128)} %bitcast.group_ref, s32[1]{0:T(128)} %bitcast.3.rows_ref.row_ref, s32[768]{0:T(1024)} %cols_ref.1, f32[16]{0:T(128)} %gain_ref.1, ...), custom_call_target="tpu_custom_call" | custom-call | tf_op jit(solution)/shard_map/pallas_call | solution.py:211
  8.3 4.0 %collective-permute-start = (bf16[4,3,48,128]{3,2,1,0:T(8,128)(2,1)}, bf16[4,3,48,128]{3,2,1,0:T(8,128)(2,1)S(1)}, u32[]{:S(2)}, u32[]{:S(2)}) collective-permute-start(bf16[4,3,48,128]{3,2,1,0:T(8,128)(2,1)} %get-tuple-element.69), channel_id=1, source_target_pairs={{0,2},{1,3},{2,0},{3,1},{4,6},{5,7},{6,4},{7,5},{8,10},{9,11},{10,... | collective-permute-start | bytes 442376 | tf_op jit(solution)/shard_map/ppermute | solution.py:587
  12.3 1.3 collective-permute-start.1
  13.6 0.2 collective-permute-start.2
  13.9 6.4 %shard_map.157 = (bf16[192,768]{1,0:T(8,128)(2,1)}, bf16[192,768]{1,0:T(8,128)(2,1)}, bf16[192,768]{1,0:T(8,128)(2,1)}, bf16[192,768]{1,0:T(8,128)(2,1)}, f32[192,768]{1,0:T(8,128)}, /*index=5*/f32[192,768]{1,0:T(8,128)}) custom-call(s32[1]{0:T(128)} %bitcast.group_ref, bf16[192,384]{1,0:T(8,128)(2,1)} %single_ref.3, bf16[192,768]{1,0:T(8,128)(2,1)} %bitcast.23, ...), custom_call_target="tpu_custom_call" | custom-call | tf_op jit(solution)/shard_map/pallas_call | solution.py:684
  20.2 0.0 copy-start.26
  20.3 3.3 %collective-permute-done = bf16[4,3,48,128]{3,2,1,0:T(8,128)(2,1)S(1)} collective-permute-done((bf16[4,3,48,128]{3,2,1,0:T(8,128)(2,1)}, bf16[4,3,48,128]{3,2,1,0:T(8,128)(2,1)S(1)}, u32[]{:S(2)}, u32[]{:S(2)}) %collective-permute-start) | collective-permute-done | bytes 147488 | tf_op jit(solution)/shard_map/ppermute | solution.py:587
  23.6 0.5 collective-permute-done.2
  24.1 0.1 pad_maximum_fusion.rest_0_
  24.1 1.6 %collective-permute-start.6 = (bf16[4,4,3,48,128]{4,3,2,1,0:T(8,128)(2,1)S(1)}, bf16[4,4,3,48,128]{4,3,2,1,0:T(8,128)(2,1)S(1)}, u32[]{:S(2)}, u32[]{:S(2)}) collective-permute-start(bf16[4,4,3,48,128]{4,3,2,1,0:T(8,128)(2,1)S(1)} %pad_maximum_fusion.rest_0_), channel_id=1, source_target_pairs={{0,16},{4,20},{8,24},{12,28},{16,0},{20,4},{24,8},{28,12},{1,17},{... | collective-permute-start | bytes 1769480 | tf_op jit(solution)/shard_map/ppermute | solution.py:593
  25.8 1.5 %collective-permute-start.4 = (bf16[4,4,3,48,128]{4,3,2,1,0:T(8,128)(2,1)S(1)}, bf16[4,4,3,48,128]{4,3,2,1,0:T(8,128)(2,1)S(1)}, u32[]{:S(2)}, u32[]{:S(2)}) collective-permute-start(bf16[4,4,3,48,128]{4,3,2,1,0:T(8,128)(2,1)S(1)} %pad_maximum_fusion.rest_0_), channel_id=1, source_target_pairs={{0,8},{4,12},{8,0},{12,4},{16,24},{20,28},{24,16},{28,20},{1,9},{5... | collective-permute-start | bytes 1769480 | tf_op jit(solution)/shard_map/ppermute | solution.py:593
  27.3 4.4 %collective-permute-start.8 = (bf16[192,768]{1,0:T(8,128)(2,1)S(1)}, bf16[192,768]{1,0:T(8,128)(2,1)S(1)}, u32[]{:S(2)}, u32[]{:S(2)}) collective-permute-start(bf16[192,768]{1,0:T(8,128)(2,1)S(1)} %copy-done.27), channel_id=1, source_target_pairs={{0,2},{1,3},{2,0},{3,1},{4,6},{5,7},{6,4},{7,5},{8,10},{9,11},{10,... | collective-permute-start | bytes 884744 | tf_op jit(solution)/shard_map/ppermute | solution.py:587
  31.7 0.5 collective-permute-start.9
  32.3 0.1 collective-permute-start.10
  32.3 5.2 %collective-permute-done.6.rest_4_ = bf16[4,4,3,48,128]{4,3,2,1,0:T(8,128)(2,1)S(1)} collective-permute-done((bf16[4,4,3,48,128]{4,3,2,1,0:T(8,128)(2,1)S(1)}, bf16[4,4,3,48,128]{4,3,2,1,0:T(8,128)(2,1)S(1)}, u32[]{:S(2)}, u32[]{:S(2)}) %collective-permute-start.6) | collective-permute-done | bytes 589856 | tf_op jit(solution)/shard_map/ppermute | solution.py:593
  37.5 1.2 collective-permute-start.12
  38.7 0.7 collective-permute-done.4.rest_2_
  39.5 1.0 collective-permute-start.11
  40.5 10.9 %collective-permute-done.8.rest_11_ = bf16[192,768]{1,0:T(8,128)(2,1)S(1)} collective-permute-done((bf16[192,768]{1,0:T(8,128)(2,1)S(1)}, bf16[192,768]{1,0:T(8,128)(2,1)S(1)}, u32[]{:S(2)}, u32[]{:S(2)}) %collective-permute-start.8) | collective-permute-done | bytes 294944 | tf_op jit(solution)/shard_map/ppermute | solution.py:587
  51.4 0.5 collective-permute-start.7
  51.9 0.4 collective-permute-done.10.rest_13_
  52.4 0.6 collective-permute-start.13
  52.9 0.1 collective-permute-start.14
  53.0 0.4 collective-permute-done.3.rest_1_
  53.4 0.8 collective-permute-done.7.rest_5_
  54.3 0.8 collective-permute-done.5.rest_3_
  55.1 0.4 collective-permute-done.13.rest_7_
  55.5 0.4 collective-permute-done.14.rest_9_
  56.0 0.2 copy-done.15
  56.2 0.7 copy-done.16
  57.0 15.2 %shard_map.159 = (bf16[192,768]{1,0:T(8,128)(2,1)}, bf16[192,768]{1,0:T(8,128)(2,1)}, bf16[192,768]{1,0:T(8,128)(2,1)}, bf16[192,768]{1,0:T(8,128)(2,1)}, bf16[4...) custom-call(s32[1]{0:T(128)} %bitcast.group_ref, ...), custom_call_target="tpu_custom_call" | custom-call | tf_op jit(solution)/shard_map/pallas_call | solution.py:502
  72.2 0.2 collective-permute-start.15
  72.4 2.9 %collective-permute-done.15 = bf16[4,8,3,48,128]{4,3,2,1,0:T(8,128)(2,1)S(1)} collective-permute-done((bf16[4,8,3,48,128]{4,3,2,1,0:T(8,128)(2,1)}, bf16[4,8,3,48,128]{4,3,2,1,0:T(8,128)(2,1)S(1)}, u32[]{:S(2)}, u32[]{:S(2)}) %collective-permute-start.15) | collective-permute-done | bytes 1179680 | tf_op jit(solution)/shard_map/ppermute | solution.py:593
  75.3 0.1 collective-permute-start.16
  75.5 1.7 %add_convert_fusion.3 = (bf16[4,4,3,48,128]{4,3,2,1,0:T(8,128)(2,1)S(1)}, bf16[4,4,3,48,128]{4,3,2,1,0:T(8,128)(2,1)S(1)}) fusion(bf16[4,8,3,48,128]{4,3,2,1,0:T(8,128)(2,1)S(1)} %collective-permute-done.15, bf16[4,16,3,48,128]{4,3,2,1,0:T(8,128)(2,1)} %get-tuple-element.91), kind=kLoop, calls=%fused_computation.3 | loop fusion | flops 2359296 | bytes 3538944 | tf_op jit(solution)/shard_map/convert_element_type | solution.py:628
  77.2 0.6 collective-permute-start.17
  77.8 0.5 collective-permute-start.18
  78.3 4.7 %collective-permute-start.21 = (bf16[192,768]{1,0:T(8,128)(2,1)S(1)}, bf16[192,768]{1,0:T(8,128)(2,1)S(1)}, u32[]{:S(2)}, u32[]{:S(2)}) collective-permute-start(bf16[192,768]{1,0:T(8,128)(2,1)S(1)} %copy-done.24), channel_id=1, source_target_pairs={{0,2},{1,3},{2,0},{3,1},{4,6},{5,7},{6,4},{7,5},{8,10},{9,11},{10,... | collective-permute-start | bytes 884744 | tf_op jit(solution)/shard_map/ppermute | solution.py:587
  83.0 3.3 %collective-permute-start.22 = (bf16[192,768]{1,0:T(8,128)(2,1)S(1)}, bf16[192,768]{1,0:T(8,128)(2,1)S(1)}, u32[]{:S(2)}, u32[]{:S(2)}) collective-permute-start(bf16[192,768]{1,0:T(8,128)(2,1)S(1)} %copy-done.23), channel_id=1, source_target_pairs={{0,3},{1,2},{2,1},{3,0},{4,7},{5,6},{6,5},{7,4},{8,11},{9,10},{10,... | collective-permute-start | bytes 884744 | tf_op jit(solution)/shard_map/ppermute | solution.py:587
  86.3 6.5 %collective-permute-done.17 = bf16[4,4,3,48,128]{4,3,2,1,0:T(8,128)(2,1)S(1)} collective-permute-done((bf16[4,4,3,48,128]{4,3,2,1,0:T(8,128)(2,1)S(1)}, bf16[4,4,3,48,128]{4,3,2,1,0:T(8,128)(2,1)S(1)}, u32[]{:S(2)}, u32[]{:S(2)}) %collective-permute-start.17) | collective-permute-done | bytes 589856 | tf_op jit(solution)/shard_map/ppermute | solution.py:593
  92.9 0.3 collective-permute-done.18
  93.1 0.2 add_convert_fusion.4
  93.3 1.6 %collective-permute-start.20 = (bf16[4,2,3,48,128]{4,3,2,1,0:T(8,128)(2,1)S(1)}, bf16[4,2,3,48,128]{4,3,2,1,0:T(8,128)(2,1)S(1)}, u32[]{:S(2)}, u32[]{:S(2)}) collective-permute-start(bf16[4,2,3,48,128]{4,3,2,1,0:T(8,128)(2,1)S(1)} %get-tuple-element.129), channel_id=1, source_target_pairs={{0,8},{4,12},{8,0},{12,4},{16,24},{20,28},{24,16},{28,20},{1,9},{5... | collective-permute-start | bytes 884744 | tf_op jit(solution)/shard_map/ppermute | solution.py:593
  94.9 0.5 collective-permute-start.19
  95.5 8.1 %collective-permute-done.21.rest_2_ = bf16[192,768]{1,0:T(8,128)(2,1)S(1)} collective-permute-done((bf16[192,768]{1,0:T(8,128)(2,1)S(1)}, bf16[192,768]{1,0:T(8,128)(2,1)S(1)}, u32[]{:S(2)}, u32[]{:S(2)}) %collective-permute-start.21) | collective-permute-done | bytes 294944 | tf_op jit(solution)/shard_map/ppermute | solution.py:587
  103.6 0.4 collective-permute-done.23.rest_1_
  104.0 0.3 add_convert_fusion
  104.3 0.0 copy-done.10
  104.4 0.4 copy-done.12
  104.7 0.7 slice_bitcast_fusion
  105.4 7.5 %collective-permute-start.27 = (bf16[4,3,48,128]{3,2,1,0:T(8,128)(2,1)S(1)}, bf16[4,3,48,128]{3,2,1,0:T(8,128)(2,1)S(1)}, u32[]{:S(2)}, u32[]{:S(2)}) collective-permute-start(bf16[4,3,48,128]{3,2,1,0:T(8,128)(2,1)S(1)} %get-tuple-element.119), channel_id=1, source_target_pairs={{0,2},{1,3},{2,0},{3,1},{4,6},{5,7},{6,4},{7,5},{8,10},{9,11},{10,... | collective-permute-start | bytes 442376 | tf_op jit(solution)/shard_map/ppermute | solution.py:587
  112.9 0.5 collective-permute-start.28
  113.4 0.0 collective-permute-start.29
  113.4 7.5 %shard_map.160 = (bf16[192,768]{1,0:T(8,128)(2,1)}, bf16[192,384]{1,0:T(8,128)(2,1)}) custom-call(s32[1]{0:T(128)} %bitcast.group_ref, bf16[192,384]{1,0:T(8,128)(2,1)} %single_ref.3, bf16[192,768]{1,0:T(8,128)(2,1)} %bitcast.24, bf16[192,768]{1,0:T(8,128)(2,1)} %bitcast.26, f32[192,768]{1,0:T(8,128)} %get-tuple-element.66.gamma_ref, ...), custom_call_target="tpu_custom_call" | custom-call | tf_op jit(solution)/shard_map/pallas_call | solution.py:725
  120.9 2.5 %collective-permute-start.26 = (bf16[192,384]{1,0:T(8,128)(2,1)}, bf16[192,384]{1,0:T(8,128)(2,1)S(1)}, u32[]{:S(2)}, u32[]{:S(2)}) collective-permute-start(bf16[192,384]{1,0:T(8,128)(2,1)} %get-tuple-element.116), channel_id=1, source_target_pairs={{0,24},{4,28},{8,16},{12,20},{16,8},{20,12},{24,0},{28,4},{1,25},{... | collective-permute-start | bytes 442376 | tf_op jit(solution)/shard_map/ppermute | solution.py:593
  123.4 0.5 collective-permute-start.25
  123.9 0.9 collective-permute-start.24
  124.8 0.6 copy-done.20
  125.4 0.1 copy-done.21
  125.5 7.7 %shard_map.161 = bf16[2,48,192,128]{3,2,1,0:T(8,128)(2,1)} custom-call(s32[1]{0:T(128)} %bitcast.group_ref, bf16[2,48,192,128]{3,2,1,0:T(8,128)(2,1)} %bitcast.21, f32[2,48,24,192]{3,2,1,0:T(8,128)} %get-tuple-element.117.stats_ref, bf16[16,128]{1,0:T(8,128)(2,1)} %bitcast.32, bf16[4,3,48,128]{3,2,1,0:T(8,128)(2,1)} %get-tuple-element.118.rest_0_, ...), custom_call_target="tpu_custom_call" | custom-call | tf_op jit(solution)/shard_map/pallas_call | solution.py:321
  133.2 0.1 add_convert_fusion.6
  133.3 0.1 collective-permute-start.30
  133.4 1.4 %collective-permute-done.30 = bf16[192,384]{1,0:T(8,128)(2,1)S(1)} collective-permute-done((bf16[192,384]{1,0:T(8,128)(2,1)S(1)}, bf16[192,384]{1,0:T(8,128)(2,1)S(1)}, u32[]{:S(2)}, u32[]{:S(2)}) %collective-permute-start.30) | collective-permute-done | bytes 147488 | tf_op jit(solution)/shard_map/ppermute | solution.py:593
  134.8 0.7 convert_add_fusion
  (70 shorter events, 0.2 us)
Async XLA Ops:
  8.3 15.3 %collective-permute-start = (bf16[4,3,48,128]{3,2,1,0:T(8,128)(2,1)}, bf16[4,3,48,128]{3,2,1,0:T(8,128)(2,1)S(1)}, u32[]{:S(2)}, u32[]{:S(2)}) collective-permute-start(bf16[4,3,48,128]{3,2,1,0:T(8,128)(2,1)} %get-tuple-element.69), channel_id=1, source_target_pairs={{0,2},{1,3},{2,0},{3,1},{4,6},{5,7},{6,4},{7,5},{8,10},{9,11},{10,... | collective-permute-start | bytes 442376 | tf_op jit(solution)/shard_map/ppermute | solution.py:587
  12.3 11.3 %collective-permute-start.1 = (bf16[4,3,48,128]{3,2,1,0:T(8,128)(2,1)}, bf16[4,3,48,128]{3,2,1,0:T(8,128)(2,1)S(1)}, u32[]{:S(2)}, u32[]{:S(2)}) collective-permute-start(bf16[4,3,48,128]{3,2,1,0:T(8,128)(2,1)} %get-tuple-element.70), channel_id=1, source_target_pairs={{0,3},{1,2},{2,1},{3,0},{4,7},{5,6},{6,5},{7,4},{8,11},{9,10},{10,... | collective-permute-start | bytes 442376 | tf_op jit(solution)/shard_map/ppermute | solution.py:587
  13.6 10.4 %collective-permute-start.2 = (bf16[4,3,48,128]{3,2,1,0:T(8,128)(2,1)}, bf16[4,3,48,128]{3,2,1,0:T(8,128)(2,1)S(1)}, u32[]{:S(2)}, u32[]{:S(2)}) collective-permute-start(bf16[4,3,48,128]{3,2,1,0:T(8,128)(2,1)} %get-tuple-element.71), channel_id=1, source_target_pairs={{0,1},{1,0},{2,3},{3,2},{4,5},{5,4},{6,7},{7,6},{8,9},{9,8},{10,11... | collective-permute-start | bytes 442376 | tf_op jit(solution)/shard_map/ppermute | solution.py:587
  13.9 10.2 %copy-start.17 = (bf16[4,3,48,128]{3,2,1,0:T(8,128)(2,1)S(1)}, bf16[4,3,48,128]{3,2,1,0:T(8,128)(2,1)}, u32[]{:S(2)}) copy-start(bf16[4,3,48,128]{3,2,1,0:T(8,128)(2,1)} %get-tuple-element.79) | copy-start | bytes 442372
  20.2 7.0 %copy-start.27 = (bf16[192,768]{1,0:T(8,128)(2,1)S(1)}, bf16[192,768]{1,0:T(8,128)(2,1)}, u32[]{:S(2)}) copy-start(bf16[192,768]{1,0:T(8,128)(2,1)} %get-tuple-element.76) | copy-start | bytes 884740
  20.2 11.5 %copy-start.26 = (bf16[192,768]{1,0:T(8,128)(2,1)S(1)}, bf16[192,768]{1,0:T(8,128)(2,1)}, u32[]{:S(2)}) copy-start(bf16[192,768]{1,0:T(8,128)(2,1)} %get-tuple-element.77) | copy-start | bytes 884740
  20.3 12.0 %copy-start.25 = (bf16[192,768]{1,0:T(8,128)(2,1)S(1)}, bf16[192,768]{1,0:T(8,128)(2,1)}, u32[]{:S(2)}) copy-start(bf16[192,768]{1,0:T(8,128)(2,1)} %get-tuple-element.78) | copy-start | bytes 884740
  24.1 31.8 %copy-start = (bf16[4,4,3,48,128]{4,3,2,1,0:T(8,128)(2,1)}, bf16[4,4,3,48,128]{4,3,2,1,0:T(8,128)(2,1)S(1)}, u32[]{:S(2)}) copy-start(bf16[4,4,3,48,128]{4,3,2,1,0:T(8,128)(2,1)S(1)} %pad_maximum_fusion.rest_0_) | copy-start | bytes 1769476
  24.1 13.3 %collective-permute-start.6 = (bf16[4,4,3,48,128]{4,3,2,1,0:T(8,128)(2,1)S(1)}, bf16[4,4,3,48,128]{4,3,2,1,0:T(8,128)(2,1)S(1)}, u32[]{:S(2)}, u32[]{:S(2)}) collective-permute-start(bf16[4,4,3,48,128]{4,3,2,1,0:T(8,128)(2,1)S(1)} %pad_maximum_fusion.rest_0_), channel_id=1, source_target_pairs={{0,16},{4,20},{8,24},{12,28},{16,0},{20,4},{24,8},{28,12},{1,17},{... | collective-permute-start | bytes 1769480 | tf_op jit(solution)/shard_map/ppermute | solution.py:593
  25.8 13.7 %collective-permute-start.4 = (bf16[4,4,3,48,128]{4,3,2,1,0:T(8,128)(2,1)S(1)}, bf16[4,4,3,48,128]{4,3,2,1,0:T(8,128)(2,1)S(1)}, u32[]{:S(2)}, u32[]{:S(2)}) collective-permute-start(bf16[4,4,3,48,128]{4,3,2,1,0:T(8,128)(2,1)S(1)} %pad_maximum_fusion.rest_0_), channel_id=1, source_target_pairs={{0,8},{4,12},{8,0},{12,4},{16,24},{20,28},{24,16},{28,20},{1,9},{5... | collective-permute-start | bytes 1769480 | tf_op jit(solution)/shard_map/ppermute | solution.py:593
  27.3 24.1 %collective-permute-start.8 = (bf16[192,768]{1,0:T(8,128)(2,1)S(1)}, bf16[192,768]{1,0:T(8,128)(2,1)S(1)}, u32[]{:S(2)}, u32[]{:S(2)}) collective-permute-start(bf16[192,768]{1,0:T(8,128)(2,1)S(1)} %copy-done.27), channel_id=1, source_target_pairs={{0,2},{1,3},{2,0},{3,1},{4,6},{5,7},{6,4},{7,5},{8,10},{9,11},{10,... | collective-permute-start | bytes 884744 | tf_op jit(solution)/shard_map/ppermute | solution.py:587
  31.7 19.7 %collective-permute-start.9 = (bf16[192,768]{1,0:T(8,128)(2,1)S(1)}, bf16[192,768]{1,0:T(8,128)(2,1)S(1)}, u32[]{:S(2)}, u32[]{:S(2)}) collective-permute-start(bf16[192,768]{1,0:T(8,128)(2,1)S(1)} %copy-done.26), channel_id=1, source_target_pairs={{0,3},{1,2},{2,1},{3,0},{4,7},{5,6},{6,5},{7,4},{8,11},{9,10},{10,... | collective-permute-start | bytes 884744 | tf_op jit(solution)/shard_map/ppermute | solution.py:587
  32.3 20.1 %collective-permute-start.10 = (bf16[192,768]{1,0:T(8,128)(2,1)S(1)}, bf16[192,768]{1,0:T(8,128)(2,1)S(1)}, u32[]{:S(2)}, u32[]{:S(2)}) collective-permute-start(bf16[192,768]{1,0:T(8,128)(2,1)S(1)} %copy-done.25), channel_id=1, source_target_pairs={{0,1},{1,0},{2,3},{3,2},{4,5},{5,4},{6,7},{7,6},{8,9},{9,8},{10,11... | collective-permute-start | bytes 884744 | tf_op jit(solution)/shard_map/ppermute | solution.py:587
  37.5 18.5 %copy-start.2 = (bf16[4,4,3,48,128]{4,3,2,1,0:T(8,128)(2,1)}, bf16[4,4,3,48,128]{4,3,2,1,0:T(8,128)(2,1)S(1)}, u32[]{:S(2)}) copy-start(bf16[4,4,3,48,128]{4,3,2,1,0:T(8,128)(2,1)S(1)} %collective-permute-done.6.rest_4_) | copy-start | bytes 1769476
  37.5 14.8 %collective-permute-start.12 = (bf16[2,4,3,48,128]{4,3,2,1,0:T(8,128)(2,1)S(1)}, bf16[2,4,3,48,128]{4,3,2,1,0:T(8,128)(2,1)S(1)}, u32[]{:S(2)}, u32[]{:S(2)}) collective-permute-start(bf16[2,4,3,48,128]{4,3,2,1,0:T(8,128)(2,1)S(1)} %slice.81), channel_id=1, source_target_pairs={{0,8},{4,12},{8,0},{12,4},{16,24},{20,28},{24,16},{28,20},{1,9},{5... | collective-permute-start | bytes 884744 | tf_op jit(solution)/shard_map/ppermute | solution.py:593
  39.5 16.5 %copy-start.3 = (bf16[4,4,3,48,128]{4,3,2,1,0:T(8,128)(2,1)}, bf16[4,4,3,48,128]{4,3,2,1,0:T(8,128)(2,1)S(1)}, u32[]{:S(2)}) copy-start(bf16[4,4,3,48,128]{4,3,2,1,0:T(8,128)(2,1)S(1)} %collective-permute-done.4.rest_2_) | copy-start | bytes 1769476
  39.5 12.9 %collective-permute-start.11 = (bf16[2,4,3,48,128]{4,3,2,1,0:T(8,128)(2,1)S(1)}, bf16[2,4,3,48,128]{4,3,2,1,0:T(8,128)(2,1)S(1)}, u32[]{:S(2)}, u32[]{:S(2)}) collective-permute-start(bf16[2,4,3,48,128]{4,3,2,1,0:T(8,128)(2,1)S(1)} %slice.80), channel_id=1, source_target_pairs={{0,16},{4,20},{8,24},{12,28},{16,0},{20,4},{24,8},{28,12},{1,17},{... | collective-permute-start | bytes 884744 | tf_op jit(solution)/shard_map/ppermute | solution.py:593
  51.4 4.6 %copy-start.7 = (bf16[192,768]{1,0:T(8,128)(2,1)}, bf16[192,768]{1,0:T(8,128)(2,1)S(1)}, u32[]{:S(2)}) copy-start(bf16[192,768]{1,0:T(8,128)(2,1)S(1)} %collective-permute-done.8.rest_11_) | copy-start | bytes 884740
  51.4 2.0 %collective-permute-start.3 = (bf16[4,4,3,48,128]{4,3,2,1,0:T(8,128)(2,1)S(1)}, bf16[4,4,3,48,128]{4,3,2,1,0:T(8,128)(2,1)S(1)}, u32[]{:S(2)}, u32[]{:S(2)}) collective-permute-start(bf16[4,4,3,48,128]{4,3,2,1,0:T(8,128)(2,1)S(1)} %pad_maximum_fusion.rest_0_), channel_id=1, source_target_pairs={{0,4},{4,0},{8,12},{12,8},{16,20},{20,16},{24,28},{28,24},{1,5},{5... | collective-permute-start | bytes 1769480 | tf_op jit(solution)/shard_map/ppermute | solution.py:593
  51.4 4.5 %copy-start.9 = (bf16[192,768]{1,0:T(8,128)(2,1)}, bf16[192,768]{1,0:T(8,128)(2,1)S(1)}, u32[]{:S(2)}) copy-start(bf16[192,768]{1,0:T(8,128)(2,1)S(1)} %collective-permute-done.9.rest_12_) | copy-start | bytes 884740
  51.4 2.8 %collective-permute-start.7 = (bf16[4,4,3,48,128]{4,3,2,1,0:T(8,128)(2,1)S(1)}, bf16[4,4,3,48,128]{4,3,2,1,0:T(8,128)(2,1)S(1)}, u32[]{:S(2)}, u32[]{:S(2)}) collective-permute-start(bf16[4,4,3,48,128]{4,3,2,1,0:T(8,128)(2,1)S(1)} %collective-permute-done.6.rest_4_), channel_id=1, source_target_pairs={{0,4},{4,0},{8,12},{12,8},{16,20},{20,16},{24,28},{28,24},{1,5},{5... | collective-permute-start | bytes 1769480 | tf_op jit(solution)/shard_map/ppermute | solution.py:593
  52.3 3.6 %copy-start.11 = (bf16[192,768]{1,0:T(8,128)(2,1)}, bf16[192,768]{1,0:T(8,128)(2,1)S(1)}, u32[]{:S(2)}) copy-start(bf16[192,768]{1,0:T(8,128)(2,1)S(1)} %collective-permute-done.10.rest_13_) | copy-start | bytes 884740
  52.3 2.8 %collective-permute-start.5 = (bf16[4,4,3,48,128]{4,3,2,1,0:T(8,128)(2,1)S(1)}, bf16[4,4,3,48,128]{4,3,2,1,0:T(8,128)(2,1)S(1)}, u32[]{:S(2)}, u32[]{:S(2)}) collective-permute-start(bf16[4,4,3,48,128]{4,3,2,1,0:T(8,128)(2,1)S(1)} %collective-permute-done.4.rest_2_), channel_id=1, source_target_pairs={{0,4},{4,0},{8,12},{12,8},{16,20},{20,16},{24,28},{28,24},{1,5},{5... | collective-permute-start | bytes 1769480 | tf_op jit(solution)/shard_map/ppermute | solution.py:593
  52.3 3.6 %copy-start.13 = (bf16[2,4,3,48,128]{4,3,2,1,0:T(8,128)(2,1)}, bf16[2,4,3,48,128]{4,3,2,1,0:T(8,128)(2,1)S(1)}, u32[]{:S(2)}) copy-start(bf16[2,4,3,48,128]{4,3,2,1,0:T(8,128)(2,1)S(1)} %collective-permute-done.12.rest_8_) | copy-start | bytes 884740
  52.4 3.6 %copy-start.14 = (bf16[2,4,3,48,128]{4,3,2,1,0:T(8,128)(2,1)}, bf16[2,4,3,48,128]{4,3,2,1,0:T(8,128)(2,1)S(1)}, u32[]{:S(2)}) copy-start(bf16[2,4,3,48,128]{4,3,2,1,0:T(8,128)(2,1)S(1)} %collective-permute-done.11.rest_6_) | copy-start | bytes 884740
  52.4 3.1 %collective-permute-start.13 = (bf16[2,4,3,48,128]{4,3,2,1,0:T(8,128)(2,1)S(1)}, bf16[2,4,3,48,128]{4,3,2,1,0:T(8,128)(2,1)S(1)}, u32[]{:S(2)}, u32[]{:S(2)}) collective-permute-start(bf16[2,4,3,48,128]{4,3,2,1,0:T(8,128)(2,1)S(1)} %collective-permute-done.11.rest_6_), channel_id=1, source_target_pairs={{0,4},{4,0},{8,12},{12,8},{16,20},{20,16},{24,28},{28,24},{1,5},{5... | collective-permute-start | bytes 884744 | tf_op jit(solution)/shard_map/ppermute | solution.py:593
  52.9 3.0 %collective-permute-start.14 = (bf16[2,4,3,48,128]{4,3,2,1,0:T(8,128)(2,1)S(1)}, bf16[2,4,3,48,128]{4,3,2,1,0:T(8,128)(2,1)S(1)}, u32[]{:S(2)}, u32[]{:S(2)}) collective-permute-start(bf16[2,4,3,48,128]{4,3,2,1,0:T(8,128)(2,1)S(1)} %collective-permute-done.12.rest_8_), channel_id=1, source_target_pairs={{0,4},{4,0},{8,12},{12,8},{16,20},{20,16},{24,28},{28,24},{1,5},{5... | collective-permute-start | bytes 884744 | tf_op jit(solution)/shard_map/ppermute | solution.py:593
  53.4 2.6 %copy-start.4 = (bf16[4,4,3,48,128]{4,3,2,1,0:T(8,128)(2,1)}, bf16[4,4,3,48,128]{4,3,2,1,0:T(8,128)(2,1)S(1)}, u32[]{:S(2)}) copy-start(bf16[4,4,3,48,128]{4,3,2,1,0:T(8,128)(2,1)S(1)} %collective-permute-done.3.rest_1_) | copy-start | bytes 1769476
  54.3 1.8 %copy-start.5 = (bf16[4,4,3,48,128]{4,3,2,1,0:T(8,128)(2,1)}, bf16[4,4,3,48,128]{4,3,2,1,0:T(8,128)(2,1)S(1)}, u32[]{:S(2)}) copy-start(bf16[4,4,3,48,128]{4,3,2,1,0:T(8,128)(2,1)S(1)} %collective-permute-done.7.rest_5_) | copy-start | bytes 1769476
  55.1 0.9 copy-start.6
  55.5 0.7 copy-start.15
  56.2 0.7 copy-start.16
  72.2 3.1 %collective-permute-start.15 = (bf16[4,8,3,48,128]{4,3,2,1,0:T(8,128)(2,1)}, bf16[4,8,3,48,128]{4,3,2,1,0:T(8,128)(2,1)S(1)}, u32[]{:S(2)}, u32[]{:S(2)}) collective-permute-start(bf16[4,8,3,48,128]{4,3,2,1,0:T(8,128)(2,1)} %get-tuple-element.92), channel_id=1, source_target_pairs={{0,4},{4,0},{8,12},{12,8},{16,20},{20,16},{24,28},{28,24},{1,5},{5... | collective-permute-start | bytes 3538952 | tf_op jit(solution)/shard_map/ppermute | solution.py:593
  75.3 11.0 %collective-permute-start.16 = (bf16[4,8,3,48,128]{4,3,2,1,0:T(8,128)(2,1)}, bf16[4,8,3,48,128]{4,3,2,1,0:T(8,128)(2,1)S(1)}, u32[]{:S(2)}, u32[]{:S(2)}) collective-permute-start(bf16[4,8,3,48,128]{4,3,2,1,0:T(8,128)(2,1)} %get-tuple-element.94), channel_id=1, source_target_pairs={{0,4},{4,0},{8,12},{12,8},{16,20},{20,16},{24,28},{28,24},{1,5},{5... | collective-permute-start | bytes 3538952 | tf_op jit(solution)/shard_map/ppermute | solution.py:593
  75.4 2.9 %copy-start.24 = (bf16[192,768]{1,0:T(8,128)(2,1)S(1)}, bf16[192,768]{1,0:T(8,128)(2,1)}, u32[]{:S(2)}) copy-start(bf16[192,768]{1,0:T(8,128)(2,1)} %get-tuple-element.99) | copy-start | bytes 884740
  75.4 7.6 %copy-start.23 = (bf16[192,768]{1,0:T(8,128)(2,1)S(1)}, bf16[192,768]{1,0:T(8,128)(2,1)}, u32[]{:S(2)}) copy-start(bf16[192,768]{1,0:T(8,128)(2,1)} %get-tuple-element.100) | copy-start | bytes 884740
  75.4 10.9 %copy-start.22 = (bf16[192,768]{1,0:T(8,128)(2,1)S(1)}, bf16[192,768]{1,0:T(8,128)(2,1)}, u32[]{:S(2)}) copy-start(bf16[192,768]{1,0:T(8,128)(2,1)} %get-tuple-element.101) | copy-start | bytes 884740
  75.4 17.7 %copy-start.1 = (bf16[4,16,3,48,128]{4,3,2,1,0:T(8,128)(2,1)S(1)}, bf16[4,16,3,48,128]{4,3,2,1,0:T(8,128)(2,1)}, u32[]{:S(2)}) copy-start(bf16[4,16,3,48,128]{4,3,2,1,0:T(8,128)(2,1)} %get-tuple-element.91) | copy-start | bytes 7077892
  77.2 15.7 %collective-permute-start.17 = (bf16[4,4,3,48,128]{4,3,2,1,0:T(8,128)(2,1)S(1)}, bf16[4,4,3,48,128]{4,3,2,1,0:T(8,128)(2,1)S(1)}, u32[]{:S(2)}, u32[]{:S(2)}) collective-permute-start(bf16[4,4,3,48,128]{4,3,2,1,0:T(8,128)(2,1)S(1)} %get-tuple-element.131), channel_id=1, source_target_pairs={{0,8},{4,12},{8,0},{12,4},{16,24},{20,28},{24,16},{28,20},{1,9},{5... | collective-permute-start | bytes 1769480 | tf_op jit(solution)/shard_map/ppermute | solution.py:593
  77.8 15.3 %collective-permute-start.18 = (bf16[4,4,3,48,128]{4,3,2,1,0:T(8,128)(2,1)S(1)}, bf16[4,4,3,48,128]{4,3,2,1,0:T(8,128)(2,1)S(1)}, u32[]{:S(2)}, u32[]{:S(2)}) collective-permute-start(bf16[4,4,3,48,128]{4,3,2,1,0:T(8,128)(2,1)S(1)} %get-tuple-element.132), channel_id=1, source_target_pairs={{0,16},{4,20},{8,24},{12,28},{16,0},{20,4},{24,8},{28,12},{1,17},{... | collective-permute-start | bytes 1769480 | tf_op jit(solution)/shard_map/ppermute | solution.py:593
  78.3 25.3 %collective-permute-start.21 = (bf16[192,768]{1,0:T(8,128)(2,1)S(1)}, bf16[192,768]{1,0:T(8,128)(2,1)S(1)}, u32[]{:S(2)}, u32[]{:S(2)}) collective-permute-start(bf16[192,768]{1,0:T(8,128)(2,1)S(1)} %copy-done.24), channel_id=1, source_target_pairs={{0,2},{1,3},{2,0},{3,1},{4,6},{5,7},{6,4},{7,5},{8,10},{9,11},{10,... | collective-permute-start | bytes 884744 | tf_op jit(solution)/shard_map/ppermute | solution.py:587
  83.0 20.5 %collective-permute-start.22 = (bf16[192,768]{1,0:T(8,128)(2,1)S(1)}, bf16[192,768]{1,0:T(8,128)(2,1)S(1)}, u32[]{:S(2)}, u32[]{:S(2)}) collective-permute-start(bf16[192,768]{1,0:T(8,128)(2,1)S(1)} %copy-done.23), channel_id=1, source_target_pairs={{0,3},{1,2},{2,1},{3,0},{4,7},{5,6},{6,5},{7,4},{8,11},{9,10},{10,... | collective-permute-start | bytes 884744 | tf_op jit(solution)/shard_map/ppermute | solution.py:587
  86.3 17.7 %collective-permute-start.23 = (bf16[192,768]{1,0:T(8,128)(2,1)S(1)}, bf16[192,768]{1,0:T(8,128)(2,1)S(1)}, u32[]{:S(2)}, u32[]{:S(2)}) collective-permute-start(bf16[192,768]{1,0:T(8,128)(2,1)S(1)} %copy-done.22), channel_id=1, source_target_pairs={{0,1},{1,0},{2,3},{3,2},{4,5},{5,4},{6,7},{7,6},{8,9},{9,8},{10,11... | collective-permute-start | bytes 884744 | tf_op jit(solution)/shard_map/ppermute | solution.py:587
  93.3 10.7 %collective-permute-start.20 = (bf16[4,2,3,48,128]{4,3,2,1,0:T(8,128)(2,1)S(1)}, bf16[4,2,3,48,128]{4,3,2,1,0:T(8,128)(2,1)S(1)}, u32[]{:S(2)}, u32[]{:S(2)}) collective-permute-start(bf16[4,2,3,48,128]{4,3,2,1,0:T(8,128)(2,1)S(1)} %get-tuple-element.129), channel_id=1, source_target_pairs={{0,8},{4,12},{8,0},{12,4},{16,24},{20,28},{24,16},{28,20},{1,9},{5... | collective-permute-start | bytes 884744 | tf_op jit(solution)/shard_map/ppermute | solution.py:593
  94.9 9.1 %collective-permute-start.19 = (bf16[4,2,3,48,128]{4,3,2,1,0:T(8,128)(2,1)S(1)}, bf16[4,2,3,48,128]{4,3,2,1,0:T(8,128)(2,1)S(1)}, u32[]{:S(2)}, u32[]{:S(2)}) collective-permute-start(bf16[4,2,3,48,128]{4,3,2,1,0:T(8,128)(2,1)S(1)} %get-tuple-element.130), channel_id=1, source_target_pairs={{0,16},{4,20},{8,24},{12,28},{16,0},{20,4},{24,8},{28,12},{1,17},{... | collective-permute-start | bytes 884744 | tf_op jit(solution)/shard_map/ppermute | solution.py:593
  103.5 0.8 copy-start.8
  103.6 0.8 copy-start.10
  104.0 0.7 copy-start.12
  105.4 18.5 %collective-permute-start.27 = (bf16[4,3,48,128]{3,2,1,0:T(8,128)(2,1)S(1)}, bf16[4,3,48,128]{3,2,1,0:T(8,128)(2,1)S(1)}, u32[]{:S(2)}, u32[]{:S(2)}) collective-permute-start(bf16[4,3,48,128]{3,2,1,0:T(8,128)(2,1)S(1)} %get-tuple-element.119), channel_id=1, source_target_pairs={{0,2},{1,3},{2,0},{3,1},{4,6},{5,7},{6,4},{7,5},{8,10},{9,11},{10,... | collective-permute-start | bytes 442376 | tf_op jit(solution)/shard_map/ppermute | solution.py:587
  112.9 11.9 %collective-permute-start.28 = (bf16[4,3,48,128]{3,2,1,0:T(8,128)(2,1)S(1)}, bf16[4,3,48,128]{3,2,1,0:T(8,128)(2,1)S(1)}, u32[]{:S(2)}, u32[]{:S(2)}) collective-permute-start(bf16[4,3,48,128]{3,2,1,0:T(8,128)(2,1)S(1)} %get-tuple-element.120), channel_id=1, source_target_pairs={{0,3},{1,2},{2,1},{3,0},{4,7},{5,6},{6,5},{7,4},{8,11},{9,10},{10,... | collective-permute-start | bytes 442376 | tf_op jit(solution)/shard_map/ppermute | solution.py:587
  113.4 11.4 %collective-permute-start.29 = (bf16[4,3,48,128]{3,2,1,0:T(8,128)(2,1)S(1)}, bf16[4,3,48,128]{3,2,1,0:T(8,128)(2,1)S(1)}, u32[]{:S(2)}, u32[]{:S(2)}) collective-permute-start(bf16[4,3,48,128]{3,2,1,0:T(8,128)(2,1)S(1)} %get-tuple-element.121), channel_id=1, source_target_pairs={{0,1},{1,0},{2,3},{3,2},{4,5},{5,4},{6,7},{7,6},{8,9},{9,8},{10,11... | collective-permute-start | bytes 442376 | tf_op jit(solution)/shard_map/ppermute | solution.py:587
  120.9 12.3 %collective-permute-start.26 = (bf16[192,384]{1,0:T(8,128)(2,1)}, bf16[192,384]{1,0:T(8,128)(2,1)S(1)}, u32[]{:S(2)}, u32[]{:S(2)}) collective-permute-start(bf16[192,384]{1,0:T(8,128)(2,1)} %get-tuple-element.116), channel_id=1, source_target_pairs={{0,24},{4,28},{8,16},{12,20},{16,8},{20,12},{24,0},{28,4},{1,25},{... | collective-permute-start | bytes 442376 | tf_op jit(solution)/shard_map/ppermute | solution.py:593
  123.4 9.8 %collective-permute-start.25 = (bf16[192,384]{1,0:T(8,128)(2,1)}, bf16[192,384]{1,0:T(8,128)(2,1)S(1)}, u32[]{:S(2)}, u32[]{:S(2)}) collective-permute-start(bf16[192,384]{1,0:T(8,128)(2,1)} %get-tuple-element.116), channel_id=1, source_target_pairs={{0,16},{4,20},{8,24},{12,28},{16,0},{20,4},{24,8},{28,12},{1,17},{... | collective-permute-start | bytes 442376 | tf_op jit(solution)/shard_map/ppermute | solution.py:593
  123.9 0.9 copy-start.19
  123.9 9.3 %collective-permute-start.24 = (bf16[192,384]{1,0:T(8,128)(2,1)}, bf16[192,384]{1,0:T(8,128)(2,1)S(1)}, u32[]{:S(2)}, u32[]{:S(2)}) collective-permute-start(bf16[192,384]{1,0:T(8,128)(2,1)} %get-tuple-element.116), channel_id=1, source_target_pairs={{0,8},{4,12},{8,0},{12,4},{16,24},{20,28},{24,16},{28,20},{1,9},{5... | collective-permute-start | bytes 442376 | tf_op jit(solution)/shard_map/ppermute | solution.py:593
  124.8 0.7 copy-start.20
  124.8 0.7 copy-start.21
  125.5 7.7 %copy-start.18 = (bf16[192,384]{1,0:T(8,128)(2,1)S(1)}, bf16[192,384]{1,0:T(8,128)(2,1)}, u32[]{:S(2)}) copy-start(bf16[192,384]{1,0:T(8,128)(2,1)} %get-tuple-element.116) | copy-start | bytes 442372
  133.3 1.4 %collective-permute-start.30 = (bf16[192,384]{1,0:T(8,128)(2,1)S(1)}, bf16[192,384]{1,0:T(8,128)(2,1)S(1)}, u32[]{:S(2)}, u32[]{:S(2)}) collective-permute-start(bf16[192,384]{1,0:T(8,128)(2,1)S(1)} %add_convert_fusion.6), channel_id=1, source_target_pairs={{0,4},{4,0},{8,12},{12,8},{16,20},{20,16},{24,28},{28,24},{1,5},{5... | collective-permute-start | bytes 442376 | tf_op jit(solution)/shard_map/ppermute | solution.py:593
